TPU v7x, 32 devices: a whole 2x2x4 slice. The times are simulated.
32 devices in a mesh: row: 4 (over y, x), col: 8 (over z, core).
Axes of the slice: x: 2, y: 2, z: 4, core: 2. Of those that a mesh axis runs over, the one named last changes fastest.
Arguments:
- polarization: bfloat16 [4096, 26624], P('row', 'col'), may hold values from -6 to 6
- metric: bfloat16 [26624, 4096], P('row', 'col'), may hold values from -0.0390625 to 0.0390625
- three_panel: bfloat16 [4096, 64, 256], P('row'), may hold values from -0.125 to 0.125
- three_near: bfloat16 [4096, 64, 256], P('col'), may hold values from -0.0078125 to 0.0078125
- green_function: bfloat16 [256, 256], replicated, may hold values from -0.375 to 0.375
- mask_panel: int32 [64, 8], replicated, may hold values 0 or 1
- mask_near: int32 [64, 8], replicated, may hold values 0 or 1
Outputs:
- screened: bfloat16 [4096, 4096], P('row', 'col')
- contracted: bfloat16 [4096, 64, 256], P('col', None, 'row')
- self_energy: float32 [64, 64], P('row', 'col')
All inputs are finite; a program needn't handle non-finite values.
Results may differ from a plain program's by a relative error of at most 0.02.
Values may be sent and summed in bfloat16 or wider, within the bound.
No kernel may reach another device: no remote copies, remote signals or barrier semaphores. Data moves between devices by JAX's collectives and lax.ppermute only.
A program may use at most 320 MiB of HBM per device.

v0:
```python
import jax
import jax.numpy as jnp
from jax import lax
from jax.sharding import PartitionSpec as P

TILE = 64
NL = 256
RB = 64
AB = 32


def expand_mask(mask, rows, cols):
    return jnp.repeat(jnp.repeat(mask, rows, axis=0), cols, axis=1)


def per_device(
    polarization, metric, three_panel, three_near, green_function, mask_panel, mask_near
):
    row_index = lax.axis_index("row")
    col_index = lax.axis_index("col")
    row_count = lax.axis_size("row")
    panel_rows = polarization.shape[0]
    near_cols = metric.shape[1]
    metric_full = lax.all_gather(metric, "row", axis=0, tiled=True)
    screened_sum = jnp.dot(
        lax.all_gather(polarization, "col", axis=1, tiled=True),
        metric_full,
        preferred_element_type=jnp.float32,
    )
    screened = screened_sum.astype(jnp.bfloat16)
    panel_blocks = panel_rows // RB
    panel_mask = lax.dynamic_slice_in_dim(mask_panel, row_index * panel_blocks, panel_blocks, 0)
    panel = three_panel * expand_mask(panel_mask, RB, AB).astype(jnp.bfloat16)[:, None, :]
    near_blocks = near_cols // RB
    near_mask = lax.dynamic_slice_in_dim(mask_near, col_index * near_blocks, near_blocks, 0)
    near = three_near * expand_mask(near_mask, RB, AB).astype(jnp.bfloat16)[:, None, :]
    near_flat = near.reshape(near_cols * TILE, NL)
    contract_part = lax.dot_general(
        screened,
        panel.reshape(panel_rows, TILE * NL),
        (((0,), (0,)), ((), ())),
        preferred_element_type=jnp.float32,
    )
    contract_part = (
        contract_part.astype(jnp.bfloat16).astype(jnp.float32).reshape(near_cols, TILE, NL)
    )
    near_share = NL // row_count
    contracted = lax.psum(contract_part.astype(jnp.bfloat16), "row")
    dressed = jnp.dot(near_flat, green_function.T, preferred_element_type=jnp.float32)
    dressed = dressed.astype(jnp.bfloat16).reshape(near_cols, TILE, NL)
    tile_part = -lax.dot_general(
        contracted, dressed, (((0, 2), (0, 2)), ((), ())), preferred_element_type=jnp.float32
    )
    column_share = lax.psum_scatter(tile_part, "col", scatter_dimension=1, tiled=True)
    row_share = TILE // row_count
    self_energy = lax.dynamic_slice_in_dim(column_share, row_index * row_share, row_share, 0)
    contracted_out = lax.dynamic_slice_in_dim(contracted, row_index * near_share, near_share, 2)
    return (screened, contracted_out, self_energy)


def solution(mesh):
    placed = (
        P("row", "col"),
        P("row", "col"),
        P("row", None, None),
        P("col", None, None),
        P(),
        P(),
        P(),
    )
    return jax.shard_map(
        per_device,
        mesh=mesh,
        in_specs=placed,
        out_specs=(P("row", "col"), P("col", None, "row"), P("row", "col")),
        check_vma=False,
    )
```

profile of v0, /device:TPU:0, one launch (start us, length us, event | category | flops | bytes accessed | tf_op | source)
XLA Modules:
  0.0 1180.2 jit_solution(7564020591593893186)
XLA Ops:
  7.2 0.0 copy-start
  7.2 0.0 all-gather.5.cloned.1.call-start
  7.2 0.7 all-gather.5.cloned.1.call-update
  7.9 0.0 all-gather.3.cloned.1.call-start
  8.0 0.7 all-gather.3.cloned.1.call-update
  8.7 0.0 all-reduce.3.cloned.1.call-start
  8.7 0.8 dynamic-slice_convert_fusion.1
  9.5 0.1 broadcast_in_dim.14
  9.6 0.1 convert_element_type.46
  9.7 0.1 broadcast_in_dim.15
  9.7 0.2 copy.16
  9.9 25.8 %broadcast_multiply_fusion = bf16[1024,64,256]{2,1,0:T(8,128)(2,1)} fusion(bf16[1024,64,256]{2,1,0:T(8,128)(2,1)} %param.9, bf16[1024,256]{1,0:T(8,128)(2,1)S(1)} %copy.16), kind=kLoop, calls=%fused_computation.2 | loop fusion | flops 16777216 | bytes 67633152 | tf_op jit(solution)/shard_map/mul | solution.py:33
  35.7 31.0 %copy.19 = bf16[128,8,64,256]{3,1,2,0:T(8,128)(2,1)} copy(bf16[128,8,64,256]{3,2,1,0:T(8,128)(2,1)} %bitcast.25) | data formatting | bytes 67108864
  66.8 190.8 %all-gather.5.cloned.1.call-done = bf16[26624,512]{1,0:T(8,128)(2,1)} async-done(((bf16[6656,512]{1,0:T(8,128)(2,1)}), bf16[26624,512]{1,0:T(8,128)(2,1)}) %all-gather.5.cloned.1.call-update) | async-done | bytes 27262992 | tf_op jit(solution)/shard_map/all_gather | solution.py:24
  257.6 463.1 %all-gather.3.cloned.1.call-done = bf16[1024,26624]{1,0:T(8,128)(2,1)} async-done(((bf16[1024,3328]{1,0:T(8,128)(2,1)}), bf16[1024,26624]{1,0:T(8,128)(2,1)}) %all-gather.3.cloned.1.call-update) | async-done | bytes 54525968 | tf_op jit(solution)/shard_map/all_gather | solution.py:26
  720.7 36.0 %convolution_convert_fusion.2 = bf16[1024,512]{1,0:T(8,128)(2,1)S(1)} fusion(bf16[1024,26624]{1,0:T(8,128)(2,1)} %all-gather.3.cloned.1.call-done, bf16[26624,512]{1,0:T(8,128)(2,1)} %all-gather.5.cloned.1.call-done), kind=kOutput, calls=%fused_computation.4 | convolution fusion | flops 27917811712 | bytes 82837504 | tf_op jit(solution)/shard_map/dot_general | solution.py:25
  756.7 0.0 copy-start.2
  756.7 32.2 %convolution_convert_fusion.1 = bf16[512,16384]{1,0:T(8,128)(2,1)} fusion(bf16[1024,512]{1,0:T(8,128)(2,1)S(1)} %convolution_convert_fusion.2, bf16[1024,16384]{1,0:T(8,128)(2,1)} %bitcast.29), kind=kOutput, calls=%fused_computation.1 | convolution fusion | flops 17188257792 | bytes 51380224 | tf_op jit(solution)/shard_map/dot_general | solution.py:38
  788.9 0.0 copy-done.2
  788.9 15.6 %copy.20 = bf16[64,8,64,256]{3,2,1,0:T(8,128)(2,1)} copy(bf16[64,8,64,256]{3,1,2,0:T(8,128)(2,1)} %bitcast.30) | data formatting | bytes 33554432
  804.5 0.0 copy-start.1
  804.5 0.0 copy-start.3
  804.5 0.0 all-reduce.3.cloned.1.call-update
  804.6 0.6 copy-done.1
  805.2 0.1 dynamic-slice_convert_fusion
  805.3 0.1 broadcast_in_dim.16
  805.4 0.1 convert_element_type.51
  805.5 0.1 copy.17
  805.7 0.0 copy-done.3
  805.7 0.6 dynamic-slice
  806.9 13.6 %broadcast_multiply_fusion.1 = bf16[512,64,256]{2,1,0:T(8,128)(2,1)} fusion(bf16[512,64,256]{2,1,0:T(8,128)(2,1)} %param.10, bf16[512,256]{1,0:T(8,128)(2,1)S(1)} %copy.17), kind=kLoop, calls=%fused_computation.3 | loop fusion | flops 8388608 | bytes 33816576 | tf_op jit(solution)/shard_map/mul | solution.py:36
  820.5 0.0 copy-done
  820.5 12.1 %convolution_convert_fusion = bf16[32768,256]{1,0:T(8,128)(2,1)} fusion(bf16[32768,256]{1,0:T(8,128)(2,1)} %bitcast.27, bf16[256,256]{1,0:T(8,128)(2,1)S(1)} %copy-done), kind=kOutput, calls=%fused_computation | convolution fusion | flops 4303355904 | bytes 33685504 | tf_op jit(solution)/shard_map/dot_general | solution.py:49
  832.7 277.6 %all-reduce.3.cloned.1.call-done = bf16[512,64,256]{2,1,0:T(8,128)(2,1)} async-done(((bf16[512,64,256]{2,1,0:T(8,128)(2,1)}), bf16[512,64,256]{2,1,0:T(8,128)(2,1)}) %all-reduce.3.cloned.1.call-update) | async-done | bytes 16777232 | tf_op jit(solution)/shard_map/psum | solution.py:48
  1110.3 9.4 constant_dynamic-slice_fusion
  1119.7 9.7 copy.18
  1129.4 15.0 %fusion = f32[64,64]{0,1:T(8,128)S(1)} fusion(bf16[512,64,256]{2,1,0:T(8,128)(2,1)} %all-reduce.3.cloned.1.call-done, bf16[512,64,256]{2,1,0:T(8,128)(2,1)} %bitcast.26), kind=kOutput, calls=%fused_computation.6 | convolution fusion | flops 1073745920 | bytes 33570816 | tf_op jit(solution)/shard_map/dot_general | solution.py:51
  1144.5 28.5 %all-reduce = f32[64,64]{0,1:T(8,128)S(1)} all-reduce(f32[64,64]{0,1:T(8,128)S(1)} %fusion), channel_id=2, replica_groups=mesh['row'=4,'col'=8] {'col'}, use_global_device_ids=true, to_apply=%region_1.0.clone | all-reduce | flops 4096 | bytes 32768
  1173.0 0.7 dynamic_slice.15
  (1 shorter events, 0.0 us)
Async XLA Ops:
  7.2 813.4 %copy-start = (bf16[256,256]{1,0:T(8,128)(2,1)S(1)}, bf16[256,256]{1,0:T(8,128)(2,1)}, u32[]{:S(2)}) copy-start(bf16[256,256]{1,0:T(8,128)(2,1)} %param.11) | copy-start | bytes 393220
  7.2 250.4 %all-gather.5.cloned.1.call-start = ((), (), s32[]{:S(2)}) async-start(), calls=%async_computation.1 | async-start | bytes 34078720 | tf_op jit(solution)/shard_map/all_gather | solution.py:24
  7.9 712.7 %all-gather.3.cloned.1.call-start = ((), (), s32[]{:S(2)}) async-start(), calls=%async_computation | async-start | bytes 61341696 | tf_op jit(solution)/shard_map/all_gather | solution.py:26
  8.7 1101.6 %all-reduce.3.cloned.1.call-start = ((), (), s32[]{:S(2)}) async-start(), calls=%async_computation.2 | async-start | bytes 33554432 | tf_op jit(solution)/shard_map/psum | solution.py:48
  756.7 32.3 %copy-start.2 = (bf16[1024,512]{1,0:T(8,128)(2,1)}, bf16[1024,512]{1,0:T(8,128)(2,1)S(1)}, u32[]{:S(2)}) copy-start(bf16[1024,512]{1,0:T(8,128)(2,1)S(1)} %convolution_convert_fusion.2) | copy-start | bytes 3145732
  804.5 0.7 copy-start.1
  804.5 1.1 copy-start.3
Sparse Core Ops, SparseCore 0:
  9.9 247.6 all-gather.4
  259.2 461.4 all-gather.2
  804.7 305.5 all-reduce.2
where the time goes:
time: 1180 us
  waiting for transfers between devices  933 us (79%)
  matrix products  95.4 us (8%)
  local copies, waits for them, and re-layouts  68.5 us (6%)
  other arithmetic  40.2 us (3%)
  blocking collectives  28.5 us (2%)
  between operations  14.5 us (1%)
    all_gather x1, waiting for transfers between devices, per_device(): lax.all_gather(polarization, 'col', axis=1, tiled=True)  463 us
    psum x1, waiting for transfers between devices, per_device(): contracted = lax.psum(contract_part.astype(jnp.bfloat16), 'row')  278 us
    all_gather x1, waiting for transfers between devices, per_device(): metric_full = lax.all_gather(metric, 'row', axis=0, tiled=True)  191 us
    unnamed x12, local copies, waits for them, and re-layouts  57.6 us
    dot_general x1, matrix products, per_device(): jnp.dot(lax.all_gather(polarization, 'col', axis=1, tiled=True), metric_f...  36 us
    dot_general x1, matrix products, per_device(): lax.dot_general(screened, panel.reshape(panel_rows, TILE * NL), (((0,), (...  32.2 us
    unnamed x1, blocking collectives  28.5 us
    mul x1, other arithmetic, per_device(): three_panel * expand_mask(panel_mask, RB, AB).astype(jnp.bfloat16)[:, Non...  25.8 us
  transfers between devices with their start and end apart: 3, of which 3 were waited for; matrix products, arithmetic and copies ran while one was open for 7% of the time, Pallas kernels for 0%

commit v1 on v0

v1 whole, which is shorter than its diff:
```python
import functools

import jax
import jax.numpy as jnp
from jax import lax
from jax.experimental import pallas as pl
from jax.experimental.pallas import tpu as pltpu
from jax.sharding import PartitionSpec as P

CHUNKS = 2
MIB = 1024 * 1024


def swap(value, axis, bit):
    size = lax.axis_size(axis)
    return lax.ppermute(value, axis, [(i, i ^ bit) for i in range(size)])


def bits_below(size):
    found = []
    while size > 1:
        size //= 2
        found.append(size)
    return found


def product_kernel(count, order_ref, *refs):
    out_ref = refs[-1]
    total = jnp.dot(refs[0][...], refs[count][0], preferred_element_type=jnp.float32)
    for e in range(1, count):
        total += jnp.dot(refs[e][...], refs[count + e][0], preferred_element_type=jnp.float32)
    out_ref[...] = total.astype(out_ref.dtype)


def product(pieces, stack, order, dtype):
    count = len(pieces)
    rows, depth = pieces[0].shape
    cols = stack.shape[2]
    block = min(256, rows)

    def stack_map(e, i, order_ref):
        return (order_ref[e], 0, 0)

    in_specs = [pl.BlockSpec((block, depth), lambda i, order_ref: (i, 0)) for _ in range(count)]
    in_specs += [pl.BlockSpec((1, depth, cols), functools.partial(stack_map, e)) for e in range(count)]
    return pl.pallas_call(
        functools.partial(product_kernel, count),
        grid_spec=pltpu.PrefetchScalarGridSpec(
            num_scalar_prefetch=1,
            grid=(rows // block,),
            in_specs=in_specs,
            out_specs=pl.BlockSpec((block, cols), lambda i, order_ref: (i, 0)),
        ),
        out_shape=jax.ShapeDtypeStruct((rows, cols), dtype),
        compiler_params=pltpu.CompilerParams(vmem_limit_bytes=40 * MIB),
        cost_estimate=pl.CostEstimate(
            flops=2 * rows * depth * count * cols,
            bytes_accessed=2 * count * depth * (rows + cols) + 4 * rows * cols,
            transcendentals=0,
        ),
    )(order, *pieces, *([stack] * count))


def per_device(
    polarization, metric, three_panel, three_near, green_function, mask_panel, mask_near
):
    r, c = lax.axis_index("row"), lax.axis_index("col")
    row_count, col_count = lax.axis_size("row"), lax.axis_size("col")
    top_row, top_col = row_count // 2, col_count // 2
    u, v = r // top_row, c // top_col
    r_low, c_low = r % top_row, c % top_col
    panel_rows, depth = polarization.shape
    near_cols = metric.shape[1]
    half = depth // 2
    per_block = metric.shape[0] // depth
    tile, near_l = three_panel.shape[1], three_panel.shape[2]
    share = near_l // row_count
    width = near_cols // CHUNKS
    on_diagonal = u == v

    metric_parts = metric.reshape(per_block, 2, half, near_cols)
    metric_mine = lax.dynamic_index_in_dim(metric_parts, u, 1, keepdims=False)
    metric_other = lax.dynamic_index_in_dim(metric_parts, 1 - u, 1, keepdims=False)
    mine = lax.dynamic_slice_in_dim(polarization, u * half, half, 1)
    other = lax.dynamic_slice_in_dim(polarization, (1 - u) * half, half, 1)

    def gather_low(piece):
        found = {0: piece}
        for bit in bits_below(top_col):
            found.update({e ^ bit: swap(p, "col", bit) for e, p in list(found.items())})
        return [found[e] for e in range(top_col)]

    def metric_chunk(j):
        kept = metric_mine[:, :, j * width : (j + 1) * width]
        arrived = swap(metric_other[:, :, j * width : (j + 1) * width], "row", top_row)
        stay = jnp.where(on_diagonal, kept, arrived)
        leave = jnp.where(on_diagonal, arrived, kept)
        both = jnp.concatenate([stay, swap(leave, "col", top_col)], axis=-1)
        found = {0: both}
        for bit in bits_below(top_row):
            found.update({f ^ bit: swap(p, "row", bit) for f, p in list(found.items())})
        return jnp.concatenate([found[f] for f in range(top_row)], axis=0)

    stacks = [metric_chunk(j) for j in range(CHUNKS)]
    crossed = swap(other, "row", top_row)
    pieces_mine = gather_low(mine)
    pieces_crossed = gather_low(crossed)
    blocks = c_low ^ jnp.arange(top_col, dtype=jnp.int32)
    order = ((blocks // per_block) ^ r_low) * per_block + blocks % per_block

    rb = panel_rows * row_count // mask_panel.shape[0]
    ab = near_l // mask_panel.shape[1]
    row_blocks = panel_rows // rb
    panel_mask = lax.dynamic_slice_in_dim(mask_panel, r * row_blocks, row_blocks, 0)
    panel_mask = jnp.repeat(jnp.repeat(panel_mask, rb, 0), ab, 1).astype(jnp.bfloat16)
    panel = three_panel * panel_mask[:, None, :]
    panel = jnp.transpose(panel, (1, 2, 0))
    shares = [
        lax.dynamic_slice_in_dim(panel, (r ^ e) * share, share, 1).reshape(tile * share, panel_rows)
        for e in range(row_count)
    ]

    near_blocks = near_cols // rb
    near_mask = lax.dynamic_slice_in_dim(mask_near, c * near_blocks, near_blocks, 0)
    near_mask = jnp.repeat(jnp.repeat(near_mask, rb, 0), ab, 1).astype(jnp.bfloat16)
    near = three_near * near_mask[:, None, :]
    green = lax.dynamic_slice_in_dim(green_function, r * share, share, 0)
    dressed = jnp.einsum("qns,ls->nlq", near, green, preferred_element_type=jnp.float32).astype(jnp.bfloat16)

    screened_chunks, contracted_chunks = [], []
    energy = jnp.zeros((tile, tile), jnp.float32)
    for j in range(CHUNKS):
        away = product(pieces_crossed, stacks[j], order, jnp.bfloat16)
        home = product(pieces_mine, stacks[j], order, jnp.float32)
        home = home + swap(away, "row", top_row).astype(jnp.float32)
        arrived = swap(home[:, width:].astype(jnp.bfloat16), "col", top_col)
        screened = (home[:, :width] + arrived.astype(jnp.float32)).astype(jnp.bfloat16)
        screened_chunks.append(screened)

        sums = {}
        for e in reversed(range(row_count)):
            sums[e] = jnp.dot(shares[e], screened, preferred_element_type=jnp.float32).astype(jnp.bfloat16)
        bits = bits_below(row_count)
        bits = bits if j % 2 else bits[::-1]
        for bit in bits:
            gone = [e for e in sums if e & bit]
            arrived = {e ^ bit: swap(sums.pop(e), "row", bit) for e in gone}
            for e, value in arrived.items():
                sums[e] = (sums[e].astype(jnp.float32) + value.astype(jnp.float32)).astype(jnp.bfloat16)
        contracted = sums[0].reshape(tile, share, width)
        contracted_chunks.append(contracted)
        energy = energy - jnp.einsum(
            "mlq,nlq->mn",
            contracted,
            dressed[:, :, j * width : (j + 1) * width],
            preferred_element_type=jnp.float32,
        )

    energy = lax.psum(energy, ("row", "col"))
    rows, cols = tile // row_count, tile // col_count
    energy = lax.dynamic_slice(energy, (r * rows, c * cols), (rows, cols))
    contracted = jnp.transpose(jnp.concatenate(contracted_chunks, axis=2), (2, 0, 1))
    return jnp.concatenate(screened_chunks, axis=1), contracted, energy


def solution(mesh):
    placed = (
        P("row", "col"),
        P("row", "col"),
        P("row", None, None),
        P("col", None, None),
        P(),
        P(),
        P(),
    )
    return jax.shard_map(
        per_device,
        mesh=mesh,
        in_specs=placed,
        out_specs=(P("row", "col"), P("col", None, "row"), P("row", "col")),
        check_vma=False,
    )
```

time: 1180 us -> 668 us (0.57)
  waiting for transfers between devices: 933 us -> 322 us
  Pallas kernels: 0 us -> 51.6 us
  matrix products: 95.4 us -> 57 us
  other arithmetic: 40.2 us -> 67.7 us
  starting transfers between devices: 0.11 us -> 26.8 us
  local copies, waits for them, and re-layouts: 68.5 us -> 91.1 us
  between operations: 14.5 us -> 1.46 us
    all_gather x2 -> x0, waiting for transfers between devices: 654 us -> none  [the longest x1 463 us: per_device(): lax.all_gather(polarization, 'col', axis=1, tiled=True)]
    ppermute x0 -> x23, waiting for transfers between devices: none -> 322 us  [swap(): return lax.ppermute(value, axis, [(i, i ^ bit) for i in range(size)])]
    psum x1 -> x0, waiting for transfers between devices: 278 us -> none  [per_device(): contracted = lax.psum(contract_part.astype(jnp.bfloat16), 'row')]
    pallas_call x0 -> x4, Pallas kernels: none -> 51.6 us  [product(): pl.pallas_call(functools.partial(product_kernel, count), grid_spec=pltpu....]
    psum x0 -> x1, blocking collectives: none -> 39.8 us  [per_device(): energy = lax.psum(energy, ('row', 'col'))]
    dot_general x4 -> x11, matrix products: 95.4 us -> 57 us  [the longest x8 30.4 us: per_device(): jnp.dot(shares[e], screened, preferred_element_type=jnp.float32)]
    unnamed x1 -> x0, blocking collectives: 28.5 us -> none
    ppermute x0 -> x23, starting transfers between devices: none -> 26.8 us  [swap(): return lax.ppermute(value, axis, [(i, i ^ bit) for i in range(size)])]
  transfers between devices with their start and end apart: 3 -> 23, of which waited for: 3 -> 12; matrix products, arithmetic and copies ran while one was open for 7% -> 29% of each run, Pallas kernels for 0% -> 8%
where the time goes in v1:
time: 668 us; the launch traced here: 658 us
  waiting for transfers between devices  322 us (48%)
  local copies, waits for them, and re-layouts  91.1 us (14%)
  other arithmetic  67.7 us (10%)
  matrix products  57 us (9%)
  Pallas kernels  51.6 us (8%)
  blocking collectives  39.8 us (6%)
  starting transfers between devices  26.8 us (4%)
    ppermute x23, waiting for transfers between devices, swap(): return lax.ppermute(value, axis, [(i, i ^ bit) for i in range(size)])  322 us
    pallas_call x4, Pallas kernels, product(): pl.pallas_call(functools.partial(product_kernel, count), grid_spec=pltpu....  51.6 us
    unnamed x35, local copies, waits for them, and re-layouts  48.3 us
    psum x1, blocking collectives, per_device(): energy = lax.psum(energy, ('row', 'col'))  39.8 us
    dot_general x8, matrix products, per_device(): jnp.dot(shares[e], screened, preferred_element_type=jnp.float32)  30.4 us
    ppermute x23, starting transfers between devices, swap(): return lax.ppermute(value, axis, [(i, i ^ bit) for i in range(size)])  26.8 us
    mul x1, other arithmetic, per_device(): panel = three_panel * panel_mask[:, None, :]  23.4 us
    another operation x1, local copies, waits for them, and re-layouts  22.9 us
  transfers between devices with their start and end apart: 23, of which 12 were waited for; matrix products, arithmetic and copies ran while one was open for 29% of the time, Pallas kernels for 8%

profile of v1, /device:TPU:0, one launch (start us, length us, event | category | flops | bytes accessed | tf_op | source)
XLA Modules:
  0.0 658.0 jit_solution(14349156719067047436)
XLA Ops:
  0.7 5.2 dynamic-slice_bitcast_fusion.1
  5.9 2.0 fusion.55
  7.8 3.0 collective-permute-start.3
  10.8 5.2 constant_dynamic-slice_fusion.4
  16.1 2.0 collective-permute-start.6
  18.1 31.1 %collective-permute-done.3 = bf16[2,1664,256]{2,1,0:T(8,128)(2,1)} collective-permute-done((bf16[2,1664,256]{2,1,0:T(8,128)(2,1)}, bf16[2,1664,256]{2,1,0:T(8,128)(2,1)}, u32[]{:S(2)}, u32[]{:S(2)}) %collective-permute-start.3) | collective-permute-done | bytes 1703968 | tf_op jit(solution)/shard_map/ppermute | solution.py:16
  49.2 36.5 %collective-permute-done.12 = bf16[2,1664,256]{2,1,0:T(8,128)(2,1)} collective-permute-done((bf16[2,1664,256]{2,1,0:T(8,128)(2,1)}, bf16[2,1664,256]{2,1,0:T(8,128)(2,1)}, u32[]{:S(2)}, u32[]{:S(2)}) %collective-permute-start.12) | collective-permute-done | bytes 1703968 | tf_op jit(solution)/shard_map/ppermute | solution.py:16
  85.7 6.0 broadcast_select_fusion.3
  91.7 3.1 collective-permute-start.13
  94.8 1.6 collective-permute-start.1
  96.4 45.2 %copy.21 = bf16[1024,64,256]{0,2,1:T(8,128)(2,1)} copy(bf16[1024,64,256]{2,1,0:T(8,128)(2,1)} %param.9) | data formatting | bytes 67108864 | tf_op args[2]
  141.6 0.7 broadcast_in_dim.17
  142.3 0.9 convert_element_type.141
  143.6 24.6 %collective-permute-done.13 = bf16[2,1664,256]{2,1,0:T(8,128)(2,1)} collective-permute-done((bf16[2,1664,256]{2,1,0:T(8,128)(2,1)}, bf16[2,1664,256]{2,1,0:T(8,128)(2,1)}, u32[]{:S(2)}, u32[]{:S(2)}) %collective-permute-start.13) | collective-permute-done | bytes 1703968 | tf_op jit(solution)/shard_map/ppermute | solution.py:16
  168.2 4.0 pad_maximum_fusion.3
  172.2 1.5 collective-permute-start.14
  173.7 0.9 broadcast_in_dim.18
  174.5 23.4 %broadcast_multiply_fusion = bf16[1024,64,256]{0,2,1:T(8,128)(2,1)} fusion(bf16[1024,64,256]{0,2,1:T(8,128)(2,1)} %copy.21, bf16[1024,256]{0,1:T(8,128)(2,1)} %bitcast.77), kind=kLoop, calls=%fused_computation.2 | loop fusion | flops 16777216 | bytes 67633152 | tf_op jit(solution)/shard_map/mul | solution.py:116
  198.1 0.7 convert_element_type.170
  198.8 1.4 broadcast_in_dim.21
  200.2 1.8 copy.22
  202.0 40.4 %collective-permute-done.4 = bf16[2,1664,256]{2,1,0:T(8,128)(2,1)} collective-permute-done((bf16[2,1664,256]{2,1,0:T(8,128)(2,1)}, bf16[2,1664,256]{2,1,0:T(8,128)(2,1)}, u32[]{:S(2)}, u32[]{:S(2)}) %collective-permute-start.4) | collective-permute-done | bytes 1703968 | tf_op jit(solution)/shard_map/ppermute | solution.py:16
  242.3 4.0 pad_maximum_fusion.2
  246.3 1.5 collective-permute-start.5
  247.8 65.3 %collective-permute-done.8.refs_2_ = bf16[1024,1664]{1,0:T(8,128)(2,1)} collective-permute-done((bf16[1024,1664]{1,0:T(8,128)(2,1)}, bf16[1024,1664]{1,0:T(8,128)(2,1)}, u32[]{:S(2)}, u32[]{:S(2)}) %collective-permute-start.8) | collective-permute-done | bytes 3407904 | tf_op jit(solution)/shard_map/ppermute | solution.py:16
  313.1 13.8 %broadcast_multiply_fusion.1 = bf16[512,64,256]{2,1,0:T(8,128)(2,1)} fusion(bf16[512,64,256]{2,1,0:T(8,128)(2,1)} %param.10, bf16[512,256]{1,0:T(8,128)(2,1)S(1)} %copy-done.6), kind=kLoop, calls=%fused_computation.3 | loop fusion | flops 8388608 | bytes 33816576 | tf_op jit(solution)/shard_map/mul | solution.py:126
  327.6 22.9 %constant_dynamic-slice_fusion.1 = (bf16[1024,64,64]{0,2,1:T(8,128)(2,1)}, bf16[1024,64,64]{0,2,1:T(8,128)(2,1)}, bf16[1024,64,64]{0,2,1:T(8,128)(2,1)}, bf16[1024,64,64]{0,2,1:T(8,128)(2,1)}) fusion(bf16[1024,64,256]{0,2,1:T(8,128)(2,1)} %broadcast_multiply_fusion, s32[]{:T(128)S(6)} %select_n.101, s32[]{:T(128)S(6)} %select_n.102, s32[]{:T(128)S(6)} %select_n.100, ...), kind=kLoop, calls=%fused_computation.67 | loop fusion | bytes 67108880 | tf_op jit(solution)/shard_map/dynamic-slice.2
  350.6 6.0 pad_maximum_fusion.1.refs_4_.refs_5_.refs_6_.refs_7_
  356.5 5.8 pad_maximum_fusion.refs_4_.refs_5_.refs_6_.refs_7_
  362.4 13.2 %shard_map.97 = bf16[1024,512]{1,0:T(8,128)(2,1)S(1)} custom-call(s32[4]{0:T(128)S(1)} %fusion.53.order_ref, bf16[1024,1664]{1,0:T(8,128)(2,1)} %collective-permute-done.6.refs_0_, bf16[1024,1664]{1,0:T(8,128)(2,1)} %collective-permute-done.7.refs_1_, bf16[1024,1664]{1,0:T(8,128)(2,1)} %collective-permute-done.8.refs_2_, ...), custom_call_target="tpu_custom_call" | custom-call | flops 6979321856 | bytes 22544384 | tf_op jit(solution)/shard_map/pallas_call | solution.py:46
  375.5 1.5 collective-permute-start.15
  377.0 13.2 %shard_map.95 = bf16[1024,512]{1,0:T(8,128)(2,1)S(1)} custom-call(s32[4]{0:T(128)S(1)} %fusion.53.order_ref, bf16[1024,1664]{1,0:T(8,128)(2,1)} %collective-permute-done.6.refs_0_, bf16[1024,1664]{1,0:T(8,128)(2,1)} %collective-permute-done.7.refs_1_, bf16[1024,1664]{1,0:T(8,128)(2,1)} %collective-permute-done.8.refs_2_, ...), custom_call_target="tpu_custom_call" | custom-call | flops 6979321856 | bytes 22544384 | tf_op jit(solution)/shard_map/pallas_call | solution.py:46
  390.9 1.7 copy-done.3
  392.6 12.4 %shard_map.96 = f32[1024,512]{1,0:T(8,128)S(1)} custom-call(s32[4]{0:T(128)S(1)} %fusion.53.order_ref, bf16[1024,1664]{1,0:T(8,128)(2,1)S(1)} %get-tuple-element.8.refs_0_, bf16[1024,1664]{1,0:T(8,128)(2,1)S(1)} %collective-permute-done.refs_1_, bf16[1024,1664]{1,0:T(8,128)(2,1)} %collective-permute-done.1.refs_2_, bf16[1024,1664]{1,0:T(8,128)(2,1)} %copy-done.3, ...), custom_call_target="tpu_custom_call" | custom-call | flops 6979321856 | bytes 22544384 | tf_op jit(solution)/shard_map/pallas_call | solution.py:46
  405.5 1.3 copy-done.4
  406.8 1.4 collective-permute-start.16
  408.3 12.9 %shard_map.94 = f32[1024,512]{1,0:T(8,128)S(1)} custom-call(s32[4]{0:T(128)S(1)} %fusion.53.order_ref, bf16[1024,1664]{1,0:T(8,128)(2,1)S(1)} %get-tuple-element.8.refs_0_, bf16[1024,1664]{1,0:T(8,128)(2,1)S(1)} %collective-permute-done.refs_1_, bf16[1024,1664]{1,0:T(8,128)(2,1)} %collective-permute-done.1.refs_2_, bf16[1024,1664]{1,0:T(8,128)(2,1)} %copy-done.3, ...), custom_call_target="tpu_custom_call" | custom-call | flops 6979321856 | bytes 22544384 | tf_op jit(solution)/shard_map/pallas_call | solution.py:46
  421.2 2.4 collective-permute-done.10
  424.0 1.5 collective-permute-start.11
  425.5 19.5 %collective-permute-done.16 = bf16[1024,256]{1,0:T(8,128)(2,1)S(1)} collective-permute-done((bf16[1024,256]{1,0:T(8,128)(2,1)S(1)}, bf16[1024,256]{1,0:T(8,128)(2,1)S(1)}, u32[]{:S(2)}, u32[]{:S(2)}) %collective-permute-start.16) | collective-permute-done | bytes 524320 | tf_op jit(solution)/shard_map/ppermute | solution.py:16
  445.2 2.4 convolution_convert_fusion
  447.7 1.5 collective-permute-start.21
  449.2 6.0 collective-permute-done.11
  455.3 2.4 convolution_convert_fusion.4
  457.8 1.5 collective-permute-start.18
  459.2 3.9 convolution_convert_fusion.2
  463.1 1.5 collective-permute-start.20
  464.7 2.4 convolution_convert_fusion.6
  467.7 28.6 %collective-permute-done.21 = bf16[4096,256]{1,0:T(8,128)(2,1)S(1)} collective-permute-done((bf16[4096,256]{1,0:T(8,128)(2,1)S(1)}, bf16[4096,256]{1,0:T(8,128)(2,1)S(1)}, u32[]{:S(2)}, u32[]{:S(2)}) %collective-permute-start.21) | collective-permute-done | bytes 2097184 | tf_op jit(solution)/shard_map/ppermute | solution.py:16
  496.3 4.0 fusion.19
  500.3 1.4 collective-permute-start.22
  501.7 4.7 collective-permute-done.18
  506.4 4.1 fusion.14
  510.5 1.4 collective-permute-start.19
  511.9 17.6 %convert_bitcast_fusion = bf16[64,64,512]{2,1,0:T(8,128)(2,1)S(1)} fusion(bf16[512,64,256]{2,1,0:T(8,128)(2,1)} %broadcast_multiply_fusion.1, bf16[256,256]{1,0:T(8,128)(2,1)S(1)} %copy-done, s32[]{:T(128)S(6)} %select_n.99), kind=kOutput, calls=%fused_computation.33 | convolution fusion | flops 1075838976 | bytes 21004292 | tf_op jit(solution)/shard_map/qns,ls->nlq/dot_general | solution.py:128
  529.9 1.1 pad_maximum_fusion.4
  530.9 10.3 %collective-permute-done.20 = bf16[4096,256]{1,0:T(8,128)(2,1)S(1)} collective-permute-done((bf16[4096,256]{1,0:T(8,128)(2,1)}, bf16[4096,256]{1,0:T(8,128)(2,1)S(1)}, u32[]{:S(2)}, u32[]{:S(2)}) %collective-permute-start.20) | collective-permute-done | bytes 2097184 | tf_op jit(solution)/shard_map/ppermute | solution.py:16
  541.2 53.1 %collective-permute-done.22 = bf16[4096,256]{1,0:T(8,128)(2,1)} collective-permute-done((bf16[4096,256]{1,0:T(8,128)(2,1)}, bf16[4096,256]{1,0:T(8,128)(2,1)}, u32[]{:S(2)}, u32[]{:S(2)}) %collective-permute-start.22) | collective-permute-done | bytes 2097184 | tf_op jit(solution)/shard_map/ppermute | solution.py:16
  594.4 6.6 %fusion.18 = bf16[4096,256]{1,0:T(8,128)(2,1)S(1)} fusion(bf16[4096,1024]{1,0:T(8,128)(2,1)} %bitcast.60, bf16[1024,256]{1,0:T(8,128)(2,1)S(1)} %fusion.48, bf16[4096,256]{1,0:T(8,128)(2,1)} %collective-permute-done.22, bf16[4096,256]{1,0:T(8,128)(2,1)S(1)} %collective-permute-done.20), kind=kOutput, calls=%fused_computation.30 | convolution fusion | flops 2156920832 | bytes 15204352 | tf_op jit(solution)/shard_map/dot_general | solution.py:142
  601.1 4.4 fusion.13
  605.5 2.4 maximum_bitcast_fusion
  607.9 4.4 fusion.43
  612.4 4.7 fusion.38
  617.1 39.8 %psum.7 = f32[64,64]{0,1:T(8,128)S(1)} all-reduce(f32[64,64]{0,1:T(8,128)S(1)} %fusion.38), channel_id=1, replica_groups=mesh['row'=4,'col'=8] {'row','col'}, use_global_device_ids=true, to_apply=%region_0.1 | all-reduce | flops 4096 | bytes 32768 | tf_op jit(solution)/shard_map/psum | solution.py:159
  (68 shorter events, 4.9 us)
Async XLA Ops:
  0.6 511.3 %copy-start = (bf16[256,256]{1,0:T(8,128)(2,1)S(1)}, bf16[256,256]{1,0:T(8,128)(2,1)}, u32[]{:S(2)}) copy-start(bf16[256,256]{1,0:T(8,128)(2,1)} %param.11) | copy-start | bytes 393220
  7.8 41.3 %collective-permute-start.3 = (bf16[2,1664,256]{2,1,0:T(8,128)(2,1)}, bf16[2,1664,256]{2,1,0:T(8,128)(2,1)}, u32[]{:S(2)}, u32[]{:S(2)}) collective-permute-start(bf16[2,1664,256]{2,1,0:T(8,128)(2,1)} %get-tuple-element.19), channel_id=1, source_target_pairs={{0,16},{8,24},{16,0},{24,8},{1,17},{9,25},{17,1},{25,9},{2,18},{10... | collective-permute-start | bytes 5111816 | tf_op jit(solution)/shard_map/ppermute | solution.py:16
  10.8 74.9 %collective-permute-start.12 = (bf16[2,1664,256]{2,1,0:T(8,128)(2,1)}, bf16[2,1664,256]{2,1,0:T(8,128)(2,1)}, u32[]{:S(2)}, u32[]{:S(2)}) collective-permute-start(bf16[2,1664,256]{2,1,0:T(8,128)(2,1)} %get-tuple-element.20), channel_id=1, source_target_pairs={{0,16},{8,24},{16,0},{24,8},{1,17},{9,25},{17,1},{25,9},{2,18},{10... | collective-permute-start | bytes 5111816 | tf_op jit(solution)/shard_map/ppermute | solution.py:16
  16.1 157.6 %collective-permute-start.6 = (bf16[1024,1664]{1,0:T(8,128)(2,1)}, bf16[1024,1664]{1,0:T(8,128)(2,1)}, u32[]{:S(2)}, u32[]{:S(2)}) collective-permute-start(bf16[1024,1664]{1,0:T(8,128)(2,1)} %get-tuple-element.7), channel_id=1, source_target_pairs={{0,16},{8,24},{16,0},{24,8},{1,17},{9,25},{17,1},{25,9},{2,18},{10... | collective-permute-start | bytes 10223624 | tf_op jit(solution)/shard_map/ppermute | solution.py:16
  91.7 76.5 %collective-permute-start.13 = (bf16[2,1664,256]{2,1,0:T(8,128)(2,1)}, bf16[2,1664,256]{2,1,0:T(8,128)(2,1)}, u32[]{:S(2)}, u32[]{:S(2)}) collective-permute-start(bf16[2,1664,256]{2,1,0:T(8,128)(2,1)} %get-tuple-element.17), channel_id=1, source_target_pairs={{0,4},{1,5},{2,6},{3,7},{4,0},{5,1},{6,2},{7,3},{8,12},{9,13},{10,... | collective-permute-start | bytes 5111816 | tf_op jit(solution)/shard_map/ppermute | solution.py:16
  94.8 46.7 %copy-start.7 = (s32[64,8]{0,1:T(8,128)S(1)}, s32[64,8]{0,1:T(8,128)}, u32[]{:S(2)}) copy-start(s32[64,8]{0,1:T(8,128)} %param.12) | copy-start | bytes 6148
  94.8 232.2 %collective-permute-start.1 = (bf16[1024,1664]{1,0:T(8,128)(2,1)S(1)}, bf16[1024,1664]{1,0:T(8,128)(2,1)}, u32[]{:S(2)}, u32[]{:S(2)}) collective-permute-start(bf16[1024,1664]{1,0:T(8,128)(2,1)S(1)} %get-tuple-element.8.refs_0_), channel_id=1, source_target_pairs={{0,2},{1,3},{2,0},{3,1},{4,6},{5,7},{6,4},{7,5},{8,10},{9,11},{10,... | collective-permute-start | bytes 10223624 | tf_op jit(solution)/shard_map/ppermute | solution.py:16
  143.2 99.2 %collective-permute-start.4 = (bf16[2,1664,256]{2,1,0:T(8,128)(2,1)}, bf16[2,1664,256]{2,1,0:T(8,128)(2,1)}, u32[]{:S(2)}, u32[]{:S(2)}) collective-permute-start(bf16[2,1664,256]{2,1,0:T(8,128)(2,1)} %get-tuple-element.12), channel_id=1, source_target_pairs={{0,4},{1,5},{2,6},{3,7},{4,0},{5,1},{6,2},{7,3},{8,12},{9,13},{10,... | collective-permute-start | bytes 5111816 | tf_op jit(solution)/shard_map/ppermute | solution.py:16
  172.2 155.4 %collective-permute-start.14 = (bf16[2,1664,512]{2,1,0:T(8,128)(2,1)}, bf16[2,1664,512]{2,1,0:T(8,128)(2,1)}, u32[]{:S(2)}, u32[]{:S(2)}) collective-permute-start(bf16[2,1664,512]{2,1,0:T(8,128)(2,1)} %pad_maximum_fusion.3), channel_id=1, source_target_pairs={{0,8},{8,0},{16,24},{24,16},{1,9},{9,1},{17,25},{25,17},{2,10},{10... | collective-permute-start | bytes 10223624 | tf_op jit(solution)/shard_map/ppermute | solution.py:16
  173.7 139.5 %collective-permute-start.8 = (bf16[1024,1664]{1,0:T(8,128)(2,1)}, bf16[1024,1664]{1,0:T(8,128)(2,1)}, u32[]{:S(2)}, u32[]{:S(2)}) collective-permute-start(bf16[1024,1664]{1,0:T(8,128)(2,1)} %collective-permute-done.6.refs_0_), channel_id=1, source_target_pairs={{0,2},{1,3},{2,0},{3,1},{4,6},{5,7},{6,4},{7,5},{8,10},{9,11},{10,... | collective-permute-start | bytes 10223624 | tf_op jit(solution)/shard_map/ppermute | solution.py:16
  174.5 23.4 %copy-start.8 = (s32[64,8]{0,1:T(8,128)S(1)}, s32[64,8]{0,1:T(8,128)}, u32[]{:S(2)}) copy-start(s32[64,8]{0,1:T(8,128)} %param.13) | copy-start | bytes 6148
  242.3 70.8 %copy-start.6 = (bf16[512,256]{1,0:T(8,128)(2,1)S(1)}, bf16[512,256]{1,0:T(8,128)(2,1)}, u32[]{:S(2)}) copy-start(bf16[512,256]{1,0:T(8,128)(2,1)} %copy.22) | copy-start | bytes 786436
  246.3 110.2 %collective-permute-start.5 = (bf16[2,1664,512]{2,1,0:T(8,128)(2,1)}, bf16[2,1664,512]{2,1,0:T(8,128)(2,1)}, u32[]{:S(2)}, u32[]{:S(2)}) collective-permute-start(bf16[2,1664,512]{2,1,0:T(8,128)(2,1)} %pad_maximum_fusion.2), channel_id=1, source_target_pairs={{0,8},{8,0},{16,24},{24,16},{1,9},{9,1},{17,25},{25,17},{2,10},{10... | collective-permute-start | bytes 10223624 | tf_op jit(solution)/shard_map/ppermute | solution.py:16
  247.8 114.5 %collective-permute-start.7 = (bf16[1024,1664]{1,0:T(8,128)(2,1)}, bf16[1024,1664]{1,0:T(8,128)(2,1)}, u32[]{:S(2)}, u32[]{:S(2)}) collective-permute-start(bf16[1024,1664]{1,0:T(8,128)(2,1)} %collective-permute-done.6.refs_0_), channel_id=1, source_target_pairs={{0,1},{1,0},{2,3},{3,2},{4,5},{5,4},{6,7},{7,6},{8,9},{9,8},{10,11... | collective-permute-start | bytes 10223624 | tf_op jit(solution)/shard_map/ppermute | solution.py:16
  313.1 49.2 %collective-permute-start.9 = (bf16[1024,1664]{1,0:T(8,128)(2,1)}, bf16[1024,1664]{1,0:T(8,128)(2,1)}, u32[]{:S(2)}, u32[]{:S(2)}) collective-permute-start(bf16[1024,1664]{1,0:T(8,128)(2,1)} %collective-permute-done.8.refs_2_), channel_id=1, source_target_pairs={{0,1},{1,0},{2,3},{3,2},{4,5},{5,4},{6,7},{7,6},{8,9},{9,8},{10,11... | collective-permute-start | bytes 10223624 | tf_op jit(solution)/shard_map/ppermute | solution.py:16
  326.9 23.6 %copy-start.2 = (bf16[2,1664,256]{2,1,0:T(8,128)(2,1)S(1)}, bf16[2,1664,256]{2,1,0:T(8,128)(2,1)}, u32[]{:S(2)}) copy-start(bf16[2,1664,256]{2,1,0:T(8,128)(2,1)} %get-tuple-element.18) | copy-start | bytes 5111812
  327.0 63.9 %collective-permute-start = (bf16[1024,1664]{1,0:T(8,128)(2,1)S(1)}, bf16[1024,1664]{1,0:T(8,128)(2,1)S(1)}, u32[]{:S(2)}, u32[]{:S(2)}) collective-permute-start(bf16[1024,1664]{1,0:T(8,128)(2,1)S(1)} %get-tuple-element.8.refs_0_), channel_id=1, source_target_pairs={{0,1},{1,0},{2,3},{3,2},{4,5},{5,4},{6,7},{7,6},{8,9},{9,8},{10,11... | collective-permute-start | bytes 10223624 | tf_op jit(solution)/shard_map/ppermute | solution.py:16
  327.5 63.3 %collective-permute-start.2 = (bf16[1024,1664]{1,0:T(8,128)(2,1)}, bf16[1024,1664]{1,0:T(8,128)(2,1)S(1)}, u32[]{:S(2)}, u32[]{:S(2)}) collective-permute-start(bf16[1024,1664]{1,0:T(8,128)(2,1)} %collective-permute-done.1.refs_2_), channel_id=1, source_target_pairs={{0,1},{1,0},{2,3},{3,2},{4,5},{5,4},{6,7},{7,6},{8,9},{9,8},{10,11... | collective-permute-start | bytes 10223624 | tf_op jit(solution)/shard_map/ppermute | solution.py:16
  350.6 6.0 copy-start.1
  375.5 29.5 %collective-permute-start.15 = (bf16[1024,512]{1,0:T(8,128)(2,1)S(1)}, bf16[1024,512]{1,0:T(8,128)(2,1)S(1)}, u32[]{:S(2)}, u32[]{:S(2)}) collective-permute-start(bf16[1024,512]{1,0:T(8,128)(2,1)S(1)} %shard_map.97), channel_id=1, source_target_pairs={{0,16},{8,24},{16,0},{24,8},{1,17},{9,25},{17,1},{25,9},{2,18},{10... | collective-permute-start | bytes 3145736 | tf_op jit(solution)/shard_map/ppermute | solution.py:16
  390.2 33.4 %collective-permute-start.10 = (bf16[1024,512]{1,0:T(8,128)(2,1)S(1)}, bf16[1024,512]{1,0:T(8,128)(2,1)S(1)}, u32[]{:S(2)}, u32[]{:S(2)}) collective-permute-start(bf16[1024,512]{1,0:T(8,128)(2,1)S(1)} %shard_map.95), channel_id=1, source_target_pairs={{0,16},{8,24},{16,0},{24,8},{1,17},{9,25},{17,1},{25,9},{2,18},{10... | collective-permute-start | bytes 3145736 | tf_op jit(solution)/shard_map/ppermute | solution.py:16
  390.9 1.8 copy-start.3
  405.1 40.1 %slice-start.6 = ((s8[8388608]{0:T(1024)(128)(4,1)}), s8[4194304]{0:T(1024)(128)(4,1)S(1)}, s32[]{:S(2)}) async-start(s8[8388608]{0:T(1024)(128)(4,1)} %bitcast.72), calls=%async_computation.6 | async-start | bytes 8388608
  405.5 1.4 copy-start.4
  406.8 38.4 %slice-start.7 = ((s8[8388608]{0:T(1024)(128)(4,1)}), s8[4194304]{0:T(1024)(128)(4,1)S(1)}, s32[]{:S(2)}) async-start(s8[8388608]{0:T(1024)(128)(4,1)} %bitcast.72), calls=%async_computation.7 | async-start | bytes 8388608
  406.8 38.2 %collective-permute-start.16 = (bf16[1024,256]{1,0:T(8,128)(2,1)S(1)}, bf16[1024,256]{1,0:T(8,128)(2,1)S(1)}, u32[]{:S(2)}, u32[]{:S(2)}) collective-permute-start(bf16[1024,256]{1,0:T(8,128)(2,1)S(1)} %slice.64), channel_id=1, source_target_pairs={{0,4},{1,5},{2,6},{3,7},{4,0},{5,1},{6,2},{7,3},{8,12},{9,13},{10,... | collective-permute-start | bytes 1572872 | tf_op jit(solution)/shard_map/ppermute | solution.py:16
  421.2 23.8 %copy-start.5 = (f32[1024,512]{1,0:T(8,128)S(1)}, f32[1024,512]{1,0:T(8,128)}, u32[]{:S(2)}) copy-start(f32[1024,512]{1,0:T(8,128)} %copy-done.4) | copy-start | bytes 6291460
  424.0 31.2 %collective-permute-start.11 = (bf16[1024,256]{1,0:T(8,128)(2,1)S(1)}, bf16[1024,256]{1,0:T(8,128)(2,1)S(1)}, u32[]{:S(2)}, u32[]{:S(2)}) collective-permute-start(bf16[1024,256]{1,0:T(8,128)(2,1)S(1)} %slice.65), channel_id=1, source_target_pairs={{0,4},{1,5},{2,6},{3,7},{4,0},{5,1},{6,2},{7,3},{8,12},{9,13},{10,... | collective-permute-start | bytes 1572872 | tf_op jit(solution)/shard_map/ppermute | solution.py:16
  445.2 14.0 %slice-start.2 = ((s8[8388608]{0:T(1024)(128)(4,1)}), s8[4194304]{0:T(1024)(128)(4,1)S(1)}, s32[]{:S(2)}) async-start(s8[8388608]{0:T(1024)(128)(4,1)} %bitcast.64), calls=%async_computation.2 | async-start | bytes 8388608
  447.7 11.6 %slice-start.3 = ((s8[8388608]{0:T(1024)(128)(4,1)}), s8[4194304]{0:T(1024)(128)(4,1)S(1)}, s32[]{:S(2)}) async-start(s8[8388608]{0:T(1024)(128)(4,1)} %bitcast.64), calls=%async_computation.3 | async-start | bytes 8388608
  447.7 48.6 %collective-permute-start.21 = (bf16[4096,256]{1,0:T(8,128)(2,1)S(1)}, bf16[4096,256]{1,0:T(8,128)(2,1)S(1)}, u32[]{:S(2)}, u32[]{:S(2)}) collective-permute-start(bf16[4096,256]{1,0:T(8,128)(2,1)S(1)} %convolution_convert_fusion), channel_id=1, source_target_pairs={{0,16},{8,24},{16,0},{24,8},{1,17},{9,25},{17,1},{25,9},{2,18},{10... | collective-permute-start | bytes 6291464 | tf_op jit(solution)/shard_map/ppermute | solution.py:16
  455.3 9.3 %slice-start.4 = ((s8[8388608]{0:T(1024)(128)(4,1)}), s8[4194304]{0:T(1024)(128)(4,1)S(1)}, s32[]{:S(2)}) async-start(s8[8388608]{0:T(1024)(128)(4,1)} %bitcast.68), calls=%async_computation.4 | async-start | bytes 8388608
  457.8 48.6 %collective-permute-start.18 = (bf16[4096,256]{1,0:T(8,128)(2,1)S(1)}, bf16[4096,256]{1,0:T(8,128)(2,1)S(1)}, u32[]{:S(2)}, u32[]{:S(2)}) collective-permute-start(bf16[4096,256]{1,0:T(8,128)(2,1)S(1)} %convolution_convert_fusion.4), channel_id=1, source_target_pairs={{0,8},{8,0},{16,24},{24,16},{1,9},{9,1},{17,25},{25,17},{2,10},{10... | collective-permute-start | bytes 6291464 | tf_op jit(solution)/shard_map/ppermute | solution.py:16
  459.2 5.4 slice-start.5
  463.1 78.1 %collective-permute-start.20 = (bf16[4096,256]{1,0:T(8,128)(2,1)}, bf16[4096,256]{1,0:T(8,128)(2,1)S(1)}, u32[]{:S(2)}, u32[]{:S(2)}) collective-permute-start(bf16[4096,256]{1,0:T(8,128)(2,1)} %convolution_convert_fusion.2), channel_id=1, source_target_pairs={{0,16},{8,24},{16,0},{24,8},{1,17},{9,25},{17,1},{25,9},{2,18},{10... | collective-permute-start | bytes 6291464 | tf_op jit(solution)/shard_map/ppermute | solution.py:16
  467.1 133.9 %collective-permute-start.17 = (bf16[4096,256]{1,0:T(8,128)(2,1)S(1)}, bf16[4096,256]{1,0:T(8,128)(2,1)S(1)}, u32[]{:S(2)}, u32[]{:S(2)}) collective-permute-start(bf16[4096,256]{1,0:T(8,128)(2,1)S(1)} %convolution_convert_fusion.6), channel_id=1, source_target_pairs={{0,8},{8,0},{16,24},{24,16},{1,9},{9,1},{17,25},{25,17},{2,10},{10... | collective-permute-start | bytes 6291464 | tf_op jit(solution)/shard_map/ppermute | solution.py:16
  500.3 94.0 %collective-permute-start.22 = (bf16[4096,256]{1,0:T(8,128)(2,1)}, bf16[4096,256]{1,0:T(8,128)(2,1)}, u32[]{:S(2)}, u32[]{:S(2)}) collective-permute-start(bf16[4096,256]{1,0:T(8,128)(2,1)} %fusion.19), channel_id=1, source_target_pairs={{0,8},{8,0},{16,24},{24,16},{1,9},{9,1},{17,25},{25,17},{2,10},{10... | collective-permute-start | bytes 6291464 | tf_op jit(solution)/shard_map/ppermute | solution.py:16
  510.5 90.6 %collective-permute-start.19 = (bf16[4096,256]{1,0:T(8,128)(2,1)}, bf16[4096,256]{1,0:T(8,128)(2,1)}, u32[]{:S(2)}, u32[]{:S(2)}) collective-permute-start(bf16[4096,256]{1,0:T(8,128)(2,1)} %fusion.14), channel_id=1, source_target_pairs={{0,16},{8,24},{16,0},{24,8},{1,17},{9,25},{17,1},{25,9},{2,18},{10... | collective-permute-start | bytes 6291464 | tf_op jit(solution)/shard_map/ppermute | solution.py:16
  529.5 71.6 %slice-start = ((s8[8388608]{0:T(1024)(128)(4,1)}), s8[4194304]{0:T(1024)(128)(4,1)S(1)}, s32[]{:S(2)}) async-start(s8[8388608]{0:T(1024)(128)(4,1)} %bitcast.61), calls=%async_computation | async-start | bytes 8388608
  594.4 6.7 %slice-start.1 = ((s8[8388608]{0:T(1024)(128)(4,1)}), s8[4194304]{0:T(1024)(128)(4,1)S(1)}, s32[]{:S(2)}) async-start(s8[8388608]{0:T(1024)(128)(4,1)} %bitcast.61), calls=%async_computation.1 | async-start | bytes 8388608

commit v2 on v1

v2 whole, which is shorter than its diff:
```python
import functools

import jax
import jax.numpy as jnp
from jax import lax
from jax.experimental import pallas as pl
from jax.experimental.pallas import tpu as pltpu
from jax.sharding import PartitionSpec as P

WIDTH = 128
PAIR = 2
GROUPS = 4
VMEM = 56
MIB = 1024 * 1024


def swap(value, axis, bit):
    size = lax.axis_size(axis)
    return lax.ppermute(value, axis, [(i, i ^ bit) for i in range(size)])


def after(value, *others):
    return lax.optimization_barrier((value, others))[0]


class Link:
    def __init__(self, in_flight):
        self.past, self.in_flight = [], in_flight

    def swap(self, value, axis, bit):
        if len(self.past) >= self.in_flight:
            value = after(value, self.past[-self.in_flight])
        self.past.append(swap(value, axis, bit))
        return self.past[-1]


def bits_below(size):
    found = []
    while size > 1:
        size //= 2
        found.append(size)
    return found


def product_kernel(count, parts, per_block, order_ref, *refs):
    pieces, sources, out_ref = refs[: count * parts], refs[count * parts : -6], refs[-6]
    held, weights, total, piece_sems, weight_sems = refs[-5:]
    width = sources[0].shape[2]
    sides = weights.shape[2] // width
    blocks = range(len(sources) // sides)

    def load(e, side, block):
        return pltpu.make_async_copy(
            sources[sides * block + side].at[order_ref[e] % per_block],
            weights.at[e, :, pl.ds(side * width, width)],
            weight_sems.at[e, side],
        )

    rows = pieces[0].shape[0]
    copies = [
        pltpu.make_async_copy(piece, held.at[i // parts, pl.ds(i % parts * rows, rows)], piece_sems.at[i])
        for i, piece in enumerate(pieces)
    ]
    for e in range(count):
        for side in range(sides):
            for block in blocks:

                @pl.when(order_ref[e] // per_block == block)
                def _():
                    load(e, side, block).start()

        for copy in copies[e * parts : (e + 1) * parts]:
            copy.start()
    for e in range(count):
        for side in range(sides):
            load(e, side, 0).wait()
        for copy in copies[e * parts : (e + 1) * parts]:
            copy.wait()
        part = jnp.dot(held[e], weights[e], preferred_element_type=jnp.float32)
        if e == 0:
            total[...] = part
        elif e < count - 1:
            total[...] += part
        else:
            out_ref[...] = (total[...] + part).astype(out_ref.dtype)


def product(pieces, sources, order, per_block, dtype):
    count, parts = len(pieces), len(pieces[0])
    rows, depth = pieces[0][0].shape
    rows *= parts
    sides = len(sources[0])
    cols = sides * sources[0][0].shape[2]
    sources = [part for block in sources for part in block]
    in_hbm = pl.BlockSpec(memory_space=pl.ANY)
    return pl.pallas_call(
        functools.partial(product_kernel, count, parts, per_block),
        in_specs=[pl.BlockSpec(memory_space=pltpu.SMEM)] + [in_hbm] * (count * parts + len(sources)),
        out_specs=pl.BlockSpec(memory_space=pltpu.VMEM),
        out_shape=jax.ShapeDtypeStruct((rows, cols), dtype),
        scratch_shapes=[
            pltpu.VMEM((count, rows, depth), jnp.bfloat16),
            pltpu.VMEM((count, depth, cols), jnp.bfloat16),
            pltpu.VMEM((rows, cols), jnp.float32),
            pltpu.SemaphoreType.DMA((count * parts,)),
            pltpu.SemaphoreType.DMA((count, sides)),
        ],
        compiler_params=pltpu.CompilerParams(vmem_limit_bytes=VMEM * MIB),
        cost_estimate=pl.CostEstimate(
            flops=2 * rows * depth * count * cols,
            bytes_accessed=2 * count * depth * (rows + cols) + 4 * rows * cols,
            transcendentals=0,
        ),
    )(order, *[part for piece in pieces for part in piece], *sources)


def turn_kernel(panel_ref, out_ref):
    out_ref[...] = jnp.transpose(panel_ref[...], (1, 2, 0))


def turn(panel, first, rows):
    _, tile, near_l = panel.shape
    tall = tile // GROUPS
    wide = min(rows, 128)
    return pl.pallas_call(
        turn_kernel,
        grid=(rows // wide, tile // tall),
        in_specs=[pl.BlockSpec((wide, tall, near_l), lambda i, g: (first // wide + i, g, 0))],
        out_specs=pl.BlockSpec((tall, near_l, wide), lambda i, g: (g, 0, i)),
        out_shape=jax.ShapeDtypeStruct((tile, near_l, rows), panel.dtype),
        compiler_params=pltpu.CompilerParams(vmem_limit_bytes=VMEM * MIB),
        cost_estimate=pl.CostEstimate(flops=0, bytes_accessed=4 * rows * tile * near_l, transcendentals=0),
    )(panel)


def contract_kernel(rb, ab, places_ref, mask_ref, screened_ref, *refs):
    panels, outs, (held, masked, sems) = refs[:-5], refs[-5:-3], refs[-3:]
    _, tall, share, rows = held.shape
    per_share = masked.shape[1]
    each = rows // len(panels)
    count, half = outs[0].shape[:2]
    steps = [(h, i, g) for h in range(2) for i in range(count) for g in range(half // tall)]

    def load(k):
        h, i, g = steps[k]
        at = pl.ds(pl.multiple_of(places_ref[h, i] * share, share), share)
        return [
            pltpu.make_async_copy(
                panel.at[pl.ds(h * half + g * tall, tall), at, :],
                held.at[k % 2, :, :, pl.ds(n * each, each)],
                sems.at[k % 2, n],
            )
            for n, panel in enumerate(panels)
        ]

    for copy in load(0):
        copy.start()
    for k, (h, i, g) in enumerate(steps):
        if k + 1 < len(steps):
            for copy in load(k + 1):
                copy.start()
        if g == 0:
            for b in range(per_share):
                for n in range(rows // rb):
                    part = screened_ref[pl.ds(n * rb, rb), :]
                    flag = mask_ref[n, places_ref[h, i] * per_share + b]
                    masked[i % 2, b, pl.ds(n * rb, rb), :] = jnp.where(flag != 0, part, jnp.zeros_like(part))
        for copy in load(k):
            copy.wait()
        for b in range(per_share):
            block = held[k % 2, :, pl.ds(b * ab, ab), :].reshape(tall * ab, rows)
            part = jnp.dot(block, masked[i % 2, b], preferred_element_type=jnp.float32)
            outs[h][i, pl.ds(g * tall, tall), pl.ds(b * ab, ab), :] = part.astype(outs[h].dtype).reshape(
                tall, ab, part.shape[1]
            )


def contract(panels, screened, mask, places, rb, ab, share):
    count = places.shape[1]
    tile, rows = panels[0].shape[0], screened.shape[0]
    tall = tile // GROUPS
    width = screened.shape[1]
    in_smem, in_hbm = pl.BlockSpec(memory_space=pltpu.SMEM), pl.BlockSpec(memory_space=pl.ANY)
    in_vmem = pl.BlockSpec(memory_space=pltpu.VMEM)
    return pl.pallas_call(
        functools.partial(contract_kernel, rb, ab),
        in_specs=[in_smem, in_smem, in_vmem] + [in_hbm] * len(panels),
        out_specs=[in_vmem] * 2,
        out_shape=[jax.ShapeDtypeStruct((count, tile // 2, share, width), jnp.bfloat16)] * 2,
        scratch_shapes=[
            pltpu.VMEM((2, tall, share, rows), jnp.bfloat16),
            pltpu.VMEM((2, share // ab, rows, width), jnp.bfloat16),
            pltpu.SemaphoreType.DMA((2, len(panels))),
        ],
        compiler_params=pltpu.CompilerParams(vmem_limit_bytes=VMEM * MIB),
        cost_estimate=pl.CostEstimate(
            flops=2 * count * tile * share * rows * width,
            bytes_accessed=2 * count * tile * share * (rows + width),
            transcendentals=0,
        ),
    )(places, mask, screened, *panels)


def scatter_sum(value, axis):
    at = lax.axis_index(axis)
    for bit in bits_below(lax.axis_size(axis)):
        halves = value.reshape(2, value.shape[0] // 2, *value.shape[1:])
        mine = (at // bit) % 2
        value = lax.dynamic_index_in_dim(halves, mine, 0, keepdims=False) + swap(
            lax.dynamic_index_in_dim(halves, 1 - mine, 0, keepdims=False), axis, bit
        )
    return value


def per_device(
    polarization, metric, three_panel, three_near, green_function, mask_panel, mask_near
):
    r, c = lax.axis_index("row"), lax.axis_index("col")
    row_count, col_count = lax.axis_size("row"), lax.axis_size("col")
    top_row, top_col = row_count // 2, col_count // 2
    u, v = r // top_row, c // top_col
    r_low, c_low = r % top_row, c % top_col
    panel_rows, depth = polarization.shape
    near_cols = metric.shape[1]
    half = depth // 2
    per_block = metric.shape[0] // depth
    tile, near_l = three_panel.shape[1], three_panel.shape[2]
    share = near_l // row_count
    width = min(WIDTH, near_cols)
    chunks = near_cols // width
    on_diagonal = u == v

    metric_parts = metric.reshape(per_block, 2, half, near_cols)
    metric_mine = lax.dynamic_index_in_dim(metric_parts, u, 1, keepdims=False)
    metric_other = lax.dynamic_index_in_dim(metric_parts, 1 - u, 1, keepdims=False)
    crossing = [metric_other[:, :, j * width : (j + 1) * width] for j in range(chunks)]
    polarization = after(polarization, crossing[0])
    mine = lax.dynamic_slice_in_dim(polarization, u * half, half, 1)
    other = lax.dynamic_slice_in_dim(polarization, (1 - u) * half, half, 1)

    first, second = jnp.split(mine, 2)
    other_first, other_second = jnp.split(other, 2)
    low = top_col // 2

    def cross(value, *others):
        return swap(after(value, *others), "row", top_row)

    arrived, came = [cross(crossing[0])], []
    near_first = swap(first, "col", low)
    crossed_first = cross(other_first, arrived[0])
    near_second = swap(after(second, near_first, arrived[0]), "col", low)
    panels = []

    def turn_next(*others):
        rows = panel_rows // GROUPS
        panels.append(turn(after(three_panel, *others), len(panels) * rows, rows))
        return panels[-1]

    def far(j, *others):
        kept = after(metric_mine, arrived[j])[:, :, j * width : (j + 1) * width]
        stay = jnp.where(on_diagonal, kept, arrived[j])
        leave = jnp.where(on_diagonal, arrived[j], kept)
        came.append([stay, swap(after(leave, *others), "col", top_col)])

    row_links = {bit: Link(2) for bit in bits_below(top_row)}

    def gather_rows(pair):
        found = {0: pair}
        for bit in bits_below(top_row):
            for f, parts in list(found.items()):
                found[f ^ bit] = [row_links[bit].swap(p, "row", bit) for p in parts]
        return [found[f] for f in range(top_row)]

    far(0)
    gathered = [gather_rows(came[0])]
    arrived.append(cross(crossing[1], arrived[0], near_first))
    crossed_second = cross(other_second, crossed_first)
    far(1, near_first, turn_next(near_first))
    gathered.append(gather_rows(came[1]))
    near_crossed_first = swap(after(crossed_first, near_second, arrived[1], came[0][1]), "col", low)
    turn_next(crossed_first, *panels)
    for j in range(2, chunks):
        arrived.append(cross(crossing[j], *([arrived[1], near_second] if j == 2 else [crossed_second])))
        far(j, came[j - 2][1], near_second, gathered[j - 2][-1], turn_next(arrived[j - 1], *panels))
        gathered.append(gather_rows(came[j]))
    near_crossed_second = swap(after(crossed_second, near_crossed_first, arrived[-1], came[1][1]), "col", low)
    while len(panels) < GROUPS:
        turn_next(crossed_second, *panels)

    def gather_low(found):
        link = Link(1)
        for bit in bits_below(low):
            for e, parts in list(found.items()):
                found[e ^ bit] = [link.swap(p, "col", bit) if bit > 1 else swap(p, "col", bit) for p in parts]
        return [found[e] for e in range(top_col)]

    pieces_mine = gather_low({0: [first, second], low: [near_first, near_second]})
    pieces_crossed = gather_low({0: [crossed_first, crossed_second], low: [near_crossed_first, near_crossed_second]})
    blocks = c_low ^ jnp.arange(top_col, dtype=jnp.int32)
    order = ((blocks // per_block) ^ r_low) * per_block + blocks % per_block

    rb = panel_rows * row_count // mask_panel.shape[0]
    ab = near_l // mask_panel.shape[1]
    row_blocks = panel_rows // rb
    panel_mask = lax.dynamic_slice_in_dim(mask_panel, r * row_blocks, row_blocks, 0)

    near_blocks = near_cols // rb
    near_mask = lax.dynamic_slice_in_dim(mask_near, c * near_blocks, near_blocks, 0)
    near_mask = jnp.repeat(jnp.repeat(near_mask, rb, 0), ab, 1).astype(jnp.bfloat16)
    near = after(three_near, near_crossed_first) * near_mask[:, None, :]
    green = lax.dynamic_slice_in_dim(green_function, r * share, share, 0)
    dressed = jnp.einsum("qns,ls->nlq", near, green, preferred_element_type=jnp.float32).astype(jnp.bfloat16)

    earlier = (*panels, dressed)
    screened_chunks, contracted_chunks = [], []
    energy = jnp.zeros((tile, tile), jnp.float32)
    hops = {bit: Link(1) for bit in bits_below(row_count)}
    pair = min(PAIR, chunks)
    wide = pair * width
    orders = [bits_below(row_count)[::-1], bits_below(row_count)]
    kept = [[e for e in range(row_count) if not e & bits[0]] for bits in orders]
    places = r ^ jnp.array(kept, jnp.int32)
    first_bits = jnp.array([[bits[0]] for bits in orders], jnp.int32)
    for j in range(0, chunks, pair):
        sources = [[gathered[j + i][f][side] for side in range(2) for i in range(pair)] for f in range(top_row)]
        away = product(pieces_crossed, sources, after(order, *earlier), per_block, jnp.bfloat16)
        home = product(pieces_mine, sources, after(order, away), per_block, jnp.float32)
        home = home + swap(away, "row", top_row).astype(jnp.float32)
        came_back = swap(home[:, wide:].astype(jnp.bfloat16), "col", top_col)
        screened = (home[:, :wide] + came_back.astype(jnp.float32)).astype(jnp.bfloat16)
        screened_chunks.append(screened)

        gone = list(contract(panels, screened, panel_mask, places ^ first_bits, rb, ab, share))
        stay = list(contract(panels, screened, panel_mask, after(places, gone), rb, ab, share))
        earlier = (home, *gone)
        left, halves = [kept[h] for h in range(2)], []
        for hop in range(len(orders[0])):
            for h, bits in enumerate(orders):
                total = stay[h].astype(jnp.float32) + hops[bits[hop]].swap(gone[h], "row", bits[hop]).astype(jnp.float32)
                total = total.astype(jnp.bfloat16)
                if hop + 1 < len(bits):
                    staying = [e for e in left[h] if not e & bits[hop + 1]]
                    gone[h] = jnp.stack([total[left[h].index(e | bits[hop + 1])] for e in staying])
                    stay[h] = jnp.stack([total[left[h].index(e)] for e in staying])
                    left[h] = staying
                else:
                    halves.append(total[0])
        contracted_chunks.append(jnp.concatenate(halves))
        parts = [
            jnp.einsum("mlq,nlq->mn", half, dressed[:, :, j * width : j * width + wide], preferred_element_type=jnp.float32)
            for half in halves
        ]
        energy = energy - jnp.concatenate(parts)

    energy = scatter_sum(scatter_sum(energy, "row").T, "col").T
    contracted = jnp.transpose(jnp.concatenate(contracted_chunks, axis=2), (2, 0, 1))
    return jnp.concatenate(screened_chunks, axis=1), contracted, energy


def solution(mesh):
    placed = (
        P("row", "col"),
        P("row", "col"),
        P("row", None, None),
        P("col", None, None),
        P(),
        P(),
        P(),
    )
    return jax.shard_map(
        per_device,
        mesh=mesh,
        in_specs=placed,
        out_specs=(P("row", "col"), P("col", None, "row"), P("row", "col")),
        check_vma=False,
    )
```

time: 668 us -> 594 us (0.89)
  Pallas kernels: 51.6 us -> 147 us
  local copies, waits for them, and re-layouts: 91.1 us -> 28.9 us
  blocking collectives: 39.8 us -> 0 us
  waiting for transfers between devices: 322 us -> 290 us
  matrix products: 57 us -> 33.2 us
  other arithmetic: 67.7 us -> 44.2 us
  starting transfers between devices: 26.8 us -> 44.6 us
    pallas_call x4 -> x12, Pallas kernels: 51.6 us -> 147 us  [the longest x4 53.8 us: product(): pl.pallas_call(functools.partial(product_kernel, count, parts, per_block)...]
    unnamed x35 -> x75, local copies, waits for them, and re-layouts: 48.3 us -> 6.52 us
    psum x1 -> x0, blocking collectives: 39.8 us -> none  [per_device(): energy = lax.psum(energy, ('row', 'col'))]
    ppermute x23 -> x47, waiting for transfers between devices: 322 us -> 290 us  [swap(): return lax.ppermute(value, axis, [(i, i ^ bit) for i in range(size)])]
    dot_general x10 -> x4, matrix products: 39.5 us -> 14 us  [per_device(): jnp.einsum('mlq,nlq->mn', half, dressed[:, :, j * width:j * width + wide]...]
    mul x2 -> x1, other arithmetic: 37.2 us -> 13.9 us  [per_device(): near = after(three_near, near_crossed_first) * near_mask[:, None, :]]
    another operation x1 -> x0, local copies, waits for them, and re-layouts: 22.9 us -> none
    concatenate x4 -> x0, other arithmetic: 19.8 us -> none  [the longest x2 11.8 us: metric_chunk(): return jnp.concatenate([found[f] for f in range(top_row)], axis=0)]
  transfers between devices with their start and end apart: 23 -> 47, of which waited for: 12 -> 22; matrix products, arithmetic and copies ran while one was open for 29% -> 15% of each run, Pallas kernels for 8% -> 25%
where the time goes in v2:
time: 594 us; the launch traced here: 590 us
  waiting for transfers between devices  290 us (49%)
  Pallas kernels  147 us (25%)
  starting transfers between devices  44.6 us (8%)
  other arithmetic  44.2 us (7%)
  matrix products  33.2 us (6%)
  local copies, waits for them, and re-layouts  28.9 us (5%)
    ppermute x47, waiting for transfers between devices, swap(): return lax.ppermute(value, axis, [(i, i ^ bit) for i in range(size)])  290 us
    pallas_call x4, Pallas kernels, product(): pl.pallas_call(functools.partial(product_kernel, count, parts, per_block)...  53.8 us
    pallas_call x4, Pallas kernels, contract(): pl.pallas_call(functools.partial(contract_kernel, rb, ab), in_specs=[in_s...  50.4 us
    ppermute x47, starting transfers between devices, swap(): return lax.ppermute(value, axis, [(i, i ^ bit) for i in range(size)])  44.6 us
    pallas_call x4, Pallas kernels, turn(): pl.pallas_call(turn_kernel, grid=(rows // wide, tile // tall), in_specs=[...  42.9 us
    dot_general x1, matrix products, per_device(): jnp.einsum('qns,ls->nlq', near, green, preferred_element_type=jnp.float32)  19.2 us
    dot_general x4, matrix products, per_device(): jnp.einsum('mlq,nlq->mn', half, dressed[:, :, j * width:j * width + wide]...  14 us
    mul x1, other arithmetic, per_device(): near = after(three_near, near_crossed_first) * near_mask[:, None, :]  13.9 us
  transfers between devices with their start and end apart: 47, of which 22 were waited for; matrix products, arithmetic and copies ran while one was open for 15% of the time, Pallas kernels for 25%

profile of v2, /device:TPU:0, one launch (start us, length us, event | category | flops | bytes accessed | tf_op | source)
XLA Modules:
  0.0 589.7 jit_solution(14774273945712197013)
XLA Ops:
  0.7 3.5 dynamic-slice_bitcast_fusion
  4.2 2.1 fusion.48
  6.2 3.0 collective-permute-start.1
  9.2 5.4 fusion.46
  15.8 1.6 collective-permute-start
  17.4 11.0 %collective-permute-done.1 = bf16[2,1664,128]{2,1,0:T(8,128)(2,1)} collective-permute-done((bf16[2,1664,128]{2,1,0:T(8,128)(2,1)}, bf16[2,1664,128]{2,1,0:T(8,128)(2,1)}, u32[]{:S(2)}, u32[]{:S(2)}) %collective-permute-start.1) | collective-permute-done | bytes 852000 | tf_op jit(solution)/shard_map/ppermute | solution.py:19
  28.4 1.7 collective-permute-start.2
  30.2 24.4 %collective-permute-done.refs_4_ = bf16[512,1664]{1,0:T(8,128)(2,1)} collective-permute-done((bf16[512,1664]{1,0:T(8,128)(2,1)S(1)}, bf16[512,1664]{1,0:T(8,128)(2,1)}, u32[]{:S(2)}, u32[]{:S(2)}) %collective-permute-start) | collective-permute-done | bytes 1703968 | tf_op jit(solution)/shard_map/ppermute | solution.py:19
  54.6 1.6 collective-permute-start.4
  57.7 2.7 collective-permute-start.6
  60.8 8.1 %collective-permute-done.2.refs_0_ = bf16[512,1664]{1,0:T(8,128)(2,1)} collective-permute-done((bf16[512,1664]{1,0:T(8,128)(2,1)}, bf16[512,1664]{1,0:T(8,128)(2,1)}, u32[]{:S(2)}, u32[]{:S(2)}) %collective-permute-start.2) | collective-permute-done | bytes 1703968 | tf_op jit(solution)/shard_map/ppermute | solution.py:19
  68.9 1.7 collective-permute-start.8
  70.7 39.3 %collective-permute-done.6.refs_10_ = bf16[2,1664,128]{2,1,0:T(8,128)(2,1)} collective-permute-done((bf16[2,1664,128]{2,1,0:T(8,128)(2,1)S(1)}, bf16[2,1664,128]{2,1,0:T(8,128)(2,1)}, u32[]{:S(2)}, u32[]{:S(2)}) %collective-permute-start.6) | collective-permute-done | bytes 852000 | tf_op jit(solution)/shard_map/ppermute | solution.py:19
  110.9 2.7 collective-permute-start.7
  113.6 10.9 %shard_map.112.refs_0_ = bf16[64,256,256]{2,1,0:T(8,128)(2,1)} custom-call(bf16[1024,64,256]{2,1,0:T(8,128)(2,1)} %panel_ref.3), custom_call_target="tpu_custom_call" | custom-call | bytes 16777216 | tf_op jit(solution)/shard_map/pallas_call | solution.py:125
  124.5 2.3 broadcast_select_fusion.4
  128.8 38.0 %collective-permute-done.12.refs_11_ = bf16[2,1664,128]{2,1,0:T(8,128)(2,1)S(1)} collective-permute-done((bf16[2,1664,128]{2,1,0:T(8,128)(2,1)S(1)}, bf16[2,1664,128]{2,1,0:T(8,128)(2,1)S(1)}, u32[]{:S(2)}, u32[]{:S(2)}) %collective-permute-start.12) | collective-permute-done | bytes 852000 | tf_op jit(solution)/shard_map/ppermute | solution.py:19
  167.3 1.6 collective-permute-start.13
  171.4 19.3 %collective-permute-done.16.refs_12_ = bf16[2,1664,128]{2,1,0:T(8,128)(2,1)S(1)} collective-permute-done((bf16[2,1664,128]{2,1,0:T(8,128)(2,1)S(1)}, bf16[2,1664,128]{2,1,0:T(8,128)(2,1)S(1)}, u32[]{:S(2)}, u32[]{:S(2)}) %collective-permute-start.16) | collective-permute-done | bytes 852000 | tf_op jit(solution)/shard_map/ppermute | solution.py:19
  195.5 1.8 copy.27
  197.8 10.6 %shard_map.113.refs_1_ = bf16[64,256,256]{2,1,0:T(8,128)(2,1)} custom-call(bf16[1024,64,256]{2,1,0:T(8,128)(2,1)} %panel_ref.3), custom_call_target="tpu_custom_call" | custom-call | bytes 16777216 | tf_op jit(solution)/shard_map/pallas_call | solution.py:125
  208.4 10.6 %shard_map.114.refs_2_ = bf16[64,256,256]{2,1,0:T(8,128)(2,1)} custom-call(bf16[1024,64,256]{2,1,0:T(8,128)(2,1)} %panel_ref.3), custom_call_target="tpu_custom_call" | custom-call | bytes 16777216 | tf_op jit(solution)/shard_map/pallas_call | solution.py:125
  220.1 2.2 broadcast_select_fusion.1
  222.3 10.7 %shard_map.115.refs_3_ = bf16[64,256,256]{2,1,0:T(8,128)(2,1)} custom-call(bf16[1024,64,256]{2,1,0:T(8,128)(2,1)} %panel_ref.3), custom_call_target="tpu_custom_call" | custom-call | bytes 16777216 | tf_op jit(solution)/shard_map/pallas_call | solution.py:125
  233.6 13.9 %broadcast_multiply_fusion = bf16[512,64,256]{2,1,0:T(8,128)(2,1)} fusion(bf16[512,64,256]{2,1,0:T(8,128)(2,1)} %param.12, bf16[512,256]{1,0:T(8,128)(2,1)S(1)} %copy-done.19), kind=kLoop, calls=%fused_computation.2 | loop fusion | flops 8388608 | bytes 33816576 | tf_op jit(solution)/shard_map/mul | solution.py:310
  247.5 6.5 %collective-permute-done.19.refs_15_ = bf16[2,1664,128]{2,1,0:T(8,128)(2,1)S(1)} collective-permute-done((bf16[2,1664,128]{2,1,0:T(8,128)(2,1)S(1)}, bf16[2,1664,128]{2,1,0:T(8,128)(2,1)S(1)}, u32[]{:S(2)}, u32[]{:S(2)}) %collective-permute-start.19) | collective-permute-done | bytes 852000 | tf_op jit(solution)/shard_map/ppermute | solution.py:19
  254.9 1.9 collective-permute-start.26
  256.8 19.2 %convert_bitcast_fusion = bf16[64,64,512]{2,1,0:T(8,128)(2,1)} fusion(bf16[512,64,256]{2,1,0:T(8,128)(2,1)} %broadcast_multiply_fusion, bf16[256,256]{1,0:T(8,128)(2,1)S(1)} %copy-done, s32[]{:T(128)S(6)} %select_n.155), kind=kOutput, calls=%fused_computation.8 | convolution fusion | flops 1075838976 | bytes 21004292 | tf_op jit(solution)/shard_map/qns,ls->nlq/dot_general | solution.py:312
  275.9 13.4 %shard_map.116 = bf16[1024,512]{1,0:T(8,128)(2,1)} custom-call(s32[4]{0:T(128)} %fusion.45.order_ref, bf16[512,1664]{1,0:T(8,128)(2,1)} %collective-permute-done.2.refs_0_, bf16[512,1664]{1,0:T(8,128)(2,1)} %collective-permute-done.8.refs_1_, bf16[512,1664]{1,0:T(8,128)(2,1)} %collective-permute-done.9.refs_2_, ...), custom_call_target="tpu_custom_call" | custom-call | flops 6979321856 | bytes 22544384 | tf_op jit(solution)/shard_map/pallas_call | solution.py:96
  289.3 5.8 collective-permute-done.26.refs_10_
  299.1 13.6 %shard_map.117 = f32[1024,512]{1,0:T(8,128)} custom-call(s32[4]{0:T(128)} %fusion.45.order_ref, bf16[512,1664]{1,0:T(8,128)(2,1)} %copy-done.16, bf16[512,1664]{1,0:T(8,128)(2,1)} %get-tuple-element.56.refs_1_, bf16[512,1664]{1,0:T(8,128)(2,1)} %collective-permute-done.20.refs_2_, bf16[512,1664]{1,0:T(8,128)(2,1)} %collective-permute-done.21.refs_3_, ...), custom_call_target="tpu_custom_call" | custom-call | flops 6979321856 | bytes 22544384 | tf_op jit(solution)/shard_map/pallas_call | solution.py:96
  312.7 7.5 %collective-permute-done.24 = bf16[1024,512]{1,0:T(8,128)(2,1)S(1)} collective-permute-done((bf16[1024,512]{1,0:T(8,128)(2,1)}, bf16[1024,512]{1,0:T(8,128)(2,1)S(1)}, u32[]{:S(2)}, u32[]{:S(2)}) %collective-permute-start.24) | collective-permute-done | bytes 1048608 | tf_op jit(solution)/shard_map/ppermute | solution.py:19
  320.2 1.9 convert_add_fusion.1
  324.3 24.5 %collective-permute-done.27.refs_11_ = bf16[2,1664,128]{2,1,0:T(8,128)(2,1)} collective-permute-done((bf16[2,1664,128]{2,1,0:T(8,128)(2,1)}, bf16[2,1664,128]{2,1,0:T(8,128)(2,1)}, u32[]{:S(2)}, u32[]{:S(2)}) %collective-permute-start.27) | collective-permute-done | bytes 852000 | tf_op jit(solution)/shard_map/ppermute | solution.py:19
  351.0 8.6 %collective-permute-done.25 = bf16[1024,256]{1,0:T(8,128)(2,1)} collective-permute-done((bf16[1024,256]{1,0:T(8,128)(2,1)}, bf16[1024,256]{1,0:T(8,128)(2,1)}, u32[]{:S(2)}, u32[]{:S(2)}) %collective-permute-start.25) | collective-permute-done | bytes 524320 | tf_op jit(solution)/shard_map/ppermute | solution.py:19
  359.6 2.0 fusion.29.screened_ref
  361.6 12.5 %shard_map.118 = (bf16[2,32,64,256]{3,2,1,0:T(8,128)(2,1)}, bf16[2,32,64,256]{3,2,1,0:T(8,128)(2,1)}) custom-call(s32[2,2]{1,0:T(2,128)} %get-tuple-element.122.places_ref, s32[16,8]{1,0:T(8,128)} %copy.42.mask_ref, bf16[1024,256]{1,0:T(8,128)(2,1)} %fusion.29.screened_ref, bf16[64,256,256]{2,1,0:T(8,128)(2,1)} %shard_map.112.refs_0_, ...), custom_call_target="tpu_custom_call" | custom-call | flops 4294967296 | bytes 20971520 | tf_op jit(solution)/shard_map/pallas_call | solution.py:185
  375.7 1.7 collective-permute-start.35
  377.4 13.3 %shard_map.119 = bf16[1024,512]{1,0:T(8,128)(2,1)} custom-call(s32[4]{0:T(128)} %fusion.45.order_ref, bf16[512,1664]{1,0:T(8,128)(2,1)} %collective-permute-done.2.refs_0_, bf16[512,1664]{1,0:T(8,128)(2,1)} %collective-permute-done.8.refs_1_, bf16[512,1664]{1,0:T(8,128)(2,1)} %collective-permute-done.9.refs_2_, ...), custom_call_target="tpu_custom_call" | custom-call | flops 6979321856 | bytes 22544384 | tf_op jit(solution)/shard_map/pallas_call | solution.py:96
  391.3 12.5 %shard_map.121 = (bf16[2,32,64,256]{3,2,1,0:T(8,128)(2,1)}, bf16[2,32,64,256]{3,2,1,0:T(8,128)(2,1)}) custom-call(s32[2,2]{1,0:T(2,128)} %get-tuple-element.90.places_ref, s32[16,8]{1,0:T(8,128)} %copy.42.mask_ref, bf16[1024,256]{1,0:T(8,128)(2,1)} %fusion.29.screened_ref, bf16[64,256,256]{2,1,0:T(8,128)(2,1)} %shard_map.112.refs_0_, ...), custom_call_target="tpu_custom_call" | custom-call | flops 4294967296 | bytes 20971520 | tf_op jit(solution)/shard_map/pallas_call | solution.py:185
  403.8 13.6 %shard_map.120 = f32[1024,512]{1,0:T(8,128)} custom-call(s32[4]{0:T(128)} %fusion.45.order_ref, bf16[512,1664]{1,0:T(8,128)(2,1)} %copy-done.16, bf16[512,1664]{1,0:T(8,128)(2,1)} %get-tuple-element.56.refs_1_, bf16[512,1664]{1,0:T(8,128)(2,1)} %collective-permute-done.20.refs_2_, bf16[512,1664]{1,0:T(8,128)(2,1)} %collective-permute-done.21.refs_3_, ...), custom_call_target="tpu_custom_call" | custom-call | flops 6979321856 | bytes 22544384 | tf_op jit(solution)/shard_map/pallas_call | solution.py:96
  417.4 28.0 %collective-permute-done.32 = bf16[1024,512]{1,0:T(8,128)(2,1)S(1)} collective-permute-done((bf16[1024,512]{1,0:T(8,128)(2,1)}, bf16[1024,512]{1,0:T(8,128)(2,1)S(1)}, u32[]{:S(2)}, u32[]{:S(2)}) %collective-permute-start.32) | collective-permute-done | bytes 1048608 | tf_op jit(solution)/shard_map/ppermute | solution.py:19
  445.5 1.9 convert_add_fusion
  449.4 1.7 collective-permute-start.36
  454.1 17.2 %collective-permute-done.33 = bf16[1024,256]{1,0:T(8,128)(2,1)S(1)} collective-permute-done((bf16[1024,256]{1,0:T(8,128)(2,1)S(1)}, bf16[1024,256]{1,0:T(8,128)(2,1)S(1)}, u32[]{:S(2)}, u32[]{:S(2)}) %collective-permute-start.33) | collective-permute-done | bytes 524320 | tf_op jit(solution)/shard_map/ppermute | solution.py:19
  472.3 12.6 %shard_map.122 = (bf16[2,32,64,256]{3,2,1,0:T(8,128)(2,1)}, bf16[2,32,64,256]{3,2,1,0:T(8,128)(2,1)}) custom-call(s32[2,2]{1,0:T(2,128)} %get-tuple-element.122.places_ref, s32[16,8]{1,0:T(8,128)} %copy.42.mask_ref, bf16[1024,256]{1,0:T(8,128)(2,1)} %fusion.28.screened_ref, bf16[64,256,256]{2,1,0:T(8,128)(2,1)} %shard_map.112.refs_0_, ...), custom_call_target="tpu_custom_call" | custom-call | flops 4294967296 | bytes 20971520 | tf_op jit(solution)/shard_map/pallas_call | solution.py:185
  484.9 1.6 collective-permute-start.39
  487.0 4.8 fusion.47
  491.8 12.7 %shard_map.123 = (bf16[2,32,64,256]{3,2,1,0:T(8,128)(2,1)}, bf16[2,32,64,256]{3,2,1,0:T(8,128)(2,1)}) custom-call(s32[2,2]{1,0:T(2,128)} %get-tuple-element.90.places_ref, s32[16,8]{1,0:T(8,128)} %copy.42.mask_ref, bf16[1024,256]{1,0:T(8,128)(2,1)} %fusion.28.screened_ref, bf16[64,256,256]{2,1,0:T(8,128)(2,1)} %shard_map.112.refs_0_, ...), custom_call_target="tpu_custom_call" | custom-call | flops 4294967296 | bytes 20971520 | tf_op jit(solution)/shard_map/pallas_call | solution.py:185
  504.5 1.7 fusion.25
  506.3 26.6 %collective-permute-done.39 = bf16[2,32,64,256]{3,2,1,0:T(8,128)(2,1)} collective-permute-done((bf16[2,32,64,256]{3,2,1,0:T(8,128)(2,1)}, bf16[2,32,64,256]{3,2,1,0:T(8,128)(2,1)}, u32[]{:S(2)}, u32[]{:S(2)}) %collective-permute-start.39) | collective-permute-done | bytes 2097184 | tf_op jit(solution)/shard_map/ppermute | solution.py:19
  532.8 2.8 add_convert_fusion
  537.6 2.5 add_convert_fusion.1
  541.8 3.5 fusion.15
  545.2 3.5 fusion.12
  548.7 11.4 %collective-permute-done.41 = bf16[1,32,64,256]{3,2,1,0:T(8,128)(2,1)S(1)} collective-permute-done((bf16[1,32,64,256]{3,2,1,0:T(8,128)(2,1)S(1)}, bf16[1,32,64,256]{3,2,1,0:T(8,128)(2,1)S(1)}, u32[]{:S(2)}, u32[]{:S(2)}) %collective-permute-start.41) | collective-permute-done | bytes 1048608 | tf_op jit(solution)/shard_map/ppermute | solution.py:19
  560.5 3.6 fusion.21
  565.9 3.5 fusion.18
  569.4 1.6 collective-permute-start.42
  571.0 2.2 collective-permute-done.42
  573.9 2.9 collective-permute-done.43
  577.1 4.5 collective-permute-done.44
  582.9 2.5 collective-permute-done.45
  585.4 3.5 maximum_bitcast_fusion
  (174 shorter events, 42.4 us)
Async XLA Ops:
  0.6 256.1 %copy-start = (bf16[256,256]{1,0:T(8,128)(2,1)S(1)}, bf16[256,256]{1,0:T(8,128)(2,1)}, u32[]{:S(2)}) copy-start(bf16[256,256]{1,0:T(8,128)(2,1)} %param.13) | copy-start | bytes 393220
  6.2 22.2 %collective-permute-start.1 = (bf16[2,1664,128]{2,1,0:T(8,128)(2,1)}, bf16[2,1664,128]{2,1,0:T(8,128)(2,1)}, u32[]{:S(2)}, u32[]{:S(2)}) collective-permute-start(bf16[2,1664,128]{2,1,0:T(8,128)(2,1)} %get-tuple-element.116), channel_id=1, source_target_pairs={{0,16},{8,24},{16,0},{24,8},{1,17},{9,25},{17,1},{25,9},{2,18},{10... | collective-permute-start | bytes 2555912 | tf_op jit(solution)/shard_map/ppermute | solution.py:19
  15.8 38.8 %collective-permute-start = (bf16[512,1664]{1,0:T(8,128)(2,1)S(1)}, bf16[512,1664]{1,0:T(8,128)(2,1)}, u32[]{:S(2)}, u32[]{:S(2)}) collective-permute-start(bf16[512,1664]{1,0:T(8,128)(2,1)S(1)} %get-tuple-element.99.refs_0_), channel_id=1, source_target_pairs={{0,2},{1,3},{2,0},{3,1},{4,6},{5,7},{6,4},{7,5},{8,10},{9,11},{10,... | collective-permute-start | bytes 5111816 | tf_op jit(solution)/shard_map/ppermute | solution.py:19
  28.4 40.5 %collective-permute-start.2 = (bf16[512,1664]{1,0:T(8,128)(2,1)}, bf16[512,1664]{1,0:T(8,128)(2,1)}, u32[]{:S(2)}, u32[]{:S(2)}) collective-permute-start(bf16[512,1664]{1,0:T(8,128)(2,1)} %get-tuple-element.52), channel_id=1, source_target_pairs={{0,16},{8,24},{16,0},{24,8},{1,17},{9,25},{17,1},{25,9},{2,18},{10... | collective-permute-start | bytes 5111816 | tf_op jit(solution)/shard_map/ppermute | solution.py:19
  54.6 56.3 %collective-permute-start.4 = (bf16[512,1664]{1,0:T(8,128)(2,1)}, bf16[512,1664]{1,0:T(8,128)(2,1)}, u32[]{:S(2)}, u32[]{:S(2)}) collective-permute-start(bf16[512,1664]{1,0:T(8,128)(2,1)} %get-tuple-element.56.refs_1_), channel_id=1, source_target_pairs={{0,2},{1,3},{2,0},{3,1},{4,6},{5,7},{6,4},{7,5},{8,10},{9,11},{10,... | collective-permute-start | bytes 5111816 | tf_op jit(solution)/shard_map/ppermute | solution.py:19
  56.2 12.7 %copy-start.18 = (bf16[512,1664]{1,0:T(8,128)(2,1)S(1)}, bf16[512,1664]{1,0:T(8,128)(2,1)}, u32[]{:S(2)}) copy-start(bf16[512,1664]{1,0:T(8,128)(2,1)} %get-tuple-element.63) | copy-start | bytes 5111812
  57.6 111.2 %copy-start.22 = (bf16[2,1664,128]{2,1,0:T(8,128)(2,1)}, bf16[2,1664,128]{2,1,0:T(8,128)(2,1)S(1)}, u32[]{:S(2)}) copy-start(bf16[2,1664,128]{2,1,0:T(8,128)(2,1)S(1)} %get-tuple-element.109.refs_8_) | copy-start | bytes 2555908
  57.7 52.3 %collective-permute-start.6 = (bf16[2,1664,128]{2,1,0:T(8,128)(2,1)S(1)}, bf16[2,1664,128]{2,1,0:T(8,128)(2,1)}, u32[]{:S(2)}, u32[]{:S(2)}) collective-permute-start(bf16[2,1664,128]{2,1,0:T(8,128)(2,1)S(1)} %get-tuple-element.110), channel_id=1, source_target_pairs={{0,4},{1,5},{2,6},{3,7},{4,0},{5,1},{6,2},{7,3},{8,12},{9,13},{10,... | collective-permute-start | bytes 2555912 | tf_op jit(solution)/shard_map/ppermute | solution.py:19
  60.3 49.6 %collective-permute-start.3 = (bf16[2,1664,128]{2,1,0:T(8,128)(2,1)S(1)}, bf16[2,1664,128]{2,1,0:T(8,128)(2,1)S(1)}, u32[]{:S(2)}, u32[]{:S(2)}) collective-permute-start(bf16[2,1664,128]{2,1,0:T(8,128)(2,1)S(1)} %copy-done.27), channel_id=1, source_target_pairs={{0,16},{8,24},{16,0},{24,8},{1,17},{9,25},{17,1},{25,9},{2,18},{10... | collective-permute-start | bytes 2555912 | tf_op jit(solution)/shard_map/ppermute | solution.py:19
  68.9 59.4 %collective-permute-start.8 = (bf16[512,1664]{1,0:T(8,128)(2,1)S(1)}, bf16[512,1664]{1,0:T(8,128)(2,1)}, u32[]{:S(2)}, u32[]{:S(2)}) collective-permute-start(bf16[512,1664]{1,0:T(8,128)(2,1)S(1)} %copy-done.18), channel_id=1, source_target_pairs={{0,16},{8,24},{16,0},{24,8},{1,17},{9,25},{17,1},{25,9},{2,18},{10... | collective-permute-start | bytes 5111816 | tf_op jit(solution)/shard_map/ppermute | solution.py:19
  110.9 56.3 %collective-permute-start.7 = (bf16[512,1664]{1,0:T(8,128)(2,1)}, bf16[512,1664]{1,0:T(8,128)(2,1)}, u32[]{:S(2)}, u32[]{:S(2)}) collective-permute-start(bf16[512,1664]{1,0:T(8,128)(2,1)} %collective-permute-done.2.refs_0_), channel_id=1, source_target_pairs={{0,2},{1,3},{2,0},{3,1},{4,6},{5,7},{6,4},{7,5},{8,10},{9,11},{10,... | collective-permute-start | bytes 5111816 | tf_op jit(solution)/shard_map/ppermute | solution.py:19
  124.5 68.7 %copy-start.30 = (s32[64,8]{0,1:T(8,128)S(1)}, s32[64,8]{0,1:T(8,128)}, u32[]{:S(2)}) copy-start(s32[64,8]{0,1:T(8,128)} %param.15) | copy-start | bytes 6148
  126.8 40.0 %collective-permute-start.12 = (bf16[2,1664,128]{2,1,0:T(8,128)(2,1)S(1)}, bf16[2,1664,128]{2,1,0:T(8,128)(2,1)S(1)}, u32[]{:S(2)}, u32[]{:S(2)}) collective-permute-start(bf16[2,1664,128]{2,1,0:T(8,128)(2,1)S(1)} %get-tuple-element.66), channel_id=1, source_target_pairs={{0,4},{1,5},{2,6},{3,7},{4,0},{5,1},{6,2},{7,3},{8,12},{9,13},{10,... | collective-permute-start | bytes 2555912 | tf_op jit(solution)/shard_map/ppermute | solution.py:19
  128.3 39.0 %collective-permute-start.11 = (bf16[2,1664,128]{2,1,0:T(8,128)(2,1)S(1)}, bf16[2,1664,128]{2,1,0:T(8,128)(2,1)S(1)}, u32[]{:S(2)}, u32[]{:S(2)}) collective-permute-start(bf16[2,1664,128]{2,1,0:T(8,128)(2,1)S(1)} %copy-done.25), channel_id=1, source_target_pairs={{0,16},{8,24},{16,0},{24,8},{1,17},{9,25},{17,1},{25,9},{2,18},{10... | collective-permute-start | bytes 2555912 | tf_op jit(solution)/shard_map/ppermute | solution.py:19
  166.8 24.0 %copy-start.33 = (bf16[2,1664,128]{2,1,0:T(8,128)(2,1)}, bf16[2,1664,128]{2,1,0:T(8,128)(2,1)S(1)}, u32[]{:S(2)}) copy-start(bf16[2,1664,128]{2,1,0:T(8,128)(2,1)S(1)} %collective-permute-done.12.refs_11_) | copy-start | bytes 2555908
  167.3 23.5 %copy-start.23 = (bf16[2,1664,128]{2,1,0:T(8,128)(2,1)}, bf16[2,1664,128]{2,1,0:T(8,128)(2,1)S(1)}, u32[]{:S(2)}) copy-start(bf16[2,1664,128]{2,1,0:T(8,128)(2,1)S(1)} %collective-permute-done.11) | copy-start | bytes 2555908
  167.3 52.4 %collective-permute-start.13 = (bf16[512,1664]{1,0:T(8,128)(2,1)}, bf16[512,1664]{1,0:T(8,128)(2,1)}, u32[]{:S(2)}, u32[]{:S(2)}) collective-permute-start(bf16[512,1664]{1,0:T(8,128)(2,1)} %collective-permute-done.8.refs_1_), channel_id=1, source_target_pairs={{0,2},{1,3},{2,0},{3,1},{4,6},{5,7},{6,4},{7,5},{8,10},{9,11},{10,... | collective-permute-start | bytes 5111816 | tf_op jit(solution)/shard_map/ppermute | solution.py:19
  168.9 21.9 %collective-permute-start.16 = (bf16[2,1664,128]{2,1,0:T(8,128)(2,1)S(1)}, bf16[2,1664,128]{2,1,0:T(8,128)(2,1)S(1)}, u32[]{:S(2)}, u32[]{:S(2)}) collective-permute-start(bf16[2,1664,128]{2,1,0:T(8,128)(2,1)S(1)} %get-tuple-element.109.refs_8_), channel_id=1, source_target_pairs={{0,8},{8,0},{16,24},{24,16},{1,9},{9,1},{17,25},{25,17},{2,10},{10... | collective-permute-start | bytes 2555912 | tf_op jit(solution)/shard_map/ppermute | solution.py:19
  170.4 48.7 %collective-permute-start.18 = (bf16[2,1664,128]{2,1,0:T(8,128)(2,1)}, bf16[2,1664,128]{2,1,0:T(8,128)(2,1)}, u32[]{:S(2)}, u32[]{:S(2)}) collective-permute-start(bf16[2,1664,128]{2,1,0:T(8,128)(2,1)} %collective-permute-done.6.refs_10_), channel_id=1, source_target_pairs={{0,8},{8,0},{16,24},{24,16},{1,9},{9,1},{17,25},{25,17},{2,10},{10... | collective-permute-start | bytes 2555912 | tf_op jit(solution)/shard_map/ppermute | solution.py:19
  170.9 48.2 %collective-permute-start.5 = (bf16[2,1664,128]{2,1,0:T(8,128)(2,1)}, bf16[2,1664,128]{2,1,0:T(8,128)(2,1)}, u32[]{:S(2)}, u32[]{:S(2)}) collective-permute-start(bf16[2,1664,128]{2,1,0:T(8,128)(2,1)} %get-tuple-element.57), channel_id=1, source_target_pairs={{0,16},{8,24},{16,0},{24,8},{1,17},{9,25},{17,1},{25,9},{2,18},{10... | collective-permute-start | bytes 2555912 | tf_op jit(solution)/shard_map/ppermute | solution.py:19
  191.7 41.3 %collective-permute-start.17 = (bf16[2,1664,128]{2,1,0:T(8,128)(2,1)}, bf16[2,1664,128]{2,1,0:T(8,128)(2,1)}, u32[]{:S(2)}, u32[]{:S(2)}) collective-permute-start(bf16[2,1664,128]{2,1,0:T(8,128)(2,1)} %get-tuple-element.68.refs_9_), channel_id=1, source_target_pairs={{0,8},{8,0},{16,24},{24,16},{1,9},{9,1},{17,25},{25,17},{2,10},{10... | collective-permute-start | bytes 2555912 | tf_op jit(solution)/shard_map/ppermute | solution.py:19
  219.1 28.4 %collective-permute-start.9 = (bf16[512,1664]{1,0:T(8,128)(2,1)}, bf16[512,1664]{1,0:T(8,128)(2,1)}, u32[]{:S(2)}, u32[]{:S(2)}) collective-permute-start(bf16[512,1664]{1,0:T(8,128)(2,1)} %collective-permute-done.2.refs_0_), channel_id=1, source_target_pairs={{0,1},{1,0},{2,3},{3,2},{4,5},{5,4},{6,7},{7,6},{8,9},{9,8},{10,11... | collective-permute-start | bytes 5111816 | tf_op jit(solution)/shard_map/ppermute | solution.py:19
  219.1 34.9 %collective-permute-start.10 = (bf16[512,1664]{1,0:T(8,128)(2,1)}, bf16[512,1664]{1,0:T(8,128)(2,1)}, u32[]{:S(2)}, u32[]{:S(2)}) collective-permute-start(bf16[512,1664]{1,0:T(8,128)(2,1)} %collective-permute-done.8.refs_1_), channel_id=1, source_target_pairs={{0,1},{1,0},{2,3},{3,2},{4,5},{5,4},{6,7},{7,6},{8,9},{9,8},{10,11... | collective-permute-start | bytes 5111816 | tf_op jit(solution)/shard_map/ppermute | solution.py:19
  219.6 34.9 %collective-permute-start.14 = (bf16[512,1664]{1,0:T(8,128)(2,1)}, bf16[512,1664]{1,0:T(8,128)(2,1)}, u32[]{:S(2)}, u32[]{:S(2)}) collective-permute-start(bf16[512,1664]{1,0:T(8,128)(2,1)} %collective-permute-done.7.refs_4_), channel_id=1, source_target_pairs={{0,1},{1,0},{2,3},{3,2},{4,5},{5,4},{6,7},{7,6},{8,9},{9,8},{10,11... | collective-permute-start | bytes 5111816 | tf_op jit(solution)/shard_map/ppermute | solution.py:19
  219.6 35.2 %collective-permute-start.15 = (bf16[512,1664]{1,0:T(8,128)(2,1)}, bf16[512,1664]{1,0:T(8,128)(2,1)}, u32[]{:S(2)}, u32[]{:S(2)}) collective-permute-start(bf16[512,1664]{1,0:T(8,128)(2,1)} %collective-permute-done.13.refs_5_), channel_id=1, source_target_pairs={{0,1},{1,0},{2,3},{3,2},{4,5},{5,4},{6,7},{7,6},{8,9},{9,8},{10,11... | collective-permute-start | bytes 5111816 | tf_op jit(solution)/shard_map/ppermute | solution.py:19
  233.0 20.9 %collective-permute-start.19 = (bf16[2,1664,128]{2,1,0:T(8,128)(2,1)S(1)}, bf16[2,1664,128]{2,1,0:T(8,128)(2,1)S(1)}, u32[]{:S(2)}, u32[]{:S(2)}) collective-permute-start(bf16[2,1664,128]{2,1,0:T(8,128)(2,1)S(1)} %copy-done.34), channel_id=1, source_target_pairs={{0,8},{8,0},{16,24},{24,16},{1,9},{9,1},{17,25},{25,17},{2,10},{10... | collective-permute-start | bytes 2555912 | tf_op jit(solution)/shard_map/ppermute | solution.py:19
  233.6 13.9 %copy-start.17 = (bf16[512,1664]{1,0:T(8,128)(2,1)S(1)}, bf16[512,1664]{1,0:T(8,128)(2,1)}, u32[]{:S(2)}) copy-start(bf16[512,1664]{1,0:T(8,128)(2,1)} %copy-done.16) | copy-start | bytes 5111812
  247.5 49.5 %collective-permute-start.20 = (bf16[512,1664]{1,0:T(8,128)(2,1)S(1)}, bf16[512,1664]{1,0:T(8,128)(2,1)}, u32[]{:S(2)}, u32[]{:S(2)}) collective-permute-start(bf16[512,1664]{1,0:T(8,128)(2,1)S(1)} %copy-done.17), channel_id=1, source_target_pairs={{0,1},{1,0},{2,3},{3,2},{4,5},{5,4},{6,7},{7,6},{8,9},{9,8},{10,11... | collective-permute-start | bytes 5111816 | tf_op jit(solution)/shard_map/ppermute | solution.py:19
  254.0 43.6 %collective-permute-start.21 = (bf16[512,1664]{1,0:T(8,128)(2,1)}, bf16[512,1664]{1,0:T(8,128)(2,1)}, u32[]{:S(2)}, u32[]{:S(2)}) collective-permute-start(bf16[512,1664]{1,0:T(8,128)(2,1)} %get-tuple-element.56.refs_1_), channel_id=1, source_target_pairs={{0,1},{1,0},{2,3},{3,2},{4,5},{5,4},{6,7},{7,6},{8,9},{9,8},{10,11... | collective-permute-start | bytes 5111816 | tf_op jit(solution)/shard_map/ppermute | solution.py:19
  254.0 43.6 %collective-permute-start.22 = (bf16[512,1664]{1,0:T(8,128)(2,1)}, bf16[512,1664]{1,0:T(8,128)(2,1)}, u32[]{:S(2)}, u32[]{:S(2)}) collective-permute-start(bf16[512,1664]{1,0:T(8,128)(2,1)} %collective-permute-done.refs_4_), channel_id=1, source_target_pairs={{0,1},{1,0},{2,3},{3,2},{4,5},{5,4},{6,7},{7,6},{8,9},{9,8},{10,11... | collective-permute-start | bytes 5111816 | tf_op jit(solution)/shard_map/ppermute | solution.py:19
  254.5 44.6 %collective-permute-start.23 = (bf16[512,1664]{1,0:T(8,128)(2,1)}, bf16[512,1664]{1,0:T(8,128)(2,1)}, u32[]{:S(2)}, u32[]{:S(2)}) collective-permute-start(bf16[512,1664]{1,0:T(8,128)(2,1)} %collective-permute-done.4.refs_5_), channel_id=1, source_target_pairs={{0,1},{1,0},{2,3},{3,2},{4,5},{5,4},{6,7},{7,6},{8,9},{9,8},{10,11... | collective-permute-start | bytes 5111816 | tf_op jit(solution)/shard_map/ppermute | solution.py:19
  254.9 40.2 %collective-permute-start.26 = (bf16[2,1664,128]{2,1,0:T(8,128)(2,1)S(1)}, bf16[2,1664,128]{2,1,0:T(8,128)(2,1)}, u32[]{:S(2)}, u32[]{:S(2)}) collective-permute-start(bf16[2,1664,128]{2,1,0:T(8,128)(2,1)S(1)} %get-tuple-element.76), channel_id=1, source_target_pairs={{0,4},{1,5},{2,6},{3,7},{4,0},{5,1},{6,2},{7,3},{8,12},{9,13},{10,... | collective-permute-start | bytes 2555912 | tf_op jit(solution)/shard_map/ppermute | solution.py:19
  275.9 19.7 %copy-start.24 = (bf16[2,1664,128]{2,1,0:T(8,128)(2,1)S(1)}, bf16[2,1664,128]{2,1,0:T(8,128)(2,1)}, u32[]{:S(2)}) copy-start(bf16[2,1664,128]{2,1,0:T(8,128)(2,1)} %copy-done.23) | copy-start | bytes 2555908
  295.1 25.1 %collective-permute-start.24 = (bf16[1024,512]{1,0:T(8,128)(2,1)}, bf16[1024,512]{1,0:T(8,128)(2,1)S(1)}, u32[]{:S(2)}, u32[]{:S(2)}) collective-permute-start(bf16[1024,512]{1,0:T(8,128)(2,1)} %shard_map.116), channel_id=1, source_target_pairs={{0,16},{8,24},{16,0},{24,8},{1,17},{9,25},{17,1},{25,9},{2,18},{10... | collective-permute-start | bytes 3145736 | tf_op jit(solution)/shard_map/ppermute | solution.py:19
  297.0 26.8 %collective-permute-start.28 = (bf16[2,1664,128]{2,1,0:T(8,128)(2,1)}, bf16[2,1664,128]{2,1,0:T(8,128)(2,1)}, u32[]{:S(2)}, u32[]{:S(2)}) collective-permute-start(bf16[2,1664,128]{2,1,0:T(8,128)(2,1)} %get-tuple-element.78.refs_8_), channel_id=1, source_target_pairs={{0,8},{8,0},{16,24},{24,16},{1,9},{9,1},{17,25},{25,17},{2,10},{10... | collective-permute-start | bytes 2555912 | tf_op jit(solution)/shard_map/ppermute | solution.py:19
  297.5 51.3 %collective-permute-start.27 = (bf16[2,1664,128]{2,1,0:T(8,128)(2,1)}, bf16[2,1664,128]{2,1,0:T(8,128)(2,1)}, u32[]{:S(2)}, u32[]{:S(2)}) collective-permute-start(bf16[2,1664,128]{2,1,0:T(8,128)(2,1)} %get-tuple-element.77), channel_id=1, source_target_pairs={{0,4},{1,5},{2,6},{3,7},{4,0},{5,1},{6,2},{7,3},{8,12},{9,13},{10,... | collective-permute-start | bytes 2555912 | tf_op jit(solution)/shard_map/ppermute | solution.py:19
  297.5 51.3 %collective-permute-start.30 = (bf16[2,1664,128]{2,1,0:T(8,128)(2,1)}, bf16[2,1664,128]{2,1,0:T(8,128)(2,1)}, u32[]{:S(2)}, u32[]{:S(2)}) collective-permute-start(bf16[2,1664,128]{2,1,0:T(8,128)(2,1)} %collective-permute-done.26.refs_10_), channel_id=1, source_target_pairs={{0,8},{8,0},{16,24},{24,16},{1,9},{9,1},{17,25},{25,17},{2,10},{10... | collective-permute-start | bytes 2555912 | tf_op jit(solution)/shard_map/ppermute | solution.py:19
  312.7 37.6 %copy-start.31 = (s32[2,2]{1,0:T(2,128)S(1)}, s32[2,2]{1,0:T(2,128)}, u32[]{:S(2)}) copy-start(s32[2,2]{1,0:T(2,128)} %constant.176.clone) | copy-start | bytes 52
  312.7 37.6 %copy-start.32 = (s32[2]{0:T(128)S(1)}, s32[2]{0:T(128)}, u32[]{:S(2)}) copy-start(s32[2]{0:T(128)} %constant.178) | copy-start | bytes 28
  323.0 36.6 %collective-permute-start.25 = (bf16[1024,256]{1,0:T(8,128)(2,1)}, bf16[1024,256]{1,0:T(8,128)(2,1)}, u32[]{:S(2)}, u32[]{:S(2)}) collective-permute-start(bf16[1024,256]{1,0:T(8,128)(2,1)} %slice.131), channel_id=1, source_target_pairs={{0,4},{1,5},{2,6},{3,7},{4,0},{5,1},{6,2},{7,3},{8,12},{9,13},{10,... | collective-permute-start | bytes 1572872 | tf_op jit(solution)/shard_map/ppermute | solution.py:19
  323.8 53.7 %collective-permute-start.29 = (bf16[2,1664,128]{2,1,0:T(8,128)(2,1)S(1)}, bf16[2,1664,128]{2,1,0:T(8,128)(2,1)}, u32[]{:S(2)}, u32[]{:S(2)}) collective-permute-start(bf16[2,1664,128]{2,1,0:T(8,128)(2,1)S(1)} %copy-done.26), channel_id=1, source_target_pairs={{0,8},{8,0},{16,24},{24,16},{1,9},{9,1},{17,25},{25,17},{2,10},{10... | collective-permute-start | bytes 2555912 | tf_op jit(solution)/shard_map/ppermute | solution.py:19
  348.8 28.6 %collective-permute-start.31 = (bf16[2,1664,128]{2,1,0:T(8,128)(2,1)}, bf16[2,1664,128]{2,1,0:T(8,128)(2,1)}, u32[]{:S(2)}, u32[]{:S(2)}) collective-permute-start(bf16[2,1664,128]{2,1,0:T(8,128)(2,1)} %collective-permute-done.27.refs_11_), channel_id=1, source_target_pairs={{0,8},{8,0},{16,24},{24,16},{1,9},{9,1},{17,25},{25,17},{2,10},{10... | collective-permute-start | bytes 2555912 | tf_op jit(solution)/shard_map/ppermute | solution.py:19
  374.2 73.4 %collective-permute-start.34 = (bf16[2,32,64,256]{3,2,1,0:T(8,128)(2,1)}, bf16[2,32,64,256]{3,2,1,0:T(8,128)(2,1)S(1)}, u32[]{:S(2)}, u32[]{:S(2)}) collective-permute-start(bf16[2,32,64,256]{3,2,1,0:T(8,128)(2,1)} %get-tuple-element.71), channel_id=1, source_target_pairs={{0,8},{8,0},{16,24},{24,16},{1,9},{9,1},{17,25},{25,17},{2,10},{10... | collective-permute-start | bytes 6291464 | tf_op jit(solution)/shard_map/ppermute | solution.py:19
  375.7 73.7 %collective-permute-start.35 = (bf16[2,32,64,256]{3,2,1,0:T(8,128)(2,1)}, bf16[2,32,64,256]{3,2,1,0:T(8,128)(2,1)S(1)}, u32[]{:S(2)}, u32[]{:S(2)}) collective-permute-start(bf16[2,32,64,256]{3,2,1,0:T(8,128)(2,1)} %get-tuple-element.72), channel_id=1, source_target_pairs={{0,16},{8,24},{16,0},{24,8},{1,17},{9,25},{17,1},{25,9},{2,18},{10... | collective-permute-start | bytes 6291464 | tf_op jit(solution)/shard_map/ppermute | solution.py:19
  390.7 54.8 %collective-permute-start.32 = (bf16[1024,512]{1,0:T(8,128)(2,1)}, bf16[1024,512]{1,0:T(8,128)(2,1)S(1)}, u32[]{:S(2)}, u32[]{:S(2)}) collective-permute-start(bf16[1024,512]{1,0:T(8,128)(2,1)} %shard_map.119), channel_id=1, source_target_pairs={{0,16},{8,24},{16,0},{24,8},{1,17},{9,25},{17,1},{25,9},{2,18},{10... | collective-permute-start | bytes 3145736 | tf_op jit(solution)/shard_map/ppermute | solution.py:19
  417.4 30.1 %copy-start.11 = (bf16[2,32,64,256]{3,2,1,0:T(8,128)(2,1)S(1)}, bf16[2,32,64,256]{3,2,1,0:T(8,128)(2,1)}, u32[]{:S(2)}) copy-start(bf16[2,32,64,256]{3,2,1,0:T(8,128)(2,1)} %get-tuple-element.84) | copy-start | bytes 6291460
  447.5 23.8 %collective-permute-start.33 = (bf16[1024,256]{1,0:T(8,128)(2,1)S(1)}, bf16[1024,256]{1,0:T(8,128)(2,1)S(1)}, u32[]{:S(2)}, u32[]{:S(2)}) collective-permute-start(bf16[1024,256]{1,0:T(8,128)(2,1)S(1)} %slice.130), channel_id=1, source_target_pairs={{0,4},{1,5},{2,6},{3,7},{4,0},{5,1},{6,2},{7,3},{8,12},{9,13},{10,... | collective-permute-start | bytes 1572872 | tf_op jit(solution)/shard_map/ppermute | solution.py:19
  449.4 35.5 %collective-permute-start.36 = (bf16[1,32,64,256]{3,2,1,0:T(8,128)(2,1)}, bf16[1,32,64,256]{3,2,1,0:T(8,128)(2,1)S(1)}, u32[]{:S(2)}, u32[]{:S(2)}) collective-permute-start(bf16[1,32,64,256]{3,2,1,0:T(8,128)(2,1)} %slice.101), channel_id=1, source_target_pairs={{0,16},{8,24},{16,0},{24,8},{1,17},{9,25},{17,1},{25,9},{2,18},{10... | collective-permute-start | bytes 3145736 | tf_op jit(solution)/shard_map/ppermute | solution.py:19
  453.5 33.0 %collective-permute-start.37 = (bf16[1,32,64,256]{3,2,1,0:T(8,128)(2,1)S(1)}, bf16[1,32,64,256]{3,2,1,0:T(8,128)(2,1)}, u32[]{:S(2)}, u32[]{:S(2)}) collective-permute-start(bf16[1,32,64,256]{3,2,1,0:T(8,128)(2,1)S(1)} %slice.103), channel_id=1, source_target_pairs={{0,8},{8,0},{16,24},{24,16},{1,9},{9,1},{17,25},{25,17},{2,10},{10... | collective-permute-start | bytes 3145736 | tf_op jit(solution)/shard_map/ppermute | solution.py:19
  484.9 47.9 %collective-permute-start.39 = (bf16[2,32,64,256]{3,2,1,0:T(8,128)(2,1)}, bf16[2,32,64,256]{3,2,1,0:T(8,128)(2,1)}, u32[]{:S(2)}, u32[]{:S(2)}) collective-permute-start(bf16[2,32,64,256]{3,2,1,0:T(8,128)(2,1)} %get-tuple-element.93), channel_id=1, source_target_pairs={{0,16},{8,24},{16,0},{24,8},{1,17},{9,25},{17,1},{25,9},{2,18},{10... | collective-permute-start | bytes 6291464 | tf_op jit(solution)/shard_map/ppermute | solution.py:19
  486.5 49.3 %collective-permute-start.38 = (bf16[2,32,64,256]{3,2,1,0:T(8,128)(2,1)}, bf16[2,32,64,256]{3,2,1,0:T(8,128)(2,1)}, u32[]{:S(2)}, u32[]{:S(2)}) collective-permute-start(bf16[2,32,64,256]{3,2,1,0:T(8,128)(2,1)} %get-tuple-element.92), channel_id=1, source_target_pairs={{0,8},{8,0},{16,24},{24,16},{1,9},{9,1},{17,25},{25,17},{2,10},{10... | collective-permute-start | bytes 6291464 | tf_op jit(solution)/shard_map/ppermute | solution.py:19
  491.8 12.7 %copy-start.5 = (bf16[2,32,64,256]{3,2,1,0:T(8,128)(2,1)S(1)}, bf16[2,32,64,256]{3,2,1,0:T(8,128)(2,1)}, u32[]{:S(2)}) copy-start(bf16[2,32,64,256]{3,2,1,0:T(8,128)(2,1)} %copy-done.4) | copy-start | bytes 6291460
  504.5 28.3 %copy-start.13 = (bf16[2,32,64,256]{3,2,1,0:T(8,128)(2,1)S(1)}, bf16[2,32,64,256]{3,2,1,0:T(8,128)(2,1)}, u32[]{:S(2)}) copy-start(bf16[2,32,64,256]{3,2,1,0:T(8,128)(2,1)} %get-tuple-element.95) | copy-start | bytes 6291460
  535.8 24.3 %collective-permute-start.41 = (bf16[1,32,64,256]{3,2,1,0:T(8,128)(2,1)S(1)}, bf16[1,32,64,256]{3,2,1,0:T(8,128)(2,1)S(1)}, u32[]{:S(2)}, u32[]{:S(2)}) collective-permute-start(bf16[1,32,64,256]{3,2,1,0:T(8,128)(2,1)S(1)} %slice.107), channel_id=1, source_target_pairs={{0,8},{8,0},{16,24},{24,16},{1,9},{9,1},{17,25},{25,17},{2,10},{10... | collective-permute-start | bytes 3145736 | tf_op jit(solution)/shard_map/ppermute | solution.py:19
  540.2 24.3 %collective-permute-start.40 = (bf16[1,32,64,256]{3,2,1,0:T(8,128)(2,1)S(1)}, bf16[1,32,64,256]{3,2,1,0:T(8,128)(2,1)S(1)}, u32[]{:S(2)}, u32[]{:S(2)}) collective-permute-start(bf16[1,32,64,256]{3,2,1,0:T(8,128)(2,1)S(1)} %slice.105), channel_id=1, source_target_pairs={{0,16},{8,24},{16,0},{24,8},{1,17},{9,25},{17,1},{25,9},{2,18},{10... | collective-permute-start | bytes 3145736 | tf_op jit(solution)/shard_map/ppermute | solution.py:19
  548.7 11.8 %copy-start.14 = (bf16[64,64,256]{2,1,0:T(8,128)(2,1)S(1)}, bf16[64,64,256]{2,1,0:T(8,128)(2,1)}, u32[]{:S(2)}) copy-start(bf16[64,64,256]{2,1,0:T(8,128)(2,1)} %get-tuple-element.111) | copy-start | bytes 6291460
  565.9 15.9 %copy-start.2 = (bf16[1024,256]{1,0:T(8,128)(2,1)S(1)}, bf16[1024,256]{1,0:T(8,128)(2,1)}, u32[]{:S(2)}) copy-start(bf16[1024,256]{1,0:T(8,128)(2,1)} %fusion.29.screened_ref) | copy-start | bytes 1572868
  565.9 15.9 %copy-start.3 = (bf16[1024,256]{1,0:T(8,128)(2,1)S(1)}, bf16[1024,256]{1,0:T(8,128)(2,1)}, u32[]{:S(2)}) copy-start(bf16[1024,256]{1,0:T(8,128)(2,1)} %fusion.28.screened_ref) | copy-start | bytes 1572868
  569.3 16.1 %copy-start.7 = (bf16[32,64,256]{2,1,0:T(8,128)(2,1)S(1)}, bf16[32,64,256]{2,1,0:T(8,128)(2,1)}, u32[]{:S(2)}) copy-start(bf16[32,64,256]{2,1,0:T(8,128)(2,1)} %copy-done.6) | copy-start | bytes 3145732
  569.4 3.8 collective-permute-start.42
  573.2 3.7 collective-permute-start.43
  577.0 4.6 collective-permute-start.44
  581.8 3.7 collective-permute-start.45
  585.4 3.5 collective-permute-start.46
  (20 other events, 91.3 us)

commit v3 on v2

--- a/solution.py
+++ b/solution.py
@@ -134,11 +134,13 @@
 
 
 def contract_kernel(rb, ab, places_ref, mask_ref, screened_ref, *refs):
-    panels, outs, (held, masked, sems) = refs[:-5], refs[-5:-3], refs[-3:]
+    count = places_ref.shape[1]
+    held, masked, sems = refs[-3:]
+    panels, outs = refs[: -3 - 2 * count], refs[-3 - 2 * count : -3]
     _, tall, share, rows = held.shape
     per_share = masked.shape[1]
     each = rows // len(panels)
-    count, half = outs[0].shape[:2]
+    half = outs[0].shape[0]
     steps = [(h, i, g) for h in range(2) for i in range(count) for g in range(half // tall)]
 
     def load(k):
@@ -170,7 +172,7 @@
         for b in range(per_share):
             block = held[k % 2, :, pl.ds(b * ab, ab), :].reshape(tall * ab, rows)
             part = jnp.dot(block, masked[i % 2, b], preferred_element_type=jnp.float32)
-            outs[h][i, pl.ds(g * tall, tall), pl.ds(b * ab, ab), :] = part.astype(outs[h].dtype).reshape(
+            outs[h * count + i][pl.ds(g * tall, tall), pl.ds(b * ab, ab), :] = part.astype(outs[0].dtype).reshape(
                 tall, ab, part.shape[1]
             )
 
@@ -182,11 +184,11 @@
     width = screened.shape[1]
     in_smem, in_hbm = pl.BlockSpec(memory_space=pltpu.SMEM), pl.BlockSpec(memory_space=pl.ANY)
     in_vmem = pl.BlockSpec(memory_space=pltpu.VMEM)
-    return pl.pallas_call(
+    found = pl.pallas_call(
         functools.partial(contract_kernel, rb, ab),
         in_specs=[in_smem, in_smem, in_vmem] + [in_hbm] * len(panels),
-        out_specs=[in_vmem] * 2,
-        out_shape=[jax.ShapeDtypeStruct((count, tile // 2, share, width), jnp.bfloat16)] * 2,
+        out_specs=[in_vmem] * (2 * count),
+        out_shape=[jax.ShapeDtypeStruct((tile // 2, share, width), jnp.bfloat16)] * (2 * count),
         scratch_shapes=[
             pltpu.VMEM((2, tall, share, rows), jnp.bfloat16),
             pltpu.VMEM((2, share // ab, rows, width), jnp.bfloat16),
@@ -199,6 +201,7 @@
             transcendentals=0,
         ),
     )(places, mask, screened, *panels)
+    return [list(found[:count]), list(found[count:])]
 
 
 def scatter_sum(value, axis):
@@ -261,6 +264,7 @@
         stay = jnp.where(on_diagonal, kept, arrived[j])
         leave = jnp.where(on_diagonal, arrived[j], kept)
         came.append([stay, swap(after(leave, *others), "col", top_col)])
+        return leave
 
     row_links = {bit: Link(2) for bit in bits_below(top_row)}
 
@@ -271,21 +275,43 @@
                 found[f ^ bit] = [row_links[bit].swap(p, "row", bit) for p in parts]
         return [found[f] for f in range(top_row)]
 
+    row_links = {bit: Link(2) for bit in bits_below(top_row)}
+    gathered = []
+
+    def gather_rows(pair):
+        found = {0: pair}
+        for bit in bits_below(top_row):
+            for f, parts in list(found.items()):
+                found[f ^ bit] = [row_links[bit].swap(p, "row", bit) for p in parts]
+        gathered.append([found[f] for f in range(top_row)])
+
+    def from_row(j, side):
+        return gathered[j][-1][side]
+
     far(0)
-    gathered = [gather_rows(came[0])]
+    gather_rows(came[0])
+    turn_next(near_first)
     arrived.append(cross(crossing[1], arrived[0], near_first))
-    crossed_second = cross(other_second, crossed_first)
-    far(1, near_first, turn_next(near_first))
-    gathered.append(gather_rows(came[1]))
-    near_crossed_first = swap(after(crossed_first, near_second, arrived[1], came[0][1]), "col", low)
-    turn_next(crossed_first, *panels)
+    crossed_second = cross(other_second, crossed_first, *panels)
+    leave = far(1, near_first)
+    gather_rows(came[1])
+    turn_next(leave, *panels)
+    near_crossed_first = swap(after(crossed_first, near_second, arrived[1], came[0][1], from_row(0, 0)), "col", low)
     for j in range(2, chunks):
-        arrived.append(cross(crossing[j], *([arrived[1], near_second] if j == 2 else [crossed_second])))
-        far(j, came[j - 2][1], near_second, gathered[j - 2][-1], turn_next(arrived[j - 1], *panels))
-        gathered.append(gather_rows(came[j]))
-    near_crossed_second = swap(after(crossed_second, near_crossed_first, arrived[-1], came[1][1]), "col", low)
+        if j == 2:
+            arrived.append(cross(crossing[j], arrived[1], *panels))
+            due = [came[0][1], near_second, from_row(0, 1), from_row(1, 0)]
+        else:
+            turn_next(near_second, came[0][1], from_row(0, 0), *panels)
+            arrived.append(cross(crossing[j], crossed_second, *panels))
+            due = [came[1][1], near_crossed_first, from_row(0, 1), from_row(1, 0)]
+        far(j, *due)
+        gather_rows(came[j])
+    near_crossed_second = swap(
+        after(crossed_second, near_crossed_first, arrived[-1], came[1][1], from_row(0, 1)), "col", low
+    )
     while len(panels) < GROUPS:
-        turn_next(crossed_second, *panels)
+        turn_next(from_row(1, 1), *panels)
 
     def gather_low(found):
         link = Link(1)
@@ -307,14 +333,15 @@
     near_blocks = near_cols // rb
     near_mask = lax.dynamic_slice_in_dim(mask_near, c * near_blocks, near_blocks, 0)
     near_mask = jnp.repeat(jnp.repeat(near_mask, rb, 0), ab, 1).astype(jnp.bfloat16)
-    near = after(three_near, near_crossed_first) * near_mask[:, None, :]
+    near = three_near * near_mask[:, None, :]
     green = lax.dynamic_slice_in_dim(green_function, r * share, share, 0)
     dressed = jnp.einsum("qns,ls->nlq", near, green, preferred_element_type=jnp.float32).astype(jnp.bfloat16)
 
-    earlier = (*panels, dressed)
+    earlier = (*panels, *[pair[1] for pair in came[2:3]])
+    due, begun = [blocks[-1] for blocks in gathered[2:3]], [pair[1] for pair in came[3:4]]
     screened_chunks, contracted_chunks = [], []
     energy = jnp.zeros((tile, tile), jnp.float32)
-    hops = {bit: Link(1) for bit in bits_below(row_count)}
+    hops = {bit: Link(2) for bit in bits_below(row_count)}
     pair = min(PAIR, chunks)
     wide = pair * width
     orders = [bits_below(row_count)[::-1], bits_below(row_count)]
@@ -324,27 +351,30 @@
     for j in range(0, chunks, pair):
         sources = [[gathered[j + i][f][side] for side in range(2) for i in range(pair)] for f in range(top_row)]
         away = product(pieces_crossed, sources, after(order, *earlier), per_block, jnp.bfloat16)
-        home = product(pieces_mine, sources, after(order, away), per_block, jnp.float32)
+        home = product(pieces_mine, sources, after(order, away, *begun), per_block, jnp.float32)
         home = home + swap(away, "row", top_row).astype(jnp.float32)
         came_back = swap(home[:, wide:].astype(jnp.bfloat16), "col", top_col)
         screened = (home[:, :wide] + came_back.astype(jnp.float32)).astype(jnp.bfloat16)
         screened_chunks.append(screened)
 
-        gone = list(contract(panels, screened, panel_mask, places ^ first_bits, rb, ab, share))
-        stay = list(contract(panels, screened, panel_mask, after(places, gone), rb, ab, share))
-        earlier = (home, *gone)
-        left, halves = [kept[h] for h in range(2)], []
+        gone = contract(panels, screened, panel_mask, after(places ^ first_bits, due), rb, ab, share)
+        stay = contract(panels, screened, panel_mask, after(places, gone), rb, ab, share)
+        earlier, due, begun = (home, *gone[0], *gone[1]), [], []
+        left = [[dict(zip(kept[h], part[h])) for part in (gone, stay)] for h in range(2)]
         for hop in range(len(orders[0])):
             for h, bits in enumerate(orders):
-                total = stay[h].astype(jnp.float32) + hops[bits[hop]].swap(gone[h], "row", bits[hop]).astype(jnp.float32)
-                total = total.astype(jnp.bfloat16)
-                if hop + 1 < len(bits):
-                    staying = [e for e in left[h] if not e & bits[hop + 1]]
-                    gone[h] = jnp.stack([total[left[h].index(e | bits[hop + 1])] for e in staying])
-                    stay[h] = jnp.stack([total[left[h].index(e)] for e in staying])
-                    left[h] = staying
-                else:
-                    halves.append(total[0])
+                going, staying = left[h]
+                next_bit = bits[hop + 1] if hop + 1 < len(bits) else 0
+                total = {}
+                for e in sorted(going, key=lambda e: -(e & next_bit)):
+                    value = hops[bits[hop]].swap(going[e], "row", bits[hop])
+                    begun += [value] if not hop and e & next_bit else []
+                    total[e] = (staying[e].astype(jnp.float32) + value.astype(jnp.float32)).astype(jnp.bfloat16)
+                left[h] = [
+                    {e & ~next_bit: value for e, value in total.items() if e & next_bit},
+                    {e: value for e, value in total.items() if not e & next_bit},
+                ]
+        halves = [left[h][1][0] for h in range(2)]
         contracted_chunks.append(jnp.concatenate(halves))
         parts = [
             jnp.einsum("mlq,nlq->mn", half, dressed[:, :, j * width : j * width + wide], preferred_element_type=jnp.float32)

time: 594 us -> 576 us (0.970)
  waiting for transfers between devices: 290 us -> 277 us
  local copies, waits for them, and re-layouts: 28.9 us -> 21.6 us
    ppermute x47 -> x51, waiting for transfers between devices: 290 us -> 277 us  [swap(): return lax.ppermute(value, axis, [(i, i ^ bit) for i in range(size)])]
    ppermute x47 -> x51, starting transfers between devices: 44.6 us -> 48.4 us  [swap(): return lax.ppermute(value, axis, [(i, i ^ bit) for i in range(size)])]
  transfers between devices with their start and end apart: 47 -> 51, of which waited for: 22 -> 23; matrix products, arithmetic and copies ran while one was open for 15% -> 14% of each run, Pallas kernels for 25% -> 26%
where the time goes in v3:
time: 576 us; the launch traced here: 572 us
  waiting for transfers between devices  277 us (48%)
  Pallas kernels  148 us (26%)
  starting transfers between devices  48.4 us (8%)
  other arithmetic  42 us (7%)
  matrix products  33.4 us (6%)
  local copies, waits for them, and re-layouts  21.6 us (4%)
    ppermute x51, waiting for transfers between devices, swap(): return lax.ppermute(value, axis, [(i, i ^ bit) for i in range(size)])  277 us
    pallas_call x4, Pallas kernels, product(): pl.pallas_call(functools.partial(product_kernel, count, parts, per_block)...  53.8 us
    pallas_call x4, Pallas kernels, contract(): pl.pallas_call(functools.partial(contract_kernel, rb, ab), in_specs=[in_s...  50.7 us
    ppermute x51, starting transfers between devices, swap(): return lax.ppermute(value, axis, [(i, i ^ bit) for i in range(size)])  48.4 us
    pallas_call x4, Pallas kernels, turn(): pl.pallas_call(turn_kernel, grid=(rows // wide, tile // tall), in_specs=[...  43.1 us
    dot_general x1, matrix products, per_device(): jnp.einsum('qns,ls->nlq', near, green, preferred_element_type=jnp.float32)  19.4 us
    dot_general x4, matrix products, per_device(): jnp.einsum('mlq,nlq->mn', half, dressed[:, :, j * width:j * width + wide]...  14.1 us
    mul x1, other arithmetic, per_device(): near = three_near * near_mask[:, None, :]  13.8 us
  transfers between devices with their start and end apart: 51, of which 23 were waited for; matrix products, arithmetic and copies ran while one was open for 14% of the time, Pallas kernels for 26%

profile of v3, /device:TPU:0, one launch (start us, length us, event | category | flops | bytes accessed | tf_op | source)
XLA Modules:
  0.0 571.9 jit_solution(12237854362096495836)
XLA Ops:
  0.7 3.5 dynamic-slice_bitcast_fusion
  4.2 2.1 fusion.44
  6.2 3.0 collective-permute-start.1
  9.2 5.4 fusion.42
  15.8 1.6 collective-permute-start
  17.4 11.0 %collective-permute-done.1 = bf16[2,1664,128]{2,1,0:T(8,128)(2,1)} collective-permute-done((bf16[2,1664,128]{2,1,0:T(8,128)(2,1)}, bf16[2,1664,128]{2,1,0:T(8,128)(2,1)}, u32[]{:S(2)}, u32[]{:S(2)}) %collective-permute-start.1) | collective-permute-done | bytes 852000 | tf_op jit(solution)/shard_map/ppermute | solution.py:19
  28.4 1.7 collective-permute-start.12
  30.2 24.4 %collective-permute-done.refs_4_ = bf16[512,1664]{1,0:T(8,128)(2,1)} collective-permute-done((bf16[512,1664]{1,0:T(8,128)(2,1)S(1)}, bf16[512,1664]{1,0:T(8,128)(2,1)}, u32[]{:S(2)}, u32[]{:S(2)}) %collective-permute-start) | collective-permute-done | bytes 1703968 | tf_op jit(solution)/shard_map/ppermute | solution.py:19
  54.6 1.6 collective-permute-start.3
  56.2 2.2 broadcast_select_fusion.5
  58.4 2.6 collective-permute-start.4
  62.5 10.8 %shard_map.112.refs_0_ = bf16[64,256,256]{2,1,0:T(8,128)(2,1)} custom-call(bf16[1024,64,256]{2,1,0:T(8,128)(2,1)} %panel_ref.3), custom_call_target="tpu_custom_call" | custom-call | bytes 16777216 | tf_op jit(solution)/shard_map/pallas_call | solution.py:125
  73.8 1.5 collective-permute-start.13
  75.3 34.7 %collective-permute-done.4.refs_10_ = bf16[2,1664,128]{2,1,0:T(8,128)(2,1)} collective-permute-done((bf16[2,1664,128]{2,1,0:T(8,128)(2,1)}, bf16[2,1664,128]{2,1,0:T(8,128)(2,1)}, u32[]{:S(2)}, u32[]{:S(2)}) %collective-permute-start.4) | collective-permute-done | bytes 852000 | tf_op jit(solution)/shard_map/ppermute | solution.py:19
  110.9 2.7 collective-permute-start.16
  116.1 11.0 %shard_map.113.refs_1_ = bf16[64,256,256]{2,1,0:T(8,128)(2,1)} custom-call(bf16[1024,64,256]{2,1,0:T(8,128)(2,1)} %panel_ref.3), custom_call_target="tpu_custom_call" | custom-call | bytes 16777216 | tf_op jit(solution)/shard_map/pallas_call | solution.py:125
  128.6 10.6 %shard_map.114.refs_2_ = bf16[64,256,256]{2,1,0:T(8,128)(2,1)} custom-call(bf16[1024,64,256]{2,1,0:T(8,128)(2,1)} %panel_ref.3), custom_call_target="tpu_custom_call" | custom-call | bytes 16777216 | tf_op jit(solution)/shard_map/pallas_call | solution.py:125
  139.7 27.1 %collective-permute-done.6.refs_11_ = bf16[2,1664,128]{2,1,0:T(8,128)(2,1)} collective-permute-done((bf16[2,1664,128]{2,1,0:T(8,128)(2,1)}, bf16[2,1664,128]{2,1,0:T(8,128)(2,1)}, u32[]{:S(2)}, u32[]{:S(2)}) %collective-permute-start.6) | collective-permute-done | bytes 852000 | tf_op jit(solution)/shard_map/ppermute | solution.py:19
  167.3 1.7 collective-permute-start.18
  171.5 14.8 %collective-permute-done.9 = bf16[2,1664,128]{2,1,0:T(8,128)(2,1)S(1)} collective-permute-done((bf16[2,1664,128]{2,1,0:T(8,128)(2,1)S(1)}, bf16[2,1664,128]{2,1,0:T(8,128)(2,1)S(1)}, u32[]{:S(2)}, u32[]{:S(2)}) %collective-permute-start.9) | collective-permute-done | bytes 852000 | tf_op jit(solution)/shard_map/ppermute | solution.py:19
  186.3 5.0 collective-permute-done.10.refs_13_
  192.3 11.5 %collective-permute-done.18.refs_5_ = bf16[512,1664]{1,0:T(8,128)(2,1)} collective-permute-done((bf16[512,1664]{1,0:T(8,128)(2,1)}, bf16[512,1664]{1,0:T(8,128)(2,1)}, u32[]{:S(2)}, u32[]{:S(2)}) %collective-permute-start.18) | collective-permute-done | bytes 1703968 | tf_op jit(solution)/shard_map/ppermute | solution.py:19
  205.1 2.4 collective-permute-start.11
  207.5 2.5 broadcast_select_fusion
  210.0 35.9 %collective-permute-done.11.refs_10_ = bf16[2,1664,128]{2,1,0:T(8,128)(2,1)} collective-permute-done((bf16[2,1664,128]{2,1,0:T(8,128)(2,1)}, bf16[2,1664,128]{2,1,0:T(8,128)(2,1)}, u32[]{:S(2)}, u32[]{:S(2)}) %collective-permute-start.11) | collective-permute-done | bytes 852000 | tf_op jit(solution)/shard_map/ppermute | solution.py:19
  247.0 10.8 %shard_map.115.refs_3_ = bf16[64,256,256]{2,1,0:T(8,128)(2,1)} custom-call(bf16[1024,64,256]{2,1,0:T(8,128)(2,1)} %panel_ref.3), custom_call_target="tpu_custom_call" | custom-call | bytes 16777216 | tf_op jit(solution)/shard_map/pallas_call | solution.py:125
  258.8 13.2 %shard_map.116 = bf16[1024,512]{1,0:T(8,128)(2,1)} custom-call(s32[4]{0:T(128)} %fusion.41.order_ref, bf16[512,1664]{1,0:T(8,128)(2,1)} %collective-permute-done.12.refs_0_, bf16[512,1664]{1,0:T(8,128)(2,1)} %collective-permute-done.13.refs_1_, bf16[512,1664]{1,0:T(8,128)(2,1)} %collective-permute-done.14.refs_2_, ...), custom_call_target="tpu_custom_call" | custom-call | flops 6979321856 | bytes 22544384 | tf_op jit(solution)/shard_map/pallas_call | solution.py:96
  272.0 14.0 %collective-permute-done.21.refs_11_ = bf16[2,1664,128]{2,1,0:T(8,128)(2,1)} collective-permute-done((bf16[2,1664,128]{2,1,0:T(8,128)(2,1)}, bf16[2,1664,128]{2,1,0:T(8,128)(2,1)}, u32[]{:S(2)}, u32[]{:S(2)}) %collective-permute-start.21) | collective-permute-done | bytes 852000 | tf_op jit(solution)/shard_map/ppermute | solution.py:19
  286.0 13.8 %broadcast_multiply_fusion = bf16[512,64,256]{2,1,0:T(8,128)(2,1)} fusion(bf16[512,64,256]{2,1,0:T(8,128)(2,1)} %param.12, bf16[512,256]{1,0:T(8,128)(2,1)S(1)} %copy.28), kind=kLoop, calls=%fused_computation.2 | loop fusion | flops 8388608 | bytes 33816576 | tf_op jit(solution)/shard_map/mul | solution.py:336
  301.8 13.6 %shard_map.117 = f32[1024,512]{1,0:T(8,128)} custom-call(s32[4]{0:T(128)} %fusion.41.order_ref, bf16[512,1664]{1,0:T(8,128)(2,1)} %copy-done.9, bf16[512,1664]{1,0:T(8,128)(2,1)} %get-tuple-element.65.refs_1_, bf16[512,1664]{1,0:T(8,128)(2,1)} %collective-permute-done.22.refs_2_, bf16[512,1664]{1,0:T(8,128)(2,1)} %collective-permute-done.23.refs_3_, ...), custom_call_target="tpu_custom_call" | custom-call | flops 6979321856 | bytes 22544384 | tf_op jit(solution)/shard_map/pallas_call | solution.py:96
  315.4 1.9 convert_add_fusion.1
  318.3 19.4 %convert_bitcast_fusion = bf16[64,64,512]{2,1,0:T(8,128)(2,1)} fusion(bf16[512,64,256]{2,1,0:T(8,128)(2,1)} %broadcast_multiply_fusion, bf16[256,256]{1,0:T(8,128)(2,1)S(1)} %copy-done, s32[]{:T(128)S(6)} %select_n.167), kind=kOutput, calls=%fused_computation.4 | convolution fusion | flops 1075838976 | bytes 21004292 | tf_op jit(solution)/shard_map/qns,ls->nlq/dot_general | solution.py:338
  338.4 1.6 collective-permute-start.30
  342.7 2.0 fusion.25.screened_ref
  344.7 12.6 %shard_map.118 = (bf16[32,64,256]{2,1,0:T(8,128)(2,1)}, bf16[32,64,256]{2,1,0:T(8,128)(2,1)}, bf16[32,64,256]{2,1,0:T(8,128)(2,1)}, bf16[32,64,256]{2,1,0:T(8,128)(2,1)}) custom-call(s32[2,2]{1,0:T(2,128)} %get-tuple-element.86.places_ref, s32[16,8]{1,0:T(8,128)} %copy.42.mask_ref, bf16[1024,256]{1,0:T(8,128)(2,1)} %fusion.25.screened_ref, ...), custom_call_target="tpu_custom_call" | custom-call | flops 4294967296 | bytes 20971520 | tf_op jit(solution)/shard_map/pallas_call | solution.py:187
  358.7 1.7 collective-permute-start.33
  361.9 16.6 %collective-permute-done.31.refs_15_ = bf16[2,1664,128]{2,1,0:T(8,128)(2,1)S(1)} collective-permute-done((bf16[2,1664,128]{2,1,0:T(8,128)(2,1)}, bf16[2,1664,128]{2,1,0:T(8,128)(2,1)S(1)}, u32[]{:S(2)}, u32[]{:S(2)}) %collective-permute-start.31) | collective-permute-done | bytes 852000 | tf_op jit(solution)/shard_map/ppermute | solution.py:19
  379.5 13.3 %shard_map.119 = bf16[1024,512]{1,0:T(8,128)(2,1)} custom-call(s32[4]{0:T(128)} %fusion.41.order_ref, bf16[512,1664]{1,0:T(8,128)(2,1)} %collective-permute-done.12.refs_0_, bf16[512,1664]{1,0:T(8,128)(2,1)} %collective-permute-done.13.refs_1_, bf16[512,1664]{1,0:T(8,128)(2,1)} %collective-permute-done.14.refs_2_, ...), custom_call_target="tpu_custom_call" | custom-call | flops 6979321856 | bytes 22544384 | tf_op jit(solution)/shard_map/pallas_call | solution.py:96
  392.8 2.1 collective-permute-start.34
  394.9 12.5 %shard_map.121 = (bf16[32,64,256]{2,1,0:T(8,128)(2,1)}, bf16[32,64,256]{2,1,0:T(8,128)(2,1)}, bf16[32,64,256]{2,1,0:T(8,128)(2,1)}, bf16[32,64,256]{2,1,0:T(8,128)(2,1)}) custom-call(s32[2,2]{1,0:T(2,128)} %get-tuple-element.95.places_ref, s32[16,8]{1,0:T(8,128)} %copy.42.mask_ref, bf16[1024,256]{1,0:T(8,128)(2,1)} %fusion.25.screened_ref, ...), custom_call_target="tpu_custom_call" | custom-call | flops 4294967296 | bytes 20971520 | tf_op jit(solution)/shard_map/pallas_call | solution.py:187
  407.4 13.7 %shard_map.120 = f32[1024,512]{1,0:T(8,128)} custom-call(s32[4]{0:T(128)} %fusion.41.order_ref, bf16[512,1664]{1,0:T(8,128)(2,1)} %copy-done.9, bf16[512,1664]{1,0:T(8,128)(2,1)} %get-tuple-element.65.refs_1_, bf16[512,1664]{1,0:T(8,128)(2,1)} %collective-permute-done.22.refs_2_, bf16[512,1664]{1,0:T(8,128)(2,1)} %collective-permute-done.23.refs_3_, ...), custom_call_target="tpu_custom_call" | custom-call | flops 6979321856 | bytes 22544384 | tf_op jit(solution)/shard_map/pallas_call | solution.py:96
  421.1 7.6 %collective-permute-done.34 = bf16[1024,512]{1,0:T(8,128)(2,1)S(1)} collective-permute-done((bf16[1024,512]{1,0:T(8,128)(2,1)}, bf16[1024,512]{1,0:T(8,128)(2,1)S(1)}, u32[]{:S(2)}, u32[]{:S(2)}) %collective-permute-start.34) | collective-permute-done | bytes 1048608 | tf_op jit(solution)/shard_map/ppermute | solution.py:19
  428.7 1.9 convert_add_fusion
  431.2 1.8 collective-permute-start.37
  434.1 21.3 %collective-permute-done.35 = bf16[1024,256]{1,0:T(8,128)(2,1)S(1)} collective-permute-done((bf16[1024,256]{1,0:T(8,128)(2,1)S(1)}, bf16[1024,256]{1,0:T(8,128)(2,1)S(1)}, u32[]{:S(2)}, u32[]{:S(2)}) %collective-permute-start.35) | collective-permute-done | bytes 524320 | tf_op jit(solution)/shard_map/ppermute | solution.py:19
  456.4 12.9 %shard_map.122 = (bf16[32,64,256]{2,1,0:T(8,128)(2,1)}, bf16[32,64,256]{2,1,0:T(8,128)(2,1)}, bf16[32,64,256]{2,1,0:T(8,128)(2,1)}, bf16[32,64,256]{2,1,0:T(8,128)(2,1)}) custom-call(s32[2,2]{1,0:T(2,128)} %get-tuple-element.86.places_ref, s32[16,8]{1,0:T(8,128)} %copy.42.mask_ref, bf16[1024,256]{1,0:T(8,128)(2,1)} %fusion.24.screened_ref, ...), custom_call_target="tpu_custom_call" | custom-call | flops 4294967296 | bytes 20971520 | tf_op jit(solution)/shard_map/pallas_call | solution.py:187
  469.3 1.8 collective-permute-start.42
  472.8 2.6 fusion.43
  475.4 12.7 %shard_map.123 = (bf16[32,64,256]{2,1,0:T(8,128)(2,1)}, bf16[32,64,256]{2,1,0:T(8,128)(2,1)}, bf16[32,64,256]{2,1,0:T(8,128)(2,1)}, bf16[32,64,256]{2,1,0:T(8,128)(2,1)}) custom-call(s32[2,2]{1,0:T(2,128)} %get-tuple-element.95.places_ref, s32[16,8]{1,0:T(8,128)} %copy.42.mask_ref, bf16[1024,256]{1,0:T(8,128)(2,1)} %fusion.24.screened_ref, ...), custom_call_target="tpu_custom_call" | custom-call | flops 4294967296 | bytes 20971520 | tf_op jit(solution)/shard_map/pallas_call | solution.py:187
  489.8 2.2 add_convert_fusion.6
  492.0 3.7 collective-permute-done.42
  495.7 1.6 add_convert_fusion.1
  499.1 1.9 add_convert_fusion.9
  502.6 3.5 fusion.15
  506.0 3.7 fusion.12
  509.8 8.3 %collective-permute-done.44 = bf16[32,64,256]{2,1,0:T(8,128)(2,1)S(1)} collective-permute-done((bf16[32,64,256]{2,1,0:T(8,128)(2,1)}, bf16[32,64,256]{2,1,0:T(8,128)(2,1)S(1)}, u32[]{:S(2)}, u32[]{:S(2)}) %collective-permute-start.44) | collective-permute-done | bytes 1048608 | tf_op jit(solution)/shard_map/ppermute | solution.py:19
  518.1 24.0 %collective-permute-done.45 = bf16[32,64,256]{2,1,0:T(8,128)(2,1)S(1)} collective-permute-done((bf16[32,64,256]{2,1,0:T(8,128)(2,1)S(1)}, bf16[32,64,256]{2,1,0:T(8,128)(2,1)S(1)}, u32[]{:S(2)}, u32[]{:S(2)}) %collective-permute-start.45) | collective-permute-done | bytes 1048608 | tf_op jit(solution)/shard_map/ppermute | solution.py:19
  543.7 3.5 fusion.21
  547.8 3.5 fusion.18
  551.7 3.4 collective-permute-done.46
  555.9 2.9 collective-permute-done.47
  559.1 4.5 collective-permute-done.48
  564.9 2.5 collective-permute-done.49
  567.4 3.5 maximum_bitcast_fusion
  (176 shorter events, 41.1 us)
Async XLA Ops:
  0.6 317.7 %copy-start = (bf16[256,256]{1,0:T(8,128)(2,1)S(1)}, bf16[256,256]{1,0:T(8,128)(2,1)}, u32[]{:S(2)}) copy-start(bf16[256,256]{1,0:T(8,128)(2,1)} %param.13) | copy-start | bytes 393220
  6.2 22.2 %collective-permute-start.1 = (bf16[2,1664,128]{2,1,0:T(8,128)(2,1)}, bf16[2,1664,128]{2,1,0:T(8,128)(2,1)}, u32[]{:S(2)}, u32[]{:S(2)}) collective-permute-start(bf16[2,1664,128]{2,1,0:T(8,128)(2,1)} %get-tuple-element.136), channel_id=1, source_target_pairs={{0,16},{8,24},{16,0},{24,8},{1,17},{9,25},{17,1},{25,9},{2,18},{10... | collective-permute-start | bytes 2555912 | tf_op jit(solution)/shard_map/ppermute | solution.py:19
  15.8 38.8 %collective-permute-start = (bf16[512,1664]{1,0:T(8,128)(2,1)S(1)}, bf16[512,1664]{1,0:T(8,128)(2,1)}, u32[]{:S(2)}, u32[]{:S(2)}) collective-permute-start(bf16[512,1664]{1,0:T(8,128)(2,1)S(1)} %get-tuple-element.119.refs_0_), channel_id=1, source_target_pairs={{0,2},{1,3},{2,0},{3,1},{4,6},{5,7},{6,4},{7,5},{8,10},{9,11},{10,... | collective-permute-start | bytes 5111816 | tf_op jit(solution)/shard_map/ppermute | solution.py:19
  28.4 45.4 %collective-permute-start.12 = (bf16[512,1664]{1,0:T(8,128)(2,1)}, bf16[512,1664]{1,0:T(8,128)(2,1)}, u32[]{:S(2)}, u32[]{:S(2)}) collective-permute-start(bf16[512,1664]{1,0:T(8,128)(2,1)} %get-tuple-element.76), channel_id=1, source_target_pairs={{0,16},{8,24},{16,0},{24,8},{1,17},{9,25},{17,1},{25,9},{2,18},{10... | collective-permute-start | bytes 5111816 | tf_op jit(solution)/shard_map/ppermute | solution.py:19
  54.6 56.3 %collective-permute-start.3 = (bf16[512,1664]{1,0:T(8,128)(2,1)}, bf16[512,1664]{1,0:T(8,128)(2,1)}, u32[]{:S(2)}, u32[]{:S(2)}) collective-permute-start(bf16[512,1664]{1,0:T(8,128)(2,1)} %get-tuple-element.65.refs_1_), channel_id=1, source_target_pairs={{0,2},{1,3},{2,0},{3,1},{4,6},{5,7},{6,4},{7,5},{8,10},{9,11},{10,... | collective-permute-start | bytes 5111816 | tf_op jit(solution)/shard_map/ppermute | solution.py:19
  58.4 51.7 %collective-permute-start.4 = (bf16[2,1664,128]{2,1,0:T(8,128)(2,1)}, bf16[2,1664,128]{2,1,0:T(8,128)(2,1)}, u32[]{:S(2)}, u32[]{:S(2)}) collective-permute-start(bf16[2,1664,128]{2,1,0:T(8,128)(2,1)} %get-tuple-element.130), channel_id=1, source_target_pairs={{0,4},{1,5},{2,6},{3,7},{4,0},{5,1},{6,2},{7,3},{8,12},{9,13},{10,... | collective-permute-start | bytes 2555912 | tf_op jit(solution)/shard_map/ppermute | solution.py:19
  61.0 49.1 %collective-permute-start.5 = (bf16[2,1664,128]{2,1,0:T(8,128)(2,1)S(1)}, bf16[2,1664,128]{2,1,0:T(8,128)(2,1)}, u32[]{:S(2)}, u32[]{:S(2)}) collective-permute-start(bf16[2,1664,128]{2,1,0:T(8,128)(2,1)S(1)} %get-tuple-element.129.refs_8_), channel_id=1, source_target_pairs={{0,8},{8,0},{16,24},{24,16},{1,9},{9,1},{17,25},{25,17},{2,10},{10... | collective-permute-start | bytes 2555912 | tf_op jit(solution)/shard_map/ppermute | solution.py:19
  73.3 36.7 %collective-permute-start.2 = (bf16[2,1664,128]{2,1,0:T(8,128)(2,1)S(1)}, bf16[2,1664,128]{2,1,0:T(8,128)(2,1)S(1)}, u32[]{:S(2)}, u32[]{:S(2)}) collective-permute-start(bf16[2,1664,128]{2,1,0:T(8,128)(2,1)S(1)} %copy-done.27), channel_id=1, source_target_pairs={{0,16},{8,24},{16,0},{24,8},{1,17},{9,25},{17,1},{25,9},{2,18},{10... | collective-permute-start | bytes 2555912 | tf_op jit(solution)/shard_map/ppermute | solution.py:19
  73.8 65.4 %collective-permute-start.13 = (bf16[512,1664]{1,0:T(8,128)(2,1)S(1)}, bf16[512,1664]{1,0:T(8,128)(2,1)}, u32[]{:S(2)}, u32[]{:S(2)}) collective-permute-start(bf16[512,1664]{1,0:T(8,128)(2,1)S(1)} %copy-done.11), channel_id=1, source_target_pairs={{0,16},{8,24},{16,0},{24,8},{1,17},{9,25},{17,1},{25,9},{2,18},{10... | collective-permute-start | bytes 5111816 | tf_op jit(solution)/shard_map/ppermute | solution.py:19
  110.9 56.3 %collective-permute-start.16 = (bf16[512,1664]{1,0:T(8,128)(2,1)}, bf16[512,1664]{1,0:T(8,128)(2,1)}, u32[]{:S(2)}, u32[]{:S(2)}) collective-permute-start(bf16[512,1664]{1,0:T(8,128)(2,1)} %collective-permute-done.12.refs_0_), channel_id=1, source_target_pairs={{0,2},{1,3},{2,0},{3,1},{4,6},{5,7},{6,4},{7,5},{8,10},{9,11},{10,... | collective-permute-start | bytes 5111816 | tf_op jit(solution)/shard_map/ppermute | solution.py:19
  113.6 26.1 %collective-permute-start.7 = (bf16[2,1664,128]{2,1,0:T(8,128)(2,1)}, bf16[2,1664,128]{2,1,0:T(8,128)(2,1)}, u32[]{:S(2)}, u32[]{:S(2)}) collective-permute-start(bf16[2,1664,128]{2,1,0:T(8,128)(2,1)} %collective-permute-done.4.refs_10_), channel_id=1, source_target_pairs={{0,8},{8,0},{16,24},{24,16},{1,9},{9,1},{17,25},{25,17},{2,10},{10... | collective-permute-start | bytes 2555912 | tf_op jit(solution)/shard_map/ppermute | solution.py:19
  116.1 53.3 %copy-start.24 = (bf16[2,1664,128]{2,1,0:T(8,128)(2,1)}, bf16[2,1664,128]{2,1,0:T(8,128)(2,1)S(1)}, u32[]{:S(2)}) copy-start(bf16[2,1664,128]{2,1,0:T(8,128)(2,1)S(1)} %get-tuple-element.73.refs_9_) | copy-start | bytes 2555908
  127.1 41.9 %copy-start.25 = (bf16[2,1664,128]{2,1,0:T(8,128)(2,1)S(1)}, bf16[2,1664,128]{2,1,0:T(8,128)(2,1)}, u32[]{:S(2)}) copy-start(bf16[2,1664,128]{2,1,0:T(8,128)(2,1)} %get-tuple-element.71) | copy-start | bytes 2555908
  127.1 39.7 %collective-permute-start.6 = (bf16[2,1664,128]{2,1,0:T(8,128)(2,1)}, bf16[2,1664,128]{2,1,0:T(8,128)(2,1)}, u32[]{:S(2)}, u32[]{:S(2)}) collective-permute-start(bf16[2,1664,128]{2,1,0:T(8,128)(2,1)} %get-tuple-element.68), channel_id=1, source_target_pairs={{0,4},{1,5},{2,6},{3,7},{4,0},{5,1},{6,2},{7,3},{8,12},{9,13},{10,... | collective-permute-start | bytes 2555912 | tf_op jit(solution)/shard_map/ppermute | solution.py:19
  139.2 28.1 %collective-permute-start.17 = (bf16[2,1664,128]{2,1,0:T(8,128)(2,1)S(1)}, bf16[2,1664,128]{2,1,0:T(8,128)(2,1)S(1)}, u32[]{:S(2)}, u32[]{:S(2)}) collective-permute-start(bf16[2,1664,128]{2,1,0:T(8,128)(2,1)S(1)} %copy-done.26), channel_id=1, source_target_pairs={{0,16},{8,24},{16,0},{24,8},{1,17},{9,25},{17,1},{25,9},{2,18},{10... | collective-permute-start | bytes 2555912 | tf_op jit(solution)/shard_map/ppermute | solution.py:19
  167.3 24.1 %copy-start.28 = (bf16[2,1664,128]{2,1,0:T(8,128)(2,1)}, bf16[2,1664,128]{2,1,0:T(8,128)(2,1)S(1)}, u32[]{:S(2)}) copy-start(bf16[2,1664,128]{2,1,0:T(8,128)(2,1)S(1)} %collective-permute-done.17) | copy-start | bytes 2555908
  167.3 36.5 %collective-permute-start.18 = (bf16[512,1664]{1,0:T(8,128)(2,1)}, bf16[512,1664]{1,0:T(8,128)(2,1)}, u32[]{:S(2)}, u32[]{:S(2)}) collective-permute-start(bf16[512,1664]{1,0:T(8,128)(2,1)} %collective-permute-done.13.refs_1_), channel_id=1, source_target_pairs={{0,2},{1,3},{2,0},{3,1},{4,6},{5,7},{6,4},{7,5},{8,10},{9,11},{10,... | collective-permute-start | bytes 5111816 | tf_op jit(solution)/shard_map/ppermute | solution.py:19
  169.0 17.4 %collective-permute-start.9 = (bf16[2,1664,128]{2,1,0:T(8,128)(2,1)S(1)}, bf16[2,1664,128]{2,1,0:T(8,128)(2,1)S(1)}, u32[]{:S(2)}, u32[]{:S(2)}) collective-permute-start(bf16[2,1664,128]{2,1,0:T(8,128)(2,1)S(1)} %copy-done.25), channel_id=1, source_target_pairs={{0,16},{8,24},{16,0},{24,8},{1,17},{9,25},{17,1},{25,9},{2,18},{10... | collective-permute-start | bytes 2555912 | tf_op jit(solution)/shard_map/ppermute | solution.py:19
  169.5 21.9 %collective-permute-start.10 = (bf16[2,1664,128]{2,1,0:T(8,128)(2,1)S(1)}, bf16[2,1664,128]{2,1,0:T(8,128)(2,1)S(1)}, u32[]{:S(2)}, u32[]{:S(2)}) collective-permute-start(bf16[2,1664,128]{2,1,0:T(8,128)(2,1)S(1)} %get-tuple-element.73.refs_9_), channel_id=1, source_target_pairs={{0,8},{8,0},{16,24},{24,16},{1,9},{9,1},{17,25},{25,17},{2,10},{10... | collective-permute-start | bytes 2555912 | tf_op jit(solution)/shard_map/ppermute | solution.py:19
  171.0 34.1 %collective-permute-start.8 = (bf16[2,1664,128]{2,1,0:T(8,128)(2,1)}, bf16[2,1664,128]{2,1,0:T(8,128)(2,1)}, u32[]{:S(2)}, u32[]{:S(2)}) collective-permute-start(bf16[2,1664,128]{2,1,0:T(8,128)(2,1)} %collective-permute-done.6.refs_11_), channel_id=1, source_target_pairs={{0,8},{8,0},{16,24},{24,16},{1,9},{9,1},{17,25},{25,17},{2,10},{10... | collective-permute-start | bytes 2555912 | tf_op jit(solution)/shard_map/ppermute | solution.py:19
  171.5 86.2 %collective-permute-start.14 = (bf16[512,1664]{1,0:T(8,128)(2,1)}, bf16[512,1664]{1,0:T(8,128)(2,1)}, u32[]{:S(2)}, u32[]{:S(2)}) collective-permute-start(bf16[512,1664]{1,0:T(8,128)(2,1)} %collective-permute-done.12.refs_0_), channel_id=1, source_target_pairs={{0,1},{1,0},{2,3},{3,2},{4,5},{5,4},{6,7},{7,6},{8,9},{9,8},{10,11... | collective-permute-start | bytes 5111816 | tf_op jit(solution)/shard_map/ppermute | solution.py:19
  186.3 71.4 %collective-permute-start.15 = (bf16[512,1664]{1,0:T(8,128)(2,1)}, bf16[512,1664]{1,0:T(8,128)(2,1)}, u32[]{:S(2)}, u32[]{:S(2)}) collective-permute-start(bf16[512,1664]{1,0:T(8,128)(2,1)} %collective-permute-done.13.refs_1_), channel_id=1, source_target_pairs={{0,1},{1,0},{2,3},{3,2},{4,5},{5,4},{6,7},{7,6},{8,9},{9,8},{10,11... | collective-permute-start | bytes 5111816 | tf_op jit(solution)/shard_map/ppermute | solution.py:19
  191.4 66.9 %collective-permute-start.19 = (bf16[512,1664]{1,0:T(8,128)(2,1)}, bf16[512,1664]{1,0:T(8,128)(2,1)}, u32[]{:S(2)}, u32[]{:S(2)}) collective-permute-start(bf16[512,1664]{1,0:T(8,128)(2,1)} %collective-permute-done.16.refs_4_), channel_id=1, source_target_pairs={{0,1},{1,0},{2,3},{3,2},{4,5},{5,4},{6,7},{7,6},{8,9},{9,8},{10,11... | collective-permute-start | bytes 5111816 | tf_op jit(solution)/shard_map/ppermute | solution.py:19
  203.8 54.6 %collective-permute-start.20 = (bf16[512,1664]{1,0:T(8,128)(2,1)}, bf16[512,1664]{1,0:T(8,128)(2,1)}, u32[]{:S(2)}, u32[]{:S(2)}) collective-permute-start(bf16[512,1664]{1,0:T(8,128)(2,1)} %collective-permute-done.18.refs_5_), channel_id=1, source_target_pairs={{0,1},{1,0},{2,3},{3,2},{4,5},{5,4},{6,7},{7,6},{8,9},{9,8},{10,11... | collective-permute-start | bytes 5111816 | tf_op jit(solution)/shard_map/ppermute | solution.py:19
  205.1 40.8 %copy-start.30 = (s32[64,8]{0,1:T(8,128)S(1)}, s32[64,8]{0,1:T(8,128)}, u32[]{:S(2)}) copy-start(s32[64,8]{0,1:T(8,128)} %param.15) | copy-start | bytes 6148
  205.1 40.8 %collective-permute-start.11 = (bf16[2,1664,128]{2,1,0:T(8,128)(2,1)}, bf16[2,1664,128]{2,1,0:T(8,128)(2,1)}, u32[]{:S(2)}, u32[]{:S(2)}) collective-permute-start(bf16[2,1664,128]{2,1,0:T(8,128)(2,1)} %get-tuple-element.74), channel_id=1, source_target_pairs={{0,4},{1,5},{2,6},{3,7},{4,0},{5,1},{6,2},{7,3},{8,12},{9,13},{10,... | collective-permute-start | bytes 2555912 | tf_op jit(solution)/shard_map/ppermute | solution.py:19
  245.9 40.0 %collective-permute-start.21 = (bf16[2,1664,128]{2,1,0:T(8,128)(2,1)}, bf16[2,1664,128]{2,1,0:T(8,128)(2,1)}, u32[]{:S(2)}, u32[]{:S(2)}) collective-permute-start(bf16[2,1664,128]{2,1,0:T(8,128)(2,1)} %get-tuple-element.82), channel_id=1, source_target_pairs={{0,4},{1,5},{2,6},{3,7},{4,0},{5,1},{6,2},{7,3},{8,12},{9,13},{10,... | collective-permute-start | bytes 2555912 | tf_op jit(solution)/shard_map/ppermute | solution.py:19
  257.7 42.0 %collective-permute-start.22 = (bf16[512,1664]{1,0:T(8,128)(2,1)S(1)}, bf16[512,1664]{1,0:T(8,128)(2,1)}, u32[]{:S(2)}, u32[]{:S(2)}) collective-permute-start(bf16[512,1664]{1,0:T(8,128)(2,1)S(1)} %copy-done.10), channel_id=1, source_target_pairs={{0,1},{1,0},{2,3},{3,2},{4,5},{5,4},{6,7},{7,6},{8,9},{9,8},{10,11... | collective-permute-start | bytes 5111816 | tf_op jit(solution)/shard_map/ppermute | solution.py:19
  257.8 43.5 %collective-permute-start.23 = (bf16[512,1664]{1,0:T(8,128)(2,1)}, bf16[512,1664]{1,0:T(8,128)(2,1)}, u32[]{:S(2)}, u32[]{:S(2)}) collective-permute-start(bf16[512,1664]{1,0:T(8,128)(2,1)} %get-tuple-element.65.refs_1_), channel_id=1, source_target_pairs={{0,1},{1,0},{2,3},{3,2},{4,5},{5,4},{6,7},{7,6},{8,9},{9,8},{10,11... | collective-permute-start | bytes 5111816 | tf_op jit(solution)/shard_map/ppermute | solution.py:19
  258.3 43.6 %collective-permute-start.24 = (bf16[512,1664]{1,0:T(8,128)(2,1)}, bf16[512,1664]{1,0:T(8,128)(2,1)}, u32[]{:S(2)}, u32[]{:S(2)}) collective-permute-start(bf16[512,1664]{1,0:T(8,128)(2,1)} %collective-permute-done.refs_4_), channel_id=1, source_target_pairs={{0,1},{1,0},{2,3},{3,2},{4,5},{5,4},{6,7},{7,6},{8,9},{9,8},{10,11... | collective-permute-start | bytes 5111816 | tf_op jit(solution)/shard_map/ppermute | solution.py:19
  258.3 43.5 %collective-permute-start.25 = (bf16[512,1664]{1,0:T(8,128)(2,1)}, bf16[512,1664]{1,0:T(8,128)(2,1)}, u32[]{:S(2)}, u32[]{:S(2)}) collective-permute-start(bf16[512,1664]{1,0:T(8,128)(2,1)} %collective-permute-done.3.refs_5_), channel_id=1, source_target_pairs={{0,1},{1,0},{2,3},{3,2},{4,5},{5,4},{6,7},{7,6},{8,9},{9,8},{10,11... | collective-permute-start | bytes 5111816 | tf_op jit(solution)/shard_map/ppermute | solution.py:19
  286.0 29.4 %collective-permute-start.26 = (bf16[1024,512]{1,0:T(8,128)(2,1)}, bf16[1024,512]{1,0:T(8,128)(2,1)S(1)}, u32[]{:S(2)}, u32[]{:S(2)}) collective-permute-start(bf16[1024,512]{1,0:T(8,128)(2,1)} %shard_map.116), channel_id=1, source_target_pairs={{0,16},{8,24},{16,0},{24,8},{1,17},{9,25},{17,1},{25,9},{2,18},{10... | collective-permute-start | bytes 3145736 | tf_op jit(solution)/shard_map/ppermute | solution.py:19
  299.8 38.7 %collective-permute-start.28 = (bf16[2,1664,128]{2,1,0:T(8,128)(2,1)}, bf16[2,1664,128]{2,1,0:T(8,128)(2,1)}, u32[]{:S(2)}, u32[]{:S(2)}) collective-permute-start(bf16[2,1664,128]{2,1,0:T(8,128)(2,1)} %get-tuple-element.84.refs_8_), channel_id=1, source_target_pairs={{0,8},{8,0},{16,24},{24,16},{1,9},{9,1},{17,25},{25,17},{2,10},{10... | collective-permute-start | bytes 2555912 | tf_op jit(solution)/shard_map/ppermute | solution.py:19
  301.3 38.8 %collective-permute-start.29 = (bf16[2,1664,128]{2,1,0:T(8,128)(2,1)}, bf16[2,1664,128]{2,1,0:T(8,128)(2,1)}, u32[]{:S(2)}, u32[]{:S(2)}) collective-permute-start(bf16[2,1664,128]{2,1,0:T(8,128)(2,1)} %collective-permute-done.11.refs_10_), channel_id=1, source_target_pairs={{0,8},{8,0},{16,24},{24,16},{1,9},{9,1},{17,25},{25,17},{2,10},{10... | collective-permute-start | bytes 2555912 | tf_op jit(solution)/shard_map/ppermute | solution.py:19
  318.2 19.5 %copy-start.29 = (s32[64,8]{0,1:T(8,128)S(1)}, s32[64,8]{0,1:T(8,128)}, u32[]{:S(2)}) copy-start(s32[64,8]{0,1:T(8,128)} %param.14) | copy-start | bytes 6148
  318.2 20.2 %copy-start.23 = (bf16[2,1664,128]{2,1,0:T(8,128)(2,1)S(1)}, bf16[2,1664,128]{2,1,0:T(8,128)(2,1)}, u32[]{:S(2)}) copy-start(bf16[2,1664,128]{2,1,0:T(8,128)(2,1)} %get-tuple-element.92.refs_9_) | copy-start | bytes 2555908
  318.2 22.5 %copy-start.31 = (s32[2,2]{1,0:T(2,128)S(1)}, s32[2,2]{1,0:T(2,128)}, u32[]{:S(2)}) copy-start(s32[2,2]{1,0:T(2,128)} %constant.176.clone) | copy-start | bytes 52
  318.2 22.5 %copy-start.32 = (s32[2]{0:T(128)S(1)}, s32[2]{0:T(128)}, u32[]{:S(2)}) copy-start(s32[2]{0:T(128)} %constant.178) | copy-start | bytes 28
  318.2 24.5 %collective-permute-start.27 = (bf16[1024,256]{1,0:T(8,128)(2,1)}, bf16[1024,256]{1,0:T(8,128)(2,1)}, u32[]{:S(2)}, u32[]{:S(2)}) collective-permute-start(bf16[1024,256]{1,0:T(8,128)(2,1)} %slice.87), channel_id=1, source_target_pairs={{0,4},{1,5},{2,6},{3,7},{4,0},{5,1},{6,2},{7,3},{8,12},{9,13},{10,... | collective-permute-start | bytes 1572872 | tf_op jit(solution)/shard_map/ppermute | solution.py:19
  338.4 22.3 %collective-permute-start.30 = (bf16[2,1664,128]{2,1,0:T(8,128)(2,1)S(1)}, bf16[2,1664,128]{2,1,0:T(8,128)(2,1)S(1)}, u32[]{:S(2)}, u32[]{:S(2)}) collective-permute-start(bf16[2,1664,128]{2,1,0:T(8,128)(2,1)S(1)} %copy-done.23), channel_id=1, source_target_pairs={{0,8},{8,0},{16,24},{24,16},{1,9},{9,1},{17,25},{25,17},{2,10},{10... | collective-permute-start | bytes 2555912 | tf_op jit(solution)/shard_map/ppermute | solution.py:19
  340.0 38.5 %collective-permute-start.31 = (bf16[2,1664,128]{2,1,0:T(8,128)(2,1)}, bf16[2,1664,128]{2,1,0:T(8,128)(2,1)S(1)}, u32[]{:S(2)}, u32[]{:S(2)}) collective-permute-start(bf16[2,1664,128]{2,1,0:T(8,128)(2,1)} %collective-permute-done.21.refs_11_), channel_id=1, source_target_pairs={{0,8},{8,0},{16,24},{24,16},{1,9},{9,1},{17,25},{25,17},{2,10},{10... | collective-permute-start | bytes 2555912 | tf_op jit(solution)/shard_map/ppermute | solution.py:19
  357.3 50.1 %collective-permute-start.32 = (bf16[32,64,256]{2,1,0:T(8,128)(2,1)}, bf16[32,64,256]{2,1,0:T(8,128)(2,1)S(1)}, u32[]{:S(2)}, u32[]{:S(2)}) collective-permute-start(bf16[32,64,256]{2,1,0:T(8,128)(2,1)} %get-tuple-element.88), channel_id=1, source_target_pairs={{0,8},{8,0},{16,24},{24,16},{1,9},{9,1},{17,25},{25,17},{2,10},{10... | collective-permute-start | bytes 3145736 | tf_op jit(solution)/shard_map/ppermute | solution.py:19
  358.7 48.7 %collective-permute-start.33 = (bf16[32,64,256]{2,1,0:T(8,128)(2,1)}, bf16[32,64,256]{2,1,0:T(8,128)(2,1)S(1)}, u32[]{:S(2)}, u32[]{:S(2)}) collective-permute-start(bf16[32,64,256]{2,1,0:T(8,128)(2,1)} %get-tuple-element.90), channel_id=1, source_target_pairs={{0,16},{8,24},{16,0},{24,8},{1,17},{9,25},{17,1},{25,9},{2,18},{10... | collective-permute-start | bytes 3145736 | tf_op jit(solution)/shard_map/ppermute | solution.py:19
  360.5 108.8 %collective-permute-start.38 = (bf16[32,64,256]{2,1,0:T(8,128)(2,1)}, bf16[32,64,256]{2,1,0:T(8,128)(2,1)}, u32[]{:S(2)}, u32[]{:S(2)}) collective-permute-start(bf16[32,64,256]{2,1,0:T(8,128)(2,1)} %get-tuple-element.89), channel_id=1, source_target_pairs={{0,16},{8,24},{16,0},{24,8},{1,17},{9,25},{17,1},{25,9},{2,18},{10... | collective-permute-start | bytes 3145736 | tf_op jit(solution)/shard_map/ppermute | solution.py:19
  360.8 17.8 %copy-start.34 = (bf16[2,1664,128]{2,1,0:T(8,128)(2,1)}, bf16[2,1664,128]{2,1,0:T(8,128)(2,1)S(1)}, u32[]{:S(2)}) copy-start(bf16[2,1664,128]{2,1,0:T(8,128)(2,1)S(1)} %collective-permute-done.30.refs_13_) | copy-start | bytes 2555908
  360.8 110.3 %collective-permute-start.36 = (bf16[32,64,256]{2,1,0:T(8,128)(2,1)}, bf16[32,64,256]{2,1,0:T(8,128)(2,1)S(1)}, u32[]{:S(2)}, u32[]{:S(2)}) collective-permute-start(bf16[32,64,256]{2,1,0:T(8,128)(2,1)} %get-tuple-element.87), channel_id=1, source_target_pairs={{0,8},{8,0},{16,24},{24,16},{1,9},{9,1},{17,25},{25,17},{2,10},{10... | collective-permute-start | bytes 3145736 | tf_op jit(solution)/shard_map/ppermute | solution.py:19
  392.8 35.9 %collective-permute-start.34 = (bf16[1024,512]{1,0:T(8,128)(2,1)}, bf16[1024,512]{1,0:T(8,128)(2,1)S(1)}, u32[]{:S(2)}, u32[]{:S(2)}) collective-permute-start(bf16[1024,512]{1,0:T(8,128)(2,1)} %shard_map.119), channel_id=1, source_target_pairs={{0,16},{8,24},{16,0},{24,8},{1,17},{9,25},{17,1},{25,9},{2,18},{10... | collective-permute-start | bytes 3145736 | tf_op jit(solution)/shard_map/ppermute | solution.py:19
  430.7 24.7 %collective-permute-start.35 = (bf16[1024,256]{1,0:T(8,128)(2,1)S(1)}, bf16[1024,256]{1,0:T(8,128)(2,1)S(1)}, u32[]{:S(2)}, u32[]{:S(2)}) collective-permute-start(bf16[1024,256]{1,0:T(8,128)(2,1)S(1)} %slice.86), channel_id=1, source_target_pairs={{0,4},{1,5},{2,6},{3,7},{4,0},{5,1},{6,2},{7,3},{8,12},{9,13},{10,... | collective-permute-start | bytes 1572872 | tf_op jit(solution)/shard_map/ppermute | solution.py:19
  431.2 56.9 %collective-permute-start.37 = (bf16[32,64,256]{2,1,0:T(8,128)(2,1)S(1)}, bf16[32,64,256]{2,1,0:T(8,128)(2,1)}, u32[]{:S(2)}, u32[]{:S(2)}) collective-permute-start(bf16[32,64,256]{2,1,0:T(8,128)(2,1)S(1)} %add_convert_fusion.10), channel_id=1, source_target_pairs={{0,16},{8,24},{16,0},{24,8},{1,17},{9,25},{17,1},{25,9},{2,18},{10... | collective-permute-start | bytes 3145736 | tf_op jit(solution)/shard_map/ppermute | solution.py:19
  433.4 55.1 %collective-permute-start.39 = (bf16[32,64,256]{2,1,0:T(8,128)(2,1)S(1)}, bf16[32,64,256]{2,1,0:T(8,128)(2,1)}, u32[]{:S(2)}, u32[]{:S(2)}) collective-permute-start(bf16[32,64,256]{2,1,0:T(8,128)(2,1)S(1)} %add_convert_fusion.7), channel_id=1, source_target_pairs={{0,8},{8,0},{16,24},{24,16},{1,9},{9,1},{17,25},{25,17},{2,10},{10... | collective-permute-start | bytes 3145736 | tf_op jit(solution)/shard_map/ppermute | solution.py:19
  456.4 16.5 %copy-start.2 = (bf16[64,64,512]{2,1,0:T(8,128)(2,1)S(1)}, bf16[64,64,512]{2,1,0:T(8,128)(2,1)}, u32[]{:S(2)}) copy-start(bf16[64,64,512]{2,1,0:T(8,128)(2,1)} %convert_bitcast_fusion) | copy-start | bytes 12582916
  469.3 26.4 %collective-permute-start.42 = (bf16[32,64,256]{2,1,0:T(8,128)(2,1)}, bf16[32,64,256]{2,1,0:T(8,128)(2,1)}, u32[]{:S(2)}, u32[]{:S(2)}) collective-permute-start(bf16[32,64,256]{2,1,0:T(8,128)(2,1)} %get-tuple-element.111), channel_id=1, source_target_pairs={{0,16},{8,24},{16,0},{24,8},{1,17},{9,25},{17,1},{25,9},{2,18},{10... | collective-permute-start | bytes 3145736 | tf_op jit(solution)/shard_map/ppermute | solution.py:19
  472.1 26.3 %collective-permute-start.41 = (bf16[32,64,256]{2,1,0:T(8,128)(2,1)}, bf16[32,64,256]{2,1,0:T(8,128)(2,1)S(1)}, u32[]{:S(2)}, u32[]{:S(2)}) collective-permute-start(bf16[32,64,256]{2,1,0:T(8,128)(2,1)} %get-tuple-element.110), channel_id=1, source_target_pairs={{0,8},{8,0},{16,24},{24,16},{1,9},{9,1},{17,25},{25,17},{2,10},{10... | collective-permute-start | bytes 3145736 | tf_op jit(solution)/shard_map/ppermute | solution.py:19
  488.1 29.9 %collective-permute-start.44 = (bf16[32,64,256]{2,1,0:T(8,128)(2,1)}, bf16[32,64,256]{2,1,0:T(8,128)(2,1)S(1)}, u32[]{:S(2)}, u32[]{:S(2)}) collective-permute-start(bf16[32,64,256]{2,1,0:T(8,128)(2,1)} %get-tuple-element.114), channel_id=1, source_target_pairs={{0,16},{8,24},{16,0},{24,8},{1,17},{9,25},{17,1},{25,9},{2,18},{10... | collective-permute-start | bytes 3145736 | tf_op jit(solution)/shard_map/ppermute | solution.py:19
  488.5 58.7 %collective-permute-start.40 = (bf16[32,64,256]{2,1,0:T(8,128)(2,1)}, bf16[32,64,256]{2,1,0:T(8,128)(2,1)S(1)}, u32[]{:S(2)}, u32[]{:S(2)}) collective-permute-start(bf16[32,64,256]{2,1,0:T(8,128)(2,1)} %get-tuple-element.108), channel_id=1, source_target_pairs={{0,8},{8,0},{16,24},{24,16},{1,9},{9,1},{17,25},{25,17},{2,10},{10... | collective-permute-start | bytes 3145736 | tf_op jit(solution)/shard_map/ppermute | solution.py:19
  498.4 43.7 %collective-permute-start.45 = (bf16[32,64,256]{2,1,0:T(8,128)(2,1)S(1)}, bf16[32,64,256]{2,1,0:T(8,128)(2,1)S(1)}, u32[]{:S(2)}, u32[]{:S(2)}) collective-permute-start(bf16[32,64,256]{2,1,0:T(8,128)(2,1)S(1)} %add_convert_fusion.1), channel_id=1, source_target_pairs={{0,8},{8,0},{16,24},{24,16},{1,9},{9,1},{17,25},{25,17},{2,10},{10... | collective-permute-start | bytes 3145736 | tf_op jit(solution)/shard_map/ppermute | solution.py:19
  501.4 45.8 %collective-permute-start.43 = (bf16[32,64,256]{2,1,0:T(8,128)(2,1)S(1)}, bf16[32,64,256]{2,1,0:T(8,128)(2,1)S(1)}, u32[]{:S(2)}, u32[]{:S(2)}) collective-permute-start(bf16[32,64,256]{2,1,0:T(8,128)(2,1)S(1)} %add_convert_fusion.4), channel_id=1, source_target_pairs={{0,16},{8,24},{16,0},{24,8},{1,17},{9,25},{17,1},{25,9},{2,18},{10... | collective-permute-start | bytes 3145736 | tf_op jit(solution)/shard_map/ppermute | solution.py:19
  506.0 36.0 %copy-start.21 = (bf16[32,64,256]{2,1,0:T(8,128)(2,1)S(1)}, bf16[32,64,256]{2,1,0:T(8,128)(2,1)}, u32[]{:S(2)}) copy-start(bf16[32,64,256]{2,1,0:T(8,128)(2,1)} %get-tuple-element.113) | copy-start | bytes 3145732
  547.8 15.9 %copy-start.3 = (bf16[1024,256]{1,0:T(8,128)(2,1)S(1)}, bf16[1024,256]{1,0:T(8,128)(2,1)}, u32[]{:S(2)}) copy-start(bf16[1024,256]{1,0:T(8,128)(2,1)} %fusion.25.screened_ref) | copy-start | bytes 1572868
  551.3 3.8 collective-permute-start.46
  555.2 3.7 collective-permute-start.47
  558.9 4.6 collective-permute-start.48
  563.7 3.7 collective-permute-start.49
  567.4 3.5 collective-permute-start.50
  (23 other events, 152.2 us)

commit v4 on v3

--- a/solution.py
+++ b/solution.py
@@ -11,6 +11,7 @@
 PAIR = 2
 GROUPS = 4
 VMEM = 56
+NO_COST = pl.CostEstimate(flops=0, bytes_accessed=0, transcendentals=0)
 MIB = 1024 * 1024
 
 
@@ -106,11 +107,7 @@
             pltpu.SemaphoreType.DMA((count, sides)),
         ],
         compiler_params=pltpu.CompilerParams(vmem_limit_bytes=VMEM * MIB),
-        cost_estimate=pl.CostEstimate(
-            flops=2 * rows * depth * count * cols,
-            bytes_accessed=2 * count * depth * (rows + cols) + 4 * rows * cols,
-            transcendentals=0,
-        ),
+        cost_estimate=NO_COST,
     )(order, *[part for piece in pieces for part in piece], *sources)
 
 
@@ -129,7 +126,7 @@
         out_specs=pl.BlockSpec((tall, near_l, wide), lambda i, g: (g, 0, i)),
         out_shape=jax.ShapeDtypeStruct((tile, near_l, rows), panel.dtype),
         compiler_params=pltpu.CompilerParams(vmem_limit_bytes=VMEM * MIB),
-        cost_estimate=pl.CostEstimate(flops=0, bytes_accessed=4 * rows * tile * near_l, transcendentals=0),
+        cost_estimate=NO_COST,
     )(panel)
 
 
@@ -195,11 +192,7 @@
             pltpu.SemaphoreType.DMA((2, len(panels))),
         ],
         compiler_params=pltpu.CompilerParams(vmem_limit_bytes=VMEM * MIB),
-        cost_estimate=pl.CostEstimate(
-            flops=2 * count * tile * share * rows * width,
-            bytes_accessed=2 * count * tile * share * (rows + width),
-            transcendentals=0,
-        ),
+        cost_estimate=NO_COST,
     )(places, mask, screened, *panels)
     return [list(found[:count]), list(found[count:])]
 
@@ -233,16 +226,15 @@
     chunks = near_cols // width
     on_diagonal = u == v
 
+    mine = lax.dynamic_slice_in_dim(polarization, u * half, half, 1)
+    other = lax.dynamic_slice_in_dim(polarization, (1 - u) * half, half, 1)
+    first, second = jnp.split(mine, 2)
+    other_first, other_second = jnp.split(other, 2)
     metric_parts = metric.reshape(per_block, 2, half, near_cols)
     metric_mine = lax.dynamic_index_in_dim(metric_parts, u, 1, keepdims=False)
     metric_other = lax.dynamic_index_in_dim(metric_parts, 1 - u, 1, keepdims=False)
     crossing = [metric_other[:, :, j * width : (j + 1) * width] for j in range(chunks)]
-    polarization = after(polarization, crossing[0])
-    mine = lax.dynamic_slice_in_dim(polarization, u * half, half, 1)
-    other = lax.dynamic_slice_in_dim(polarization, (1 - u) * half, half, 1)
-
-    first, second = jnp.split(mine, 2)
-    other_first, other_second = jnp.split(other, 2)
+
     low = top_col // 2
 
     def cross(value, *others):
@@ -310,6 +302,7 @@
     near_crossed_second = swap(
         after(crossed_second, near_crossed_first, arrived[-1], came[1][1], from_row(0, 1)), "col", low
     )
+    near_crossed_second = after(near_crossed_second, *[pair[1] for pair in came[2:3]])
     while len(panels) < GROUPS:
         turn_next(from_row(1, 1), *panels)
 
@@ -329,13 +322,6 @@
     ab = near_l // mask_panel.shape[1]
     row_blocks = panel_rows // rb
     panel_mask = lax.dynamic_slice_in_dim(mask_panel, r * row_blocks, row_blocks, 0)
-
-    near_blocks = near_cols // rb
-    near_mask = lax.dynamic_slice_in_dim(mask_near, c * near_blocks, near_blocks, 0)
-    near_mask = jnp.repeat(jnp.repeat(near_mask, rb, 0), ab, 1).astype(jnp.bfloat16)
-    near = three_near * near_mask[:, None, :]
-    green = lax.dynamic_slice_in_dim(green_function, r * share, share, 0)
-    dressed = jnp.einsum("qns,ls->nlq", near, green, preferred_element_type=jnp.float32).astype(jnp.bfloat16)
 
     earlier = (*panels, *[pair[1] for pair in came[2:3]])
     due, begun = [blocks[-1] for blocks in gathered[2:3]], [pair[1] for pair in came[3:4]]
@@ -375,15 +361,21 @@
                     {e: value for e, value in total.items() if not e & next_bit},
                 ]
         halves = [left[h][1][0] for h in range(2)]
-        contracted_chunks.append(jnp.concatenate(halves))
-        parts = [
-            jnp.einsum("mlq,nlq->mn", half, dressed[:, :, j * width : j * width + wide], preferred_element_type=jnp.float32)
-            for half in halves
-        ]
-        energy = energy - jnp.concatenate(parts)
-
+        contracted_chunks.append(halves)
+
+    near_blocks = near_cols // rb
+    near_mask = lax.dynamic_slice_in_dim(mask_near, c * near_blocks, near_blocks, 0)
+    near_mask = jnp.repeat(jnp.repeat(near_mask, rb, 0), ab, 1).astype(jnp.bfloat16)
+    near = after(three_near, *stay[0], *stay[1]) * near_mask[:, None, :]
+    green = lax.dynamic_slice_in_dim(green_function, r * share, share, 0)
+    dressed = jnp.einsum("qns,ls->nlq", near, green, preferred_element_type=jnp.float32).astype(jnp.bfloat16)
+    for j, halves in enumerate(contracted_chunks):
+        beside = dressed[:, :, j * wide : (j + 1) * wide]
+        energy = energy - jnp.concatenate(
+            [jnp.einsum("mlq,nlq->mn", half, beside, preferred_element_type=jnp.float32) for half in halves]
+        )
     energy = scatter_sum(scatter_sum(energy, "row").T, "col").T
-    contracted = jnp.transpose(jnp.concatenate(contracted_chunks, axis=2), (2, 0, 1))
+    contracted = jnp.transpose(jnp.concatenate([jnp.concatenate(halves) for halves in contracted_chunks], axis=2), (2, 0, 1))
     return jnp.concatenate(screened_chunks, axis=1), contracted, energy
 
 

time: 576 us -> 577 us (level)
  transfers between devices with their start and end apart: 51 -> 51, of which waited for: 23 -> 21; matrix products, arithmetic and copies ran while one was open for 14% -> 13% of each run, Pallas kernels for 26% -> 26%
where the time goes in v4:
time: 577 us; the launch traced here: 570 us
  waiting for transfers between devices  275 us (48%)
  Pallas kernels  147 us (25%)
  starting transfers between devices  51.7 us (9%)
  other arithmetic  41.5 us (7%)
  matrix products  31.7 us (5%)
  local copies, waits for them, and re-layouts  20.6 us (4%)
    ppermute x51, waiting for transfers between devices, swap(): return lax.ppermute(value, axis, [(i, i ^ bit) for i in range(size)])  275 us
    pallas_call x4, Pallas kernels, product(): pl.pallas_call(functools.partial(product_kernel, count, parts, per_block)...  54.2 us
    ppermute x51, starting transfers between devices, swap(): return lax.ppermute(value, axis, [(i, i ^ bit) for i in range(size)])  51.7 us
    pallas_call x4, Pallas kernels, contract(): pl.pallas_call(functools.partial(contract_kernel, rb, ab), in_specs=[in_s...  50.1 us
    pallas_call x4, Pallas kernels, turn(): pl.pallas_call(turn_kernel, grid=(rows // wide, tile // tall), in_specs=[...  42.8 us
    dot_general x1, matrix products, per_device(): jnp.einsum('qns,ls->nlq', near, green, preferred_element_type=jnp.float32)  17.6 us
    dot_general x4, matrix products, per_device(): jnp.einsum('mlq,nlq->mn', half, beside, preferred_element_type=jnp.float32)  14.1 us
    mul x1, other arithmetic, per_device(): near = after(three_near, *stay[0], *stay[1]) * near_mask[:, None, :]  13.8 us
  transfers between devices with their start and end apart: 51, of which 21 were waited for; matrix products, arithmetic and copies ran while one was open for 13% of the time, Pallas kernels for 26%

profile of v4, /device:TPU:0, one launch (start us, length us, event | category | flops | bytes accessed | tf_op | source)
XLA Modules:
  0.0 569.8 jit_solution(14621126824792740085)
XLA Ops:
  0.7 5.2 dynamic-slice_bitcast_fusion
  5.9 2.0 fusion.44
  7.9 3.0 collective-permute-start.1
  10.9 5.2 fusion.42
  16.2 1.6 collective-permute-start
  17.7 12.4 %collective-permute-done.1 = bf16[2,1664,128]{2,1,0:T(8,128)(2,1)} collective-permute-done((bf16[2,1664,128]{2,1,0:T(8,128)(2,1)}, bf16[2,1664,128]{2,1,0:T(8,128)(2,1)}, u32[]{:S(2)}, u32[]{:S(2)}) %collective-permute-start.1) | collective-permute-done | bytes 852000 | tf_op jit(solution)/shard_map/ppermute | solution.py:20
  30.2 1.7 collective-permute-start.12
  31.9 23.0 %collective-permute-done.refs_4_ = bf16[512,1664]{1,0:T(8,128)(2,1)} collective-permute-done((bf16[512,1664]{1,0:T(8,128)(2,1)S(1)}, bf16[512,1664]{1,0:T(8,128)(2,1)}, u32[]{:S(2)}, u32[]{:S(2)}) %collective-permute-start) | collective-permute-done | bytes 1703968 | tf_op jit(solution)/shard_map/ppermute | solution.py:20
  54.9 1.6 collective-permute-start.3
  56.5 2.4 broadcast_select_fusion.5
  59.0 2.6 collective-permute-start.4
  63.0 10.7 %shard_map.112.refs_0_ = bf16[64,256,256]{2,1,0:T(8,128)(2,1)} custom-call(bf16[1024,64,256]{2,1,0:T(8,128)(2,1)} %panel_ref.3), custom_call_target="tpu_custom_call" | custom-call | tf_op jit(solution)/shard_map/pallas_call | solution.py:122
  74.2 1.5 collective-permute-start.13
  75.7 34.4 %collective-permute-done.4.refs_10_ = bf16[2,1664,128]{2,1,0:T(8,128)(2,1)} collective-permute-done((bf16[2,1664,128]{2,1,0:T(8,128)(2,1)}, bf16[2,1664,128]{2,1,0:T(8,128)(2,1)}, u32[]{:S(2)}, u32[]{:S(2)}) %collective-permute-start.4) | collective-permute-done | bytes 852000 | tf_op jit(solution)/shard_map/ppermute | solution.py:20
  111.0 2.7 collective-permute-start.16
  116.6 10.7 %shard_map.113.refs_1_ = bf16[64,256,256]{2,1,0:T(8,128)(2,1)} custom-call(bf16[1024,64,256]{2,1,0:T(8,128)(2,1)} %panel_ref.3), custom_call_target="tpu_custom_call" | custom-call | tf_op jit(solution)/shard_map/pallas_call | solution.py:122
  128.7 10.6 %shard_map.114.refs_2_ = bf16[64,256,256]{2,1,0:T(8,128)(2,1)} custom-call(bf16[1024,64,256]{2,1,0:T(8,128)(2,1)} %panel_ref.3), custom_call_target="tpu_custom_call" | custom-call | tf_op jit(solution)/shard_map/pallas_call | solution.py:122
  139.9 1.5 collective-permute-start.9
  141.9 25.0 %collective-permute-done.6.refs_11_ = bf16[2,1664,128]{2,1,0:T(8,128)(2,1)} collective-permute-done((bf16[2,1664,128]{2,1,0:T(8,128)(2,1)}, bf16[2,1664,128]{2,1,0:T(8,128)(2,1)}, u32[]{:S(2)}, u32[]{:S(2)}) %collective-permute-start.6) | collective-permute-done | bytes 852000 | tf_op jit(solution)/shard_map/ppermute | solution.py:20
  167.4 1.6 collective-permute-start.18
  169.0 6.5 %collective-permute-done.9 = bf16[2,1664,128]{2,1,0:T(8,128)(2,1)S(1)} collective-permute-done((bf16[2,1664,128]{2,1,0:T(8,128)(2,1)}, bf16[2,1664,128]{2,1,0:T(8,128)(2,1)S(1)}, u32[]{:S(2)}, u32[]{:S(2)}) %collective-permute-start.9) | collective-permute-done | bytes 852000 | tf_op jit(solution)/shard_map/ppermute | solution.py:20
  177.8 43.5 %collective-permute-done.11.refs_10_ = bf16[2,1664,128]{2,1,0:T(8,128)(2,1)S(1)} collective-permute-done((bf16[2,1664,128]{2,1,0:T(8,128)(2,1)S(1)}, bf16[2,1664,128]{2,1,0:T(8,128)(2,1)S(1)}, u32[]{:S(2)}, u32[]{:S(2)}) %collective-permute-start.11) | collective-permute-done | bytes 852000 | tf_op jit(solution)/shard_map/ppermute | solution.py:20
  222.1 1.6 collective-permute-start.28
  225.9 17.9 %collective-permute-done.28.refs_12_ = bf16[2,1664,128]{2,1,0:T(8,128)(2,1)S(1)} collective-permute-done((bf16[2,1664,128]{2,1,0:T(8,128)(2,1)S(1)}, bf16[2,1664,128]{2,1,0:T(8,128)(2,1)S(1)}, u32[]{:S(2)}, u32[]{:S(2)}) %collective-permute-start.28) | collective-permute-done | bytes 852000 | tf_op jit(solution)/shard_map/ppermute | solution.py:20
  243.9 3.1 collective-permute-start.21
  247.0 14.7 %collective-permute-done.29.refs_14_ = bf16[2,1664,128]{2,1,0:T(8,128)(2,1)S(1)} collective-permute-done((bf16[2,1664,128]{2,1,0:T(8,128)(2,1)S(1)}, bf16[2,1664,128]{2,1,0:T(8,128)(2,1)S(1)}, u32[]{:S(2)}, u32[]{:S(2)}) %collective-permute-start.29) | collective-permute-done | bytes 852000 | tf_op jit(solution)/shard_map/ppermute | solution.py:20
  265.6 10.9 %shard_map.115.refs_3_ = bf16[64,256,256]{2,1,0:T(8,128)(2,1)} custom-call(bf16[1024,64,256]{2,1,0:T(8,128)(2,1)} %panel_ref.3), custom_call_target="tpu_custom_call" | custom-call | tf_op jit(solution)/shard_map/pallas_call | solution.py:122
  276.5 13.3 %shard_map.116 = bf16[1024,512]{1,0:T(8,128)(2,1)} custom-call(s32[4]{0:T(128)} %fusion.41.order_ref, bf16[512,1664]{1,0:T(8,128)(2,1)} %collective-permute-done.12.refs_0_, bf16[512,1664]{1,0:T(8,128)(2,1)} %collective-permute-done.13.refs_1_, bf16[512,1664]{1,0:T(8,128)(2,1)} %copy-done.9, bf16[512,1664]{1,0:T(8,128)(2,1)} %copy-done.10, ...), custom_call_target="tpu_custom_call" | custom-call | tf_op jit(solution)/shard_map/pallas_call | solution.py:97
  290.4 1.6 collective-permute-start.30
  292.4 13.6 %shard_map.117 = f32[1024,512]{1,0:T(8,128)} custom-call(s32[4]{0:T(128)} %fusion.41.order_ref, bf16[512,1664]{1,0:T(8,128)(2,1)} %copy-done.1, bf16[512,1664]{1,0:T(8,128)(2,1)} %copy-done.2, bf16[512,1664]{1,0:T(8,128)(2,1)} %collective-permute-done.22.refs_2_, bf16[512,1664]{1,0:T(8,128)(2,1)} %collective-permute-done.23.refs_3_, ...), custom_call_target="tpu_custom_call" | custom-call | tf_op jit(solution)/shard_map/pallas_call | solution.py:97
  306.0 9.3 %collective-permute-done.26 = bf16[1024,512]{1,0:T(8,128)(2,1)S(1)} collective-permute-done((bf16[1024,512]{1,0:T(8,128)(2,1)}, bf16[1024,512]{1,0:T(8,128)(2,1)S(1)}, u32[]{:S(2)}, u32[]{:S(2)}) %collective-permute-start.26) | collective-permute-done | bytes 1048608 | tf_op jit(solution)/shard_map/ppermute | solution.py:20
  315.4 1.9 convert_add_fusion.1
  318.2 2.7 collective-permute-start.27
  322.3 21.8 %collective-permute-done.27 = bf16[1024,256]{1,0:T(8,128)(2,1)} collective-permute-done((bf16[1024,256]{1,0:T(8,128)(2,1)}, bf16[1024,256]{1,0:T(8,128)(2,1)}, u32[]{:S(2)}, u32[]{:S(2)}) %collective-permute-start.27) | collective-permute-done | bytes 524320 | tf_op jit(solution)/shard_map/ppermute | solution.py:20
  344.0 2.0 fusion.25.screened_ref
  346.1 12.5 %shard_map.118 = (bf16[32,64,256]{2,1,0:T(8,128)(2,1)}, bf16[32,64,256]{2,1,0:T(8,128)(2,1)}, bf16[32,64,256]{2,1,0:T(8,128)(2,1)}, bf16[32,64,256]{2,1,0:T(8,128)(2,1)}) custom-call(s32[2,2]{1,0:T(2,128)} %get-tuple-element.87.places_ref, s32[16,8]{1,0:T(8,128)} %copy.42.mask_ref, bf16[1024,256]{1,0:T(8,128)(2,1)} %fusion.25.screened_ref, ...), custom_call_target="tpu_custom_call" | custom-call | tf_op jit(solution)/shard_map/pallas_call | solution.py:184
  358.6 1.7 collective-permute-start.32
  361.7 13.7 %shard_map.119 = bf16[1024,512]{1,0:T(8,128)(2,1)} custom-call(s32[4]{0:T(128)} %fusion.41.order_ref, bf16[512,1664]{1,0:T(8,128)(2,1)} %collective-permute-done.12.refs_0_, bf16[512,1664]{1,0:T(8,128)(2,1)} %collective-permute-done.13.refs_1_, bf16[512,1664]{1,0:T(8,128)(2,1)} %copy-done.9, bf16[512,1664]{1,0:T(8,128)(2,1)} %copy-done.10, ...), custom_call_target="tpu_custom_call" | custom-call | tf_op jit(solution)/shard_map/pallas_call | solution.py:97
  375.4 1.6 collective-permute-start.34
  378.5 12.6 %shard_map.121 = (bf16[32,64,256]{2,1,0:T(8,128)(2,1)}, bf16[32,64,256]{2,1,0:T(8,128)(2,1)}, bf16[32,64,256]{2,1,0:T(8,128)(2,1)}, bf16[32,64,256]{2,1,0:T(8,128)(2,1)}) custom-call(s32[2,2]{1,0:T(2,128)} %get-tuple-element.96.places_ref, s32[16,8]{1,0:T(8,128)} %copy.42.mask_ref, bf16[1024,256]{1,0:T(8,128)(2,1)} %fusion.25.screened_ref, ...), custom_call_target="tpu_custom_call" | custom-call | tf_op jit(solution)/shard_map/pallas_call | solution.py:184
  391.1 13.6 %shard_map.120 = f32[1024,512]{1,0:T(8,128)} custom-call(s32[4]{0:T(128)} %fusion.41.order_ref, bf16[512,1664]{1,0:T(8,128)(2,1)} %copy-done.1, bf16[512,1664]{1,0:T(8,128)(2,1)} %copy-done.2, bf16[512,1664]{1,0:T(8,128)(2,1)} %collective-permute-done.22.refs_2_, bf16[512,1664]{1,0:T(8,128)(2,1)} %collective-permute-done.23.refs_3_, ...), custom_call_target="tpu_custom_call" | custom-call | tf_op jit(solution)/shard_map/pallas_call | solution.py:97
  404.8 4.3 collective-permute-done.34
  409.1 1.9 convert_add_fusion
  411.1 1.7 add_convert_fusion.10
  414.3 17.6 %collective-permute-done.35 = bf16[1024,256]{1,0:T(8,128)(2,1)S(1)} collective-permute-done((bf16[1024,256]{1,0:T(8,128)(2,1)S(1)}, bf16[1024,256]{1,0:T(8,128)(2,1)S(1)}, u32[]{:S(2)}, u32[]{:S(2)}) %collective-permute-start.35) | collective-permute-done | bytes 524320 | tf_op jit(solution)/shard_map/ppermute | solution.py:20
  433.1 12.5 %shard_map.122 = (bf16[32,64,256]{2,1,0:T(8,128)(2,1)}, bf16[32,64,256]{2,1,0:T(8,128)(2,1)}, bf16[32,64,256]{2,1,0:T(8,128)(2,1)}, bf16[32,64,256]{2,1,0:T(8,128)(2,1)}) custom-call(s32[2,2]{1,0:T(2,128)} %get-tuple-element.87.places_ref, s32[16,8]{1,0:T(8,128)} %copy.42.mask_ref, bf16[1024,256]{1,0:T(8,128)(2,1)} %fusion.24.screened_ref, ...), custom_call_target="tpu_custom_call" | custom-call | tf_op jit(solution)/shard_map/pallas_call | solution.py:184
  447.2 12.5 %shard_map.123 = (bf16[32,64,256]{2,1,0:T(8,128)(2,1)}, bf16[32,64,256]{2,1,0:T(8,128)(2,1)}, bf16[32,64,256]{2,1,0:T(8,128)(2,1)}, bf16[32,64,256]{2,1,0:T(8,128)(2,1)}) custom-call(s32[2,2]{1,0:T(2,128)} %get-tuple-element.96.places_ref, s32[16,8]{1,0:T(8,128)} %copy.42.mask_ref, bf16[1024,256]{1,0:T(8,128)(2,1)} %fusion.24.screened_ref, ...), custom_call_target="tpu_custom_call" | custom-call | tf_op jit(solution)/shard_map/pallas_call | solution.py:184
  460.6 13.8 %broadcast_multiply_fusion = bf16[512,64,256]{2,1,0:T(8,128)(2,1)} fusion(bf16[512,64,256]{2,1,0:T(8,128)(2,1)} %param.12, bf16[512,256]{1,0:T(8,128)(2,1)S(1)} %copy.28), kind=kLoop, calls=%fused_computation.2 | loop fusion | flops 8388608 | bytes 33816576 | tf_op jit(solution)/shard_map/mul | solution.py:369
  474.3 17.6 %convert_bitcast_fusion = bf16[64,64,512]{2,1,0:T(8,128)(2,1)S(1)} fusion(bf16[512,64,256]{2,1,0:T(8,128)(2,1)} %broadcast_multiply_fusion, bf16[256,256]{1,0:T(8,128)(2,1)S(1)} %copy-done, s32[]{:T(128)S(6)} %select_n.167), kind=kOutput, calls=%fused_computation.4 | convolution fusion | flops 1075838976 | bytes 21004292 | tf_op jit(solution)/shard_map/qns,ls->nlq/dot_general | solution.py:371
  494.3 1.6 collective-permute-start.40
  495.9 1.9 add_convert_fusion.6
  499.3 1.9 add_convert_fusion.9
  501.2 1.6 add_convert_fusion.4
  503.4 3.5 fusion.15
  506.9 3.5 fusion.12
  510.4 8.8 %collective-permute-done.44 = bf16[32,64,256]{2,1,0:T(8,128)(2,1)S(1)} collective-permute-done((bf16[32,64,256]{2,1,0:T(8,128)(2,1)S(1)}, bf16[32,64,256]{2,1,0:T(8,128)(2,1)S(1)}, u32[]{:S(2)}, u32[]{:S(2)}) %collective-permute-start.44) | collective-permute-done | bytes 1048608 | tf_op jit(solution)/shard_map/ppermute | solution.py:20
  519.2 21.6 %collective-permute-done.45 = bf16[32,64,256]{2,1,0:T(8,128)(2,1)S(1)} collective-permute-done((bf16[32,64,256]{2,1,0:T(8,128)(2,1)S(1)}, bf16[32,64,256]{2,1,0:T(8,128)(2,1)S(1)}, u32[]{:S(2)}, u32[]{:S(2)}) %collective-permute-start.45) | collective-permute-done | bytes 1048608 | tf_op jit(solution)/shard_map/ppermute | solution.py:20
  541.4 3.7 fusion.21
  545.8 3.5 fusion.18
  550.1 3.0 collective-permute-done.46
  554.5 2.2 collective-permute-done.47
  557.0 4.5 collective-permute-done.48
  562.8 2.5 collective-permute-done.49
  565.3 3.4 maximum_bitcast_fusion
  (186 shorter events, 39.3 us)
Async XLA Ops:
  0.6 473.7 %copy-start = (bf16[256,256]{1,0:T(8,128)(2,1)S(1)}, bf16[256,256]{1,0:T(8,128)(2,1)}, u32[]{:S(2)}) copy-start(bf16[256,256]{1,0:T(8,128)(2,1)} %param.13) | copy-start | bytes 393220
  7.9 22.2 %collective-permute-start.1 = (bf16[2,1664,128]{2,1,0:T(8,128)(2,1)}, bf16[2,1664,128]{2,1,0:T(8,128)(2,1)}, u32[]{:S(2)}, u32[]{:S(2)}) collective-permute-start(bf16[2,1664,128]{2,1,0:T(8,128)(2,1)} %get-tuple-element.137), channel_id=1, source_target_pairs={{0,16},{8,24},{16,0},{24,8},{1,17},{9,25},{17,1},{25,9},{2,18},{10... | collective-permute-start | bytes 2555912 | tf_op jit(solution)/shard_map/ppermute | solution.py:20
  16.2 245.5 %copy-start.1 = (bf16[512,1664]{1,0:T(8,128)(2,1)}, bf16[512,1664]{1,0:T(8,128)(2,1)S(1)}, u32[]{:S(2)}) copy-start(bf16[512,1664]{1,0:T(8,128)(2,1)S(1)} %get-tuple-element.121.refs_0_) | copy-start | bytes 5111812
  16.2 245.6 %copy-start.2 = (bf16[512,1664]{1,0:T(8,128)(2,1)}, bf16[512,1664]{1,0:T(8,128)(2,1)S(1)}, u32[]{:S(2)}) copy-start(bf16[512,1664]{1,0:T(8,128)(2,1)S(1)} %get-tuple-element.65.refs_1_) | copy-start | bytes 5111812
  16.2 38.8 %collective-permute-start = (bf16[512,1664]{1,0:T(8,128)(2,1)S(1)}, bf16[512,1664]{1,0:T(8,128)(2,1)}, u32[]{:S(2)}, u32[]{:S(2)}) collective-permute-start(bf16[512,1664]{1,0:T(8,128)(2,1)S(1)} %get-tuple-element.121.refs_0_), channel_id=1, source_target_pairs={{0,2},{1,3},{2,0},{3,1},{4,6},{5,7},{6,4},{7,5},{8,10},{9,11},{10,... | collective-permute-start | bytes 5111816 | tf_op jit(solution)/shard_map/ppermute | solution.py:20
  30.2 44.0 %collective-permute-start.12 = (bf16[512,1664]{1,0:T(8,128)(2,1)}, bf16[512,1664]{1,0:T(8,128)(2,1)}, u32[]{:S(2)}, u32[]{:S(2)}) collective-permute-start(bf16[512,1664]{1,0:T(8,128)(2,1)} %get-tuple-element.76), channel_id=1, source_target_pairs={{0,16},{8,24},{16,0},{24,8},{1,17},{9,25},{17,1},{25,9},{2,18},{10... | collective-permute-start | bytes 5111816 | tf_op jit(solution)/shard_map/ppermute | solution.py:20
  54.9 56.1 %collective-permute-start.3 = (bf16[512,1664]{1,0:T(8,128)(2,1)S(1)}, bf16[512,1664]{1,0:T(8,128)(2,1)}, u32[]{:S(2)}, u32[]{:S(2)}) collective-permute-start(bf16[512,1664]{1,0:T(8,128)(2,1)S(1)} %get-tuple-element.65.refs_1_), channel_id=1, source_target_pairs={{0,2},{1,3},{2,0},{3,1},{4,6},{5,7},{6,4},{7,5},{8,10},{9,11},{10,... | collective-permute-start | bytes 5111816 | tf_op jit(solution)/shard_map/ppermute | solution.py:20
  59.0 51.2 %collective-permute-start.4 = (bf16[2,1664,128]{2,1,0:T(8,128)(2,1)}, bf16[2,1664,128]{2,1,0:T(8,128)(2,1)}, u32[]{:S(2)}, u32[]{:S(2)}) collective-permute-start(bf16[2,1664,128]{2,1,0:T(8,128)(2,1)} %get-tuple-element.132), channel_id=1, source_target_pairs={{0,4},{1,5},{2,6},{3,7},{4,0},{5,1},{6,2},{7,3},{8,12},{9,13},{10,... | collective-permute-start | bytes 2555912 | tf_op jit(solution)/shard_map/ppermute | solution.py:20
  61.5 53.7 %copy-start.3 = (bf16[2,1664,512]{2,1,0:T(8,128)(2,1)S(1)}, bf16[2,1664,512]{2,1,0:T(8,128)(2,1)}, u32[]{:S(2)}) copy-start(bf16[2,1664,512]{2,1,0:T(8,128)(2,1)} %get-tuple-element.82) | copy-start | bytes 10223620
  61.5 48.6 %collective-permute-start.5 = (bf16[2,1664,128]{2,1,0:T(8,128)(2,1)S(1)}, bf16[2,1664,128]{2,1,0:T(8,128)(2,1)}, u32[]{:S(2)}, u32[]{:S(2)}) collective-permute-start(bf16[2,1664,128]{2,1,0:T(8,128)(2,1)S(1)} %get-tuple-element.131.refs_8_), channel_id=1, source_target_pairs={{0,8},{8,0},{16,24},{24,16},{1,9},{9,1},{17,25},{25,17},{2,10},{10... | collective-permute-start | bytes 2555912 | tf_op jit(solution)/shard_map/ppermute | solution.py:20
  73.7 36.4 %collective-permute-start.2 = (bf16[2,1664,128]{2,1,0:T(8,128)(2,1)}, bf16[2,1664,128]{2,1,0:T(8,128)(2,1)S(1)}, u32[]{:S(2)}, u32[]{:S(2)}) collective-permute-start(bf16[2,1664,128]{2,1,0:T(8,128)(2,1)} %get-tuple-element.62), channel_id=1, source_target_pairs={{0,16},{8,24},{16,0},{24,8},{1,17},{9,25},{17,1},{25,9},{2,18},{10... | collective-permute-start | bytes 2555912 | tf_op jit(solution)/shard_map/ppermute | solution.py:20
  74.2 65.1 %collective-permute-start.13 = (bf16[512,1664]{1,0:T(8,128)(2,1)}, bf16[512,1664]{1,0:T(8,128)(2,1)}, u32[]{:S(2)}, u32[]{:S(2)}) collective-permute-start(bf16[512,1664]{1,0:T(8,128)(2,1)} %get-tuple-element.77), channel_id=1, source_target_pairs={{0,16},{8,24},{16,0},{24,8},{1,17},{9,25},{17,1},{25,9},{2,18},{10... | collective-permute-start | bytes 5111816 | tf_op jit(solution)/shard_map/ppermute | solution.py:20
  111.0 56.3 %collective-permute-start.16 = (bf16[512,1664]{1,0:T(8,128)(2,1)}, bf16[512,1664]{1,0:T(8,128)(2,1)}, u32[]{:S(2)}, u32[]{:S(2)}) collective-permute-start(bf16[512,1664]{1,0:T(8,128)(2,1)} %collective-permute-done.12.refs_0_), channel_id=1, source_target_pairs={{0,2},{1,3},{2,0},{3,1},{4,6},{5,7},{6,4},{7,5},{8,10},{9,11},{10,... | collective-permute-start | bytes 5111816 | tf_op jit(solution)/shard_map/ppermute | solution.py:20
  113.7 27.7 %collective-permute-start.7 = (bf16[2,1664,128]{2,1,0:T(8,128)(2,1)}, bf16[2,1664,128]{2,1,0:T(8,128)(2,1)S(1)}, u32[]{:S(2)}, u32[]{:S(2)}) collective-permute-start(bf16[2,1664,128]{2,1,0:T(8,128)(2,1)} %collective-permute-done.4.refs_10_), channel_id=1, source_target_pairs={{0,8},{8,0},{16,24},{24,16},{1,9},{9,1},{17,25},{25,17},{2,10},{10... | collective-permute-start | bytes 2555912 | tf_op jit(solution)/shard_map/ppermute | solution.py:20
  127.2 39.7 %collective-permute-start.6 = (bf16[2,1664,128]{2,1,0:T(8,128)(2,1)}, bf16[2,1664,128]{2,1,0:T(8,128)(2,1)}, u32[]{:S(2)}, u32[]{:S(2)}) collective-permute-start(bf16[2,1664,128]{2,1,0:T(8,128)(2,1)} %get-tuple-element.68), channel_id=1, source_target_pairs={{0,4},{1,5},{2,6},{3,7},{4,0},{5,1},{6,2},{7,3},{8,12},{9,13},{10,... | collective-permute-start | bytes 2555912 | tf_op jit(solution)/shard_map/ppermute | solution.py:20
  139.4 28.0 %collective-permute-start.17 = (bf16[2,1664,128]{2,1,0:T(8,128)(2,1)}, bf16[2,1664,128]{2,1,0:T(8,128)(2,1)S(1)}, u32[]{:S(2)}, u32[]{:S(2)}) collective-permute-start(bf16[2,1664,128]{2,1,0:T(8,128)(2,1)} %get-tuple-element.79), channel_id=1, source_target_pairs={{0,16},{8,24},{16,0},{24,8},{1,17},{9,25},{17,1},{25,9},{2,18},{10... | collective-permute-start | bytes 2555912 | tf_op jit(solution)/shard_map/ppermute | solution.py:20
  139.9 35.7 %collective-permute-start.9 = (bf16[2,1664,128]{2,1,0:T(8,128)(2,1)}, bf16[2,1664,128]{2,1,0:T(8,128)(2,1)S(1)}, u32[]{:S(2)}, u32[]{:S(2)}) collective-permute-start(bf16[2,1664,128]{2,1,0:T(8,128)(2,1)} %get-tuple-element.71), channel_id=1, source_target_pairs={{0,16},{8,24},{16,0},{24,8},{1,17},{9,25},{17,1},{25,9},{2,18},{10... | collective-permute-start | bytes 2555912 | tf_op jit(solution)/shard_map/ppermute | solution.py:20
  141.4 27.6 %copy-start.18 = (bf16[2,1664,128]{2,1,0:T(8,128)(2,1)}, bf16[2,1664,128]{2,1,0:T(8,128)(2,1)S(1)}, u32[]{:S(2)}) copy-start(bf16[2,1664,128]{2,1,0:T(8,128)(2,1)S(1)} %collective-permute-done.7.refs_14_) | copy-start | bytes 2555908
  141.4 34.4 %collective-permute-start.10 = (bf16[2,1664,128]{2,1,0:T(8,128)(2,1)}, bf16[2,1664,128]{2,1,0:T(8,128)(2,1)S(1)}, u32[]{:S(2)}, u32[]{:S(2)}) collective-permute-start(bf16[2,1664,128]{2,1,0:T(8,128)(2,1)} %get-tuple-element.73.refs_9_), channel_id=1, source_target_pairs={{0,8},{8,0},{16,24},{24,16},{1,9},{9,1},{17,25},{25,17},{2,10},{10... | collective-permute-start | bytes 2555912 | tf_op jit(solution)/shard_map/ppermute | solution.py:20
  167.4 54.7 %collective-permute-start.18 = (bf16[512,1664]{1,0:T(8,128)(2,1)}, bf16[512,1664]{1,0:T(8,128)(2,1)S(1)}, u32[]{:S(2)}, u32[]{:S(2)}) collective-permute-start(bf16[512,1664]{1,0:T(8,128)(2,1)} %collective-permute-done.13.refs_1_), channel_id=1, source_target_pairs={{0,2},{1,3},{2,0},{3,1},{4,6},{5,7},{6,4},{7,5},{8,10},{9,11},{10,... | collective-permute-start | bytes 5111816 | tf_op jit(solution)/shard_map/ppermute | solution.py:20
  169.0 54.6 %collective-permute-start.14 = (bf16[512,1664]{1,0:T(8,128)(2,1)}, bf16[512,1664]{1,0:T(8,128)(2,1)S(1)}, u32[]{:S(2)}, u32[]{:S(2)}) collective-permute-start(bf16[512,1664]{1,0:T(8,128)(2,1)} %collective-permute-done.12.refs_0_), channel_id=1, source_target_pairs={{0,1},{1,0},{2,3},{3,2},{4,5},{5,4},{6,7},{7,6},{8,9},{9,8},{10,11... | collective-permute-start | bytes 5111816 | tf_op jit(solution)/shard_map/ppermute | solution.py:20
  175.7 86.5 %copy-start.6 = (bf16[2,1664,128]{2,1,0:T(8,128)(2,1)}, bf16[2,1664,128]{2,1,0:T(8,128)(2,1)S(1)}, u32[]{:S(2)}) copy-start(bf16[2,1664,128]{2,1,0:T(8,128)(2,1)S(1)} %get-tuple-element.85.refs_8_) | copy-start | bytes 2555908
  175.8 45.5 %collective-permute-start.11 = (bf16[2,1664,128]{2,1,0:T(8,128)(2,1)S(1)}, bf16[2,1664,128]{2,1,0:T(8,128)(2,1)S(1)}, u32[]{:S(2)}, u32[]{:S(2)}) collective-permute-start(bf16[2,1664,128]{2,1,0:T(8,128)(2,1)S(1)} %get-tuple-element.74), channel_id=1, source_target_pairs={{0,4},{1,5},{2,6},{3,7},{4,0},{5,1},{6,2},{7,3},{8,12},{9,13},{10,... | collective-permute-start | bytes 2555912 | tf_op jit(solution)/shard_map/ppermute | solution.py:20
  177.3 44.8 %collective-permute-start.8 = (bf16[2,1664,128]{2,1,0:T(8,128)(2,1)}, bf16[2,1664,128]{2,1,0:T(8,128)(2,1)S(1)}, u32[]{:S(2)}, u32[]{:S(2)}) collective-permute-start(bf16[2,1664,128]{2,1,0:T(8,128)(2,1)} %collective-permute-done.6.refs_11_), channel_id=1, source_target_pairs={{0,8},{8,0},{16,24},{24,16},{1,9},{9,1},{17,25},{25,17},{2,10},{10... | collective-permute-start | bytes 2555912 | tf_op jit(solution)/shard_map/ppermute | solution.py:20
  177.8 83.9 %collective-permute-start.15 = (bf16[512,1664]{1,0:T(8,128)(2,1)}, bf16[512,1664]{1,0:T(8,128)(2,1)S(1)}, u32[]{:S(2)}, u32[]{:S(2)}) collective-permute-start(bf16[512,1664]{1,0:T(8,128)(2,1)} %collective-permute-done.13.refs_1_), channel_id=1, source_target_pairs={{0,1},{1,0},{2,3},{3,2},{4,5},{5,4},{6,7},{7,6},{8,9},{9,8},{10,11... | collective-permute-start | bytes 5111816 | tf_op jit(solution)/shard_map/ppermute | solution.py:20
  221.3 41.1 %copy-start.15 = (bf16[2,1664,128]{2,1,0:T(8,128)(2,1)}, bf16[2,1664,128]{2,1,0:T(8,128)(2,1)S(1)}, u32[]{:S(2)}) copy-start(bf16[2,1664,128]{2,1,0:T(8,128)(2,1)S(1)} %collective-permute-done.11.refs_10_) | copy-start | bytes 2555908
  221.3 41.0 %collective-permute-start.19 = (bf16[512,1664]{1,0:T(8,128)(2,1)}, bf16[512,1664]{1,0:T(8,128)(2,1)S(1)}, u32[]{:S(2)}, u32[]{:S(2)}) collective-permute-start(bf16[512,1664]{1,0:T(8,128)(2,1)} %collective-permute-done.16.refs_4_), channel_id=1, source_target_pairs={{0,1},{1,0},{2,3},{3,2},{4,5},{5,4},{6,7},{7,6},{8,9},{9,8},{10,11... | collective-permute-start | bytes 5111816 | tf_op jit(solution)/shard_map/ppermute | solution.py:20
  222.0 40.2 %copy-start.8 = (bf16[512,1664]{1,0:T(8,128)(2,1)}, bf16[512,1664]{1,0:T(8,128)(2,1)S(1)}, u32[]{:S(2)}) copy-start(bf16[512,1664]{1,0:T(8,128)(2,1)S(1)} %collective-permute-done.18.refs_5_) | copy-start | bytes 5111812
  222.0 40.3 %collective-permute-start.20 = (bf16[512,1664]{1,0:T(8,128)(2,1)S(1)}, bf16[512,1664]{1,0:T(8,128)(2,1)S(1)}, u32[]{:S(2)}, u32[]{:S(2)}) collective-permute-start(bf16[512,1664]{1,0:T(8,128)(2,1)S(1)} %collective-permute-done.18.refs_5_), channel_id=1, source_target_pairs={{0,1},{1,0},{2,3},{3,2},{4,5},{5,4},{6,7},{7,6},{8,9},{9,8},{10,11... | collective-permute-start | bytes 5111816 | tf_op jit(solution)/shard_map/ppermute | solution.py:20
  222.1 21.8 %collective-permute-start.28 = (bf16[2,1664,128]{2,1,0:T(8,128)(2,1)S(1)}, bf16[2,1664,128]{2,1,0:T(8,128)(2,1)S(1)}, u32[]{:S(2)}, u32[]{:S(2)}) collective-permute-start(bf16[2,1664,128]{2,1,0:T(8,128)(2,1)S(1)} %get-tuple-element.85.refs_8_), channel_id=1, source_target_pairs={{0,8},{8,0},{16,24},{24,16},{1,9},{9,1},{17,25},{25,17},{2,10},{10... | collective-permute-start | bytes 2555912 | tf_op jit(solution)/shard_map/ppermute | solution.py:20
  223.6 38.8 %copy-start.9 = (bf16[512,1664]{1,0:T(8,128)(2,1)}, bf16[512,1664]{1,0:T(8,128)(2,1)S(1)}, u32[]{:S(2)}) copy-start(bf16[512,1664]{1,0:T(8,128)(2,1)S(1)} %collective-permute-done.14.refs_2_) | copy-start | bytes 5111812
  223.6 38.1 %collective-permute-start.29 = (bf16[2,1664,128]{2,1,0:T(8,128)(2,1)S(1)}, bf16[2,1664,128]{2,1,0:T(8,128)(2,1)S(1)}, u32[]{:S(2)}, u32[]{:S(2)}) collective-permute-start(bf16[2,1664,128]{2,1,0:T(8,128)(2,1)S(1)} %collective-permute-done.11.refs_10_), channel_id=1, source_target_pairs={{0,8},{8,0},{16,24},{24,16},{1,9},{9,1},{17,25},{25,17},{2,10},{10... | collective-permute-start | bytes 2555912 | tf_op jit(solution)/shard_map/ppermute | solution.py:20
  243.9 18.5 %copy-start.16 = (bf16[2,1664,128]{2,1,0:T(8,128)(2,1)}, bf16[2,1664,128]{2,1,0:T(8,128)(2,1)S(1)}, u32[]{:S(2)}) copy-start(bf16[2,1664,128]{2,1,0:T(8,128)(2,1)S(1)} %collective-permute-done.28.refs_12_) | copy-start | bytes 2555908
  243.9 45.9 %collective-permute-start.21 = (bf16[2,1664,128]{2,1,0:T(8,128)(2,1)}, bf16[2,1664,128]{2,1,0:T(8,128)(2,1)}, u32[]{:S(2)}, u32[]{:S(2)}) collective-permute-start(bf16[2,1664,128]{2,1,0:T(8,128)(2,1)} %get-tuple-element.83), channel_id=1, source_target_pairs={{0,4},{1,5},{2,6},{3,7},{4,0},{5,1},{6,2},{7,3},{8,12},{9,13},{10,... | collective-permute-start | bytes 2555912 | tf_op jit(solution)/shard_map/ppermute | solution.py:20
  261.7 28.7 %collective-permute-start.22 = (bf16[512,1664]{1,0:T(8,128)(2,1)S(1)}, bf16[512,1664]{1,0:T(8,128)(2,1)}, u32[]{:S(2)}, u32[]{:S(2)}) collective-permute-start(bf16[512,1664]{1,0:T(8,128)(2,1)S(1)} %get-tuple-element.121.refs_0_), channel_id=1, source_target_pairs={{0,1},{1,0},{2,3},{3,2},{4,5},{5,4},{6,7},{7,6},{8,9},{9,8},{10,11... | collective-permute-start | bytes 5111816 | tf_op jit(solution)/shard_map/ppermute | solution.py:20
  261.7 30.3 %collective-permute-start.23 = (bf16[512,1664]{1,0:T(8,128)(2,1)S(1)}, bf16[512,1664]{1,0:T(8,128)(2,1)}, u32[]{:S(2)}, u32[]{:S(2)}) collective-permute-start(bf16[512,1664]{1,0:T(8,128)(2,1)S(1)} %get-tuple-element.65.refs_1_), channel_id=1, source_target_pairs={{0,1},{1,0},{2,3},{3,2},{4,5},{5,4},{6,7},{7,6},{8,9},{9,8},{10,11... | collective-permute-start | bytes 5111816 | tf_op jit(solution)/shard_map/ppermute | solution.py:20
  262.3 30.1 %collective-permute-start.24 = (bf16[512,1664]{1,0:T(8,128)(2,1)}, bf16[512,1664]{1,0:T(8,128)(2,1)}, u32[]{:S(2)}, u32[]{:S(2)}) collective-permute-start(bf16[512,1664]{1,0:T(8,128)(2,1)} %collective-permute-done.refs_4_), channel_id=1, source_target_pairs={{0,1},{1,0},{2,3},{3,2},{4,5},{5,4},{6,7},{7,6},{8,9},{9,8},{10,11... | collective-permute-start | bytes 5111816 | tf_op jit(solution)/shard_map/ppermute | solution.py:20
  264.8 27.5 %collective-permute-start.25 = (bf16[512,1664]{1,0:T(8,128)(2,1)}, bf16[512,1664]{1,0:T(8,128)(2,1)}, u32[]{:S(2)}, u32[]{:S(2)}) collective-permute-start(bf16[512,1664]{1,0:T(8,128)(2,1)} %collective-permute-done.3.refs_5_), channel_id=1, source_target_pairs={{0,1},{1,0},{2,3},{3,2},{4,5},{5,4},{6,7},{7,6},{8,9},{9,8},{10,11... | collective-permute-start | bytes 5111816 | tf_op jit(solution)/shard_map/ppermute | solution.py:20
  289.8 25.6 %collective-permute-start.26 = (bf16[1024,512]{1,0:T(8,128)(2,1)}, bf16[1024,512]{1,0:T(8,128)(2,1)S(1)}, u32[]{:S(2)}, u32[]{:S(2)}) collective-permute-start(bf16[1024,512]{1,0:T(8,128)(2,1)} %shard_map.116), channel_id=1, source_target_pairs={{0,16},{8,24},{16,0},{24,8},{1,17},{9,25},{17,1},{25,9},{2,18},{10... | collective-permute-start | bytes 3145736 | tf_op jit(solution)/shard_map/ppermute | solution.py:20
  290.4 70.4 %collective-permute-start.30 = (bf16[2,1664,128]{2,1,0:T(8,128)(2,1)}, bf16[2,1664,128]{2,1,0:T(8,128)(2,1)S(1)}, u32[]{:S(2)}, u32[]{:S(2)}) collective-permute-start(bf16[2,1664,128]{2,1,0:T(8,128)(2,1)} %get-tuple-element.93.refs_9_), channel_id=1, source_target_pairs={{0,8},{8,0},{16,24},{24,16},{1,9},{9,1},{17,25},{25,17},{2,10},{10... | collective-permute-start | bytes 2555912 | tf_op jit(solution)/shard_map/ppermute | solution.py:20
  292.0 68.8 %collective-permute-start.31 = (bf16[2,1664,128]{2,1,0:T(8,128)(2,1)}, bf16[2,1664,128]{2,1,0:T(8,128)(2,1)}, u32[]{:S(2)}, u32[]{:S(2)}) collective-permute-start(bf16[2,1664,128]{2,1,0:T(8,128)(2,1)} %collective-permute-done.21.refs_11_), channel_id=1, source_target_pairs={{0,8},{8,0},{16,24},{24,16},{1,9},{9,1},{17,25},{25,17},{2,10},{10... | collective-permute-start | bytes 2555912 | tf_op jit(solution)/shard_map/ppermute | solution.py:20
  318.2 25.9 %collective-permute-start.27 = (bf16[1024,256]{1,0:T(8,128)(2,1)}, bf16[1024,256]{1,0:T(8,128)(2,1)}, u32[]{:S(2)}, u32[]{:S(2)}) collective-permute-start(bf16[1024,256]{1,0:T(8,128)(2,1)} %slice.85), channel_id=1, source_target_pairs={{0,4},{1,5},{2,6},{3,7},{4,0},{5,1},{6,2},{7,3},{8,12},{9,13},{10,... | collective-permute-start | bytes 1572872 | tf_op jit(solution)/shard_map/ppermute | solution.py:20
  358.6 32.5 %collective-permute-start.32 = (bf16[32,64,256]{2,1,0:T(8,128)(2,1)}, bf16[32,64,256]{2,1,0:T(8,128)(2,1)}, u32[]{:S(2)}, u32[]{:S(2)}) collective-permute-start(bf16[32,64,256]{2,1,0:T(8,128)(2,1)} %get-tuple-element.89), channel_id=1, source_target_pairs={{0,8},{8,0},{16,24},{24,16},{1,9},{9,1},{17,25},{25,17},{2,10},{10... | collective-permute-start | bytes 3145736 | tf_op jit(solution)/shard_map/ppermute | solution.py:20
  360.3 30.8 %collective-permute-start.33 = (bf16[32,64,256]{2,1,0:T(8,128)(2,1)}, bf16[32,64,256]{2,1,0:T(8,128)(2,1)S(1)}, u32[]{:S(2)}, u32[]{:S(2)}) collective-permute-start(bf16[32,64,256]{2,1,0:T(8,128)(2,1)} %get-tuple-element.91), channel_id=1, source_target_pairs={{0,16},{8,24},{16,0},{24,8},{1,17},{9,25},{17,1},{25,9},{2,18},{10... | collective-permute-start | bytes 3145736 | tf_op jit(solution)/shard_map/ppermute | solution.py:20
  360.8 16.2 %copy-start.36 = (s32[64,8]{0,1:T(8,128)S(1)}, s32[64,8]{0,1:T(8,128)}, u32[]{:S(2)}) copy-start(s32[64,8]{0,1:T(8,128)} %param.15) | copy-start | bytes 6148
  375.4 33.6 %collective-permute-start.34 = (bf16[1024,512]{1,0:T(8,128)(2,1)}, bf16[1024,512]{1,0:T(8,128)(2,1)S(1)}, u32[]{:S(2)}, u32[]{:S(2)}) collective-permute-start(bf16[1024,512]{1,0:T(8,128)(2,1)} %shard_map.119), channel_id=1, source_target_pairs={{0,16},{8,24},{16,0},{24,8},{1,17},{9,25},{17,1},{25,9},{2,18},{10... | collective-permute-start | bytes 3145736 | tf_op jit(solution)/shard_map/ppermute | solution.py:20
  377.4 68.2 %collective-permute-start.38 = (bf16[32,64,256]{2,1,0:T(8,128)(2,1)}, bf16[32,64,256]{2,1,0:T(8,128)(2,1)S(1)}, u32[]{:S(2)}, u32[]{:S(2)}) collective-permute-start(bf16[32,64,256]{2,1,0:T(8,128)(2,1)} %get-tuple-element.90), channel_id=1, source_target_pairs={{0,16},{8,24},{16,0},{24,8},{1,17},{9,25},{17,1},{25,9},{2,18},{10... | collective-permute-start | bytes 3145736 | tf_op jit(solution)/shard_map/ppermute | solution.py:20
  378.0 81.6 %collective-permute-start.36 = (bf16[32,64,256]{2,1,0:T(8,128)(2,1)}, bf16[32,64,256]{2,1,0:T(8,128)(2,1)S(1)}, u32[]{:S(2)}, u32[]{:S(2)}) collective-permute-start(bf16[32,64,256]{2,1,0:T(8,128)(2,1)} %get-tuple-element.88), channel_id=1, source_target_pairs={{0,8},{8,0},{16,24},{24,16},{1,9},{9,1},{17,25},{25,17},{2,10},{10... | collective-permute-start | bytes 3145736 | tf_op jit(solution)/shard_map/ppermute | solution.py:20
  411.1 20.9 %collective-permute-start.35 = (bf16[1024,256]{1,0:T(8,128)(2,1)S(1)}, bf16[1024,256]{1,0:T(8,128)(2,1)S(1)}, u32[]{:S(2)}, u32[]{:S(2)}) collective-permute-start(bf16[1024,256]{1,0:T(8,128)(2,1)S(1)} %slice.84), channel_id=1, source_target_pairs={{0,4},{1,5},{2,6},{3,7},{4,0},{5,1},{6,2},{7,3},{8,12},{9,13},{10,... | collective-permute-start | bytes 1572872 | tf_op jit(solution)/shard_map/ppermute | solution.py:20
  412.8 79.7 %collective-permute-start.37 = (bf16[32,64,256]{2,1,0:T(8,128)(2,1)S(1)}, bf16[32,64,256]{2,1,0:T(8,128)(2,1)}, u32[]{:S(2)}, u32[]{:S(2)}) collective-permute-start(bf16[32,64,256]{2,1,0:T(8,128)(2,1)S(1)} %add_convert_fusion.10), channel_id=1, source_target_pairs={{0,16},{8,24},{16,0},{24,8},{1,17},{9,25},{17,1},{25,9},{2,18},{10... | collective-permute-start | bytes 3145736 | tf_op jit(solution)/shard_map/ppermute | solution.py:20
  413.8 80.4 %collective-permute-start.39 = (bf16[32,64,256]{2,1,0:T(8,128)(2,1)S(1)}, bf16[32,64,256]{2,1,0:T(8,128)(2,1)S(1)}, u32[]{:S(2)}, u32[]{:S(2)}) collective-permute-start(bf16[32,64,256]{2,1,0:T(8,128)(2,1)S(1)} %add_convert_fusion.7), channel_id=1, source_target_pairs={{0,8},{8,0},{16,24},{24,16},{1,9},{9,1},{17,25},{25,17},{2,10},{10... | collective-permute-start | bytes 3145736 | tf_op jit(solution)/shard_map/ppermute | solution.py:20
  446.7 51.2 %collective-permute-start.42 = (bf16[32,64,256]{2,1,0:T(8,128)(2,1)}, bf16[32,64,256]{2,1,0:T(8,128)(2,1)S(1)}, u32[]{:S(2)}, u32[]{:S(2)}) collective-permute-start(bf16[32,64,256]{2,1,0:T(8,128)(2,1)} %get-tuple-element.112), channel_id=1, source_target_pairs={{0,16},{8,24},{16,0},{24,8},{1,17},{9,25},{17,1},{25,9},{2,18},{10... | collective-permute-start | bytes 3145736 | tf_op jit(solution)/shard_map/ppermute | solution.py:20
  459.7 38.6 %collective-permute-start.41 = (bf16[32,64,256]{2,1,0:T(8,128)(2,1)}, bf16[32,64,256]{2,1,0:T(8,128)(2,1)}, u32[]{:S(2)}, u32[]{:S(2)}) collective-permute-start(bf16[32,64,256]{2,1,0:T(8,128)(2,1)} %get-tuple-element.111), channel_id=1, source_target_pairs={{0,8},{8,0},{16,24},{24,16},{1,9},{9,1},{17,25},{25,17},{2,10},{10... | collective-permute-start | bytes 3145736 | tf_op jit(solution)/shard_map/ppermute | solution.py:20
  493.1 26.1 %collective-permute-start.44 = (bf16[32,64,256]{2,1,0:T(8,128)(2,1)S(1)}, bf16[32,64,256]{2,1,0:T(8,128)(2,1)S(1)}, u32[]{:S(2)}, u32[]{:S(2)}) collective-permute-start(bf16[32,64,256]{2,1,0:T(8,128)(2,1)S(1)} %copy-done.40), channel_id=1, source_target_pairs={{0,16},{8,24},{16,0},{24,8},{1,17},{9,25},{17,1},{25,9},{2,18},{10... | collective-permute-start | bytes 3145736 | tf_op jit(solution)/shard_map/ppermute | solution.py:20
  494.3 50.9 %collective-permute-start.40 = (bf16[32,64,256]{2,1,0:T(8,128)(2,1)S(1)}, bf16[32,64,256]{2,1,0:T(8,128)(2,1)S(1)}, u32[]{:S(2)}, u32[]{:S(2)}) collective-permute-start(bf16[32,64,256]{2,1,0:T(8,128)(2,1)S(1)} %copy-done.39), channel_id=1, source_target_pairs={{0,8},{8,0},{16,24},{24,16},{1,9},{9,1},{17,25},{25,17},{2,10},{10... | collective-permute-start | bytes 3145736 | tf_op jit(solution)/shard_map/ppermute | solution.py:20
  498.3 42.6 %collective-permute-start.45 = (bf16[32,64,256]{2,1,0:T(8,128)(2,1)S(1)}, bf16[32,64,256]{2,1,0:T(8,128)(2,1)S(1)}, u32[]{:S(2)}, u32[]{:S(2)}) collective-permute-start(bf16[32,64,256]{2,1,0:T(8,128)(2,1)S(1)} %add_convert_fusion.1), channel_id=1, source_target_pairs={{0,8},{8,0},{16,24},{24,16},{1,9},{9,1},{17,25},{25,17},{2,10},{10... | collective-permute-start | bytes 3145736 | tf_op jit(solution)/shard_map/ppermute | solution.py:20
  502.8 42.3 %collective-permute-start.43 = (bf16[32,64,256]{2,1,0:T(8,128)(2,1)S(1)}, bf16[32,64,256]{2,1,0:T(8,128)(2,1)S(1)}, u32[]{:S(2)}, u32[]{:S(2)}) collective-permute-start(bf16[32,64,256]{2,1,0:T(8,128)(2,1)S(1)} %add_convert_fusion.4), channel_id=1, source_target_pairs={{0,16},{8,24},{16,0},{24,8},{1,17},{9,25},{17,1},{25,9},{2,18},{10... | collective-permute-start | bytes 3145736 | tf_op jit(solution)/shard_map/ppermute | solution.py:20
  506.9 33.9 %copy-start.33 = (bf16[32,64,256]{2,1,0:T(8,128)(2,1)S(1)}, bf16[32,64,256]{2,1,0:T(8,128)(2,1)}, u32[]{:S(2)}) copy-start(bf16[32,64,256]{2,1,0:T(8,128)(2,1)} %get-tuple-element.114) | copy-start | bytes 3145732
  545.8 15.9 %copy-start.4 = (bf16[1024,256]{1,0:T(8,128)(2,1)S(1)}, bf16[1024,256]{1,0:T(8,128)(2,1)}, u32[]{:S(2)}) copy-start(bf16[1024,256]{1,0:T(8,128)(2,1)} %fusion.25.screened_ref) | copy-start | bytes 1572868
  549.3 3.8 collective-permute-start.46
  553.1 3.7 collective-permute-start.47
  556.9 4.6 collective-permute-start.48
  561.7 3.7 collective-permute-start.49
  565.3 3.5 collective-permute-start.50
  (28 other events, 141.7 us)

commit v5 on v4

--- a/solution.py
+++ b/solution.py
@@ -126,7 +126,7 @@
         out_specs=pl.BlockSpec((tall, near_l, wide), lambda i, g: (g, 0, i)),
         out_shape=jax.ShapeDtypeStruct((tile, near_l, rows), panel.dtype),
         compiler_params=pltpu.CompilerParams(vmem_limit_bytes=VMEM * MIB),
-        cost_estimate=NO_COST,
+        cost_estimate=pl.CostEstimate(flops=0, bytes_accessed=8 * rows * tile * near_l, transcendentals=0),
     )(panel)
 
 
@@ -235,6 +235,11 @@
     metric_other = lax.dynamic_index_in_dim(metric_parts, 1 - u, 1, keepdims=False)
     crossing = [metric_other[:, :, j * width : (j + 1) * width] for j in range(chunks)]
 
+    rb = panel_rows * row_count // mask_panel.shape[0]
+    ab = near_l // mask_panel.shape[1]
+    row_blocks = panel_rows // rb
+    panel_mask = lax.dynamic_slice_in_dim(mask_panel, r * row_blocks, row_blocks, 0)
+
     low = top_col // 2
 
     def cross(value, *others):
@@ -290,21 +295,29 @@
     turn_next(leave, *panels)
     near_crossed_first = swap(after(crossed_first, near_second, arrived[1], came[0][1], from_row(0, 0)), "col", low)
     for j in range(2, chunks):
+        due = [came[j - 2][1], near_second, from_row(0, 1), from_row(1, 0)]
         if j == 2:
             arrived.append(cross(crossing[j], arrived[1], *panels))
-            due = [came[0][1], near_second, from_row(0, 1), from_row(1, 0)]
         else:
-            turn_next(near_second, came[0][1], from_row(0, 0), *panels)
+            due.append(near_crossed_first)
+            while len(panels) < GROUPS:
+                turn_next(near_second, came[0][1], from_row(0, 0), *panels)
             arrived.append(cross(crossing[j], crossed_second, *panels))
-            due = [came[1][1], near_crossed_first, from_row(0, 1), from_row(1, 0)]
         far(j, *due)
-        gather_rows(came[j])
+    while len(panels) < GROUPS:
+        turn_next(near_second, *panels)
+
+    near_blocks = near_cols // rb
+    near_mask = lax.dynamic_slice_in_dim(mask_near, c * near_blocks, near_blocks, 0)
+    near_mask = jnp.repeat(jnp.repeat(near_mask, rb, 0), ab, 1).astype(jnp.bfloat16)
+    near = after(three_near, near_crossed_first, came[1][1]) * near_mask[:, None, :]
+    green = lax.dynamic_slice_in_dim(green_function, r * share, share, 0)
+    dressed = jnp.einsum("qns,ls->nlq", near, green, preferred_element_type=jnp.float32).astype(jnp.bfloat16)
+
     near_crossed_second = swap(
         after(crossed_second, near_crossed_first, arrived[-1], came[1][1], from_row(0, 1)), "col", low
     )
-    near_crossed_second = after(near_crossed_second, *[pair[1] for pair in came[2:3]])
-    while len(panels) < GROUPS:
-        turn_next(from_row(1, 1), *panels)
+    near_crossed_second = after(near_crossed_second, dressed, *panels, *[pair[1] for pair in came[2:3]])
 
     def gather_low(found):
         link = Link(1)
@@ -318,13 +331,8 @@
     blocks = c_low ^ jnp.arange(top_col, dtype=jnp.int32)
     order = ((blocks // per_block) ^ r_low) * per_block + blocks % per_block
 
-    rb = panel_rows * row_count // mask_panel.shape[0]
-    ab = near_l // mask_panel.shape[1]
-    row_blocks = panel_rows // rb
-    panel_mask = lax.dynamic_slice_in_dim(mask_panel, r * row_blocks, row_blocks, 0)
-
-    earlier = (*panels, *[pair[1] for pair in came[2:3]])
-    due, begun = [blocks[-1] for blocks in gathered[2:3]], [pair[1] for pair in came[3:4]]
+    earlier, due = (), [pair[1] for pair in came[3:4]]
+    ready = pieces_crossed[-1][-1]
     screened_chunks, contracted_chunks = [], []
     energy = jnp.zeros((tile, tile), jnp.float32)
     hops = {bit: Link(2) for bit in bits_below(row_count)}
@@ -335,17 +343,20 @@
     places = r ^ jnp.array(kept, jnp.int32)
     first_bits = jnp.array([[bits[0]] for bits in orders], jnp.int32)
     for j in range(0, chunks, pair):
+        for i in range(len(gathered), min(j + pair + 1, chunks)):
+            gather_rows([after(part, ready) for part in came[i]])
         sources = [[gathered[j + i][f][side] for side in range(2) for i in range(pair)] for f in range(top_row)]
         away = product(pieces_crossed, sources, after(order, *earlier), per_block, jnp.bfloat16)
-        home = product(pieces_mine, sources, after(order, away, *begun), per_block, jnp.float32)
-        home = home + swap(away, "row", top_row).astype(jnp.float32)
+        ready = away
+        home = product(pieces_mine, sources, after(order, away), per_block, jnp.float32)
+        home = after(home, *due) + swap(away, "row", top_row).astype(jnp.float32)
         came_back = swap(home[:, wide:].astype(jnp.bfloat16), "col", top_col)
         screened = (home[:, :wide] + came_back.astype(jnp.float32)).astype(jnp.bfloat16)
         screened_chunks.append(screened)
 
-        gone = contract(panels, screened, panel_mask, after(places ^ first_bits, due), rb, ab, share)
+        gone = contract(panels, screened, panel_mask, places ^ first_bits, rb, ab, share)
         stay = contract(panels, screened, panel_mask, after(places, gone), rb, ab, share)
-        earlier, due, begun = (home, *gone[0], *gone[1]), [], []
+        earlier, due = (home, *gone[0], *gone[1]), []
         left = [[dict(zip(kept[h], part[h])) for part in (gone, stay)] for h in range(2)]
         for hop in range(len(orders[0])):
             for h, bits in enumerate(orders):
@@ -354,7 +365,7 @@
                 total = {}
                 for e in sorted(going, key=lambda e: -(e & next_bit)):
                     value = hops[bits[hop]].swap(going[e], "row", bits[hop])
-                    begun += [value] if not hop and e & next_bit else []
+                    due += [value] if not hop and e & next_bit else []
                     total[e] = (staying[e].astype(jnp.float32) + value.astype(jnp.float32)).astype(jnp.bfloat16)
                 left[h] = [
                     {e & ~next_bit: value for e, value in total.items() if e & next_bit},
@@ -363,19 +374,13 @@
         halves = [left[h][1][0] for h in range(2)]
         contracted_chunks.append(halves)
 
-    near_blocks = near_cols // rb
-    near_mask = lax.dynamic_slice_in_dim(mask_near, c * near_blocks, near_blocks, 0)
-    near_mask = jnp.repeat(jnp.repeat(near_mask, rb, 0), ab, 1).astype(jnp.bfloat16)
-    near = after(three_near, *stay[0], *stay[1]) * near_mask[:, None, :]
-    green = lax.dynamic_slice_in_dim(green_function, r * share, share, 0)
-    dressed = jnp.einsum("qns,ls->nlq", near, green, preferred_element_type=jnp.float32).astype(jnp.bfloat16)
     for j, halves in enumerate(contracted_chunks):
         beside = dressed[:, :, j * wide : (j + 1) * wide]
         energy = energy - jnp.concatenate(
             [jnp.einsum("mlq,nlq->mn", half, beside, preferred_element_type=jnp.float32) for half in halves]
         )
-    energy = scatter_sum(scatter_sum(energy, "row").T, "col").T
     contracted = jnp.transpose(jnp.concatenate([jnp.concatenate(halves) for halves in contracted_chunks], axis=2), (2, 0, 1))
+    energy = scatter_sum(after(scatter_sum(energy, "row"), contracted).T, "col").T
     return jnp.concatenate(screened_chunks, axis=1), contracted, energy
 
 

time: 577 us -> 528 us (0.915)
  waiting for transfers between devices: 275 us -> 218 us
    ppermute x51, waiting for transfers between devices: 275 us -> 218 us  [swap(): return lax.ppermute(value, axis, [(i, i ^ bit) for i in range(size)])]
  transfers between devices with their start and end apart: 51 -> 51, of which waited for: 21 -> 21; matrix products, arithmetic and copies ran while one was open for 13% -> 17% of each run, Pallas kernels for 26% -> 28%
where the time goes in v5:
time: 528 us; the launch traced here: 524 us
  waiting for transfers between devices  218 us (41%)
  Pallas kernels  147 us (28%)
  starting transfers between devices  52.6 us (10%)
  other arithmetic  46 us (9%)
  matrix products  33 us (6%)
  local copies, waits for them, and re-layouts  26 us (5%)
    ppermute x51, waiting for transfers between devices, swap(): return lax.ppermute(value, axis, [(i, i ^ bit) for i in range(size)])  218 us
    pallas_call x4, Pallas kernels, product(): pl.pallas_call(functools.partial(product_kernel, count, parts, per_block)...  53.7 us
    ppermute x51, starting transfers between devices, swap(): return lax.ppermute(value, axis, [(i, i ^ bit) for i in range(size)])  52.6 us
    pallas_call x4, Pallas kernels, contract(): pl.pallas_call(functools.partial(contract_kernel, rb, ab), in_specs=[in_s...  50.1 us
    pallas_call x4, Pallas kernels, turn(): pl.pallas_call(turn_kernel, grid=(rows // wide, tile // tall), in_specs=[...  42.9 us
    dot_general x1, matrix products, per_device(): jnp.einsum('qns,ls->nlq', near, green, preferred_element_type=jnp.float32)  19.1 us
    dot_general x4, matrix products, per_device(): jnp.einsum('mlq,nlq->mn', half, beside, preferred_element_type=jnp.float32)  13.8 us
    mul x1, other arithmetic, per_device(): after(three_near, near_crossed_first, came[1][1]) * near_mask[:, None, :]  13.8 us
  transfers between devices with their start and end apart: 51, of which 21 were waited for; matrix products, arithmetic and copies ran while one was open for 17% of the time, Pallas kernels for 28%

profile of v5, /device:TPU:0, one launch (start us, length us, event | category | flops | bytes accessed | tf_op | source)
XLA Modules:
  0.0 524.2 jit_solution(2325045046077552742)
XLA Ops:
  0.7 5.3 %dynamic-slice_bitcast_fusion = (bf16[2,1664,512]{2,1,0:T(8,128)(2,1)}, bf16[2,1664,512]{2,1,0:T(8,128)(2,1)S(1)}) fusion(bf16[2,2,1664,512]{3,2,1,0:T(8,128)(2,1)} %bitcast.61, s32[]{:T(128)S(6)} %select_n.157, s32[]{:T(128)S(6)} %select_n.153), kind=kLoop, calls=%fused_computation.5 | loop fusion | bytes 13631496 | tf_op jit(solution)/shard_map/jit(dynamic_index_in_dim)/squeeze | solution.py:234
  6.0 2.1 fusion.43
  8.0 3.0 collective-permute-start
  11.0 5.2 fusion.41
  16.2 1.6 collective-permute-start.2
  17.8 12.5 %collective-permute-done = bf16[2,1664,128]{2,1,0:T(8,128)(2,1)} collective-permute-done((bf16[2,1664,128]{2,1,0:T(8,128)(2,1)}, bf16[2,1664,128]{2,1,0:T(8,128)(2,1)}, u32[]{:S(2)}, u32[]{:S(2)}) %collective-permute-start) | collective-permute-done | bytes 852000 | tf_op jit(solution)/shard_map/ppermute | solution.py:20
  30.2 1.7 collective-permute-start.1
  32.0 23.0 %collective-permute-done.2.refs_4_ = bf16[512,1664]{1,0:T(8,128)(2,1)} collective-permute-done((bf16[512,1664]{1,0:T(8,128)(2,1)S(1)}, bf16[512,1664]{1,0:T(8,128)(2,1)}, u32[]{:S(2)}, u32[]{:S(2)}) %collective-permute-start.2) | collective-permute-done | bytes 1703968 | tf_op jit(solution)/shard_map/ppermute | solution.py:20
  55.0 1.6 collective-permute-start.6
  57.1 2.4 broadcast_select_fusion.6
  59.5 2.6 collective-permute-start.8
  62.1 10.9 %shard_map.112.refs_0_ = bf16[64,256,256]{2,1,0:T(8,128)(2,1)} custom-call(bf16[1024,64,256]{2,1,0:T(8,128)(2,1)} %panel_ref.3), custom_call_target="tpu_custom_call" | custom-call | bytes 33554432 | tf_op jit(solution)/shard_map/pallas_call | solution.py:122
  76.0 12.8 %collective-permute-done.7 = bf16[2,1664,128]{2,1,0:T(8,128)(2,1)S(1)} collective-permute-done((bf16[2,1664,128]{2,1,0:T(8,128)(2,1)}, bf16[2,1664,128]{2,1,0:T(8,128)(2,1)S(1)}, u32[]{:S(2)}, u32[]{:S(2)}) %collective-permute-start.7) | collective-permute-done | bytes 852000 | tf_op jit(solution)/shard_map/ppermute | solution.py:20
  88.8 2.5 broadcast_select_fusion.3
  91.3 10.7 %shard_map.113.refs_1_ = bf16[64,256,256]{2,1,0:T(8,128)(2,1)} custom-call(bf16[1024,64,256]{2,1,0:T(8,128)(2,1)} %panel_ref.3), custom_call_target="tpu_custom_call" | custom-call | bytes 33554432 | tf_op jit(solution)/shard_map/pallas_call | solution.py:122
  102.0 8.1 %collective-permute-done.8.refs_10_ = bf16[2,1664,128]{2,1,0:T(8,128)(2,1)} collective-permute-done((bf16[2,1664,128]{2,1,0:T(8,128)(2,1)}, bf16[2,1664,128]{2,1,0:T(8,128)(2,1)}, u32[]{:S(2)}, u32[]{:S(2)}) %collective-permute-start.8) | collective-permute-done | bytes 852000 | tf_op jit(solution)/shard_map/ppermute | solution.py:20
  111.1 2.7 collective-permute-start.10
  116.3 10.6 %shard_map.114.refs_2_ = bf16[64,256,256]{2,1,0:T(8,128)(2,1)} custom-call(bf16[1024,64,256]{2,1,0:T(8,128)(2,1)} %panel_ref.3), custom_call_target="tpu_custom_call" | custom-call | bytes 33554432 | tf_op jit(solution)/shard_map/pallas_call | solution.py:122
  126.9 1.6 collective-permute-start.12
  128.5 10.6 %shard_map.115.refs_3_ = bf16[64,256,256]{2,1,0:T(8,128)(2,1)} custom-call(bf16[1024,64,256]{2,1,0:T(8,128)(2,1)} %panel_ref.3), custom_call_target="tpu_custom_call" | custom-call | bytes 33554432 | tf_op jit(solution)/shard_map/pallas_call | solution.py:122
  139.1 2.7 collective-permute-done.15
  146.5 1.8 copy.27
  148.3 2.6 broadcast_select_fusion.1
  150.8 2.6 collective-permute-start.17
  153.5 16.5 %collective-permute-done.12.refs_11_ = bf16[2,1664,128]{2,1,0:T(8,128)(2,1)} collective-permute-done((bf16[2,1664,128]{2,1,0:T(8,128)(2,1)}, bf16[2,1664,128]{2,1,0:T(8,128)(2,1)}, u32[]{:S(2)}, u32[]{:S(2)}) %collective-permute-start.12) | collective-permute-done | bytes 852000 | tf_op jit(solution)/shard_map/ppermute | solution.py:20
  171.5 2.5 collective-permute-start.14
  174.0 13.8 %broadcast_multiply_fusion = bf16[512,64,256]{2,1,0:T(8,128)(2,1)} fusion(bf16[512,64,256]{2,1,0:T(8,128)(2,1)} %param.12, bf16[512,256]{1,0:T(8,128)(2,1)S(1)} %copy-done.20), kind=kLoop, calls=%fused_computation.2 | loop fusion | flops 8388608 | bytes 33816576 | tf_op jit(solution)/shard_map/mul | solution.py:313
  187.8 17.3 %collective-permute-done.17.refs_10_ = bf16[2,1664,128]{2,1,0:T(8,128)(2,1)} collective-permute-done((bf16[2,1664,128]{2,1,0:T(8,128)(2,1)S(1)}, bf16[2,1664,128]{2,1,0:T(8,128)(2,1)}, u32[]{:S(2)}, u32[]{:S(2)}) %collective-permute-start.17) | collective-permute-done | bytes 852000 | tf_op jit(solution)/shard_map/ppermute | solution.py:20
  205.1 19.1 %convert_bitcast_fusion = bf16[64,64,512]{2,1,0:T(8,128)(2,1)} fusion(bf16[512,64,256]{2,1,0:T(8,128)(2,1)} %broadcast_multiply_fusion, bf16[256,256]{1,0:T(8,128)(2,1)S(1)} %copy-done, s32[]{:T(128)S(6)} %select_n.161), kind=kOutput, calls=%fused_computation.4 | convolution fusion | flops 1075838976 | bytes 21004292 | tf_op jit(solution)/shard_map/qns,ls->nlq/dot_general | solution.py:315
  224.3 5.8 %collective-permute-done.14.refs_5_ = bf16[512,1664]{1,0:T(8,128)(2,1)} collective-permute-done((bf16[512,1664]{1,0:T(8,128)(2,1)S(1)}, bf16[512,1664]{1,0:T(8,128)(2,1)}, u32[]{:S(2)}, u32[]{:S(2)}) %collective-permute-start.14) | collective-permute-done | bytes 1703968 | tf_op jit(solution)/shard_map/ppermute | solution.py:20
  235.6 13.2 %shard_map.116 = bf16[1024,512]{1,0:T(8,128)(2,1)} custom-call(s32[4]{0:T(128)} %fusion.40.order_ref, bf16[512,1664]{1,0:T(8,128)(2,1)} %collective-permute-done.1.refs_0_, bf16[512,1664]{1,0:T(8,128)(2,1)} %copy-done.8, bf16[512,1664]{1,0:T(8,128)(2,1)} %copy-done.10, bf16[512,1664]{1,0:T(8,128)(2,1)} %copy-done.11, ...), custom_call_target="tpu_custom_call" | custom-call | tf_op jit(solution)/shard_map/pallas_call | solution.py:97
  249.4 2.5 broadcast_select_fusion
  254.4 13.6 %shard_map.117 = f32[1024,512]{1,0:T(8,128)} custom-call(s32[4]{0:T(128)} %fusion.40.order_ref, bf16[512,1664]{1,0:T(8,128)(2,1)} %copy-done.3, bf16[512,1664]{1,0:T(8,128)(2,1)} %copy-done.2, bf16[512,1664]{1,0:T(8,128)(2,1)} %collective-permute-done.21.refs_2_, bf16[512,1664]{1,0:T(8,128)(2,1)} %collective-permute-done.22.refs_3_, ...), custom_call_target="tpu_custom_call" | custom-call | tf_op jit(solution)/shard_map/pallas_call | solution.py:97
  268.0 23.7 %collective-permute-done.25.refs_11_ = bf16[2,1664,128]{2,1,0:T(8,128)(2,1)S(1)} collective-permute-done((bf16[2,1664,128]{2,1,0:T(8,128)(2,1)S(1)}, bf16[2,1664,128]{2,1,0:T(8,128)(2,1)S(1)}, u32[]{:S(2)}, u32[]{:S(2)}) %collective-permute-start.25) | collective-permute-done | bytes 852000 | tf_op jit(solution)/shard_map/ppermute | solution.py:20
  292.2 1.6 collective-permute-start.31
  293.8 1.9 convert_add_fusion.1
  298.4 22.9 %collective-permute-done.27 = bf16[1024,256]{1,0:T(8,128)(2,1)} collective-permute-done((bf16[1024,256]{1,0:T(8,128)(2,1)}, bf16[1024,256]{1,0:T(8,128)(2,1)}, u32[]{:S(2)}, u32[]{:S(2)}) %collective-permute-start.27) | collective-permute-done | bytes 524320 | tf_op jit(solution)/shard_map/ppermute | solution.py:20
  321.3 2.0 fusion.25.screened_ref
  323.3 12.5 %shard_map.118 = (bf16[32,64,256]{2,1,0:T(8,128)(2,1)}, bf16[32,64,256]{2,1,0:T(8,128)(2,1)}, bf16[32,64,256]{2,1,0:T(8,128)(2,1)}, bf16[32,64,256]{2,1,0:T(8,128)(2,1)}) custom-call(s32[2,2]{1,0:T(2,128)} %get-tuple-element.154.places_ref, s32[16,8]{1,0:T(8,128)} %copy.42.mask_ref, bf16[1024,256]{1,0:T(8,128)(2,1)} %fusion.25.screened_ref, ...), custom_call_target="tpu_custom_call" | custom-call | tf_op jit(solution)/shard_map/pallas_call | solution.py:184
  338.8 13.2 %shard_map.119 = bf16[1024,512]{1,0:T(8,128)(2,1)} custom-call(s32[4]{0:T(128)} %fusion.40.order_ref, bf16[512,1664]{1,0:T(8,128)(2,1)} %collective-permute-done.1.refs_0_, bf16[512,1664]{1,0:T(8,128)(2,1)} %copy-done.8, bf16[512,1664]{1,0:T(8,128)(2,1)} %copy-done.10, bf16[512,1664]{1,0:T(8,128)(2,1)} %copy-done.11, ...), custom_call_target="tpu_custom_call" | custom-call | tf_op jit(solution)/shard_map/pallas_call | solution.py:97
  354.8 12.5 %shard_map.121 = (bf16[32,64,256]{2,1,0:T(8,128)(2,1)}, bf16[32,64,256]{2,1,0:T(8,128)(2,1)}, bf16[32,64,256]{2,1,0:T(8,128)(2,1)}, bf16[32,64,256]{2,1,0:T(8,128)(2,1)}) custom-call(s32[2,2]{1,0:T(2,128)} %get-tuple-element.106.places_ref, s32[16,8]{1,0:T(8,128)} %copy.42.mask_ref, bf16[1024,256]{1,0:T(8,128)(2,1)} %fusion.25.screened_ref, ...), custom_call_target="tpu_custom_call" | custom-call | tf_op jit(solution)/shard_map/pallas_call | solution.py:184
  367.4 13.6 %shard_map.120 = f32[1024,512]{1,0:T(8,128)} custom-call(s32[4]{0:T(128)} %fusion.40.order_ref, bf16[512,1664]{1,0:T(8,128)(2,1)} %copy-done.3, bf16[512,1664]{1,0:T(8,128)(2,1)} %copy-done.2, bf16[512,1664]{1,0:T(8,128)(2,1)} %collective-permute-done.21.refs_2_, bf16[512,1664]{1,0:T(8,128)(2,1)} %collective-permute-done.22.refs_3_, ...), custom_call_target="tpu_custom_call" | custom-call | tf_op jit(solution)/shard_map/pallas_call | solution.py:97
  381.0 5.0 collective-permute-done.34
  386.0 1.9 convert_add_fusion
  391.3 19.2 %collective-permute-done.35 = bf16[1024,256]{1,0:T(8,128)(2,1)S(1)} collective-permute-done((bf16[1024,256]{1,0:T(8,128)(2,1)S(1)}, bf16[1024,256]{1,0:T(8,128)(2,1)S(1)}, u32[]{:S(2)}, u32[]{:S(2)}) %collective-permute-start.35) | collective-permute-done | bytes 524320 | tf_op jit(solution)/shard_map/ppermute | solution.py:20
  411.5 12.5 %shard_map.122 = (bf16[32,64,256]{2,1,0:T(8,128)(2,1)}, bf16[32,64,256]{2,1,0:T(8,128)(2,1)}, bf16[32,64,256]{2,1,0:T(8,128)(2,1)}, bf16[32,64,256]{2,1,0:T(8,128)(2,1)}) custom-call(s32[2,2]{1,0:T(2,128)} %get-tuple-element.154.places_ref, s32[16,8]{1,0:T(8,128)} %copy.42.mask_ref, bf16[1024,256]{1,0:T(8,128)(2,1)} %fusion.24.screened_ref, ...), custom_call_target="tpu_custom_call" | custom-call | tf_op jit(solution)/shard_map/pallas_call | solution.py:184
  424.0 1.6 collective-permute-start.42
  428.0 2.8 fusion.42
  430.8 12.6 %shard_map.123 = (bf16[32,64,256]{2,1,0:T(8,128)(2,1)}, bf16[32,64,256]{2,1,0:T(8,128)(2,1)}, bf16[32,64,256]{2,1,0:T(8,128)(2,1)}, bf16[32,64,256]{2,1,0:T(8,128)(2,1)}) custom-call(s32[2,2]{1,0:T(2,128)} %get-tuple-element.106.places_ref, s32[16,8]{1,0:T(8,128)} %copy.42.mask_ref, bf16[1024,256]{1,0:T(8,128)(2,1)} %fusion.24.screened_ref, ...), custom_call_target="tpu_custom_call" | custom-call | tf_op jit(solution)/shard_map/pallas_call | solution.py:184
  444.6 2.5 add_convert_fusion.6
  447.1 6.4 %collective-permute-done.42 = bf16[32,64,256]{2,1,0:T(8,128)(2,1)} collective-permute-done((bf16[32,64,256]{2,1,0:T(8,128)(2,1)}, bf16[32,64,256]{2,1,0:T(8,128)(2,1)}, u32[]{:S(2)}, u32[]{:S(2)}) %collective-permute-start.42) | collective-permute-done | bytes 1048608 | tf_op jit(solution)/shard_map/ppermute | solution.py:20
  453.5 1.6 add_convert_fusion.1
  456.1 2.3 add_convert_fusion.9
  458.9 1.6 collective-permute-start.43
  460.4 3.5 fusion.15
  463.9 3.5 fusion.12
  467.4 8.5 %collective-permute-done.44 = bf16[32,64,256]{2,1,0:T(8,128)(2,1)S(1)} collective-permute-done((bf16[32,64,256]{2,1,0:T(8,128)(2,1)}, bf16[32,64,256]{2,1,0:T(8,128)(2,1)S(1)}, u32[]{:S(2)}, u32[]{:S(2)}) %collective-permute-start.44) | collective-permute-done | bytes 1048608 | tf_op jit(solution)/shard_map/ppermute | solution.py:20
  475.9 20.6 %collective-permute-done.45 = bf16[32,64,256]{2,1,0:T(8,128)(2,1)S(1)} collective-permute-done((bf16[32,64,256]{2,1,0:T(8,128)(2,1)S(1)}, bf16[32,64,256]{2,1,0:T(8,128)(2,1)S(1)}, u32[]{:S(2)}, u32[]{:S(2)}) %collective-permute-start.45) | collective-permute-done | bytes 1048608 | tf_op jit(solution)/shard_map/ppermute | solution.py:20
  497.1 3.5 fusion.21
  501.4 3.5 fusion.18
  505.5 3.2 collective-permute-done.46
  510.2 3.5 maximum_bitcast_fusion
  513.9 4.5 collective-permute-done.48
  518.7 3.5 collective-permute-done.49
  (180 shorter events, 45.5 us)
Async XLA Ops:
  0.6 204.5 %copy-start = (bf16[256,256]{1,0:T(8,128)(2,1)S(1)}, bf16[256,256]{1,0:T(8,128)(2,1)}, u32[]{:S(2)}) copy-start(bf16[256,256]{1,0:T(8,128)(2,1)} %param.13) | copy-start | bytes 393220
  8.0 22.2 %collective-permute-start = (bf16[2,1664,128]{2,1,0:T(8,128)(2,1)}, bf16[2,1664,128]{2,1,0:T(8,128)(2,1)}, u32[]{:S(2)}, u32[]{:S(2)}) collective-permute-start(bf16[2,1664,128]{2,1,0:T(8,128)(2,1)} %get-tuple-element.148), channel_id=1, source_target_pairs={{0,16},{8,24},{16,0},{24,8},{1,17},{9,25},{17,1},{25,9},{2,18},{10... | collective-permute-start | bytes 2555912 | tf_op jit(solution)/shard_map/ppermute | solution.py:20
  16.2 213.9 %copy-start.3 = (bf16[512,1664]{1,0:T(8,128)(2,1)}, bf16[512,1664]{1,0:T(8,128)(2,1)S(1)}, u32[]{:S(2)}) copy-start(bf16[512,1664]{1,0:T(8,128)(2,1)S(1)} %get-tuple-element.132.refs_0_) | copy-start | bytes 5111812
  16.2 214.5 %copy-start.2 = (bf16[512,1664]{1,0:T(8,128)(2,1)}, bf16[512,1664]{1,0:T(8,128)(2,1)S(1)}, u32[]{:S(2)}) copy-start(bf16[512,1664]{1,0:T(8,128)(2,1)S(1)} %get-tuple-element.69.refs_1_) | copy-start | bytes 5111812
  16.2 38.8 %collective-permute-start.2 = (bf16[512,1664]{1,0:T(8,128)(2,1)S(1)}, bf16[512,1664]{1,0:T(8,128)(2,1)}, u32[]{:S(2)}, u32[]{:S(2)}) collective-permute-start(bf16[512,1664]{1,0:T(8,128)(2,1)S(1)} %get-tuple-element.132.refs_0_), channel_id=1, source_target_pairs={{0,2},{1,3},{2,0},{3,1},{4,6},{5,7},{6,4},{7,5},{8,10},{9,11},{10,... | collective-permute-start | bytes 5111816 | tf_op jit(solution)/shard_map/ppermute | solution.py:20
  30.2 42.8 %collective-permute-start.1 = (bf16[512,1664]{1,0:T(8,128)(2,1)}, bf16[512,1664]{1,0:T(8,128)(2,1)}, u32[]{:S(2)}, u32[]{:S(2)}) collective-permute-start(bf16[512,1664]{1,0:T(8,128)(2,1)} %get-tuple-element.66), channel_id=1, source_target_pairs={{0,16},{8,24},{16,0},{24,8},{1,17},{9,25},{17,1},{25,9},{2,18},{10... | collective-permute-start | bytes 5111816 | tf_op jit(solution)/shard_map/ppermute | solution.py:20
  55.0 56.1 %collective-permute-start.6 = (bf16[512,1664]{1,0:T(8,128)(2,1)S(1)}, bf16[512,1664]{1,0:T(8,128)(2,1)}, u32[]{:S(2)}, u32[]{:S(2)}) collective-permute-start(bf16[512,1664]{1,0:T(8,128)(2,1)S(1)} %get-tuple-element.69.refs_1_), channel_id=1, source_target_pairs={{0,2},{1,3},{2,0},{3,1},{4,6},{5,7},{6,4},{7,5},{8,10},{9,11},{10,... | collective-permute-start | bytes 5111816 | tf_op jit(solution)/shard_map/ppermute | solution.py:20
  56.5 32.3 %collective-permute-start.7 = (bf16[2,1664,128]{2,1,0:T(8,128)(2,1)}, bf16[2,1664,128]{2,1,0:T(8,128)(2,1)S(1)}, u32[]{:S(2)}, u32[]{:S(2)}) collective-permute-start(bf16[2,1664,128]{2,1,0:T(8,128)(2,1)} %get-tuple-element.70), channel_id=1, source_target_pairs={{0,16},{8,24},{16,0},{24,8},{1,17},{9,25},{17,1},{25,9},{2,18},{10... | collective-permute-start | bytes 2555912 | tf_op jit(solution)/shard_map/ppermute | solution.py:20
  59.5 15.0 %copy-start.7 = (bf16[2,1664,128]{2,1,0:T(8,128)(2,1)}, bf16[2,1664,128]{2,1,0:T(8,128)(2,1)S(1)}, u32[]{:S(2)}) copy-start(bf16[2,1664,128]{2,1,0:T(8,128)(2,1)S(1)} %get-tuple-element.141.refs_8_) | copy-start | bytes 2555908
  59.5 50.7 %collective-permute-start.8 = (bf16[2,1664,128]{2,1,0:T(8,128)(2,1)}, bf16[2,1664,128]{2,1,0:T(8,128)(2,1)}, u32[]{:S(2)}, u32[]{:S(2)}) collective-permute-start(bf16[2,1664,128]{2,1,0:T(8,128)(2,1)} %get-tuple-element.142), channel_id=1, source_target_pairs={{0,4},{1,5},{2,6},{3,7},{4,0},{5,1},{6,2},{7,3},{8,12},{9,13},{10,... | collective-permute-start | bytes 2555912 | tf_op jit(solution)/shard_map/ppermute | solution.py:20
  73.0 53.9 %collective-permute-start.3 = (bf16[512,1664]{1,0:T(8,128)(2,1)}, bf16[512,1664]{1,0:T(8,128)(2,1)S(1)}, u32[]{:S(2)}, u32[]{:S(2)}) collective-permute-start(bf16[512,1664]{1,0:T(8,128)(2,1)} %get-tuple-element.68), channel_id=1, source_target_pairs={{0,16},{8,24},{16,0},{24,8},{1,17},{9,25},{17,1},{25,9},{2,18},{10... | collective-permute-start | bytes 5111816 | tf_op jit(solution)/shard_map/ppermute | solution.py:20
  74.5 35.7 %collective-permute-start.9 = (bf16[2,1664,128]{2,1,0:T(8,128)(2,1)S(1)}, bf16[2,1664,128]{2,1,0:T(8,128)(2,1)S(1)}, u32[]{:S(2)}, u32[]{:S(2)}) collective-permute-start(bf16[2,1664,128]{2,1,0:T(8,128)(2,1)S(1)} %get-tuple-element.141.refs_8_), channel_id=1, source_target_pairs={{0,8},{8,0},{16,24},{24,16},{1,9},{9,1},{17,25},{25,17},{2,10},{10... | collective-permute-start | bytes 2555912 | tf_op jit(solution)/shard_map/ppermute | solution.py:20
  91.3 22.5 %copy-start.32 = (bf16[2,1664,128]{2,1,0:T(8,128)(2,1)S(1)}, bf16[2,1664,128]{2,1,0:T(8,128)(2,1)}, u32[]{:S(2)}) copy-start(bf16[2,1664,128]{2,1,0:T(8,128)(2,1)} %get-tuple-element.81) | copy-start | bytes 2555908
  110.2 16.7 %copy-start.15 = (bf16[2,1664,128]{2,1,0:T(8,128)(2,1)}, bf16[2,1664,128]{2,1,0:T(8,128)(2,1)S(1)}, u32[]{:S(2)}) copy-start(bf16[2,1664,128]{2,1,0:T(8,128)(2,1)S(1)} %collective-permute-done.9.refs_12_) | copy-start | bytes 2555908
  111.1 60.4 %collective-permute-start.10 = (bf16[512,1664]{1,0:T(8,128)(2,1)}, bf16[512,1664]{1,0:T(8,128)(2,1)}, u32[]{:S(2)}, u32[]{:S(2)}) collective-permute-start(bf16[512,1664]{1,0:T(8,128)(2,1)} %collective-permute-done.1.refs_0_), channel_id=1, source_target_pairs={{0,2},{1,3},{2,0},{3,1},{4,6},{5,7},{6,4},{7,5},{8,10},{9,11},{10,... | collective-permute-start | bytes 5111816 | tf_op jit(solution)/shard_map/ppermute | solution.py:20
  113.8 28.1 %collective-permute-start.15 = (bf16[2,1664,128]{2,1,0:T(8,128)(2,1)S(1)}, bf16[2,1664,128]{2,1,0:T(8,128)(2,1)S(1)}, u32[]{:S(2)}, u32[]{:S(2)}) collective-permute-start(bf16[2,1664,128]{2,1,0:T(8,128)(2,1)S(1)} %copy-done.32), channel_id=1, source_target_pairs={{0,16},{8,24},{16,0},{24,8},{1,17},{9,25},{17,1},{25,9},{2,18},{10... | collective-permute-start | bytes 2555912 | tf_op jit(solution)/shard_map/ppermute | solution.py:20
  114.3 36.6 %collective-permute-start.13 = (bf16[2,1664,128]{2,1,0:T(8,128)(2,1)}, bf16[2,1664,128]{2,1,0:T(8,128)(2,1)}, u32[]{:S(2)}, u32[]{:S(2)}) collective-permute-start(bf16[2,1664,128]{2,1,0:T(8,128)(2,1)} %collective-permute-done.8.refs_10_), channel_id=1, source_target_pairs={{0,8},{8,0},{16,24},{24,16},{1,9},{9,1},{17,25},{25,17},{2,10},{10... | collective-permute-start | bytes 2555912 | tf_op jit(solution)/shard_map/ppermute | solution.py:20
  115.8 35.1 %collective-permute-start.16 = (bf16[2,1664,128]{2,1,0:T(8,128)(2,1)}, bf16[2,1664,128]{2,1,0:T(8,128)(2,1)}, u32[]{:S(2)}, u32[]{:S(2)}) collective-permute-start(bf16[2,1664,128]{2,1,0:T(8,128)(2,1)} %get-tuple-element.83.refs_9_), channel_id=1, source_target_pairs={{0,8},{8,0},{16,24},{24,16},{1,9},{9,1},{17,25},{25,17},{2,10},{10... | collective-permute-start | bytes 2555912 | tf_op jit(solution)/shard_map/ppermute | solution.py:20
  126.9 17.3 %copy-start.35 = (s32[64,8]{0,1:T(8,128)S(1)}, s32[64,8]{0,1:T(8,128)}, u32[]{:S(2)}) copy-start(s32[64,8]{0,1:T(8,128)} %param.15) | copy-start | bytes 6148
  126.9 43.1 %collective-permute-start.12 = (bf16[2,1664,128]{2,1,0:T(8,128)(2,1)}, bf16[2,1664,128]{2,1,0:T(8,128)(2,1)}, u32[]{:S(2)}, u32[]{:S(2)}) collective-permute-start(bf16[2,1664,128]{2,1,0:T(8,128)(2,1)} %get-tuple-element.78), channel_id=1, source_target_pairs={{0,4},{1,5},{2,6},{3,7},{4,0},{5,1},{6,2},{7,3},{8,12},{9,13},{10,... | collective-permute-start | bytes 2555912 | tf_op jit(solution)/shard_map/ppermute | solution.py:20
  142.8 28.8 %collective-permute-start.11 = (bf16[2,1664,128]{2,1,0:T(8,128)(2,1)}, bf16[2,1664,128]{2,1,0:T(8,128)(2,1)}, u32[]{:S(2)}, u32[]{:S(2)}) collective-permute-start(bf16[2,1664,128]{2,1,0:T(8,128)(2,1)} %get-tuple-element.77), channel_id=1, source_target_pairs={{0,16},{8,24},{16,0},{24,8},{1,17},{9,25},{17,1},{25,9},{2,18},{10... | collective-permute-start | bytes 2555912 | tf_op jit(solution)/shard_map/ppermute | solution.py:20
  148.2 23.3 %copy-start.9 = (bf16[512,1664]{1,0:T(8,128)(2,1)S(1)}, bf16[512,1664]{1,0:T(8,128)(2,1)}, u32[]{:S(2)}) copy-start(bf16[512,1664]{1,0:T(8,128)(2,1)} %copy-done.8) | copy-start | bytes 5111812
  148.3 25.8 %copy-start.20 = (bf16[512,256]{1,0:T(8,128)(2,1)S(1)}, bf16[512,256]{1,0:T(8,128)(2,1)}, u32[]{:S(2)}) copy-start(bf16[512,256]{1,0:T(8,128)(2,1)} %copy.27) | copy-start | bytes 786436
  150.8 79.3 %collective-permute-start.4 = (bf16[512,1664]{1,0:T(8,128)(2,1)}, bf16[512,1664]{1,0:T(8,128)(2,1)S(1)}, u32[]{:S(2)}, u32[]{:S(2)}) collective-permute-start(bf16[512,1664]{1,0:T(8,128)(2,1)} %collective-permute-done.1.refs_0_), channel_id=1, source_target_pairs={{0,1},{1,0},{2,3},{3,2},{4,5},{5,4},{6,7},{7,6},{8,9},{9,8},{10,11... | collective-permute-start | bytes 5111816 | tf_op jit(solution)/shard_map/ppermute | solution.py:20
  150.8 54.3 %collective-permute-start.17 = (bf16[2,1664,128]{2,1,0:T(8,128)(2,1)S(1)}, bf16[2,1664,128]{2,1,0:T(8,128)(2,1)}, u32[]{:S(2)}, u32[]{:S(2)}) collective-permute-start(bf16[2,1664,128]{2,1,0:T(8,128)(2,1)S(1)} %get-tuple-element.84), channel_id=1, source_target_pairs={{0,4},{1,5},{2,6},{3,7},{4,0},{5,1},{6,2},{7,3},{8,12},{9,13},{10,... | collective-permute-start | bytes 2555912 | tf_op jit(solution)/shard_map/ppermute | solution.py:20
  170.0 60.6 %collective-permute-start.20 = (bf16[2,1664,128]{2,1,0:T(8,128)(2,1)}, bf16[2,1664,128]{2,1,0:T(8,128)(2,1)S(1)}, u32[]{:S(2)}, u32[]{:S(2)}) collective-permute-start(bf16[2,1664,128]{2,1,0:T(8,128)(2,1)} %collective-permute-done.12.refs_11_), channel_id=1, source_target_pairs={{0,8},{8,0},{16,24},{24,16},{1,9},{9,1},{17,25},{25,17},{2,10},{10... | collective-permute-start | bytes 2555912 | tf_op jit(solution)/shard_map/ppermute | solution.py:20
  171.5 59.3 %collective-permute-start.5 = (bf16[512,1664]{1,0:T(8,128)(2,1)S(1)}, bf16[512,1664]{1,0:T(8,128)(2,1)S(1)}, u32[]{:S(2)}, u32[]{:S(2)}) collective-permute-start(bf16[512,1664]{1,0:T(8,128)(2,1)S(1)} %copy-done.9), channel_id=1, source_target_pairs={{0,1},{1,0},{2,3},{3,2},{4,5},{5,4},{6,7},{7,6},{8,9},{9,8},{10,11... | collective-permute-start | bytes 5111816 | tf_op jit(solution)/shard_map/ppermute | solution.py:20
  171.5 58.6 %collective-permute-start.14 = (bf16[512,1664]{1,0:T(8,128)(2,1)S(1)}, bf16[512,1664]{1,0:T(8,128)(2,1)}, u32[]{:S(2)}, u32[]{:S(2)}) collective-permute-start(bf16[512,1664]{1,0:T(8,128)(2,1)S(1)} %copy-done.9), channel_id=1, source_target_pairs={{0,2},{1,3},{2,0},{3,1},{4,6},{5,7},{6,4},{7,5},{8,10},{9,11},{10,... | collective-permute-start | bytes 5111816 | tf_op jit(solution)/shard_map/ppermute | solution.py:20
  205.1 27.4 %collective-permute-start.18 = (bf16[512,1664]{1,0:T(8,128)(2,1)}, bf16[512,1664]{1,0:T(8,128)(2,1)S(1)}, u32[]{:S(2)}, u32[]{:S(2)}) collective-permute-start(bf16[512,1664]{1,0:T(8,128)(2,1)} %collective-permute-done.10.refs_4_), channel_id=1, source_target_pairs={{0,1},{1,0},{2,3},{3,2},{4,5},{5,4},{6,7},{7,6},{8,9},{9,8},{10,11... | collective-permute-start | bytes 5111816 | tf_op jit(solution)/shard_map/ppermute | solution.py:20
  230.1 5.5 %collective-permute-start.19 = (bf16[512,1664]{1,0:T(8,128)(2,1)}, bf16[512,1664]{1,0:T(8,128)(2,1)}, u32[]{:S(2)}, u32[]{:S(2)}) collective-permute-start(bf16[512,1664]{1,0:T(8,128)(2,1)} %collective-permute-done.14.refs_5_), channel_id=1, source_target_pairs={{0,1},{1,0},{2,3},{3,2},{4,5},{5,4},{6,7},{7,6},{8,9},{9,8},{10,11... | collective-permute-start | bytes 5111816 | tf_op jit(solution)/shard_map/ppermute | solution.py:20
  230.1 21.8 %collective-permute-start.21 = (bf16[512,1664]{1,0:T(8,128)(2,1)S(1)}, bf16[512,1664]{1,0:T(8,128)(2,1)}, u32[]{:S(2)}, u32[]{:S(2)}) collective-permute-start(bf16[512,1664]{1,0:T(8,128)(2,1)S(1)} %get-tuple-element.132.refs_0_), channel_id=1, source_target_pairs={{0,1},{1,0},{2,3},{3,2},{4,5},{5,4},{6,7},{7,6},{8,9},{9,8},{10,11... | collective-permute-start | bytes 5111816 | tf_op jit(solution)/shard_map/ppermute | solution.py:20
  230.7 21.7 %collective-permute-start.22 = (bf16[512,1664]{1,0:T(8,128)(2,1)S(1)}, bf16[512,1664]{1,0:T(8,128)(2,1)}, u32[]{:S(2)}, u32[]{:S(2)}) collective-permute-start(bf16[512,1664]{1,0:T(8,128)(2,1)S(1)} %get-tuple-element.69.refs_1_), channel_id=1, source_target_pairs={{0,1},{1,0},{2,3},{3,2},{4,5},{5,4},{6,7},{7,6},{8,9},{9,8},{10,11... | collective-permute-start | bytes 5111816 | tf_op jit(solution)/shard_map/ppermute | solution.py:20
  231.3 21.7 %collective-permute-start.23 = (bf16[512,1664]{1,0:T(8,128)(2,1)}, bf16[512,1664]{1,0:T(8,128)(2,1)}, u32[]{:S(2)}, u32[]{:S(2)}) collective-permute-start(bf16[512,1664]{1,0:T(8,128)(2,1)} %collective-permute-done.2.refs_4_), channel_id=1, source_target_pairs={{0,1},{1,0},{2,3},{3,2},{4,5},{5,4},{6,7},{7,6},{8,9},{9,8},{10,11... | collective-permute-start | bytes 5111816 | tf_op jit(solution)/shard_map/ppermute | solution.py:20
  233.6 20.7 %collective-permute-start.24 = (bf16[512,1664]{1,0:T(8,128)(2,1)}, bf16[512,1664]{1,0:T(8,128)(2,1)}, u32[]{:S(2)}, u32[]{:S(2)}) collective-permute-start(bf16[512,1664]{1,0:T(8,128)(2,1)} %collective-permute-done.6.refs_5_), channel_id=1, source_target_pairs={{0,1},{1,0},{2,3},{3,2},{4,5},{5,4},{6,7},{7,6},{8,9},{9,8},{10,11... | collective-permute-start | bytes 5111816 | tf_op jit(solution)/shard_map/ppermute | solution.py:20
  248.9 45.0 %collective-permute-start.26 = (bf16[1024,512]{1,0:T(8,128)(2,1)}, bf16[1024,512]{1,0:T(8,128)(2,1)S(1)}, u32[]{:S(2)}, u32[]{:S(2)}) collective-permute-start(bf16[1024,512]{1,0:T(8,128)(2,1)} %shard_map.116), channel_id=1, source_target_pairs={{0,16},{8,24},{16,0},{24,8},{1,17},{9,25},{17,1},{25,9},{2,18},{10... | collective-permute-start | bytes 3145736 | tf_op jit(solution)/shard_map/ppermute | solution.py:20
  251.9 39.8 %collective-permute-start.25 = (bf16[2,1664,128]{2,1,0:T(8,128)(2,1)S(1)}, bf16[2,1664,128]{2,1,0:T(8,128)(2,1)S(1)}, u32[]{:S(2)}, u32[]{:S(2)}) collective-permute-start(bf16[2,1664,128]{2,1,0:T(8,128)(2,1)S(1)} %get-tuple-element.89), channel_id=1, source_target_pairs={{0,4},{1,5},{2,6},{3,7},{4,0},{5,1},{6,2},{7,3},{8,12},{9,13},{10,... | collective-permute-start | bytes 2555912 | tf_op jit(solution)/shard_map/ppermute | solution.py:20
  252.3 39.4 %collective-permute-start.28 = (bf16[2,1664,128]{2,1,0:T(8,128)(2,1)S(1)}, bf16[2,1664,128]{2,1,0:T(8,128)(2,1)S(1)}, u32[]{:S(2)}, u32[]{:S(2)}) collective-permute-start(bf16[2,1664,128]{2,1,0:T(8,128)(2,1)S(1)} %copy-done.6), channel_id=1, source_target_pairs={{0,8},{8,0},{16,24},{24,16},{1,9},{9,1},{17,25},{25,17},{2,10},{10... | collective-permute-start | bytes 2555912 | tf_op jit(solution)/shard_map/ppermute | solution.py:20
  253.0 39.2 %collective-permute-start.30 = (bf16[2,1664,128]{2,1,0:T(8,128)(2,1)}, bf16[2,1664,128]{2,1,0:T(8,128)(2,1)S(1)}, u32[]{:S(2)}, u32[]{:S(2)}) collective-permute-start(bf16[2,1664,128]{2,1,0:T(8,128)(2,1)} %collective-permute-done.17.refs_10_), channel_id=1, source_target_pairs={{0,8},{8,0},{16,24},{24,16},{1,9},{9,1},{17,25},{25,17},{2,10},{10... | collective-permute-start | bytes 2555912 | tf_op jit(solution)/shard_map/ppermute | solution.py:20
  291.7 47.0 %collective-permute-start.29 = (bf16[2,1664,128]{2,1,0:T(8,128)(2,1)}, bf16[2,1664,128]{2,1,0:T(8,128)(2,1)}, u32[]{:S(2)}, u32[]{:S(2)}) collective-permute-start(bf16[2,1664,128]{2,1,0:T(8,128)(2,1)} %get-tuple-element.101.refs_9_), channel_id=1, source_target_pairs={{0,8},{8,0},{16,24},{24,16},{1,9},{9,1},{17,25},{25,17},{2,10},{10... | collective-permute-start | bytes 2555912 | tf_op jit(solution)/shard_map/ppermute | solution.py:20
  292.2 46.6 %collective-permute-start.31 = (bf16[2,1664,128]{2,1,0:T(8,128)(2,1)S(1)}, bf16[2,1664,128]{2,1,0:T(8,128)(2,1)}, u32[]{:S(2)}, u32[]{:S(2)}) collective-permute-start(bf16[2,1664,128]{2,1,0:T(8,128)(2,1)S(1)} %collective-permute-done.25.refs_11_), channel_id=1, source_target_pairs={{0,8},{8,0},{16,24},{24,16},{1,9},{9,1},{17,25},{25,17},{2,10},{10... | collective-permute-start | bytes 2555912 | tf_op jit(solution)/shard_map/ppermute | solution.py:20
  296.7 24.6 %collective-permute-start.27 = (bf16[1024,256]{1,0:T(8,128)(2,1)}, bf16[1024,256]{1,0:T(8,128)(2,1)}, u32[]{:S(2)}, u32[]{:S(2)}) collective-permute-start(bf16[1024,256]{1,0:T(8,128)(2,1)} %slice.85), channel_id=1, source_target_pairs={{0,4},{1,5},{2,6},{3,7},{4,0},{5,1},{6,2},{7,3},{8,12},{9,13},{10,... | collective-permute-start | bytes 1572872 | tf_op jit(solution)/shard_map/ppermute | solution.py:20
  335.8 45.2 %collective-permute-start.32 = (bf16[32,64,256]{2,1,0:T(8,128)(2,1)}, bf16[32,64,256]{2,1,0:T(8,128)(2,1)S(1)}, u32[]{:S(2)}, u32[]{:S(2)}) collective-permute-start(bf16[32,64,256]{2,1,0:T(8,128)(2,1)} %get-tuple-element.92), channel_id=1, source_target_pairs={{0,8},{8,0},{16,24},{24,16},{1,9},{9,1},{17,25},{25,17},{2,10},{10... | collective-permute-start | bytes 3145736 | tf_op jit(solution)/shard_map/ppermute | solution.py:20
  337.3 43.7 %collective-permute-start.33 = (bf16[32,64,256]{2,1,0:T(8,128)(2,1)}, bf16[32,64,256]{2,1,0:T(8,128)(2,1)S(1)}, u32[]{:S(2)}, u32[]{:S(2)}) collective-permute-start(bf16[32,64,256]{2,1,0:T(8,128)(2,1)} %get-tuple-element.94), channel_id=1, source_target_pairs={{0,16},{8,24},{16,0},{24,8},{1,17},{9,25},{17,1},{25,9},{2,18},{10... | collective-permute-start | bytes 3145736 | tf_op jit(solution)/shard_map/ppermute | solution.py:20
  352.0 34.0 %collective-permute-start.34 = (bf16[1024,512]{1,0:T(8,128)(2,1)}, bf16[1024,512]{1,0:T(8,128)(2,1)S(1)}, u32[]{:S(2)}, u32[]{:S(2)}) collective-permute-start(bf16[1024,512]{1,0:T(8,128)(2,1)} %shard_map.119), channel_id=1, source_target_pairs={{0,16},{8,24},{16,0},{24,8},{1,17},{9,25},{17,1},{25,9},{2,18},{10... | collective-permute-start | bytes 3145736 | tf_op jit(solution)/shard_map/ppermute | solution.py:20
  352.6 71.4 %collective-permute-start.38 = (bf16[32,64,256]{2,1,0:T(8,128)(2,1)}, bf16[32,64,256]{2,1,0:T(8,128)(2,1)}, u32[]{:S(2)}, u32[]{:S(2)}) collective-permute-start(bf16[32,64,256]{2,1,0:T(8,128)(2,1)} %get-tuple-element.93), channel_id=1, source_target_pairs={{0,16},{8,24},{16,0},{24,8},{1,17},{9,25},{17,1},{25,9},{2,18},{10... | collective-permute-start | bytes 3145736 | tf_op jit(solution)/shard_map/ppermute | solution.py:20
  354.1 71.5 %collective-permute-start.36 = (bf16[32,64,256]{2,1,0:T(8,128)(2,1)}, bf16[32,64,256]{2,1,0:T(8,128)(2,1)S(1)}, u32[]{:S(2)}, u32[]{:S(2)}) collective-permute-start(bf16[32,64,256]{2,1,0:T(8,128)(2,1)} %get-tuple-element.91), channel_id=1, source_target_pairs={{0,8},{8,0},{16,24},{24,16},{1,9},{9,1},{17,25},{25,17},{2,10},{10... | collective-permute-start | bytes 3145736 | tf_op jit(solution)/shard_map/ppermute | solution.py:20
  388.0 22.4 %collective-permute-start.35 = (bf16[1024,256]{1,0:T(8,128)(2,1)S(1)}, bf16[1024,256]{1,0:T(8,128)(2,1)S(1)}, u32[]{:S(2)}, u32[]{:S(2)}) collective-permute-start(bf16[1024,256]{1,0:T(8,128)(2,1)S(1)} %slice.84), channel_id=1, source_target_pairs={{0,4},{1,5},{2,6},{3,7},{4,0},{5,1},{6,2},{7,3},{8,12},{9,13},{10,... | collective-permute-start | bytes 1572872 | tf_op jit(solution)/shard_map/ppermute | solution.py:20
  388.7 54.7 %collective-permute-start.37 = (bf16[32,64,256]{2,1,0:T(8,128)(2,1)S(1)}, bf16[32,64,256]{2,1,0:T(8,128)(2,1)}, u32[]{:S(2)}, u32[]{:S(2)}) collective-permute-start(bf16[32,64,256]{2,1,0:T(8,128)(2,1)S(1)} %add_convert_fusion.10), channel_id=1, source_target_pairs={{0,16},{8,24},{16,0},{24,8},{1,17},{9,25},{17,1},{25,9},{2,18},{10... | collective-permute-start | bytes 3145736 | tf_op jit(solution)/shard_map/ppermute | solution.py:20
  390.6 53.3 %collective-permute-start.39 = (bf16[32,64,256]{2,1,0:T(8,128)(2,1)S(1)}, bf16[32,64,256]{2,1,0:T(8,128)(2,1)}, u32[]{:S(2)}, u32[]{:S(2)}) collective-permute-start(bf16[32,64,256]{2,1,0:T(8,128)(2,1)S(1)} %add_convert_fusion.7), channel_id=1, source_target_pairs={{0,8},{8,0},{16,24},{24,16},{1,9},{9,1},{17,25},{25,17},{2,10},{10... | collective-permute-start | bytes 3145736 | tf_op jit(solution)/shard_map/ppermute | solution.py:20
  424.0 29.5 %collective-permute-start.42 = (bf16[32,64,256]{2,1,0:T(8,128)(2,1)}, bf16[32,64,256]{2,1,0:T(8,128)(2,1)}, u32[]{:S(2)}, u32[]{:S(2)}) collective-permute-start(bf16[32,64,256]{2,1,0:T(8,128)(2,1)} %get-tuple-element.122), channel_id=1, source_target_pairs={{0,16},{8,24},{16,0},{24,8},{1,17},{9,25},{17,1},{25,9},{2,18},{10... | collective-permute-start | bytes 3145736 | tf_op jit(solution)/shard_map/ppermute | solution.py:20
  426.6 28.6 %collective-permute-start.41 = (bf16[32,64,256]{2,1,0:T(8,128)(2,1)}, bf16[32,64,256]{2,1,0:T(8,128)(2,1)S(1)}, u32[]{:S(2)}, u32[]{:S(2)}) collective-permute-start(bf16[32,64,256]{2,1,0:T(8,128)(2,1)} %get-tuple-element.121), channel_id=1, source_target_pairs={{0,8},{8,0},{16,24},{24,16},{1,9},{9,1},{17,25},{25,17},{2,10},{10... | collective-permute-start | bytes 3145736 | tf_op jit(solution)/shard_map/ppermute | solution.py:20
  443.4 32.5 %collective-permute-start.44 = (bf16[32,64,256]{2,1,0:T(8,128)(2,1)}, bf16[32,64,256]{2,1,0:T(8,128)(2,1)S(1)}, u32[]{:S(2)}, u32[]{:S(2)}) collective-permute-start(bf16[32,64,256]{2,1,0:T(8,128)(2,1)} %get-tuple-element.125), channel_id=1, source_target_pairs={{0,16},{8,24},{16,0},{24,8},{1,17},{9,25},{17,1},{25,9},{2,18},{10... | collective-permute-start | bytes 3145736 | tf_op jit(solution)/shard_map/ppermute | solution.py:20
  444.0 56.6 %collective-permute-start.40 = (bf16[32,64,256]{2,1,0:T(8,128)(2,1)}, bf16[32,64,256]{2,1,0:T(8,128)(2,1)S(1)}, u32[]{:S(2)}, u32[]{:S(2)}) collective-permute-start(bf16[32,64,256]{2,1,0:T(8,128)(2,1)} %get-tuple-element.119), channel_id=1, source_target_pairs={{0,8},{8,0},{16,24},{24,16},{1,9},{9,1},{17,25},{25,17},{2,10},{10... | collective-permute-start | bytes 3145736 | tf_op jit(solution)/shard_map/ppermute | solution.py:20
  455.2 41.4 %collective-permute-start.45 = (bf16[32,64,256]{2,1,0:T(8,128)(2,1)S(1)}, bf16[32,64,256]{2,1,0:T(8,128)(2,1)S(1)}, u32[]{:S(2)}, u32[]{:S(2)}) collective-permute-start(bf16[32,64,256]{2,1,0:T(8,128)(2,1)S(1)} %add_convert_fusion.1), channel_id=1, source_target_pairs={{0,8},{8,0},{16,24},{24,16},{1,9},{9,1},{17,25},{25,17},{2,10},{10... | collective-permute-start | bytes 3145736 | tf_op jit(solution)/shard_map/ppermute | solution.py:20
  458.9 41.7 %collective-permute-start.43 = (bf16[32,64,256]{2,1,0:T(8,128)(2,1)S(1)}, bf16[32,64,256]{2,1,0:T(8,128)(2,1)S(1)}, u32[]{:S(2)}, u32[]{:S(2)}) collective-permute-start(bf16[32,64,256]{2,1,0:T(8,128)(2,1)S(1)} %add_convert_fusion.4), channel_id=1, source_target_pairs={{0,16},{8,24},{16,0},{24,8},{1,17},{9,25},{17,1},{25,9},{2,18},{10... | collective-permute-start | bytes 3145736 | tf_op jit(solution)/shard_map/ppermute | solution.py:20
  463.9 32.6 %copy-start.31 = (bf16[32,64,256]{2,1,0:T(8,128)(2,1)S(1)}, bf16[32,64,256]{2,1,0:T(8,128)(2,1)}, u32[]{:S(2)}) copy-start(bf16[32,64,256]{2,1,0:T(8,128)(2,1)} %get-tuple-element.124) | copy-start | bytes 3145732
  504.9 3.8 collective-permute-start.46
  508.7 13.6 %copy-start.4 = (bf16[1024,256]{1,0:T(8,128)(2,1)S(1)}, bf16[1024,256]{1,0:T(8,128)(2,1)}, u32[]{:S(2)}) copy-start(bf16[1024,256]{1,0:T(8,128)(2,1)} %fusion.25.screened_ref) | copy-start | bytes 1572868
  508.7 13.6 %copy-start.5 = (bf16[1024,256]{1,0:T(8,128)(2,1)S(1)}, bf16[1024,256]{1,0:T(8,128)(2,1)}, u32[]{:S(2)}) copy-start(bf16[1024,256]{1,0:T(8,128)(2,1)} %fusion.24.screened_ref) | copy-start | bytes 1572868
  508.7 5.0 collective-permute-start.47
  510.2 13.8 %copy-start.1 = (bf16[256,256]{1,0:T(8,128)(2,1)S(1)}, bf16[256,256]{1,0:T(8,128)(2,1)}, u32[]{:S(2)}) copy-start(bf16[256,256]{1,0:T(8,128)(2,1)} %param.13) | copy-start | bytes 393220
  513.8 4.6 collective-permute-start.48
  518.6 3.7 collective-permute-start.49
  522.2 1.2 collective-permute-start.50
  (25 other events, 105.3 us)

commit v6 on v5

--- a/solution.py
+++ b/solution.py
@@ -8,11 +8,10 @@
 from jax.sharding import PartitionSpec as P
 
 WIDTH = 128
-PAIR = 2
 GROUPS = 4
 VMEM = 56
+MIB = 1024 * 1024
 NO_COST = pl.CostEstimate(flops=0, bytes_accessed=0, transcendentals=0)
-MIB = 1024 * 1024
 
 
 def swap(value, axis, bit):
@@ -222,8 +221,10 @@
     per_block = metric.shape[0] // depth
     tile, near_l = three_panel.shape[1], three_panel.shape[2]
     share = near_l // row_count
-    width = min(WIDTH, near_cols)
-    chunks = near_cols // width
+    wide = near_cols // 2 if near_cols >= 4 * WIDTH else near_cols
+    width = wide // 2
+    bounds = [(0, width), (width, width)] + ([(wide, wide)] if wide < near_cols else [])
+    chunks = len(bounds)
     on_diagonal = u == v
 
     mine = lax.dynamic_slice_in_dim(polarization, u * half, half, 1)
@@ -233,7 +234,7 @@
     metric_parts = metric.reshape(per_block, 2, half, near_cols)
     metric_mine = lax.dynamic_index_in_dim(metric_parts, u, 1, keepdims=False)
     metric_other = lax.dynamic_index_in_dim(metric_parts, 1 - u, 1, keepdims=False)
-    crossing = [metric_other[:, :, j * width : (j + 1) * width] for j in range(chunks)]
+    crossing = [metric_other[:, :, at : at + size] for at, size in bounds]
 
     rb = panel_rows * row_count // mask_panel.shape[0]
     ab = near_l // mask_panel.shape[1]
@@ -257,7 +258,8 @@
         return panels[-1]
 
     def far(j, *others):
-        kept = after(metric_mine, arrived[j])[:, :, j * width : (j + 1) * width]
+        at, size = bounds[j]
+        kept = after(metric_mine, arrived[j])[:, :, at : at + size]
         stay = jnp.where(on_diagonal, kept, arrived[j])
         leave = jnp.where(on_diagonal, arrived[j], kept)
         came.append([stay, swap(after(leave, *others), "col", top_col)])
@@ -295,17 +297,11 @@
     turn_next(leave, *panels)
     near_crossed_first = swap(after(crossed_first, near_second, arrived[1], came[0][1], from_row(0, 0)), "col", low)
     for j in range(2, chunks):
-        due = [came[j - 2][1], near_second, from_row(0, 1), from_row(1, 0)]
-        if j == 2:
-            arrived.append(cross(crossing[j], arrived[1], *panels))
-        else:
-            due.append(near_crossed_first)
-            while len(panels) < GROUPS:
-                turn_next(near_second, came[0][1], from_row(0, 0), *panels)
-            arrived.append(cross(crossing[j], crossed_second, *panels))
-        far(j, *due)
+        arrived.append(cross(crossing[j], arrived[1], *panels))
+        far(j, came[j - 2][1], near_second, from_row(0, 1), from_row(1, 0))
+        gather_rows(came[j][:1])
     while len(panels) < GROUPS:
-        turn_next(near_second, *panels)
+        turn_next(near_second, came[0][1], from_row(0, 0), *panels)
 
     near_blocks = near_cols // rb
     near_mask = lax.dynamic_slice_in_dim(mask_near, c * near_blocks, near_blocks, 0)
@@ -317,7 +313,8 @@
     near_crossed_second = swap(
         after(crossed_second, near_crossed_first, arrived[-1], came[1][1], from_row(0, 1)), "col", low
     )
-    near_crossed_second = after(near_crossed_second, dressed, *panels, *[pair[1] for pair in came[2:3]])
+    due = [part for j in range(2, chunks) for part in (came[j][1], from_row(j, 0))]
+    near_crossed_second = after(near_crossed_second, dressed, *panels, *due)
 
     def gather_low(found):
         link = Link(1)
@@ -331,32 +328,38 @@
     blocks = c_low ^ jnp.arange(top_col, dtype=jnp.int32)
     order = ((blocks // per_block) ^ r_low) * per_block + blocks % per_block
 
-    earlier, due = (), [pair[1] for pair in came[3:4]]
-    ready = pieces_crossed[-1][-1]
     screened_chunks, contracted_chunks = [], []
     energy = jnp.zeros((tile, tile), jnp.float32)
     hops = {bit: Link(2) for bit in bits_below(row_count)}
-    pair = min(PAIR, chunks)
-    wide = pair * width
     orders = [bits_below(row_count)[::-1], bits_below(row_count)]
     kept = [[e for e in range(row_count) if not e & bits[0]] for bits in orders]
     places = r ^ jnp.array(kept, jnp.int32)
     first_bits = jnp.array([[bits[0]] for bits in orders], jnp.int32)
-    for j in range(0, chunks, pair):
-        for i in range(len(gathered), min(j + pair + 1, chunks)):
-            gather_rows([after(part, ready) for part in came[i]])
-        sources = [[gathered[j + i][f][side] for side in range(2) for i in range(pair)] for f in range(top_row)]
-        away = product(pieces_crossed, sources, after(order, *earlier), per_block, jnp.bfloat16)
-        ready = away
-        home = product(pieces_mine, sources, after(order, away), per_block, jnp.float32)
-        home = after(home, *due) + swap(away, "row", top_row).astype(jnp.float32)
-        came_back = swap(home[:, wide:].astype(jnp.bfloat16), "col", top_col)
-        screened = (home[:, :wide] + came_back.astype(jnp.float32)).astype(jnp.bfloat16)
+    groups = [[0, 1]] + [[j] for j in range(2, chunks)]
+
+    def sources_of(k):
+        return [[gathered[i][f][side] for side in range(2) for i in groups[k]] for f in range(top_row)]
+
+    away = product(pieces_crossed, sources_of(0), order, per_block, jnp.bfloat16)
+    for j in range(2, chunks):
+        early = gathered.pop(2)
+        gather_rows([after(came[j][1], pieces_crossed[-1][-1])])
+        gathered.append([a + b for a, b in zip(early, gathered.pop())])
+    home = product(pieces_mine, sources_of(0), after(order, away), per_block, jnp.float32)
+    due = []
+    for k in range(len(groups)):
+        total = after(home, *due) + swap(away, "row", top_row).astype(jnp.float32)
+        came_back = swap(total[:, wide:].astype(jnp.bfloat16), "col", top_col)
+        screened = (total[:, :wide] + came_back.astype(jnp.float32)).astype(jnp.bfloat16)
         screened_chunks.append(screened)
 
-        gone = contract(panels, screened, panel_mask, places ^ first_bits, rb, ab, share)
-        stay = contract(panels, screened, panel_mask, after(places, gone), rb, ab, share)
-        earlier, due = (home, *gone[0], *gone[1]), []
+        if k + 1 < len(groups):
+            away = product(pieces_crossed, sources_of(k + 1), after(order, home), per_block, jnp.bfloat16)
+        gone = contract(panels, screened, panel_mask, after(places ^ first_bits, away), rb, ab, share)
+        if k + 1 < len(groups):
+            home = product(pieces_mine, sources_of(k + 1), after(order, away, gone), per_block, jnp.float32)
+        stay = contract(panels, screened, panel_mask, after(places, home, gone), rb, ab, share)
+        due = []
         left = [[dict(zip(kept[h], part[h])) for part in (gone, stay)] for h in range(2)]
         for hop in range(len(orders[0])):
             for h, bits in enumerate(orders):

time: 528 us -> 582 us (1.10)
  waiting for transfers between devices: 218 us -> 275 us
    ppermute x51 -> x47, waiting for transfers between devices: 218 us -> 275 us  [swap(): return lax.ppermute(value, axis, [(i, i ^ bit) for i in range(size)])]
    ppermute x51 -> x47, starting transfers between devices: 52.6 us -> 50.1 us  [swap(): return lax.ppermute(value, axis, [(i, i ^ bit) for i in range(size)])]
  transfers between devices with their start and end apart: 51 -> 47, of which waited for: 21 -> 21; matrix products, arithmetic and copies ran while one was open for 17% -> 15% of each run, Pallas kernels for 28% -> 21%
where the time goes in v6:
time: 582 us; the launch traced here: 577 us
  waiting for transfers between devices  275 us (47%)
  Pallas kernels  146 us (25%)
  starting transfers between devices  50.1 us (9%)
  other arithmetic  42.4 us (7%)
  matrix products  33.1 us (6%)
  local copies, waits for them, and re-layouts  29.9 us (5%)
    ppermute x47, waiting for transfers between devices, swap(): return lax.ppermute(value, axis, [(i, i ^ bit) for i in range(size)])  275 us
    pallas_call x4, Pallas kernels, product(): pl.pallas_call(functools.partial(product_kernel, count, parts, per_block)...  52.5 us
    pallas_call x4, Pallas kernels, contract(): pl.pallas_call(functools.partial(contract_kernel, rb, ab), in_specs=[in_s...  50.4 us
    ppermute x47, starting transfers between devices, swap(): return lax.ppermute(value, axis, [(i, i ^ bit) for i in range(size)])  50.1 us
    pallas_call x4, Pallas kernels, turn(): pl.pallas_call(turn_kernel, grid=(rows // wide, tile // tall), in_specs=[...  42.9 us
    dot_general x1, matrix products, per_device(): jnp.einsum('qns,ls->nlq', near, green, preferred_element_type=jnp.float32)  19.2 us
    dot_general x4, matrix products, per_device(): jnp.einsum('mlq,nlq->mn', half, beside, preferred_element_type=jnp.float32)  14 us
    mul x1, other arithmetic, per_device(): after(three_near, near_crossed_first, came[1][1]) * near_mask[:, None, :]  13.8 us
  transfers between devices with their start and end apart: 47, of which 21 were waited for; matrix products, arithmetic and copies ran while one was open for 15% of the time, Pallas kernels for 21%

profile of v6, /device:TPU:0, one launch (start us, length us, event | category | flops | bytes accessed | tf_op | source)
XLA Modules:
  0.0 577.5 jit_solution(5258276642181785139)
XLA Ops:
  0.7 5.3 fusion.41
  5.9 3.0 collective-permute-start.2
  9.0 5.2 dynamic-slice_bitcast_fusion
  17.1 18.9 %collective-permute-done = bf16[2,1664,128]{2,1,0:T(8,128)(2,1)S(1)} collective-permute-done((bf16[2,1664,128]{2,1,0:T(8,128)(2,1)S(1)}, bf16[2,1664,128]{2,1,0:T(8,128)(2,1)S(1)}, u32[]{:S(2)}, u32[]{:S(2)}) %collective-permute-start) | collective-permute-done | bytes 852000 | tf_op jit(solution)/shard_map/ppermute | solution.py:19
  36.0 10.3 %collective-permute-done.2.refs_4_ = bf16[512,1664]{1,0:T(8,128)(2,1)} collective-permute-done((bf16[512,1664]{1,0:T(8,128)(2,1)S(1)}, bf16[512,1664]{1,0:T(8,128)(2,1)}, u32[]{:S(2)}, u32[]{:S(2)}) %collective-permute-start.2) | collective-permute-done | bytes 1703968 | tf_op jit(solution)/shard_map/ppermute | solution.py:19
  46.3 1.7 collective-permute-start.7
  48.0 2.8 slice.52
  51.1 1.7 collective-permute-start.6
  52.9 1.5 broadcast_select_fusion.4
  54.4 1.6 collective-permute-start.9
  56.0 2.6 collective-permute-start.8
  58.5 10.9 %shard_map.112.refs_0_ = bf16[64,256,256]{2,1,0:T(8,128)(2,1)} custom-call(bf16[1024,64,256]{2,1,0:T(8,128)(2,1)} %panel_ref.3), custom_call_target="tpu_custom_call" | custom-call | bytes 33554432 | tf_op jit(solution)/shard_map/pallas_call | solution.py:121
  69.4 2.7 broadcast_select_fusion.2
  72.2 10.8 %shard_map.113.refs_1_ = bf16[64,256,256]{2,1,0:T(8,128)(2,1)} custom-call(bf16[1024,64,256]{2,1,0:T(8,128)(2,1)} %panel_ref.3), custom_call_target="tpu_custom_call" | custom-call | bytes 33554432 | tf_op jit(solution)/shard_map/pallas_call | solution.py:121
  84.5 21.7 %collective-permute-done.8.refs_10_ = bf16[2,1664,128]{2,1,0:T(8,128)(2,1)} collective-permute-done((bf16[2,1664,128]{2,1,0:T(8,128)(2,1)S(1)}, bf16[2,1664,128]{2,1,0:T(8,128)(2,1)}, u32[]{:S(2)}, u32[]{:S(2)}) %collective-permute-start.8) | collective-permute-done | bytes 852000 | tf_op jit(solution)/shard_map/ppermute | solution.py:19
  107.3 2.5 collective-permute-start.10
  113.4 28.0 %collective-permute-done.11 = bf16[2,1664,256]{2,1,0:T(8,128)(2,1)S(1)} collective-permute-done((bf16[2,1664,256]{2,1,0:T(8,128)(2,1)S(1)}, bf16[2,1664,256]{2,1,0:T(8,128)(2,1)S(1)}, u32[]{:S(2)}, u32[]{:S(2)}) %collective-permute-start.11) | collective-permute-done | bytes 1703968 | tf_op jit(solution)/shard_map/ppermute | solution.py:19
  142.6 2.8 collective-permute-start.12
  145.4 3.9 broadcast_select_fusion
  153.4 1.8 copy.27
  155.2 10.6 %shard_map.114.refs_2_ = bf16[64,256,256]{2,1,0:T(8,128)(2,1)} custom-call(bf16[1024,64,256]{2,1,0:T(8,128)(2,1)} %panel_ref.3), custom_call_target="tpu_custom_call" | custom-call | bytes 33554432 | tf_op jit(solution)/shard_map/pallas_call | solution.py:121
  165.8 10.7 %shard_map.115.refs_3_ = bf16[64,256,256]{2,1,0:T(8,128)(2,1)} custom-call(bf16[1024,64,256]{2,1,0:T(8,128)(2,1)} %panel_ref.3), custom_call_target="tpu_custom_call" | custom-call | bytes 33554432 | tf_op jit(solution)/shard_map/pallas_call | solution.py:121
  176.5 42.2 %collective-permute-done.12.refs_11_ = bf16[2,1664,128]{2,1,0:T(8,128)(2,1)} collective-permute-done((bf16[2,1664,128]{2,1,0:T(8,128)(2,1)}, bf16[2,1664,128]{2,1,0:T(8,128)(2,1)}, u32[]{:S(2)}, u32[]{:S(2)}) %collective-permute-start.12) | collective-permute-done | bytes 852000 | tf_op jit(solution)/shard_map/ppermute | solution.py:19
  218.7 1.6 collective-permute-start.20
  220.4 13.8 %broadcast_multiply_fusion = bf16[512,64,256]{2,1,0:T(8,128)(2,1)} fusion(bf16[512,64,256]{2,1,0:T(8,128)(2,1)} %param.12, bf16[512,256]{1,0:T(8,128)(2,1)S(1)} %copy-done.19), kind=kLoop, calls=%fused_computation.2 | loop fusion | flops 8388608 | bytes 33816576 | tf_op jit(solution)/shard_map/mul | solution.py:309
  234.3 18.5 %collective-permute-done.16.refs_9_ = bf16[2,1664,256]{2,1,0:T(8,128)(2,1)} collective-permute-done((bf16[2,1664,256]{2,1,0:T(8,128)(2,1)}, bf16[2,1664,256]{2,1,0:T(8,128)(2,1)}, u32[]{:S(2)}, u32[]{:S(2)}) %collective-permute-start.16) | collective-permute-done | bytes 1703968 | tf_op jit(solution)/shard_map/ppermute | solution.py:19
  252.8 19.2 %convert_bitcast_fusion = bf16[64,64,512]{2,1,0:T(8,128)(2,1)} fusion(bf16[512,64,256]{2,1,0:T(8,128)(2,1)} %broadcast_multiply_fusion, bf16[256,256]{1,0:T(8,128)(2,1)S(1)} %copy-done, s32[]{:T(128)S(6)} %select_n.157), kind=kOutput, calls=%fused_computation.4 | convolution fusion | flops 1075838976 | bytes 21004292 | tf_op jit(solution)/shard_map/qns,ls->nlq/dot_general | solution.py:311
  272.0 17.2 %collective-permute-done.14.refs_5_ = bf16[512,1664]{1,0:T(8,128)(2,1)} collective-permute-done((bf16[512,1664]{1,0:T(8,128)(2,1)}, bf16[512,1664]{1,0:T(8,128)(2,1)}, u32[]{:S(2)}, u32[]{:S(2)}) %collective-permute-start.14) | collective-permute-done | bytes 1703968 | tf_op jit(solution)/shard_map/ppermute | solution.py:19
  294.5 13.2 %shard_map.116 = bf16[1024,512]{1,0:T(8,128)(2,1)} custom-call(s32[4]{0:T(128)} %fusion.40.order_ref, bf16[512,1664]{1,0:T(8,128)(2,1)} %collective-permute-done.1.refs_0_, bf16[512,1664]{1,0:T(8,128)(2,1)} %collective-permute-done.3.refs_1_, bf16[512,1664]{1,0:T(8,128)(2,1)} %copy-done.9, bf16[512,1664]{1,0:T(8,128)(2,1)} %copy-done.10, ...), custom_call_target="tpu_custom_call" | custom-call | tf_op jit(solution)/shard_map/pallas_call | solution.py:96
  308.9 1.6 collective-permute-start.27
  310.5 13.6 %shard_map.117 = f32[1024,512]{1,0:T(8,128)} custom-call(s32[4]{0:T(128)} %fusion.40.order_ref, bf16[512,1664]{1,0:T(8,128)(2,1)} %copy-done.3, bf16[512,1664]{1,0:T(8,128)(2,1)} %copy-done.2, bf16[512,1664]{1,0:T(8,128)(2,1)} %collective-permute-done.21.refs_2_, bf16[512,1664]{1,0:T(8,128)(2,1)} %collective-permute-done.22.refs_3_, ...), custom_call_target="tpu_custom_call" | custom-call | tf_op jit(solution)/shard_map/pallas_call | solution.py:96
  324.1 9.0 %collective-permute-done.25 = bf16[1024,512]{1,0:T(8,128)(2,1)S(1)} collective-permute-done((bf16[1024,512]{1,0:T(8,128)(2,1)}, bf16[1024,512]{1,0:T(8,128)(2,1)S(1)}, u32[]{:S(2)}, u32[]{:S(2)}) %collective-permute-start.25) | collective-permute-done | bytes 1048608 | tf_op jit(solution)/shard_map/ppermute | solution.py:19
  333.2 1.9 convert_add_fusion.1
  339.1 22.7 %collective-permute-done.26 = bf16[1024,256]{1,0:T(8,128)(2,1)S(1)} collective-permute-done((bf16[1024,256]{1,0:T(8,128)(2,1)S(1)}, bf16[1024,256]{1,0:T(8,128)(2,1)S(1)}, u32[]{:S(2)}, u32[]{:S(2)}) %collective-permute-start.26) | collective-permute-done | bytes 524320 | tf_op jit(solution)/shard_map/ppermute | solution.py:19
  361.8 2.1 fusion.25.screened_ref
  365.1 12.7 %shard_map.118 = bf16[1024,512]{1,0:T(8,128)(2,1)} custom-call(s32[4]{0:T(128)} %fusion.40.order_ref, bf16[512,1664]{1,0:T(8,128)(2,1)} %collective-permute-done.1.refs_0_, bf16[512,1664]{1,0:T(8,128)(2,1)} %collective-permute-done.3.refs_1_, bf16[512,1664]{1,0:T(8,128)(2,1)} %copy-done.9, bf16[512,1664]{1,0:T(8,128)(2,1)} %copy-done.10, ...), custom_call_target="tpu_custom_call" | custom-call | tf_op jit(solution)/shard_map/pallas_call | solution.py:96
  377.8 12.6 %shard_map.119 = (bf16[32,64,256]{2,1,0:T(8,128)(2,1)}, bf16[32,64,256]{2,1,0:T(8,128)(2,1)}, bf16[32,64,256]{2,1,0:T(8,128)(2,1)}, bf16[32,64,256]{2,1,0:T(8,128)(2,1)}) custom-call(s32[2,2]{1,0:T(2,128)} %get-tuple-element.83.places_ref, s32[16,8]{1,0:T(8,128)} %copy.42.mask_ref, bf16[1024,256]{1,0:T(8,128)(2,1)} %fusion.25.screened_ref, ...), custom_call_target="tpu_custom_call" | custom-call | tf_op jit(solution)/shard_map/pallas_call | solution.py:183
  391.6 1.9 collective-permute-start.28
  395.6 13.0 %shard_map.120 = f32[1024,512]{1,0:T(8,128)} custom-call(s32[4]{0:T(128)} %fusion.40.order_ref, bf16[512,1664]{1,0:T(8,128)(2,1)} %copy-done.3, bf16[512,1664]{1,0:T(8,128)(2,1)} %copy-done.2, bf16[512,1664]{1,0:T(8,128)(2,1)} %collective-permute-done.21.refs_2_, bf16[512,1664]{1,0:T(8,128)(2,1)} %collective-permute-done.22.refs_3_, ...), custom_call_target="tpu_custom_call" | custom-call | tf_op jit(solution)/shard_map/pallas_call | solution.py:96
  408.6 12.7 %shard_map.121 = (bf16[32,64,256]{2,1,0:T(8,128)(2,1)}, bf16[32,64,256]{2,1,0:T(8,128)(2,1)}, bf16[32,64,256]{2,1,0:T(8,128)(2,1)}, bf16[32,64,256]{2,1,0:T(8,128)(2,1)}) custom-call(s32[2,2]{1,0:T(2,128)} %get-tuple-element.90.places_ref, s32[16,8]{1,0:T(8,128)} %copy.42.mask_ref, bf16[1024,256]{1,0:T(8,128)(2,1)} %fusion.25.screened_ref, ...), custom_call_target="tpu_custom_call" | custom-call | tf_op jit(solution)/shard_map/pallas_call | solution.py:183
  421.3 17.9 %collective-permute-done.30 = bf16[1024,512]{1,0:T(8,128)(2,1)S(1)} collective-permute-done((bf16[1024,512]{1,0:T(8,128)(2,1)S(1)}, bf16[1024,512]{1,0:T(8,128)(2,1)S(1)}, u32[]{:S(2)}, u32[]{:S(2)}) %collective-permute-start.30) | collective-permute-done | bytes 1048608 | tf_op jit(solution)/shard_map/ppermute | solution.py:19
  442.1 1.7 collective-permute-start.33
  443.8 18.8 %collective-permute-done.31 = bf16[1024,256]{1,0:T(8,128)(2,1)S(1)} collective-permute-done((bf16[1024,256]{1,0:T(8,128)(2,1)S(1)}, bf16[1024,256]{1,0:T(8,128)(2,1)S(1)}, u32[]{:S(2)}, u32[]{:S(2)}) %collective-permute-start.31) | collective-permute-done | bytes 524320 | tf_op jit(solution)/shard_map/ppermute | solution.py:19
  463.6 12.5 %shard_map.122 = (bf16[32,64,256]{2,1,0:T(8,128)(2,1)}, bf16[32,64,256]{2,1,0:T(8,128)(2,1)}, bf16[32,64,256]{2,1,0:T(8,128)(2,1)}, bf16[32,64,256]{2,1,0:T(8,128)(2,1)}) custom-call(s32[2,2]{1,0:T(2,128)} %get-tuple-element.83.places_ref, s32[16,8]{1,0:T(8,128)} %copy.42.mask_ref, bf16[1024,256]{1,0:T(8,128)(2,1)} %fusion.24.screened_ref, ...), custom_call_target="tpu_custom_call" | custom-call | tf_op jit(solution)/shard_map/pallas_call | solution.py:183
  478.2 1.5 collective-permute-start.38
  479.7 2.8 fusion.42
  482.5 12.6 %shard_map.123 = (bf16[32,64,256]{2,1,0:T(8,128)(2,1)}, bf16[32,64,256]{2,1,0:T(8,128)(2,1)}, bf16[32,64,256]{2,1,0:T(8,128)(2,1)}, bf16[32,64,256]{2,1,0:T(8,128)(2,1)}) custom-call(s32[2,2]{1,0:T(2,128)} %get-tuple-element.90.places_ref, s32[16,8]{1,0:T(8,128)} %copy.42.mask_ref, bf16[1024,256]{1,0:T(8,128)(2,1)} %fusion.24.screened_ref, ...), custom_call_target="tpu_custom_call" | custom-call | tf_op jit(solution)/shard_map/pallas_call | solution.py:183
  495.2 1.5 collective-permute-start.40
  496.8 2.5 add_convert_fusion.9
  499.3 3.4 collective-permute-done.37
  502.7 1.6 add_convert_fusion.4
  504.3 2.4 collective-permute-done.38
  507.8 1.9 add_convert_fusion.6
  510.6 1.9 collective-permute-start.41
  512.5 3.5 fusion.12
  515.9 3.5 fusion.15
  519.4 5.6 collective-permute-done.36
  525.0 25.0 %collective-permute-done.39 = bf16[32,64,256]{2,1,0:T(8,128)(2,1)S(1)} collective-permute-done((bf16[32,64,256]{2,1,0:T(8,128)(2,1)S(1)}, bf16[32,64,256]{2,1,0:T(8,128)(2,1)S(1)}, u32[]{:S(2)}, u32[]{:S(2)}) %collective-permute-start.39) | collective-permute-done | bytes 1048608 | tf_op jit(solution)/shard_map/ppermute | solution.py:19
  550.6 3.5 fusion.18
  554.7 3.6 fusion.21
  559.0 3.1 collective-permute-done.42
  563.5 3.5 maximum_bitcast_fusion
  567.2 4.5 collective-permute-done.44
  572.7 2.8 collective-permute-done.45
  (170 shorter events, 43.9 us)
Async XLA Ops:
  0.6 252.2 %copy-start = (bf16[256,256]{1,0:T(8,128)(2,1)S(1)}, bf16[256,256]{1,0:T(8,128)(2,1)}, u32[]{:S(2)}) copy-start(bf16[256,256]{1,0:T(8,128)(2,1)} %param.13) | copy-start | bytes 393220
  5.9 283.3 %copy-start.3 = (bf16[512,1664]{1,0:T(8,128)(2,1)}, bf16[512,1664]{1,0:T(8,128)(2,1)S(1)}, u32[]{:S(2)}) copy-start(bf16[512,1664]{1,0:T(8,128)(2,1)S(1)} %get-tuple-element.116.refs_0_) | copy-start | bytes 5111812
  5.9 283.8 %copy-start.2 = (bf16[512,1664]{1,0:T(8,128)(2,1)}, bf16[512,1664]{1,0:T(8,128)(2,1)S(1)}, u32[]{:S(2)}) copy-start(bf16[512,1664]{1,0:T(8,128)(2,1)S(1)} %get-tuple-element.61.refs_1_) | copy-start | bytes 5111812
  5.9 40.3 %collective-permute-start.2 = (bf16[512,1664]{1,0:T(8,128)(2,1)S(1)}, bf16[512,1664]{1,0:T(8,128)(2,1)}, u32[]{:S(2)}, u32[]{:S(2)}) collective-permute-start(bf16[512,1664]{1,0:T(8,128)(2,1)S(1)} %get-tuple-element.116.refs_0_), channel_id=1, source_target_pairs={{0,2},{1,3},{2,0},{3,1},{4,6},{5,7},{6,4},{7,5},{8,10},{9,11},{10,... | collective-permute-start | bytes 5111816 | tf_op jit(solution)/shard_map/ppermute | solution.py:19
  14.2 32.1 %copy-start.4 = (bf16[2,1664,512]{2,1,0:T(8,128)(2,1)}, bf16[2,1664,512]{2,1,0:T(8,128)(2,1)S(1)}, u32[]{:S(2)}) copy-start(bf16[2,1664,512]{2,1,0:T(8,128)(2,1)S(1)} %get-tuple-element.114) | copy-start | bytes 10223620
  15.6 20.4 %collective-permute-start = (bf16[2,1664,128]{2,1,0:T(8,128)(2,1)S(1)}, bf16[2,1664,128]{2,1,0:T(8,128)(2,1)S(1)}, u32[]{:S(2)}, u32[]{:S(2)}) collective-permute-start(bf16[2,1664,128]{2,1,0:T(8,128)(2,1)S(1)} %get-tuple-element.128), channel_id=1, source_target_pairs={{0,16},{8,24},{16,0},{24,8},{1,17},{9,25},{17,1},{25,9},{2,18},{10... | collective-permute-start | bytes 2555912 | tf_op jit(solution)/shard_map/ppermute | solution.py:19
  46.3 23.2 %collective-permute-start.7 = (bf16[2,1664,128]{2,1,0:T(8,128)(2,1)}, bf16[2,1664,128]{2,1,0:T(8,128)(2,1)}, u32[]{:S(2)}, u32[]{:S(2)}) collective-permute-start(bf16[2,1664,128]{2,1,0:T(8,128)(2,1)} %get-tuple-element.62), channel_id=1, source_target_pairs={{0,16},{8,24},{16,0},{24,8},{1,17},{9,25},{17,1},{25,9},{2,18},{10... | collective-permute-start | bytes 2555912 | tf_op jit(solution)/shard_map/ppermute | solution.py:19
  50.8 55.4 %collective-permute-start.1 = (bf16[512,1664]{1,0:T(8,128)(2,1)}, bf16[512,1664]{1,0:T(8,128)(2,1)}, u32[]{:S(2)}, u32[]{:S(2)}) collective-permute-start(bf16[512,1664]{1,0:T(8,128)(2,1)} %get-tuple-element.58), channel_id=1, source_target_pairs={{0,16},{8,24},{16,0},{24,8},{1,17},{9,25},{17,1},{25,9},{2,18},{10... | collective-permute-start | bytes 5111816 | tf_op jit(solution)/shard_map/ppermute | solution.py:19
  51.1 56.2 %collective-permute-start.6 = (bf16[512,1664]{1,0:T(8,128)(2,1)S(1)}, bf16[512,1664]{1,0:T(8,128)(2,1)}, u32[]{:S(2)}, u32[]{:S(2)}) collective-permute-start(bf16[512,1664]{1,0:T(8,128)(2,1)S(1)} %get-tuple-element.61.refs_1_), channel_id=1, source_target_pairs={{0,2},{1,3},{2,0},{3,1},{4,6},{5,7},{6,4},{7,5},{8,10},{9,11},{10,... | collective-permute-start | bytes 5111816 | tf_op jit(solution)/shard_map/ppermute | solution.py:19
  54.4 15.1 %copy-start.8 = (bf16[2,1664,128]{2,1,0:T(8,128)(2,1)}, bf16[2,1664,128]{2,1,0:T(8,128)(2,1)S(1)}, u32[]{:S(2)}) copy-start(bf16[2,1664,128]{2,1,0:T(8,128)(2,1)S(1)} %get-tuple-element.123.refs_8_) | copy-start | bytes 2555908
  54.4 30.1 %collective-permute-start.9 = (bf16[2,1664,128]{2,1,0:T(8,128)(2,1)S(1)}, bf16[2,1664,128]{2,1,0:T(8,128)(2,1)S(1)}, u32[]{:S(2)}, u32[]{:S(2)}) collective-permute-start(bf16[2,1664,128]{2,1,0:T(8,128)(2,1)S(1)} %get-tuple-element.123.refs_8_), channel_id=1, source_target_pairs={{0,8},{8,0},{16,24},{24,16},{1,9},{9,1},{17,25},{25,17},{2,10},{10... | collective-permute-start | bytes 2555912 | tf_op jit(solution)/shard_map/ppermute | solution.py:19
  56.0 50.2 %collective-permute-start.8 = (bf16[2,1664,128]{2,1,0:T(8,128)(2,1)S(1)}, bf16[2,1664,128]{2,1,0:T(8,128)(2,1)}, u32[]{:S(2)}, u32[]{:S(2)}) collective-permute-start(bf16[2,1664,128]{2,1,0:T(8,128)(2,1)S(1)} %get-tuple-element.124), channel_id=1, source_target_pairs={{0,4},{1,5},{2,6},{3,7},{4,0},{5,1},{6,2},{7,3},{8,12},{9,13},{10,... | collective-permute-start | bytes 2555912 | tf_op jit(solution)/shard_map/ppermute | solution.py:19
  82.9 58.5 %collective-permute-start.11 = (bf16[2,1664,256]{2,1,0:T(8,128)(2,1)S(1)}, bf16[2,1664,256]{2,1,0:T(8,128)(2,1)S(1)}, u32[]{:S(2)}, u32[]{:S(2)}) collective-permute-start(bf16[2,1664,256]{2,1,0:T(8,128)(2,1)S(1)} %copy-done.17), channel_id=1, source_target_pairs={{0,16},{8,24},{16,0},{24,8},{1,17},{9,25},{17,1},{25,9},{2,18},{10... | collective-permute-start | bytes 5111816 | tf_op jit(solution)/shard_map/ppermute | solution.py:19
  84.5 22.9 %copy-start.15 = (bf16[2,1664,128]{2,1,0:T(8,128)(2,1)}, bf16[2,1664,128]{2,1,0:T(8,128)(2,1)S(1)}, u32[]{:S(2)}) copy-start(bf16[2,1664,128]{2,1,0:T(8,128)(2,1)S(1)} %collective-permute-done.9.refs_12_) | copy-start | bytes 2555908
  107.3 111.4 %collective-permute-start.10 = (bf16[512,1664]{1,0:T(8,128)(2,1)}, bf16[512,1664]{1,0:T(8,128)(2,1)}, u32[]{:S(2)}, u32[]{:S(2)}) collective-permute-start(bf16[512,1664]{1,0:T(8,128)(2,1)} %collective-permute-done.1.refs_0_), channel_id=1, source_target_pairs={{0,2},{1,3},{2,0},{3,1},{4,6},{5,7},{6,4},{7,5},{8,10},{9,11},{10,... | collective-permute-start | bytes 5111816 | tf_op jit(solution)/shard_map/ppermute | solution.py:19
  109.8 110.4 %collective-permute-start.3 = (bf16[512,1664]{1,0:T(8,128)(2,1)}, bf16[512,1664]{1,0:T(8,128)(2,1)}, u32[]{:S(2)}, u32[]{:S(2)}) collective-permute-start(bf16[512,1664]{1,0:T(8,128)(2,1)} %get-tuple-element.60), channel_id=1, source_target_pairs={{0,16},{8,24},{16,0},{24,8},{1,17},{9,25},{17,1},{25,9},{2,18},{10... | collective-permute-start | bytes 5111816 | tf_op jit(solution)/shard_map/ppermute | solution.py:19
  111.3 38.0 %collective-permute-start.15 = (bf16[2,1664,128]{2,1,0:T(8,128)(2,1)}, bf16[2,1664,128]{2,1,0:T(8,128)(2,1)}, u32[]{:S(2)}, u32[]{:S(2)}) collective-permute-start(bf16[2,1664,128]{2,1,0:T(8,128)(2,1)} %get-tuple-element.74.refs_9_), channel_id=1, source_target_pairs={{0,8},{8,0},{16,24},{24,16},{1,9},{9,1},{17,25},{25,17},{2,10},{10... | collective-permute-start | bytes 2555912 | tf_op jit(solution)/shard_map/ppermute | solution.py:19
  112.8 38.0 %collective-permute-start.13 = (bf16[2,1664,128]{2,1,0:T(8,128)(2,1)}, bf16[2,1664,128]{2,1,0:T(8,128)(2,1)}, u32[]{:S(2)}, u32[]{:S(2)}) collective-permute-start(bf16[2,1664,128]{2,1,0:T(8,128)(2,1)} %collective-permute-done.8.refs_10_), channel_id=1, source_target_pairs={{0,8},{8,0},{16,24},{24,16},{1,9},{9,1},{17,25},{25,17},{2,10},{10... | collective-permute-start | bytes 2555912 | tf_op jit(solution)/shard_map/ppermute | solution.py:19
  142.6 76.0 %collective-permute-start.12 = (bf16[2,1664,128]{2,1,0:T(8,128)(2,1)}, bf16[2,1664,128]{2,1,0:T(8,128)(2,1)}, u32[]{:S(2)}, u32[]{:S(2)}) collective-permute-start(bf16[2,1664,128]{2,1,0:T(8,128)(2,1)} %get-tuple-element.68), channel_id=1, source_target_pairs={{0,4},{1,5},{2,6},{3,7},{4,0},{5,1},{6,2},{7,3},{8,12},{9,13},{10,... | collective-permute-start | bytes 2555912 | tf_op jit(solution)/shard_map/ppermute | solution.py:19
  149.3 84.9 %collective-permute-start.17 = (bf16[2,1664,256]{2,1,0:T(8,128)(2,1)}, bf16[2,1664,256]{2,1,0:T(8,128)(2,1)}, u32[]{:S(2)}, u32[]{:S(2)}) collective-permute-start(bf16[2,1664,256]{2,1,0:T(8,128)(2,1)} %get-tuple-element.76.refs_8_), channel_id=1, source_target_pairs={{0,8},{8,0},{16,24},{24,16},{1,9},{9,1},{17,25},{25,17},{2,10},{10... | collective-permute-start | bytes 5111816 | tf_op jit(solution)/shard_map/ppermute | solution.py:19
  150.8 102.0 %collective-permute-start.16 = (bf16[2,1664,256]{2,1,0:T(8,128)(2,1)}, bf16[2,1664,256]{2,1,0:T(8,128)(2,1)}, u32[]{:S(2)}, u32[]{:S(2)}) collective-permute-start(bf16[2,1664,256]{2,1,0:T(8,128)(2,1)} %get-tuple-element.75), channel_id=1, source_target_pairs={{0,4},{1,5},{2,6},{3,7},{4,0},{5,1},{6,2},{7,3},{8,12},{9,13},{10,... | collective-permute-start | bytes 5111816 | tf_op jit(solution)/shard_map/ppermute | solution.py:19
  165.8 54.6 %copy-start.19 = (bf16[512,256]{1,0:T(8,128)(2,1)S(1)}, bf16[512,256]{1,0:T(8,128)(2,1)}, u32[]{:S(2)}) copy-start(bf16[512,256]{1,0:T(8,128)(2,1)} %copy.27) | copy-start | bytes 786436
  218.7 71.1 %collective-permute-start.4 = (bf16[512,1664]{1,0:T(8,128)(2,1)}, bf16[512,1664]{1,0:T(8,128)(2,1)S(1)}, u32[]{:S(2)}, u32[]{:S(2)}) collective-permute-start(bf16[512,1664]{1,0:T(8,128)(2,1)} %collective-permute-done.1.refs_0_), channel_id=1, source_target_pairs={{0,1},{1,0},{2,3},{3,2},{4,5},{5,4},{6,7},{7,6},{8,9},{9,8},{10,11... | collective-permute-start | bytes 5111816 | tf_op jit(solution)/shard_map/ppermute | solution.py:19
  218.7 70.6 %collective-permute-start.20 = (bf16[2,1664,128]{2,1,0:T(8,128)(2,1)}, bf16[2,1664,128]{2,1,0:T(8,128)(2,1)S(1)}, u32[]{:S(2)}, u32[]{:S(2)}) collective-permute-start(bf16[2,1664,128]{2,1,0:T(8,128)(2,1)} %collective-permute-done.12.refs_11_), channel_id=1, source_target_pairs={{0,8},{8,0},{16,24},{24,16},{1,9},{9,1},{17,25},{25,17},{2,10},{10... | collective-permute-start | bytes 2555912 | tf_op jit(solution)/shard_map/ppermute | solution.py:19
  220.3 69.0 %collective-permute-start.14 = (bf16[512,1664]{1,0:T(8,128)(2,1)}, bf16[512,1664]{1,0:T(8,128)(2,1)}, u32[]{:S(2)}, u32[]{:S(2)}) collective-permute-start(bf16[512,1664]{1,0:T(8,128)(2,1)} %collective-permute-done.3.refs_1_), channel_id=1, source_target_pairs={{0,2},{1,3},{2,0},{3,1},{4,6},{5,7},{6,4},{7,5},{8,10},{9,11},{10,... | collective-permute-start | bytes 5111816 | tf_op jit(solution)/shard_map/ppermute | solution.py:19
  234.2 56.9 %collective-permute-start.5 = (bf16[512,1664]{1,0:T(8,128)(2,1)}, bf16[512,1664]{1,0:T(8,128)(2,1)S(1)}, u32[]{:S(2)}, u32[]{:S(2)}) collective-permute-start(bf16[512,1664]{1,0:T(8,128)(2,1)} %collective-permute-done.3.refs_1_), channel_id=1, source_target_pairs={{0,1},{1,0},{2,3},{3,2},{4,5},{5,4},{6,7},{7,6},{8,9},{9,8},{10,11... | collective-permute-start | bytes 5111816 | tf_op jit(solution)/shard_map/ppermute | solution.py:19
  252.8 39.6 %collective-permute-start.18 = (bf16[512,1664]{1,0:T(8,128)(2,1)}, bf16[512,1664]{1,0:T(8,128)(2,1)}, u32[]{:S(2)}, u32[]{:S(2)}) collective-permute-start(bf16[512,1664]{1,0:T(8,128)(2,1)} %collective-permute-done.10.refs_4_), channel_id=1, source_target_pairs={{0,1},{1,0},{2,3},{3,2},{4,5},{5,4},{6,7},{7,6},{8,9},{9,8},{10,11... | collective-permute-start | bytes 5111816 | tf_op jit(solution)/shard_map/ppermute | solution.py:19
  289.2 5.2 collective-permute-start.19
  289.3 19.6 %collective-permute-start.21 = (bf16[512,1664]{1,0:T(8,128)(2,1)S(1)}, bf16[512,1664]{1,0:T(8,128)(2,1)}, u32[]{:S(2)}, u32[]{:S(2)}) collective-permute-start(bf16[512,1664]{1,0:T(8,128)(2,1)S(1)} %get-tuple-element.116.refs_0_), channel_id=1, source_target_pairs={{0,1},{1,0},{2,3},{3,2},{4,5},{5,4},{6,7},{7,6},{8,9},{9,8},{10,11... | collective-permute-start | bytes 5111816 | tf_op jit(solution)/shard_map/ppermute | solution.py:19
  289.8 20.7 %collective-permute-start.22 = (bf16[512,1664]{1,0:T(8,128)(2,1)S(1)}, bf16[512,1664]{1,0:T(8,128)(2,1)}, u32[]{:S(2)}, u32[]{:S(2)}) collective-permute-start(bf16[512,1664]{1,0:T(8,128)(2,1)S(1)} %get-tuple-element.61.refs_1_), channel_id=1, source_target_pairs={{0,1},{1,0},{2,3},{3,2},{4,5},{5,4},{6,7},{7,6},{8,9},{9,8},{10,11... | collective-permute-start | bytes 5111816 | tf_op jit(solution)/shard_map/ppermute | solution.py:19
  292.3 18.2 %collective-permute-start.23 = (bf16[512,1664]{1,0:T(8,128)(2,1)}, bf16[512,1664]{1,0:T(8,128)(2,1)}, u32[]{:S(2)}, u32[]{:S(2)}) collective-permute-start(bf16[512,1664]{1,0:T(8,128)(2,1)} %collective-permute-done.2.refs_4_), channel_id=1, source_target_pairs={{0,1},{1,0},{2,3},{3,2},{4,5},{5,4},{6,7},{7,6},{8,9},{9,8},{10,11... | collective-permute-start | bytes 5111816 | tf_op jit(solution)/shard_map/ppermute | solution.py:19
  292.4 18.1 %collective-permute-start.24 = (bf16[512,1664]{1,0:T(8,128)(2,1)}, bf16[512,1664]{1,0:T(8,128)(2,1)}, u32[]{:S(2)}, u32[]{:S(2)}) collective-permute-start(bf16[512,1664]{1,0:T(8,128)(2,1)} %collective-permute-done.6.refs_5_), channel_id=1, source_target_pairs={{0,1},{1,0},{2,3},{3,2},{4,5},{5,4},{6,7},{7,6},{8,9},{9,8},{10,11... | collective-permute-start | bytes 5111816 | tf_op jit(solution)/shard_map/ppermute | solution.py:19
  307.7 25.5 %collective-permute-start.25 = (bf16[1024,512]{1,0:T(8,128)(2,1)}, bf16[1024,512]{1,0:T(8,128)(2,1)S(1)}, u32[]{:S(2)}, u32[]{:S(2)}) collective-permute-start(bf16[1024,512]{1,0:T(8,128)(2,1)} %shard_map.116), channel_id=1, source_target_pairs={{0,16},{8,24},{16,0},{24,8},{1,17},{9,25},{17,1},{25,9},{2,18},{10... | collective-permute-start | bytes 3145736 | tf_op jit(solution)/shard_map/ppermute | solution.py:19
  308.9 55.1 %collective-permute-start.27 = (bf16[2,1664,256]{2,1,0:T(8,128)(2,1)}, bf16[2,1664,256]{2,1,0:T(8,128)(2,1)S(1)}, u32[]{:S(2)}, u32[]{:S(2)}) collective-permute-start(bf16[2,1664,256]{2,1,0:T(8,128)(2,1)} %collective-permute-done.16.refs_9_), channel_id=1, source_target_pairs={{0,8},{8,0},{16,24},{24,16},{1,9},{9,1},{17,25},{25,17},{2,10},{10... | collective-permute-start | bytes 5111816 | tf_op jit(solution)/shard_map/ppermute | solution.py:19
  324.1 13.6 %copy-start.33 = (s32[64,8]{0,1:T(8,128)S(1)}, s32[64,8]{0,1:T(8,128)}, u32[]{:S(2)}) copy-start(s32[64,8]{0,1:T(8,128)} %param.14) | copy-start | bytes 6148
  324.1 14.3 %copy-start.35 = (s32[2,2]{1,0:T(2,128)S(1)}, s32[2,2]{1,0:T(2,128)}, u32[]{:S(2)}) copy-start(s32[2,2]{1,0:T(2,128)} %constant.176.clone) | copy-start | bytes 52
  324.1 14.3 %copy-start.36 = (s32[2]{0:T(128)S(1)}, s32[2]{0:T(128)}, u32[]{:S(2)}) copy-start(s32[2]{0:T(128)} %constant.178) | copy-start | bytes 28
  336.5 25.3 %collective-permute-start.26 = (bf16[1024,256]{1,0:T(8,128)(2,1)S(1)}, bf16[1024,256]{1,0:T(8,128)(2,1)S(1)}, u32[]{:S(2)}, u32[]{:S(2)}) collective-permute-start(bf16[1024,256]{1,0:T(8,128)(2,1)S(1)} %slice.74), channel_id=1, source_target_pairs={{0,4},{1,5},{2,6},{3,7},{4,0},{5,1},{6,2},{7,3},{8,12},{9,13},{10,... | collective-permute-start | bytes 1572872 | tf_op jit(solution)/shard_map/ppermute | solution.py:19
  377.8 15.7 %copy-start.22 = (bf16[1024,512]{1,0:T(8,128)(2,1)S(1)}, bf16[1024,512]{1,0:T(8,128)(2,1)}, u32[]{:S(2)}) copy-start(bf16[1024,512]{1,0:T(8,128)(2,1)} %shard_map.118) | copy-start | bytes 3145732
  390.4 30.9 %collective-permute-start.29 = (bf16[32,64,256]{2,1,0:T(8,128)(2,1)}, bf16[32,64,256]{2,1,0:T(8,128)(2,1)S(1)}, u32[]{:S(2)}, u32[]{:S(2)}) collective-permute-start(bf16[32,64,256]{2,1,0:T(8,128)(2,1)} %get-tuple-element.87), channel_id=1, source_target_pairs={{0,16},{8,24},{16,0},{24,8},{1,17},{9,25},{17,1},{25,9},{2,18},{10... | collective-permute-start | bytes 3145736 | tf_op jit(solution)/shard_map/ppermute | solution.py:19
  391.6 29.7 %collective-permute-start.28 = (bf16[32,64,256]{2,1,0:T(8,128)(2,1)}, bf16[32,64,256]{2,1,0:T(8,128)(2,1)S(1)}, u32[]{:S(2)}, u32[]{:S(2)}) collective-permute-start(bf16[32,64,256]{2,1,0:T(8,128)(2,1)} %get-tuple-element.85), channel_id=1, source_target_pairs={{0,8},{8,0},{16,24},{24,16},{1,9},{9,1},{17,25},{25,17},{2,10},{10... | collective-permute-start | bytes 3145736 | tf_op jit(solution)/shard_map/ppermute | solution.py:19
  393.4 45.8 %collective-permute-start.30 = (bf16[1024,512]{1,0:T(8,128)(2,1)S(1)}, bf16[1024,512]{1,0:T(8,128)(2,1)S(1)}, u32[]{:S(2)}, u32[]{:S(2)}) collective-permute-start(bf16[1024,512]{1,0:T(8,128)(2,1)S(1)} %copy-done.22), channel_id=1, source_target_pairs={{0,16},{8,24},{16,0},{24,8},{1,17},{9,25},{17,1},{25,9},{2,18},{10... | collective-permute-start | bytes 3145736 | tf_op jit(solution)/shard_map/ppermute | solution.py:19
  394.0 82.2 %collective-permute-start.32 = (bf16[32,64,256]{2,1,0:T(8,128)(2,1)}, bf16[32,64,256]{2,1,0:T(8,128)(2,1)}, u32[]{:S(2)}, u32[]{:S(2)}) collective-permute-start(bf16[32,64,256]{2,1,0:T(8,128)(2,1)} %get-tuple-element.84), channel_id=1, source_target_pairs={{0,8},{8,0},{16,24},{24,16},{1,9},{9,1},{17,25},{25,17},{2,10},{10... | collective-permute-start | bytes 3145736 | tf_op jit(solution)/shard_map/ppermute | solution.py:19
  394.6 82.6 %collective-permute-start.34 = (bf16[32,64,256]{2,1,0:T(8,128)(2,1)}, bf16[32,64,256]{2,1,0:T(8,128)(2,1)S(1)}, u32[]{:S(2)}, u32[]{:S(2)}) collective-permute-start(bf16[32,64,256]{2,1,0:T(8,128)(2,1)} %get-tuple-element.86), channel_id=1, source_target_pairs={{0,16},{8,24},{16,0},{24,8},{1,17},{9,25},{17,1},{25,9},{2,18},{10... | collective-permute-start | bytes 3145736 | tf_op jit(solution)/shard_map/ppermute | solution.py:19
  408.6 30.7 %copy-start.7 = (f32[1024,512]{1,0:T(8,128)S(1)}, f32[1024,512]{1,0:T(8,128)}, u32[]{:S(2)}) copy-start(f32[1024,512]{1,0:T(8,128)} %shard_map.120) | copy-start | bytes 6291460
  421.3 18.5 %copy-start.26 = (bf16[32,64,256]{2,1,0:T(8,128)(2,1)S(1)}, bf16[32,64,256]{2,1,0:T(8,128)(2,1)}, u32[]{:S(2)}) copy-start(bf16[32,64,256]{2,1,0:T(8,128)(2,1)} %get-tuple-element.95) | copy-start | bytes 3145732
  439.7 22.9 %collective-permute-start.31 = (bf16[1024,256]{1,0:T(8,128)(2,1)S(1)}, bf16[1024,256]{1,0:T(8,128)(2,1)S(1)}, u32[]{:S(2)}, u32[]{:S(2)}) collective-permute-start(bf16[1024,256]{1,0:T(8,128)(2,1)S(1)} %slice.73), channel_id=1, source_target_pairs={{0,4},{1,5},{2,6},{3,7},{4,0},{5,1},{6,2},{7,3},{8,12},{9,13},{10,... | collective-permute-start | bytes 1572872 | tf_op jit(solution)/shard_map/ppermute | solution.py:19
  440.2 55.0 %collective-permute-start.35 = (bf16[32,64,256]{2,1,0:T(8,128)(2,1)S(1)}, bf16[32,64,256]{2,1,0:T(8,128)(2,1)}, u32[]{:S(2)}, u32[]{:S(2)}) collective-permute-start(bf16[32,64,256]{2,1,0:T(8,128)(2,1)S(1)} %add_convert_fusion.7), channel_id=1, source_target_pairs={{0,8},{8,0},{16,24},{24,16},{1,9},{9,1},{17,25},{25,17},{2,10},{10... | collective-permute-start | bytes 3145736 | tf_op jit(solution)/shard_map/ppermute | solution.py:19
  442.1 53.2 %collective-permute-start.33 = (bf16[32,64,256]{2,1,0:T(8,128)(2,1)S(1)}, bf16[32,64,256]{2,1,0:T(8,128)(2,1)}, u32[]{:S(2)}, u32[]{:S(2)}) collective-permute-start(bf16[32,64,256]{2,1,0:T(8,128)(2,1)S(1)} %add_convert_fusion.10), channel_id=1, source_target_pairs={{0,16},{8,24},{16,0},{24,8},{1,17},{9,25},{17,1},{25,9},{2,18},{10... | collective-permute-start | bytes 3145736 | tf_op jit(solution)/shard_map/ppermute | solution.py:19
  476.2 26.5 %collective-permute-start.37 = (bf16[32,64,256]{2,1,0:T(8,128)(2,1)}, bf16[32,64,256]{2,1,0:T(8,128)(2,1)}, u32[]{:S(2)}, u32[]{:S(2)}) collective-permute-start(bf16[32,64,256]{2,1,0:T(8,128)(2,1)} %get-tuple-element.105), channel_id=1, source_target_pairs={{0,8},{8,0},{16,24},{24,16},{1,9},{9,1},{17,25},{25,17},{2,10},{10... | collective-permute-start | bytes 3145736 | tf_op jit(solution)/shard_map/ppermute | solution.py:19
  478.2 28.5 %collective-permute-start.38 = (bf16[32,64,256]{2,1,0:T(8,128)(2,1)}, bf16[32,64,256]{2,1,0:T(8,128)(2,1)S(1)}, u32[]{:S(2)}, u32[]{:S(2)}) collective-permute-start(bf16[32,64,256]{2,1,0:T(8,128)(2,1)} %get-tuple-element.106), channel_id=1, source_target_pairs={{0,16},{8,24},{16,0},{24,8},{1,17},{9,25},{17,1},{25,9},{2,18},{10... | collective-permute-start | bytes 3145736 | tf_op jit(solution)/shard_map/ppermute | solution.py:19
  495.1 29.9 %collective-permute-start.36 = (bf16[32,64,256]{2,1,0:T(8,128)(2,1)}, bf16[32,64,256]{2,1,0:T(8,128)(2,1)S(1)}, u32[]{:S(2)}, u32[]{:S(2)}) collective-permute-start(bf16[32,64,256]{2,1,0:T(8,128)(2,1)} %get-tuple-element.103), channel_id=1, source_target_pairs={{0,8},{8,0},{16,24},{24,16},{1,9},{9,1},{17,25},{25,17},{2,10},{10... | collective-permute-start | bytes 3145736 | tf_op jit(solution)/shard_map/ppermute | solution.py:19
  495.2 58.8 %collective-permute-start.40 = (bf16[32,64,256]{2,1,0:T(8,128)(2,1)}, bf16[32,64,256]{2,1,0:T(8,128)(2,1)S(1)}, u32[]{:S(2)}, u32[]{:S(2)}) collective-permute-start(bf16[32,64,256]{2,1,0:T(8,128)(2,1)} %get-tuple-element.109), channel_id=1, source_target_pairs={{0,16},{8,24},{16,0},{24,8},{1,17},{9,25},{17,1},{25,9},{2,18},{10... | collective-permute-start | bytes 3145736 | tf_op jit(solution)/shard_map/ppermute | solution.py:19
  506.7 43.3 %collective-permute-start.39 = (bf16[32,64,256]{2,1,0:T(8,128)(2,1)S(1)}, bf16[32,64,256]{2,1,0:T(8,128)(2,1)S(1)}, u32[]{:S(2)}, u32[]{:S(2)}) collective-permute-start(bf16[32,64,256]{2,1,0:T(8,128)(2,1)S(1)} %add_convert_fusion.4), channel_id=1, source_target_pairs={{0,16},{8,24},{16,0},{24,8},{1,17},{9,25},{17,1},{25,9},{2,18},{10... | collective-permute-start | bytes 3145736 | tf_op jit(solution)/shard_map/ppermute | solution.py:19
  510.6 43.5 %collective-permute-start.41 = (bf16[32,64,256]{2,1,0:T(8,128)(2,1)S(1)}, bf16[32,64,256]{2,1,0:T(8,128)(2,1)S(1)}, u32[]{:S(2)}, u32[]{:S(2)}) collective-permute-start(bf16[32,64,256]{2,1,0:T(8,128)(2,1)S(1)} %add_convert_fusion.1), channel_id=1, source_target_pairs={{0,8},{8,0},{16,24},{24,16},{1,9},{9,1},{17,25},{25,17},{2,10},{10... | collective-permute-start | bytes 3145736 | tf_op jit(solution)/shard_map/ppermute | solution.py:19
  515.9 34.1 %copy-start.31 = (bf16[32,64,256]{2,1,0:T(8,128)(2,1)S(1)}, bf16[32,64,256]{2,1,0:T(8,128)(2,1)}, u32[]{:S(2)}) copy-start(bf16[32,64,256]{2,1,0:T(8,128)(2,1)} %get-tuple-element.102) | copy-start | bytes 3145732
  558.4 3.8 collective-permute-start.42
  562.2 13.3 %copy-start.5 = (bf16[1024,256]{1,0:T(8,128)(2,1)S(1)}, bf16[1024,256]{1,0:T(8,128)(2,1)}, u32[]{:S(2)}) copy-start(bf16[1024,256]{1,0:T(8,128)(2,1)} %fusion.25.screened_ref) | copy-start | bytes 1572868
  562.2 13.4 %copy-start.6 = (bf16[1024,256]{1,0:T(8,128)(2,1)S(1)}, bf16[1024,256]{1,0:T(8,128)(2,1)}, u32[]{:S(2)}) copy-start(bf16[1024,256]{1,0:T(8,128)(2,1)} %fusion.24.screened_ref) | copy-start | bytes 1572868
  562.2 4.8 collective-permute-start.43
  563.5 13.8 %copy-start.1 = (bf16[256,256]{1,0:T(8,128)(2,1)S(1)}, bf16[256,256]{1,0:T(8,128)(2,1)}, u32[]{:S(2)}) copy-start(bf16[256,256]{1,0:T(8,128)(2,1)} %param.13) | copy-start | bytes 393220
  567.0 4.6 collective-permute-start.44
  571.8 3.7 collective-permute-start.45
  575.5 1.2 collective-permute-start.46
  (20 other events, 78.4 us)

commit v7 on v5

--- a/solution.py
+++ b/solution.py
@@ -303,7 +303,7 @@
             while len(panels) < GROUPS:
                 turn_next(near_second, came[0][1], from_row(0, 0), *panels)
             arrived.append(cross(crossing[j], crossed_second, *panels))
-        far(j, *due)
+        leave = far(j, *due)
     while len(panels) < GROUPS:
         turn_next(near_second, *panels)
 
@@ -331,8 +331,6 @@
     blocks = c_low ^ jnp.arange(top_col, dtype=jnp.int32)
     order = ((blocks // per_block) ^ r_low) * per_block + blocks % per_block
 
-    earlier, due = (), [pair[1] for pair in came[3:4]]
-    ready = pieces_crossed[-1][-1]
     screened_chunks, contracted_chunks = [], []
     energy = jnp.zeros((tile, tile), jnp.float32)
     hops = {bit: Link(2) for bit in bits_below(row_count)}
@@ -342,21 +340,37 @@
     kept = [[e for e in range(row_count) if not e & bits[0]] for bits in orders]
     places = r ^ jnp.array(kept, jnp.int32)
     first_bits = jnp.array([[bits[0]] for bits in orders], jnp.int32)
-    for j in range(0, chunks, pair):
-        for i in range(len(gathered), min(j + pair + 1, chunks)):
+    pairs = chunks // pair
+
+    def sources_of(k):
+        at = range(k * pair, (k + 1) * pair)
+        return [[gathered[i][f][side] for side in range(2) for i in at] for f in range(top_row)]
+
+    def gather_next(upto, ready):
+        for i in range(len(gathered), min(upto, chunks)):
             gather_rows([after(part, ready) for part in came[i]])
-        sources = [[gathered[j + i][f][side] for side in range(2) for i in range(pair)] for f in range(top_row)]
-        away = product(pieces_crossed, sources, after(order, *earlier), per_block, jnp.bfloat16)
-        ready = away
-        home = product(pieces_mine, sources, after(order, away), per_block, jnp.float32)
-        home = after(home, *due) + swap(away, "row", top_row).astype(jnp.float32)
-        came_back = swap(home[:, wide:].astype(jnp.bfloat16), "col", top_col)
-        screened = (home[:, :wide] + came_back.astype(jnp.float32)).astype(jnp.bfloat16)
+
+    gather_next(pair + 1, pieces_crossed[-1][-1])
+    away = product(pieces_crossed, sources_of(0), after(order, leave), per_block, jnp.bfloat16)
+    home = product(pieces_mine, sources_of(0), after(order, away), per_block, jnp.float32)
+    crossing_back = swap(away, "row", top_row)
+    due = [part[1] for part in came[3:4]]
+    for k in range(pairs):
+        total = after(home, *due) + crossing_back.astype(jnp.float32)
+        came_back = swap(total[:, wide:].astype(jnp.bfloat16), "col", top_col)
+        if k + 1 < pairs:
+            gather_next((k + 2) * pair, away)
+            away = product(pieces_crossed, sources_of(k + 1), after(order, home), per_block, jnp.bfloat16)
+            crossing_back = swap(away, "row", top_row)
+            came_back = after(came_back, away)
+        screened = (total[:, :wide] + came_back.astype(jnp.float32)).astype(jnp.bfloat16)
         screened_chunks.append(screened)
-
-        gone = contract(panels, screened, panel_mask, places ^ first_bits, rb, ab, share)
-        stay = contract(panels, screened, panel_mask, after(places, gone), rb, ab, share)
-        earlier, due = (home, *gone[0], *gone[1]), []
+        gone = contract(panels, screened, panel_mask, after(places ^ first_bits, away), rb, ab, share)
+        if k + 1 < pairs:
+            home = product(pieces_mine, sources_of(k + 1), after(order, away, gone, crossing_back), per_block, jnp.float32)
+            gone[1] = [after(value, crossing_back) for value in gone[1]]
+        stay = contract(panels, screened, panel_mask, after(places, home, gone), rb, ab, share)
+        due = []
         left = [[dict(zip(kept[h], part[h])) for part in (gone, stay)] for h in range(2)]
         for hop in range(len(orders[0])):
             for h, bits in enumerate(orders):
@@ -365,7 +379,7 @@
                 total = {}
                 for e in sorted(going, key=lambda e: -(e & next_bit)):
                     value = hops[bits[hop]].swap(going[e], "row", bits[hop])
-                    due += [value] if not hop and e & next_bit else []
+                    due += [value] if not hop and not h and e & next_bit else []
                     total[e] = (staying[e].astype(jnp.float32) + value.astype(jnp.float32)).astype(jnp.bfloat16)
                 left[h] = [
                     {e & ~next_bit: value for e, value in total.items() if e & next_bit},

time: 528 us -> 547 us (1.036)
  waiting for transfers between devices: 218 us -> 239 us
    ppermute x51, waiting for transfers between devices: 218 us -> 239 us  [swap(): return lax.ppermute(value, axis, [(i, i ^ bit) for i in range(size)])]
  transfers between devices with their start and end apart: 51 -> 51, of which waited for: 21 -> 25; matrix products, arithmetic and copies ran while one was open for 17% -> 16% of each run, Pallas kernels for 28% -> 27%
where the time goes in v7:
time: 547 us; the launch traced here: 543 us
  waiting for transfers between devices  239 us (44%)
  Pallas kernels  147 us (27%)
  starting transfers between devices  47.7 us (9%)
  other arithmetic  46.6 us (9%)
  matrix products  33.3 us (6%)
  local copies, waits for them, and re-layouts  27.5 us (5%)
    ppermute x51, waiting for transfers between devices, swap(): return lax.ppermute(value, axis, [(i, i ^ bit) for i in range(size)])  239 us
    pallas_call x4, Pallas kernels, product(): pl.pallas_call(functools.partial(product_kernel, count, parts, per_block)...  53.8 us
    pallas_call x4, Pallas kernels, contract(): pl.pallas_call(functools.partial(contract_kernel, rb, ab), in_specs=[in_s...  50.5 us
    ppermute x51, starting transfers between devices, swap(): return lax.ppermute(value, axis, [(i, i ^ bit) for i in range(size)])  47.7 us
    pallas_call x4, Pallas kernels, turn(): pl.pallas_call(turn_kernel, grid=(rows // wide, tile // tall), in_specs=[...  42.9 us
    dot_general x1, matrix products, per_device(): jnp.einsum('qns,ls->nlq', near, green, preferred_element_type=jnp.float32)  19.5 us
    dot_general x4, matrix products, per_device(): jnp.einsum('mlq,nlq->mn', half, beside, preferred_element_type=jnp.float32)  13.8 us
    mul x1, other arithmetic, per_device(): after(three_near, near_crossed_first, came[1][1]) * near_mask[:, None, :]  13.8 us
  transfers between devices with their start and end apart: 51, of which 25 were waited for; matrix products, arithmetic and copies ran while one was open for 16% of the time, Pallas kernels for 27%

profile of v7, /device:TPU:0, one launch (start us, length us, event | category | flops | bytes accessed | tf_op | source)
XLA Modules:
  0.0 542.8 jit_solution(12467527249222592876)
XLA Ops:
  0.7 5.3 dynamic-slice_bitcast_fusion
  5.9 2.0 fusion.43
  8.0 3.0 collective-permute-start
  11.0 5.2 fusion.41
  17.8 12.5 %collective-permute-done = bf16[2,1664,128]{2,1,0:T(8,128)(2,1)} collective-permute-done((bf16[2,1664,128]{2,1,0:T(8,128)(2,1)}, bf16[2,1664,128]{2,1,0:T(8,128)(2,1)}, u32[]{:S(2)}, u32[]{:S(2)}) %collective-permute-start) | collective-permute-done | bytes 852000 | tf_op jit(solution)/shard_map/ppermute | solution.py:20
  30.2 1.7 collective-permute-start.1
  32.0 23.0 %collective-permute-done.2.refs_4_ = bf16[512,1664]{1,0:T(8,128)(2,1)} collective-permute-done((bf16[512,1664]{1,0:T(8,128)(2,1)S(1)}, bf16[512,1664]{1,0:T(8,128)(2,1)}, u32[]{:S(2)}, u32[]{:S(2)}) %collective-permute-start.2) | collective-permute-done | bytes 1703968 | tf_op jit(solution)/shard_map/ppermute | solution.py:20
  57.0 2.4 broadcast_select_fusion.5
  59.5 2.6 collective-permute-start.6
  62.1 10.9 %shard_map.112.refs_0_ = bf16[64,256,256]{2,1,0:T(8,128)(2,1)} custom-call(bf16[1024,64,256]{2,1,0:T(8,128)(2,1)} %panel_ref.3), custom_call_target="tpu_custom_call" | custom-call | bytes 33554432 | tf_op jit(solution)/shard_map/pallas_call | solution.py:122
  76.0 12.8 %collective-permute-done.4 = bf16[2,1664,128]{2,1,0:T(8,128)(2,1)S(1)} collective-permute-done((bf16[2,1664,128]{2,1,0:T(8,128)(2,1)}, bf16[2,1664,128]{2,1,0:T(8,128)(2,1)S(1)}, u32[]{:S(2)}, u32[]{:S(2)}) %collective-permute-start.4) | collective-permute-done | bytes 852000 | tf_op jit(solution)/shard_map/ppermute | solution.py:20
  88.8 2.5 broadcast_select_fusion.2
  91.3 10.7 %shard_map.113.refs_1_ = bf16[64,256,256]{2,1,0:T(8,128)(2,1)} custom-call(bf16[1024,64,256]{2,1,0:T(8,128)(2,1)} %panel_ref.3), custom_call_target="tpu_custom_call" | custom-call | bytes 33554432 | tf_op jit(solution)/shard_map/pallas_call | solution.py:122
  102.0 8.1 %collective-permute-done.6.refs_10_ = bf16[2,1664,128]{2,1,0:T(8,128)(2,1)} collective-permute-done((bf16[2,1664,128]{2,1,0:T(8,128)(2,1)}, bf16[2,1664,128]{2,1,0:T(8,128)(2,1)}, u32[]{:S(2)}, u32[]{:S(2)}) %collective-permute-start.6) | collective-permute-done | bytes 852000 | tf_op jit(solution)/shard_map/ppermute | solution.py:20
  111.1 2.7 collective-permute-start.11
  116.3 10.6 %shard_map.114.refs_2_ = bf16[64,256,256]{2,1,0:T(8,128)(2,1)} custom-call(bf16[1024,64,256]{2,1,0:T(8,128)(2,1)} %panel_ref.3), custom_call_target="tpu_custom_call" | custom-call | bytes 33554432 | tf_op jit(solution)/shard_map/pallas_call | solution.py:122
  128.5 10.6 %shard_map.115.refs_3_ = bf16[64,256,256]{2,1,0:T(8,128)(2,1)} custom-call(bf16[1024,64,256]{2,1,0:T(8,128)(2,1)} %panel_ref.3), custom_call_target="tpu_custom_call" | custom-call | bytes 33554432 | tf_op jit(solution)/shard_map/pallas_call | solution.py:122
  139.1 2.7 collective-permute-done.15
  146.4 1.8 copy.27
  148.2 2.6 broadcast_select_fusion.1
  150.8 2.6 collective-permute-start.17
  153.5 16.5 %collective-permute-done.12.refs_11_ = bf16[2,1664,128]{2,1,0:T(8,128)(2,1)} collective-permute-done((bf16[2,1664,128]{2,1,0:T(8,128)(2,1)}, bf16[2,1664,128]{2,1,0:T(8,128)(2,1)}, u32[]{:S(2)}, u32[]{:S(2)}) %collective-permute-start.12) | collective-permute-done | bytes 852000 | tf_op jit(solution)/shard_map/ppermute | solution.py:20
  171.5 2.5 collective-permute-start.14
  174.0 13.8 %broadcast_multiply_fusion = bf16[512,64,256]{2,1,0:T(8,128)(2,1)} fusion(bf16[512,64,256]{2,1,0:T(8,128)(2,1)} %param.12, bf16[512,256]{1,0:T(8,128)(2,1)S(1)} %copy-done.22), kind=kLoop, calls=%fused_computation.2 | loop fusion | flops 8388608 | bytes 33816576 | tf_op jit(solution)/shard_map/mul | solution.py:313
  187.8 17.2 %collective-permute-done.17.refs_10_ = bf16[2,1664,128]{2,1,0:T(8,128)(2,1)S(1)} collective-permute-done((bf16[2,1664,128]{2,1,0:T(8,128)(2,1)S(1)}, bf16[2,1664,128]{2,1,0:T(8,128)(2,1)S(1)}, u32[]{:S(2)}, u32[]{:S(2)}) %collective-permute-start.17) | collective-permute-done | bytes 852000 | tf_op jit(solution)/shard_map/ppermute | solution.py:20
  205.0 19.5 %convert_bitcast_fusion = bf16[64,64,512]{2,1,0:T(8,128)(2,1)} fusion(bf16[512,64,256]{2,1,0:T(8,128)(2,1)} %broadcast_multiply_fusion, bf16[256,256]{1,0:T(8,128)(2,1)S(1)} %copy-done, s32[]{:T(128)S(6)} %select_n.162), kind=kOutput, calls=%fused_computation.4 | convolution fusion | flops 1075838976 | bytes 21004292 | tf_op jit(solution)/shard_map/qns,ls->nlq/dot_general | solution.py:315
  224.5 5.6 %collective-permute-done.14.refs_5_ = bf16[512,1664]{1,0:T(8,128)(2,1)} collective-permute-done((bf16[512,1664]{1,0:T(8,128)(2,1)S(1)}, bf16[512,1664]{1,0:T(8,128)(2,1)}, u32[]{:S(2)}, u32[]{:S(2)}) %collective-permute-start.14) | collective-permute-done | bytes 1703968 | tf_op jit(solution)/shard_map/ppermute | solution.py:20
  234.2 2.7 broadcast_select_fusion
  236.9 13.4 %shard_map.116 = bf16[1024,512]{1,0:T(8,128)(2,1)} custom-call(s32[4]{0:T(128)} %fusion.40.order_ref, bf16[512,1664]{1,0:T(8,128)(2,1)} %collective-permute-done.1.refs_0_, bf16[512,1664]{1,0:T(8,128)(2,1)} %copy-done.8, bf16[512,1664]{1,0:T(8,128)(2,1)} %copy-done.10, bf16[512,1664]{1,0:T(8,128)(2,1)} %copy-done.11, ...), custom_call_target="tpu_custom_call" | custom-call | tf_op jit(solution)/shard_map/pallas_call | solution.py:97
  254.6 13.6 %shard_map.117 = f32[1024,512]{1,0:T(8,128)} custom-call(s32[4]{0:T(128)} %fusion.40.order_ref, bf16[512,1664]{1,0:T(8,128)(2,1)} %copy-done.3, bf16[512,1664]{1,0:T(8,128)(2,1)} %copy-done.2, bf16[512,1664]{1,0:T(8,128)(2,1)} %collective-permute-done.21.refs_2_, bf16[512,1664]{1,0:T(8,128)(2,1)} %collective-permute-done.22.refs_3_, ...), custom_call_target="tpu_custom_call" | custom-call | tf_op jit(solution)/shard_map/pallas_call | solution.py:97
  268.2 22.8 %collective-permute-done.25.refs_11_ = bf16[2,1664,128]{2,1,0:T(8,128)(2,1)S(1)} collective-permute-done((bf16[2,1664,128]{2,1,0:T(8,128)(2,1)}, bf16[2,1664,128]{2,1,0:T(8,128)(2,1)S(1)}, u32[]{:S(2)}, u32[]{:S(2)}) %collective-permute-start.25) | collective-permute-done | bytes 852000 | tf_op jit(solution)/shard_map/ppermute | solution.py:20
  291.5 1.6 collective-permute-start.29
  293.1 2.2 convert_add_fusion.1
  298.0 15.0 %collective-permute-done.31.refs_15_ = bf16[2,1664,128]{2,1,0:T(8,128)(2,1)} collective-permute-done((bf16[2,1664,128]{2,1,0:T(8,128)(2,1)S(1)}, bf16[2,1664,128]{2,1,0:T(8,128)(2,1)}, u32[]{:S(2)}, u32[]{:S(2)}) %collective-permute-start.31) | collective-permute-done | bytes 852000 | tf_op jit(solution)/shard_map/ppermute | solution.py:20
  313.0 17.3 %collective-permute-done.29.refs_13_ = bf16[2,1664,128]{2,1,0:T(8,128)(2,1)} collective-permute-done((bf16[2,1664,128]{2,1,0:T(8,128)(2,1)}, bf16[2,1664,128]{2,1,0:T(8,128)(2,1)}, u32[]{:S(2)}, u32[]{:S(2)}) %collective-permute-start.29) | collective-permute-done | bytes 852000 | tf_op jit(solution)/shard_map/ppermute | solution.py:20
  330.3 13.3 %shard_map.118 = bf16[1024,512]{1,0:T(8,128)(2,1)} custom-call(s32[4]{0:T(128)} %fusion.40.order_ref, bf16[512,1664]{1,0:T(8,128)(2,1)} %collective-permute-done.1.refs_0_, bf16[512,1664]{1,0:T(8,128)(2,1)} %copy-done.8, bf16[512,1664]{1,0:T(8,128)(2,1)} %copy-done.10, bf16[512,1664]{1,0:T(8,128)(2,1)} %copy-done.11, ...), custom_call_target="tpu_custom_call" | custom-call | tf_op jit(solution)/shard_map/pallas_call | solution.py:97
  345.2 2.0 fusion.25.screened_ref
  347.2 12.8 %shard_map.119 = (bf16[32,64,256]{2,1,0:T(8,128)(2,1)}, bf16[32,64,256]{2,1,0:T(8,128)(2,1)}, bf16[32,64,256]{2,1,0:T(8,128)(2,1)}, bf16[32,64,256]{2,1,0:T(8,128)(2,1)}) custom-call(s32[2,2]{1,0:T(2,128)} %get-tuple-element.107.places_ref, s32[16,8]{1,0:T(8,128)} %copy.42.mask_ref, bf16[1024,256]{1,0:T(8,128)(2,1)} %fusion.25.screened_ref, ...), custom_call_target="tpu_custom_call" | custom-call | tf_op jit(solution)/shard_map/pallas_call | solution.py:184
  362.0 6.1 %collective-permute-done.32 = bf16[1024,512]{1,0:T(8,128)(2,1)S(1)} collective-permute-done((bf16[1024,512]{1,0:T(8,128)(2,1)}, bf16[1024,512]{1,0:T(8,128)(2,1)S(1)}, u32[]{:S(2)}, u32[]{:S(2)}) %collective-permute-start.32) | collective-permute-done | bytes 1048608 | tf_op jit(solution)/shard_map/ppermute | solution.py:20
  369.6 13.6 %shard_map.120 = f32[1024,512]{1,0:T(8,128)} custom-call(s32[4]{0:T(128)} %fusion.40.order_ref, bf16[512,1664]{1,0:T(8,128)(2,1)} %copy-done.3, bf16[512,1664]{1,0:T(8,128)(2,1)} %copy-done.2, bf16[512,1664]{1,0:T(8,128)(2,1)} %collective-permute-done.21.refs_2_, bf16[512,1664]{1,0:T(8,128)(2,1)} %collective-permute-done.22.refs_3_, ...), custom_call_target="tpu_custom_call" | custom-call | tf_op jit(solution)/shard_map/pallas_call | solution.py:97
  383.2 3.1 collective-permute-done.33
  386.3 1.9 convert_add_fusion
  389.0 12.5 %shard_map.121 = (bf16[32,64,256]{2,1,0:T(8,128)(2,1)}, bf16[32,64,256]{2,1,0:T(8,128)(2,1)}, bf16[32,64,256]{2,1,0:T(8,128)(2,1)}, bf16[32,64,256]{2,1,0:T(8,128)(2,1)}) custom-call(s32[2,2]{1,0:T(2,128)} %get-tuple-element.116.places_ref, s32[16,8]{1,0:T(8,128)} %copy.42.mask_ref, bf16[1024,256]{1,0:T(8,128)(2,1)} %fusion.25.screened_ref, ...), custom_call_target="tpu_custom_call" | custom-call | tf_op jit(solution)/shard_map/pallas_call | solution.py:184
  401.5 8.2 %collective-permute-done.34 = bf16[1024,256]{1,0:T(8,128)(2,1)S(1)} collective-permute-done((bf16[1024,256]{1,0:T(8,128)(2,1)S(1)}, bf16[1024,256]{1,0:T(8,128)(2,1)S(1)}, u32[]{:S(2)}, u32[]{:S(2)}) %collective-permute-start.34) | collective-permute-done | bytes 524320 | tf_op jit(solution)/shard_map/ppermute | solution.py:20
  410.7 12.6 %shard_map.122 = (bf16[32,64,256]{2,1,0:T(8,128)(2,1)}, bf16[32,64,256]{2,1,0:T(8,128)(2,1)}, bf16[32,64,256]{2,1,0:T(8,128)(2,1)}, bf16[32,64,256]{2,1,0:T(8,128)(2,1)}) custom-call(s32[2,2]{1,0:T(2,128)} %get-tuple-element.107.places_ref, s32[16,8]{1,0:T(8,128)} %copy.42.mask_ref, bf16[1024,256]{1,0:T(8,128)(2,1)} %fusion.24.screened_ref, ...), custom_call_target="tpu_custom_call" | custom-call | tf_op jit(solution)/shard_map/pallas_call | solution.py:184
  426.0 1.8 collective-permute-start.39
  430.3 2.8 fusion.42
  433.1 12.6 %shard_map.123 = (bf16[32,64,256]{2,1,0:T(8,128)(2,1)}, bf16[32,64,256]{2,1,0:T(8,128)(2,1)}, bf16[32,64,256]{2,1,0:T(8,128)(2,1)}, bf16[32,64,256]{2,1,0:T(8,128)(2,1)}) custom-call(s32[2,2]{1,0:T(2,128)} %get-tuple-element.116.places_ref, s32[16,8]{1,0:T(8,128)} %copy.42.mask_ref, bf16[1024,256]{1,0:T(8,128)(2,1)} %fusion.24.screened_ref, ...), custom_call_target="tpu_custom_call" | custom-call | tf_op jit(solution)/shard_map/pallas_call | solution.py:184
  445.7 4.9 collective-permute-done.41
  450.6 1.6 add_convert_fusion.4
  452.2 20.0 %collective-permute-done.39 = bf16[32,64,256]{2,1,0:T(8,128)(2,1)} collective-permute-done((bf16[32,64,256]{2,1,0:T(8,128)(2,1)}, bf16[32,64,256]{2,1,0:T(8,128)(2,1)}, u32[]{:S(2)}, u32[]{:S(2)}) %collective-permute-start.39) | collective-permute-done | bytes 1048608 | tf_op jit(solution)/shard_map/ppermute | solution.py:20
  473.0 3.0 collective-permute-done.37
  477.0 2.3 add_convert_fusion.9
  479.4 1.8 add_convert_fusion.6
  481.1 3.5 fusion.12
  484.6 3.5 fusion.15
  488.1 10.2 %collective-permute-done.40 = bf16[32,64,256]{2,1,0:T(8,128)(2,1)S(1)} collective-permute-done((bf16[32,64,256]{2,1,0:T(8,128)(2,1)S(1)}, bf16[32,64,256]{2,1,0:T(8,128)(2,1)S(1)}, u32[]{:S(2)}, u32[]{:S(2)}) %collective-permute-start.40) | collective-permute-done | bytes 1048608 | tf_op jit(solution)/shard_map/ppermute | solution.py:20
  499.2 3.5 fusion.18
  502.6 17.3 %collective-permute-done.44 = bf16[32,64,256]{2,1,0:T(8,128)(2,1)S(1)} collective-permute-done((bf16[32,64,256]{2,1,0:T(8,128)(2,1)S(1)}, bf16[32,64,256]{2,1,0:T(8,128)(2,1)S(1)}, u32[]{:S(2)}, u32[]{:S(2)}) %collective-permute-start.44) | collective-permute-done | bytes 1048608 | tf_op jit(solution)/shard_map/ppermute | solution.py:20
  520.7 3.5 fusion.21
  524.8 3.2 collective-permute-done.46
  528.8 3.5 maximum_bitcast_fusion
  532.5 4.5 collective-permute-done.48
  537.3 3.5 collective-permute-done.49
  (188 shorter events, 48.3 us)
Async XLA Ops:
  0.6 204.4 %copy-start = (bf16[256,256]{1,0:T(8,128)(2,1)S(1)}, bf16[256,256]{1,0:T(8,128)(2,1)}, u32[]{:S(2)}) copy-start(bf16[256,256]{1,0:T(8,128)(2,1)} %param.13) | copy-start | bytes 393220
  8.0 22.2 %collective-permute-start = (bf16[2,1664,128]{2,1,0:T(8,128)(2,1)}, bf16[2,1664,128]{2,1,0:T(8,128)(2,1)}, u32[]{:S(2)}, u32[]{:S(2)}) collective-permute-start(bf16[2,1664,128]{2,1,0:T(8,128)(2,1)} %get-tuple-element.157), channel_id=1, source_target_pairs={{0,16},{8,24},{16,0},{24,8},{1,17},{9,25},{17,1},{25,9},{2,18},{10... | collective-permute-start | bytes 2555912 | tf_op jit(solution)/shard_map/ppermute | solution.py:20
  16.2 213.9 %copy-start.3 = (bf16[512,1664]{1,0:T(8,128)(2,1)}, bf16[512,1664]{1,0:T(8,128)(2,1)S(1)}, u32[]{:S(2)}) copy-start(bf16[512,1664]{1,0:T(8,128)(2,1)S(1)} %get-tuple-element.140.refs_0_) | copy-start | bytes 5111812
  16.2 214.5 %copy-start.2 = (bf16[512,1664]{1,0:T(8,128)(2,1)}, bf16[512,1664]{1,0:T(8,128)(2,1)S(1)}, u32[]{:S(2)}) copy-start(bf16[512,1664]{1,0:T(8,128)(2,1)S(1)} %get-tuple-element.77.refs_1_) | copy-start | bytes 5111812
  16.2 38.8 %collective-permute-start.2 = (bf16[512,1664]{1,0:T(8,128)(2,1)S(1)}, bf16[512,1664]{1,0:T(8,128)(2,1)}, u32[]{:S(2)}, u32[]{:S(2)}) collective-permute-start(bf16[512,1664]{1,0:T(8,128)(2,1)S(1)} %get-tuple-element.140.refs_0_), channel_id=1, source_target_pairs={{0,2},{1,3},{2,0},{3,1},{4,6},{5,7},{6,4},{7,5},{8,10},{9,11},{10,... | collective-permute-start | bytes 5111816 | tf_op jit(solution)/shard_map/ppermute | solution.py:20
  30.2 42.8 %collective-permute-start.1 = (bf16[512,1664]{1,0:T(8,128)(2,1)}, bf16[512,1664]{1,0:T(8,128)(2,1)}, u32[]{:S(2)}, u32[]{:S(2)}) collective-permute-start(bf16[512,1664]{1,0:T(8,128)(2,1)} %get-tuple-element.71), channel_id=1, source_target_pairs={{0,16},{8,24},{16,0},{24,8},{1,17},{9,25},{17,1},{25,9},{2,18},{10... | collective-permute-start | bytes 5111816 | tf_op jit(solution)/shard_map/ppermute | solution.py:20
  55.0 56.1 %collective-permute-start.5 = (bf16[512,1664]{1,0:T(8,128)(2,1)S(1)}, bf16[512,1664]{1,0:T(8,128)(2,1)}, u32[]{:S(2)}, u32[]{:S(2)}) collective-permute-start(bf16[512,1664]{1,0:T(8,128)(2,1)S(1)} %get-tuple-element.77.refs_1_), channel_id=1, source_target_pairs={{0,2},{1,3},{2,0},{3,1},{4,6},{5,7},{6,4},{7,5},{8,10},{9,11},{10,... | collective-permute-start | bytes 5111816 | tf_op jit(solution)/shard_map/ppermute | solution.py:20
  56.5 32.3 %collective-permute-start.4 = (bf16[2,1664,128]{2,1,0:T(8,128)(2,1)}, bf16[2,1664,128]{2,1,0:T(8,128)(2,1)S(1)}, u32[]{:S(2)}, u32[]{:S(2)}) collective-permute-start(bf16[2,1664,128]{2,1,0:T(8,128)(2,1)} %get-tuple-element.74), channel_id=1, source_target_pairs={{0,16},{8,24},{16,0},{24,8},{1,17},{9,25},{17,1},{25,9},{2,18},{10... | collective-permute-start | bytes 2555912 | tf_op jit(solution)/shard_map/ppermute | solution.py:20
  59.5 50.7 %collective-permute-start.6 = (bf16[2,1664,128]{2,1,0:T(8,128)(2,1)}, bf16[2,1664,128]{2,1,0:T(8,128)(2,1)}, u32[]{:S(2)}, u32[]{:S(2)}) collective-permute-start(bf16[2,1664,128]{2,1,0:T(8,128)(2,1)} %get-tuple-element.152), channel_id=1, source_target_pairs={{0,4},{1,5},{2,6},{3,7},{4,0},{5,1},{6,2},{7,3},{8,12},{9,13},{10,... | collective-permute-start | bytes 2555912 | tf_op jit(solution)/shard_map/ppermute | solution.py:20
  73.0 53.9 %collective-permute-start.3 = (bf16[512,1664]{1,0:T(8,128)(2,1)}, bf16[512,1664]{1,0:T(8,128)(2,1)S(1)}, u32[]{:S(2)}, u32[]{:S(2)}) collective-permute-start(bf16[512,1664]{1,0:T(8,128)(2,1)} %get-tuple-element.73), channel_id=1, source_target_pairs={{0,16},{8,24},{16,0},{24,8},{1,17},{9,25},{17,1},{25,9},{2,18},{10... | collective-permute-start | bytes 5111816 | tf_op jit(solution)/shard_map/ppermute | solution.py:20
  74.5 35.7 %collective-permute-start.7 = (bf16[2,1664,128]{2,1,0:T(8,128)(2,1)S(1)}, bf16[2,1664,128]{2,1,0:T(8,128)(2,1)S(1)}, u32[]{:S(2)}, u32[]{:S(2)}) collective-permute-start(bf16[2,1664,128]{2,1,0:T(8,128)(2,1)S(1)} %get-tuple-element.151.refs_8_), channel_id=1, source_target_pairs={{0,8},{8,0},{16,24},{24,16},{1,9},{9,1},{17,25},{25,17},{2,10},{10... | collective-permute-start | bytes 2555912 | tf_op jit(solution)/shard_map/ppermute | solution.py:20
  91.3 22.4 %copy-start.34 = (bf16[2,1664,128]{2,1,0:T(8,128)(2,1)S(1)}, bf16[2,1664,128]{2,1,0:T(8,128)(2,1)}, u32[]{:S(2)}) copy-start(bf16[2,1664,128]{2,1,0:T(8,128)(2,1)} %get-tuple-element.88) | copy-start | bytes 2555908
  111.1 60.4 %collective-permute-start.11 = (bf16[512,1664]{1,0:T(8,128)(2,1)}, bf16[512,1664]{1,0:T(8,128)(2,1)}, u32[]{:S(2)}, u32[]{:S(2)}) collective-permute-start(bf16[512,1664]{1,0:T(8,128)(2,1)} %collective-permute-done.1.refs_0_), channel_id=1, source_target_pairs={{0,2},{1,3},{2,0},{3,1},{4,6},{5,7},{6,4},{7,5},{8,10},{9,11},{10,... | collective-permute-start | bytes 5111816 | tf_op jit(solution)/shard_map/ppermute | solution.py:20
  113.7 28.1 %collective-permute-start.15 = (bf16[2,1664,128]{2,1,0:T(8,128)(2,1)S(1)}, bf16[2,1664,128]{2,1,0:T(8,128)(2,1)S(1)}, u32[]{:S(2)}, u32[]{:S(2)}) collective-permute-start(bf16[2,1664,128]{2,1,0:T(8,128)(2,1)S(1)} %copy-done.34), channel_id=1, source_target_pairs={{0,16},{8,24},{16,0},{24,8},{1,17},{9,25},{17,1},{25,9},{2,18},{10... | collective-permute-start | bytes 2555912 | tf_op jit(solution)/shard_map/ppermute | solution.py:20
  114.2 36.6 %collective-permute-start.13 = (bf16[2,1664,128]{2,1,0:T(8,128)(2,1)}, bf16[2,1664,128]{2,1,0:T(8,128)(2,1)}, u32[]{:S(2)}, u32[]{:S(2)}) collective-permute-start(bf16[2,1664,128]{2,1,0:T(8,128)(2,1)} %collective-permute-done.6.refs_10_), channel_id=1, source_target_pairs={{0,8},{8,0},{16,24},{24,16},{1,9},{9,1},{17,25},{25,17},{2,10},{10... | collective-permute-start | bytes 2555912 | tf_op jit(solution)/shard_map/ppermute | solution.py:20
  115.7 35.1 %collective-permute-start.16 = (bf16[2,1664,128]{2,1,0:T(8,128)(2,1)}, bf16[2,1664,128]{2,1,0:T(8,128)(2,1)}, u32[]{:S(2)}, u32[]{:S(2)}) collective-permute-start(bf16[2,1664,128]{2,1,0:T(8,128)(2,1)} %get-tuple-element.90.refs_9_), channel_id=1, source_target_pairs={{0,8},{8,0},{16,24},{24,16},{1,9},{9,1},{17,25},{25,17},{2,10},{10... | collective-permute-start | bytes 2555912 | tf_op jit(solution)/shard_map/ppermute | solution.py:20
  126.9 43.1 %collective-permute-start.12 = (bf16[2,1664,128]{2,1,0:T(8,128)(2,1)}, bf16[2,1664,128]{2,1,0:T(8,128)(2,1)}, u32[]{:S(2)}, u32[]{:S(2)}) collective-permute-start(bf16[2,1664,128]{2,1,0:T(8,128)(2,1)} %get-tuple-element.85), channel_id=1, source_target_pairs={{0,4},{1,5},{2,6},{3,7},{4,0},{5,1},{6,2},{7,3},{8,12},{9,13},{10,... | collective-permute-start | bytes 2555912 | tf_op jit(solution)/shard_map/ppermute | solution.py:20
  142.8 28.8 %collective-permute-start.8 = (bf16[2,1664,128]{2,1,0:T(8,128)(2,1)}, bf16[2,1664,128]{2,1,0:T(8,128)(2,1)}, u32[]{:S(2)}, u32[]{:S(2)}) collective-permute-start(bf16[2,1664,128]{2,1,0:T(8,128)(2,1)} %get-tuple-element.81), channel_id=1, source_target_pairs={{0,16},{8,24},{16,0},{24,8},{1,17},{9,25},{17,1},{25,9},{2,18},{10... | collective-permute-start | bytes 2555912 | tf_op jit(solution)/shard_map/ppermute | solution.py:20
  148.2 23.3 %copy-start.9 = (bf16[512,1664]{1,0:T(8,128)(2,1)S(1)}, bf16[512,1664]{1,0:T(8,128)(2,1)}, u32[]{:S(2)}) copy-start(bf16[512,1664]{1,0:T(8,128)(2,1)} %copy-done.8) | copy-start | bytes 5111812
  148.2 25.8 %copy-start.22 = (bf16[512,256]{1,0:T(8,128)(2,1)S(1)}, bf16[512,256]{1,0:T(8,128)(2,1)}, u32[]{:S(2)}) copy-start(bf16[512,256]{1,0:T(8,128)(2,1)} %copy.27) | copy-start | bytes 786436
  150.8 79.9 %collective-permute-start.9 = (bf16[512,1664]{1,0:T(8,128)(2,1)}, bf16[512,1664]{1,0:T(8,128)(2,1)S(1)}, u32[]{:S(2)}, u32[]{:S(2)}) collective-permute-start(bf16[512,1664]{1,0:T(8,128)(2,1)} %collective-permute-done.1.refs_0_), channel_id=1, source_target_pairs={{0,1},{1,0},{2,3},{3,2},{4,5},{5,4},{6,7},{7,6},{8,9},{9,8},{10,11... | collective-permute-start | bytes 5111816 | tf_op jit(solution)/shard_map/ppermute | solution.py:20
  150.8 54.1 %collective-permute-start.17 = (bf16[2,1664,128]{2,1,0:T(8,128)(2,1)S(1)}, bf16[2,1664,128]{2,1,0:T(8,128)(2,1)S(1)}, u32[]{:S(2)}, u32[]{:S(2)}) collective-permute-start(bf16[2,1664,128]{2,1,0:T(8,128)(2,1)S(1)} %get-tuple-element.91), channel_id=1, source_target_pairs={{0,4},{1,5},{2,6},{3,7},{4,0},{5,1},{6,2},{7,3},{8,12},{9,13},{10,... | collective-permute-start | bytes 2555912 | tf_op jit(solution)/shard_map/ppermute | solution.py:20
  170.0 60.1 %collective-permute-start.20 = (bf16[2,1664,128]{2,1,0:T(8,128)(2,1)}, bf16[2,1664,128]{2,1,0:T(8,128)(2,1)S(1)}, u32[]{:S(2)}, u32[]{:S(2)}) collective-permute-start(bf16[2,1664,128]{2,1,0:T(8,128)(2,1)} %collective-permute-done.12.refs_11_), channel_id=1, source_target_pairs={{0,8},{8,0},{16,24},{24,16},{1,9},{9,1},{17,25},{25,17},{2,10},{10... | collective-permute-start | bytes 2555912 | tf_op jit(solution)/shard_map/ppermute | solution.py:20
  171.5 59.3 %collective-permute-start.10 = (bf16[512,1664]{1,0:T(8,128)(2,1)S(1)}, bf16[512,1664]{1,0:T(8,128)(2,1)S(1)}, u32[]{:S(2)}, u32[]{:S(2)}) collective-permute-start(bf16[512,1664]{1,0:T(8,128)(2,1)S(1)} %copy-done.9), channel_id=1, source_target_pairs={{0,1},{1,0},{2,3},{3,2},{4,5},{5,4},{6,7},{7,6},{8,9},{9,8},{10,11... | collective-permute-start | bytes 5111816 | tf_op jit(solution)/shard_map/ppermute | solution.py:20
  171.5 58.6 %collective-permute-start.14 = (bf16[512,1664]{1,0:T(8,128)(2,1)S(1)}, bf16[512,1664]{1,0:T(8,128)(2,1)}, u32[]{:S(2)}, u32[]{:S(2)}) collective-permute-start(bf16[512,1664]{1,0:T(8,128)(2,1)S(1)} %copy-done.9), channel_id=1, source_target_pairs={{0,2},{1,3},{2,0},{3,1},{4,6},{5,7},{6,4},{7,5},{8,10},{9,11},{10,... | collective-permute-start | bytes 5111816 | tf_op jit(solution)/shard_map/ppermute | solution.py:20
  205.0 28.3 %collective-permute-start.18 = (bf16[512,1664]{1,0:T(8,128)(2,1)}, bf16[512,1664]{1,0:T(8,128)(2,1)}, u32[]{:S(2)}, u32[]{:S(2)}) collective-permute-start(bf16[512,1664]{1,0:T(8,128)(2,1)} %collective-permute-done.11.refs_4_), channel_id=1, source_target_pairs={{0,1},{1,0},{2,3},{3,2},{4,5},{5,4},{6,7},{7,6},{8,9},{9,8},{10,11... | collective-permute-start | bytes 5111816 | tf_op jit(solution)/shard_map/ppermute | solution.py:20
  230.1 6.9 %collective-permute-start.19 = (bf16[512,1664]{1,0:T(8,128)(2,1)}, bf16[512,1664]{1,0:T(8,128)(2,1)}, u32[]{:S(2)}, u32[]{:S(2)}) collective-permute-start(bf16[512,1664]{1,0:T(8,128)(2,1)} %collective-permute-done.14.refs_5_), channel_id=1, source_target_pairs={{0,1},{1,0},{2,3},{3,2},{4,5},{5,4},{6,7},{7,6},{8,9},{9,8},{10,11... | collective-permute-start | bytes 5111816 | tf_op jit(solution)/shard_map/ppermute | solution.py:20
  230.1 20.8 %collective-permute-start.21 = (bf16[512,1664]{1,0:T(8,128)(2,1)S(1)}, bf16[512,1664]{1,0:T(8,128)(2,1)}, u32[]{:S(2)}, u32[]{:S(2)}) collective-permute-start(bf16[512,1664]{1,0:T(8,128)(2,1)S(1)} %get-tuple-element.140.refs_0_), channel_id=1, source_target_pairs={{0,1},{1,0},{2,3},{3,2},{4,5},{5,4},{6,7},{7,6},{8,9},{9,8},{10,11... | collective-permute-start | bytes 5111816 | tf_op jit(solution)/shard_map/ppermute | solution.py:20
  230.7 20.7 %collective-permute-start.22 = (bf16[512,1664]{1,0:T(8,128)(2,1)S(1)}, bf16[512,1664]{1,0:T(8,128)(2,1)}, u32[]{:S(2)}, u32[]{:S(2)}) collective-permute-start(bf16[512,1664]{1,0:T(8,128)(2,1)S(1)} %get-tuple-element.77.refs_1_), channel_id=1, source_target_pairs={{0,1},{1,0},{2,3},{3,2},{4,5},{5,4},{6,7},{7,6},{8,9},{9,8},{10,11... | collective-permute-start | bytes 5111816 | tf_op jit(solution)/shard_map/ppermute | solution.py:20
  233.1 18.9 %collective-permute-start.23 = (bf16[512,1664]{1,0:T(8,128)(2,1)}, bf16[512,1664]{1,0:T(8,128)(2,1)}, u32[]{:S(2)}, u32[]{:S(2)}) collective-permute-start(bf16[512,1664]{1,0:T(8,128)(2,1)} %collective-permute-done.2.refs_4_), channel_id=1, source_target_pairs={{0,1},{1,0},{2,3},{3,2},{4,5},{5,4},{6,7},{7,6},{8,9},{9,8},{10,11... | collective-permute-start | bytes 5111816 | tf_op jit(solution)/shard_map/ppermute | solution.py:20
  233.3 20.1 %collective-permute-start.24 = (bf16[512,1664]{1,0:T(8,128)(2,1)}, bf16[512,1664]{1,0:T(8,128)(2,1)S(1)}, u32[]{:S(2)}, u32[]{:S(2)}) collective-permute-start(bf16[512,1664]{1,0:T(8,128)(2,1)} %collective-permute-done.5.refs_5_), channel_id=1, source_target_pairs={{0,1},{1,0},{2,3},{3,2},{4,5},{5,4},{6,7},{7,6},{8,9},{9,8},{10,11... | collective-permute-start | bytes 5111816 | tf_op jit(solution)/shard_map/ppermute | solution.py:20
  250.4 42.8 %collective-permute-start.26 = (bf16[1024,512]{1,0:T(8,128)(2,1)}, bf16[1024,512]{1,0:T(8,128)(2,1)}, u32[]{:S(2)}, u32[]{:S(2)}) collective-permute-start(bf16[1024,512]{1,0:T(8,128)(2,1)} %shard_map.116), channel_id=1, source_target_pairs={{0,16},{8,24},{16,0},{24,8},{1,17},{9,25},{17,1},{25,9},{2,18},{10... | collective-permute-start | bytes 3145736 | tf_op jit(solution)/shard_map/ppermute | solution.py:20
  250.9 40.1 %collective-permute-start.25 = (bf16[2,1664,128]{2,1,0:T(8,128)(2,1)}, bf16[2,1664,128]{2,1,0:T(8,128)(2,1)S(1)}, u32[]{:S(2)}, u32[]{:S(2)}) collective-permute-start(bf16[2,1664,128]{2,1,0:T(8,128)(2,1)} %get-tuple-element.95), channel_id=1, source_target_pairs={{0,4},{1,5},{2,6},{3,7},{4,0},{5,1},{6,2},{7,3},{8,12},{9,13},{10,... | collective-permute-start | bytes 2555912 | tf_op jit(solution)/shard_map/ppermute | solution.py:20
  251.4 39.6 %collective-permute-start.30 = (bf16[2,1664,128]{2,1,0:T(8,128)(2,1)S(1)}, bf16[2,1664,128]{2,1,0:T(8,128)(2,1)S(1)}, u32[]{:S(2)}, u32[]{:S(2)}) collective-permute-start(bf16[2,1664,128]{2,1,0:T(8,128)(2,1)S(1)} %copy-done.16), channel_id=1, source_target_pairs={{0,8},{8,0},{16,24},{24,16},{1,9},{9,1},{17,25},{25,17},{2,10},{10... | collective-permute-start | bytes 2555912 | tf_op jit(solution)/shard_map/ppermute | solution.py:20
  252.1 39.5 %collective-permute-start.28 = (bf16[2,1664,128]{2,1,0:T(8,128)(2,1)S(1)}, bf16[2,1664,128]{2,1,0:T(8,128)(2,1)S(1)}, u32[]{:S(2)}, u32[]{:S(2)}) collective-permute-start(bf16[2,1664,128]{2,1,0:T(8,128)(2,1)S(1)} %copy-done.6), channel_id=1, source_target_pairs={{0,8},{8,0},{16,24},{24,16},{1,9},{9,1},{17,25},{25,17},{2,10},{10... | collective-permute-start | bytes 2555912 | tf_op jit(solution)/shard_map/ppermute | solution.py:20
  291.0 22.0 %collective-permute-start.31 = (bf16[2,1664,128]{2,1,0:T(8,128)(2,1)S(1)}, bf16[2,1664,128]{2,1,0:T(8,128)(2,1)}, u32[]{:S(2)}, u32[]{:S(2)}) collective-permute-start(bf16[2,1664,128]{2,1,0:T(8,128)(2,1)S(1)} %collective-permute-done.25.refs_11_), channel_id=1, source_target_pairs={{0,8},{8,0},{16,24},{24,16},{1,9},{9,1},{17,25},{25,17},{2,10},{10... | collective-permute-start | bytes 2555912 | tf_op jit(solution)/shard_map/ppermute | solution.py:20
  291.5 38.8 %collective-permute-start.29 = (bf16[2,1664,128]{2,1,0:T(8,128)(2,1)}, bf16[2,1664,128]{2,1,0:T(8,128)(2,1)}, u32[]{:S(2)}, u32[]{:S(2)}) collective-permute-start(bf16[2,1664,128]{2,1,0:T(8,128)(2,1)} %get-tuple-element.103.refs_9_), channel_id=1, source_target_pairs={{0,8},{8,0},{16,24},{24,16},{1,9},{9,1},{17,25},{25,17},{2,10},{10... | collective-permute-start | bytes 2555912 | tf_op jit(solution)/shard_map/ppermute | solution.py:20
  296.2 48.9 %collective-permute-start.27 = (bf16[1024,256]{1,0:T(8,128)(2,1)}, bf16[1024,256]{1,0:T(8,128)(2,1)}, u32[]{:S(2)}, u32[]{:S(2)}) collective-permute-start(bf16[1024,256]{1,0:T(8,128)(2,1)} %slice.85), channel_id=1, source_target_pairs={{0,4},{1,5},{2,6},{3,7},{4,0},{5,1},{6,2},{7,3},{8,12},{9,13},{10,... | collective-permute-start | bytes 1572872 | tf_op jit(solution)/shard_map/ppermute | solution.py:20
  343.6 24.5 %collective-permute-start.32 = (bf16[1024,512]{1,0:T(8,128)(2,1)}, bf16[1024,512]{1,0:T(8,128)(2,1)S(1)}, u32[]{:S(2)}, u32[]{:S(2)}) collective-permute-start(bf16[1024,512]{1,0:T(8,128)(2,1)} %shard_map.118), channel_id=1, source_target_pairs={{0,16},{8,24},{16,0},{24,8},{1,17},{9,25},{17,1},{25,9},{2,18},{10... | collective-permute-start | bytes 3145736 | tf_op jit(solution)/shard_map/ppermute | solution.py:20
  359.9 26.4 %collective-permute-start.33 = (bf16[32,64,256]{2,1,0:T(8,128)(2,1)}, bf16[32,64,256]{2,1,0:T(8,128)(2,1)S(1)}, u32[]{:S(2)}, u32[]{:S(2)}) collective-permute-start(bf16[32,64,256]{2,1,0:T(8,128)(2,1)} %get-tuple-element.109), channel_id=1, source_target_pairs={{0,8},{8,0},{16,24},{24,16},{1,9},{9,1},{17,25},{25,17},{2,10},{10... | collective-permute-start | bytes 3145736 | tf_op jit(solution)/shard_map/ppermute | solution.py:20
  360.5 62.8 %collective-permute-start.35 = (bf16[32,64,256]{2,1,0:T(8,128)(2,1)}, bf16[32,64,256]{2,1,0:T(8,128)(2,1)S(1)}, u32[]{:S(2)}, u32[]{:S(2)}) collective-permute-start(bf16[32,64,256]{2,1,0:T(8,128)(2,1)} %get-tuple-element.108), channel_id=1, source_target_pairs={{0,8},{8,0},{16,24},{24,16},{1,9},{9,1},{17,25},{25,17},{2,10},{10... | collective-permute-start | bytes 3145736 | tf_op jit(solution)/shard_map/ppermute | solution.py:20
  368.1 56.5 %collective-permute-start.36 = (bf16[32,64,256]{2,1,0:T(8,128)(2,1)}, bf16[32,64,256]{2,1,0:T(8,128)(2,1)S(1)}, u32[]{:S(2)}, u32[]{:S(2)}) collective-permute-start(bf16[32,64,256]{2,1,0:T(8,128)(2,1)} %get-tuple-element.115), channel_id=1, source_target_pairs={{0,16},{8,24},{16,0},{24,8},{1,17},{9,25},{17,1},{25,9},{2,18},{10... | collective-permute-start | bytes 3145736 | tf_op jit(solution)/shard_map/ppermute | solution.py:20
  388.3 21.4 %collective-permute-start.34 = (bf16[1024,256]{1,0:T(8,128)(2,1)S(1)}, bf16[1024,256]{1,0:T(8,128)(2,1)S(1)}, u32[]{:S(2)}, u32[]{:S(2)}) collective-permute-start(bf16[1024,256]{1,0:T(8,128)(2,1)S(1)} %slice.84), channel_id=1, source_target_pairs={{0,4},{1,5},{2,6},{3,7},{4,0},{5,1},{6,2},{7,3},{8,12},{9,13},{10,... | collective-permute-start | bytes 1572872 | tf_op jit(solution)/shard_map/ppermute | solution.py:20
  388.4 39.4 %collective-permute-start.38 = (bf16[32,64,256]{2,1,0:T(8,128)(2,1)}, bf16[32,64,256]{2,1,0:T(8,128)(2,1)S(1)}, u32[]{:S(2)}, u32[]{:S(2)}) collective-permute-start(bf16[32,64,256]{2,1,0:T(8,128)(2,1)} %get-tuple-element.114), channel_id=1, source_target_pairs={{0,16},{8,24},{16,0},{24,8},{1,17},{9,25},{17,1},{25,9},{2,18},{10... | collective-permute-start | bytes 3145736 | tf_op jit(solution)/shard_map/ppermute | solution.py:20
  424.3 26.2 %collective-permute-start.41 = (bf16[32,64,256]{2,1,0:T(8,128)(2,1)}, bf16[32,64,256]{2,1,0:T(8,128)(2,1)S(1)}, u32[]{:S(2)}, u32[]{:S(2)}) collective-permute-start(bf16[32,64,256]{2,1,0:T(8,128)(2,1)} %get-tuple-element.131), channel_id=1, source_target_pairs={{0,8},{8,0},{16,24},{24,16},{1,9},{9,1},{17,25},{25,17},{2,10},{10... | collective-permute-start | bytes 3145736 | tf_op jit(solution)/shard_map/ppermute | solution.py:20
  426.0 46.2 %collective-permute-start.39 = (bf16[32,64,256]{2,1,0:T(8,128)(2,1)}, bf16[32,64,256]{2,1,0:T(8,128)(2,1)}, u32[]{:S(2)}, u32[]{:S(2)}) collective-permute-start(bf16[32,64,256]{2,1,0:T(8,128)(2,1)} %add_convert_fusion.7), channel_id=1, source_target_pairs={{0,8},{8,0},{16,24},{24,16},{1,9},{9,1},{17,25},{25,17},{2,10},{10... | collective-permute-start | bytes 3145736 | tf_op jit(solution)/shard_map/ppermute | solution.py:20
  427.8 44.7 %collective-permute-start.42 = (bf16[32,64,256]{2,1,0:T(8,128)(2,1)}, bf16[32,64,256]{2,1,0:T(8,128)(2,1)S(1)}, u32[]{:S(2)}, u32[]{:S(2)}) collective-permute-start(bf16[32,64,256]{2,1,0:T(8,128)(2,1)} %get-tuple-element.132), channel_id=1, source_target_pairs={{0,16},{8,24},{16,0},{24,8},{1,17},{9,25},{17,1},{25,9},{2,18},{10... | collective-permute-start | bytes 3145736 | tf_op jit(solution)/shard_map/ppermute | solution.py:20
  429.2 46.8 %collective-permute-start.37 = (bf16[32,64,256]{2,1,0:T(8,128)(2,1)S(1)}, bf16[32,64,256]{2,1,0:T(8,128)(2,1)}, u32[]{:S(2)}, u32[]{:S(2)}) collective-permute-start(bf16[32,64,256]{2,1,0:T(8,128)(2,1)S(1)} %add_convert_fusion.10), channel_id=1, source_target_pairs={{0,16},{8,24},{16,0},{24,8},{1,17},{9,25},{17,1},{25,9},{2,18},{10... | collective-permute-start | bytes 3145736 | tf_op jit(solution)/shard_map/ppermute | solution.py:20
  445.6 26.6 %copy-start.41 = (bf16[32,64,256]{2,1,0:T(8,128)(2,1)S(1)}, bf16[32,64,256]{2,1,0:T(8,128)(2,1)}, u32[]{:S(2)}) copy-start(bf16[32,64,256]{2,1,0:T(8,128)(2,1)} %get-tuple-element.129) | copy-start | bytes 3145732
  445.7 30.3 %copy-start.40 = (bf16[32,64,256]{2,1,0:T(8,128)(2,1)S(1)}, bf16[32,64,256]{2,1,0:T(8,128)(2,1)}, u32[]{:S(2)}) copy-start(bf16[32,64,256]{2,1,0:T(8,128)(2,1)} %get-tuple-element.135) | copy-start | bytes 3145732
  445.7 30.8 %copy-start.24 = (bf16[32,64,256]{2,1,0:T(8,128)(2,1)S(1)}, bf16[32,64,256]{2,1,0:T(8,128)(2,1)}, u32[]{:S(2)}) copy-start(bf16[32,64,256]{2,1,0:T(8,128)(2,1)} %get-tuple-element.136) | copy-start | bytes 3145732
  452.2 24.8 %copy-start.27 = (bf16[32,64,256]{2,1,0:T(8,128)(2,1)S(1)}, bf16[32,64,256]{2,1,0:T(8,128)(2,1)}, u32[]{:S(2)}) copy-start(bf16[32,64,256]{2,1,0:T(8,128)(2,1)} %copy-done.26) | copy-start | bytes 3145732
  452.2 24.8 %copy-start.31 = (bf16[32,64,256]{2,1,0:T(8,128)(2,1)S(1)}, bf16[32,64,256]{2,1,0:T(8,128)(2,1)}, u32[]{:S(2)}) copy-start(bf16[32,64,256]{2,1,0:T(8,128)(2,1)} %get-tuple-element.117) | copy-start | bytes 3145732
  472.2 26.1 %collective-permute-start.40 = (bf16[32,64,256]{2,1,0:T(8,128)(2,1)S(1)}, bf16[32,64,256]{2,1,0:T(8,128)(2,1)S(1)}, u32[]{:S(2)}, u32[]{:S(2)}) collective-permute-start(bf16[32,64,256]{2,1,0:T(8,128)(2,1)S(1)} %copy-done.41), channel_id=1, source_target_pairs={{0,8},{8,0},{16,24},{24,16},{1,9},{9,1},{17,25},{25,17},{2,10},{10... | collective-permute-start | bytes 3145736 | tf_op jit(solution)/shard_map/ppermute | solution.py:20
  472.5 26.1 %collective-permute-start.43 = (bf16[32,64,256]{2,1,0:T(8,128)(2,1)S(1)}, bf16[32,64,256]{2,1,0:T(8,128)(2,1)S(1)}, u32[]{:S(2)}, u32[]{:S(2)}) collective-permute-start(bf16[32,64,256]{2,1,0:T(8,128)(2,1)S(1)} %add_convert_fusion.4), channel_id=1, source_target_pairs={{0,16},{8,24},{16,0},{24,8},{1,17},{9,25},{17,1},{25,9},{2,18},{10... | collective-permute-start | bytes 3145736 | tf_op jit(solution)/shard_map/ppermute | solution.py:20
  476.0 43.9 %collective-permute-start.44 = (bf16[32,64,256]{2,1,0:T(8,128)(2,1)S(1)}, bf16[32,64,256]{2,1,0:T(8,128)(2,1)S(1)}, u32[]{:S(2)}, u32[]{:S(2)}) collective-permute-start(bf16[32,64,256]{2,1,0:T(8,128)(2,1)S(1)} %copy-done.40), channel_id=1, source_target_pairs={{0,16},{8,24},{16,0},{24,8},{1,17},{9,25},{17,1},{25,9},{2,18},{10... | collective-permute-start | bytes 3145736 | tf_op jit(solution)/shard_map/ppermute | solution.py:20
  476.9 43.1 %collective-permute-start.45 = (bf16[32,64,256]{2,1,0:T(8,128)(2,1)S(1)}, bf16[32,64,256]{2,1,0:T(8,128)(2,1)S(1)}, u32[]{:S(2)}, u32[]{:S(2)}) collective-permute-start(bf16[32,64,256]{2,1,0:T(8,128)(2,1)S(1)} %add_convert_fusion.1), channel_id=1, source_target_pairs={{0,8},{8,0},{16,24},{24,16},{1,9},{9,1},{17,25},{25,17},{2,10},{10... | collective-permute-start | bytes 3145736 | tf_op jit(solution)/shard_map/ppermute | solution.py:20
  499.2 21.5 %copy-start.13 = (bf16[32,64,256]{2,1,0:T(8,128)(2,1)}, bf16[32,64,256]{2,1,0:T(8,128)(2,1)S(1)}, u32[]{:S(2)}) copy-start(bf16[32,64,256]{2,1,0:T(8,128)(2,1)S(1)} %add_convert_fusion.3) | copy-start | bytes 3145732
  499.2 20.8 %copy-start.32 = (bf16[32,64,256]{2,1,0:T(8,128)(2,1)S(1)}, bf16[32,64,256]{2,1,0:T(8,128)(2,1)}, u32[]{:S(2)}) copy-start(bf16[32,64,256]{2,1,0:T(8,128)(2,1)} %get-tuple-element.134) | copy-start | bytes 3145732
  524.2 3.8 collective-permute-start.46
  528.0 4.3 collective-permute-start.47
  532.4 4.6 collective-permute-start.48
  537.2 3.7 collective-permute-start.49
  540.9 1.2 collective-permute-start.50
  (29 other events, 227.6 us)

commit v8 on v7

--- a/solution.py
+++ b/solution.py
@@ -273,14 +273,17 @@
         return [found[f] for f in range(top_row)]
 
     row_links = {bit: Link(2) for bit in bits_below(top_row)}
-    gathered = []
-
-    def gather_rows(pair):
+    gathered, stays = [], []
+
+    def rows_of(pair):
         found = {0: pair}
         for bit in bits_below(top_row):
             for f, parts in list(found.items()):
                 found[f ^ bit] = [row_links[bit].swap(p, "row", bit) for p in parts]
-        gathered.append([found[f] for f in range(top_row)])
+        return [found[f] for f in range(top_row)]
+
+    def gather_rows(pair):
+        gathered.append(rows_of(pair))
 
     def from_row(j, side):
         return gathered[j][-1][side]
@@ -304,6 +307,7 @@
                 turn_next(near_second, came[0][1], from_row(0, 0), *panels)
             arrived.append(cross(crossing[j], crossed_second, *panels))
         leave = far(j, *due)
+        stays.append(rows_of([after(came[j][0], from_row(1, 1))]))
     while len(panels) < GROUPS:
         turn_next(near_second, *panels)
 
@@ -311,13 +315,14 @@
     near_mask = lax.dynamic_slice_in_dim(mask_near, c * near_blocks, near_blocks, 0)
     near_mask = jnp.repeat(jnp.repeat(near_mask, rb, 0), ab, 1).astype(jnp.bfloat16)
     near = after(three_near, near_crossed_first, came[1][1]) * near_mask[:, None, :]
-    green = lax.dynamic_slice_in_dim(green_function, r * share, share, 0)
+    early = [blocks[-1][0] for blocks in stays]
+    green = lax.dynamic_slice_in_dim(after(green_function, *early[:1]), r * share, share, 0)
     dressed = jnp.einsum("qns,ls->nlq", near, green, preferred_element_type=jnp.float32).astype(jnp.bfloat16)
 
     near_crossed_second = swap(
         after(crossed_second, near_crossed_first, arrived[-1], came[1][1], from_row(0, 1)), "col", low
     )
-    near_crossed_second = after(near_crossed_second, dressed, *panels, *[pair[1] for pair in came[2:3]])
+    near_crossed_second = after(near_crossed_second, dressed, *panels, *early, *[pair[1] for pair in came[2:3]])
 
     def gather_low(found):
         link = Link(1)
@@ -348,7 +353,8 @@
 
     def gather_next(upto, ready):
         for i in range(len(gathered), min(upto, chunks)):
-            gather_rows([after(part, ready) for part in came[i]])
+            later = rows_of([after(came[i][1], ready)])
+            gathered.append([a + b for a, b in zip(stays[i - 2], later)])
 
     gather_next(pair + 1, pieces_crossed[-1][-1])
     away = product(pieces_crossed, sources_of(0), after(order, leave), per_block, jnp.bfloat16)
@@ -388,11 +394,12 @@
         halves = [left[h][1][0] for h in range(2)]
         contracted_chunks.append(halves)
 
-    for j, halves in enumerate(contracted_chunks):
+    for j, (front, back) in enumerate(contracted_chunks):
         beside = dressed[:, :, j * wide : (j + 1) * wide]
-        energy = energy - jnp.concatenate(
-            [jnp.einsum("mlq,nlq->mn", half, beside, preferred_element_type=jnp.float32) for half in halves]
-        )
+        of_back = jnp.einsum("mlq,nlq->mn", back, beside, preferred_element_type=jnp.float32)
+        of_front = jnp.einsum("mlq,nlq->mn", after(front, of_back), beside, preferred_element_type=jnp.float32)
+        energy = energy - jnp.concatenate([of_front, of_back])
+
     contracted = jnp.transpose(jnp.concatenate([jnp.concatenate(halves) for halves in contracted_chunks], axis=2), (2, 0, 1))
     energy = scatter_sum(after(scatter_sum(energy, "row"), contracted).T, "col").T
     return jnp.concatenate(screened_chunks, axis=1), contracted, energy

time: 547 us -> 524 us (0.958)
  waiting for transfers between devices: 239 us -> 218 us
    ppermute x51, waiting for transfers between devices: 239 us -> 218 us  [swap(): return lax.ppermute(value, axis, [(i, i ^ bit) for i in range(size)])]
  transfers between devices with their start and end apart: 51 -> 51, of which waited for: 25 -> 19; matrix products, arithmetic and copies ran while one was open for 16% -> 17% of each run, Pallas kernels for 27% -> 28%
where the time goes in v8:
time: 524 us; the launch traced here: 520 us
  waiting for transfers between devices  218 us (42%)
  Pallas kernels  147 us (28%)
  starting transfers between devices  51.1 us (10%)
  other arithmetic  42.9 us (8%)
  matrix products  33 us (6%)
  local copies, waits for them, and re-layouts  26.4 us (5%)
    ppermute x51, waiting for transfers between devices, swap(): return lax.ppermute(value, axis, [(i, i ^ bit) for i in range(size)])  218 us
    pallas_call x4, Pallas kernels, product(): pl.pallas_call(functools.partial(product_kernel, count, parts, per_block)...  53.6 us
    ppermute x51, starting transfers between devices, swap(): return lax.ppermute(value, axis, [(i, i ^ bit) for i in range(size)])  51.1 us
    pallas_call x4, Pallas kernels, contract(): pl.pallas_call(functools.partial(contract_kernel, rb, ab), in_specs=[in_s...  50.3 us
    pallas_call x4, Pallas kernels, turn(): pl.pallas_call(turn_kernel, grid=(rows // wide, tile // tall), in_specs=[...  42.9 us
    dot_general x1, matrix products, per_device(): jnp.einsum('qns,ls->nlq', near, green, preferred_element_type=jnp.float32)  19.1 us
    mul x1, other arithmetic, per_device(): after(three_near, near_crossed_first, came[1][1]) * near_mask[:, None, :]  13.8 us
  transfers between devices with their start and end apart: 51, of which 19 were waited for; matrix products, arithmetic and copies ran while one was open for 17% of the time, Pallas kernels for 28%

profile of v8, /device:TPU:0, one launch (start us, length us, event | category | flops | bytes accessed | tf_op | source)
XLA Modules:
  0.0 520.2 jit_solution(2199990612436233307)
XLA Ops:
  0.7 5.3 %fusion.41 = (bf16[512,1664]{1,0:T(8,128)(2,1)S(1)}, bf16[512,1664]{1,0:T(8,128)(2,1)S(1)}, bf16[512,1664]{1,0:T(8,128)(2,1)}, bf16[512,1664]{1,0:T(8,128)(2,1)}) fusion(bf16[1024,3328]{1,0:T(8,128)(2,1)} %param.9, s32[]{:T(128)S(6)} %add.207, s32[]{:T(128)S(6)} %select_n.156, s32[]{:T(128)S(6)} %select_n.155), kind=kLoop, calls=%fused_computation.86 | loop fusion | bytes 13631500 | tf_op jit(solution)/shard_map/split | solution.py:231
  6.0 3.0 collective-permute-start.2
  9.0 5.2 %dynamic-slice_bitcast_fusion = (bf16[2,1664,512]{2,1,0:T(8,128)(2,1)}, bf16[2,1664,512]{2,1,0:T(8,128)(2,1)S(1)}) fusion(bf16[2,2,1664,512]{3,2,1,0:T(8,128)(2,1)} %bitcast.61, s32[]{:T(128)S(6)} %select_n.157, s32[]{:T(128)S(6)} %select_n.154), kind=kLoop, calls=%fused_computation.5 | loop fusion | bytes 13631496 | tf_op jit(solution)/shard_map/jit(dynamic_index_in_dim)/squeeze | solution.py:234
  14.2 1.8 fusion.43
  16.0 1.5 collective-permute-start
  17.5 19.0 %collective-permute-done = bf16[2,1664,128]{2,1,0:T(8,128)(2,1)} collective-permute-done((bf16[2,1664,128]{2,1,0:T(8,128)(2,1)S(1)}, bf16[2,1664,128]{2,1,0:T(8,128)(2,1)}, u32[]{:S(2)}, u32[]{:S(2)}) %collective-permute-start) | collective-permute-done | bytes 852000 | tf_op jit(solution)/shard_map/ppermute | solution.py:20
  38.0 8.3 %collective-permute-done.2.refs_4_ = bf16[512,1664]{1,0:T(8,128)(2,1)} collective-permute-done((bf16[512,1664]{1,0:T(8,128)(2,1)S(1)}, bf16[512,1664]{1,0:T(8,128)(2,1)}, u32[]{:S(2)}, u32[]{:S(2)}) %collective-permute-start.2) | collective-permute-done | bytes 1703968 | tf_op jit(solution)/shard_map/ppermute | solution.py:20
  46.3 1.7 collective-permute-start.5
  48.0 1.5 broadcast_select_fusion.5
  49.6 2.7 collective-permute-start.6
  55.2 10.9 %shard_map.112.refs_0_ = bf16[64,256,256]{2,1,0:T(8,128)(2,1)} custom-call(bf16[1024,64,256]{2,1,0:T(8,128)(2,1)} %panel_ref.3), custom_call_target="tpu_custom_call" | custom-call | bytes 33554432 | tf_op jit(solution)/shard_map/pallas_call | solution.py:122
  66.1 10.8 %collective-permute-done.1.refs_0_ = bf16[512,1664]{1,0:T(8,128)(2,1)} collective-permute-done((bf16[512,1664]{1,0:T(8,128)(2,1)}, bf16[512,1664]{1,0:T(8,128)(2,1)}, u32[]{:S(2)}, u32[]{:S(2)}) %collective-permute-start.1) | collective-permute-done | bytes 1703968 | tf_op jit(solution)/shard_map/ppermute | solution.py:20
  76.9 1.5 collective-permute-start.3
  78.4 23.4 %collective-permute-done.6.refs_10_ = bf16[2,1664,128]{2,1,0:T(8,128)(2,1)S(1)} collective-permute-done((bf16[2,1664,128]{2,1,0:T(8,128)(2,1)S(1)}, bf16[2,1664,128]{2,1,0:T(8,128)(2,1)S(1)}, u32[]{:S(2)}, u32[]{:S(2)}) %collective-permute-start.6) | collective-permute-done | bytes 852000 | tf_op jit(solution)/shard_map/ppermute | solution.py:20
  103.4 2.5 broadcast_select_fusion.2
  105.9 3.4 collective-permute-start.12
  109.4 10.8 %shard_map.113.refs_1_ = bf16[64,256,256]{2,1,0:T(8,128)(2,1)} custom-call(bf16[1024,64,256]{2,1,0:T(8,128)(2,1)} %panel_ref.3), custom_call_target="tpu_custom_call" | custom-call | bytes 33554432 | tf_op jit(solution)/shard_map/pallas_call | solution.py:122
  120.2 1.5 collective-permute-start.15
  122.3 22.3 %collective-permute-done.12.refs_11_ = bf16[2,1664,128]{2,1,0:T(8,128)(2,1)} collective-permute-done((bf16[2,1664,128]{2,1,0:T(8,128)(2,1)S(1)}, bf16[2,1664,128]{2,1,0:T(8,128)(2,1)}, u32[]{:S(2)}, u32[]{:S(2)}) %collective-permute-start.12) | collective-permute-done | bytes 852000 | tf_op jit(solution)/shard_map/ppermute | solution.py:20
  145.1 10.6 %shard_map.114.refs_2_ = bf16[64,256,256]{2,1,0:T(8,128)(2,1)} custom-call(bf16[1024,64,256]{2,1,0:T(8,128)(2,1)} %panel_ref.3), custom_call_target="tpu_custom_call" | custom-call | bytes 33554432 | tf_op jit(solution)/shard_map/pallas_call | solution.py:122
  155.8 10.6 %shard_map.115.refs_3_ = bf16[64,256,256]{2,1,0:T(8,128)(2,1)} custom-call(bf16[1024,64,256]{2,1,0:T(8,128)(2,1)} %panel_ref.3), custom_call_target="tpu_custom_call" | custom-call | bytes 33554432 | tf_op jit(solution)/shard_map/pallas_call | solution.py:122
  166.4 1.5 collective-permute-start.8
  170.2 1.8 copy.27
  172.0 1.6 broadcast_select_fusion
  175.4 9.6 %collective-permute-done.8 = bf16[2,1664,128]{2,1,0:T(8,128)(2,1)} collective-permute-done((bf16[2,1664,128]{2,1,0:T(8,128)(2,1)}, bf16[2,1664,128]{2,1,0:T(8,128)(2,1)}, u32[]{:S(2)}, u32[]{:S(2)}) %collective-permute-start.8) | collective-permute-done | bytes 852000 | tf_op jit(solution)/shard_map/ppermute | solution.py:20
  185.7 13.8 %broadcast_multiply_fusion = bf16[512,64,256]{2,1,0:T(8,128)(2,1)} fusion(bf16[512,64,256]{2,1,0:T(8,128)(2,1)} %param.12, bf16[512,256]{1,0:T(8,128)(2,1)S(1)} %copy-done.23), kind=kLoop, calls=%fused_computation.2 | loop fusion | flops 8388608 | bytes 33816576 | tf_op jit(solution)/shard_map/mul | solution.py:317
  199.5 2.4 broadcast_select_fusion.1
  203.4 19.1 %convert_bitcast_fusion = bf16[64,64,512]{2,1,0:T(8,128)(2,1)} fusion(bf16[512,64,256]{2,1,0:T(8,128)(2,1)} %broadcast_multiply_fusion, bf16[256,256]{1,0:T(8,128)(2,1)S(1)} %copy-done, s32[]{:T(128)S(6)} %select_n.164), kind=kOutput, calls=%fused_computation.4 | convolution fusion | flops 1075838976 | bytes 21004292 | tf_op jit(solution)/shard_map/qns,ls->nlq/dot_general | solution.py:320
  223.6 15.5 %collective-permute-done.14.refs_5_ = bf16[512,1664]{1,0:T(8,128)(2,1)S(1)} collective-permute-done((bf16[512,1664]{1,0:T(8,128)(2,1)}, bf16[512,1664]{1,0:T(8,128)(2,1)S(1)}, u32[]{:S(2)}, u32[]{:S(2)}) %collective-permute-start.14) | collective-permute-done | bytes 1703968 | tf_op jit(solution)/shard_map/ppermute | solution.py:20
  239.1 2.8 collective-permute-start.27
  246.9 13.2 %shard_map.116 = bf16[1024,512]{1,0:T(8,128)(2,1)} custom-call(s32[4]{0:T(128)} %fusion.40.order_ref, bf16[512,1664]{1,0:T(8,128)(2,1)} %collective-permute-done.1.refs_0_, bf16[512,1664]{1,0:T(8,128)(2,1)} %collective-permute-done.3.refs_1_, bf16[512,1664]{1,0:T(8,128)(2,1)} %copy-done.10, bf16[512,1664]{1,0:T(8,128)(2,1)} %copy-done.11, ...), custom_call_target="tpu_custom_call" | custom-call | tf_op jit(solution)/shard_map/pallas_call | solution.py:97
  260.1 20.0 %collective-permute-done.27.refs_11_ = bf16[2,1664,128]{2,1,0:T(8,128)(2,1)} collective-permute-done((bf16[2,1664,128]{2,1,0:T(8,128)(2,1)}, bf16[2,1664,128]{2,1,0:T(8,128)(2,1)}, u32[]{:S(2)}, u32[]{:S(2)}) %collective-permute-start.27) | collective-permute-done | bytes 852000 | tf_op jit(solution)/shard_map/ppermute | solution.py:20
  280.1 1.5 collective-permute-start.28
  283.6 13.6 %shard_map.117 = f32[1024,512]{1,0:T(8,128)} custom-call(s32[4]{0:T(128)} %fusion.40.order_ref, bf16[512,1664]{1,0:T(8,128)(2,1)} %copy-done.3, bf16[512,1664]{1,0:T(8,128)(2,1)} %copy-done.2, bf16[512,1664]{1,0:T(8,128)(2,1)} %collective-permute-done.23.refs_2_, bf16[512,1664]{1,0:T(8,128)(2,1)} %collective-permute-done.24.refs_3_, ...), custom_call_target="tpu_custom_call" | custom-call | tf_op jit(solution)/shard_map/pallas_call | solution.py:97
  297.3 7.9 %collective-permute-done.28 = bf16[1024,512]{1,0:T(8,128)(2,1)S(1)} collective-permute-done((bf16[1024,512]{1,0:T(8,128)(2,1)}, bf16[1024,512]{1,0:T(8,128)(2,1)S(1)}, u32[]{:S(2)}, u32[]{:S(2)}) %collective-permute-start.28) | collective-permute-done | bytes 1048608 | tf_op jit(solution)/shard_map/ppermute | solution.py:20
  305.2 1.9 convert_add_fusion.1
  308.6 11.9 %collective-permute-done.30.refs_14_ = bf16[2,1664,128]{2,1,0:T(8,128)(2,1)} collective-permute-done((bf16[2,1664,128]{2,1,0:T(8,128)(2,1)}, bf16[2,1664,128]{2,1,0:T(8,128)(2,1)}, u32[]{:S(2)}, u32[]{:S(2)}) %collective-permute-start.30) | collective-permute-done | bytes 852000 | tf_op jit(solution)/shard_map/ppermute | solution.py:20
  320.6 13.2 %shard_map.118 = bf16[1024,512]{1,0:T(8,128)(2,1)} custom-call(s32[4]{0:T(128)} %fusion.40.order_ref, bf16[512,1664]{1,0:T(8,128)(2,1)} %collective-permute-done.1.refs_0_, bf16[512,1664]{1,0:T(8,128)(2,1)} %collective-permute-done.3.refs_1_, bf16[512,1664]{1,0:T(8,128)(2,1)} %copy-done.10, bf16[512,1664]{1,0:T(8,128)(2,1)} %copy-done.11, ...), custom_call_target="tpu_custom_call" | custom-call | tf_op jit(solution)/shard_map/pallas_call | solution.py:97
  335.1 2.0 fusion.25.screened_ref
  337.2 12.5 %shard_map.119 = (bf16[32,64,256]{2,1,0:T(8,128)(2,1)}, bf16[32,64,256]{2,1,0:T(8,128)(2,1)}, bf16[32,64,256]{2,1,0:T(8,128)(2,1)}, bf16[32,64,256]{2,1,0:T(8,128)(2,1)}) custom-call(s32[2,2]{1,0:T(2,128)} %get-tuple-element.111.places_ref, s32[16,8]{1,0:T(8,128)} %copy.42.mask_ref, bf16[1024,256]{1,0:T(8,128)(2,1)} %fusion.25.screened_ref, ...), custom_call_target="tpu_custom_call" | custom-call | tf_op jit(solution)/shard_map/pallas_call | solution.py:184
  349.7 1.6 collective-permute-start.33
  351.3 6.4 %collective-permute-done.32 = bf16[1024,512]{1,0:T(8,128)(2,1)S(1)} collective-permute-done((bf16[1024,512]{1,0:T(8,128)(2,1)}, bf16[1024,512]{1,0:T(8,128)(2,1)S(1)}, u32[]{:S(2)}, u32[]{:S(2)}) %collective-permute-start.32) | collective-permute-done | bytes 1048608 | tf_op jit(solution)/shard_map/ppermute | solution.py:20
  358.3 1.6 collective-permute-start.35
  361.3 13.6 %shard_map.120 = f32[1024,512]{1,0:T(8,128)} custom-call(s32[4]{0:T(128)} %fusion.40.order_ref, bf16[512,1664]{1,0:T(8,128)(2,1)} %copy-done.3, bf16[512,1664]{1,0:T(8,128)(2,1)} %copy-done.2, bf16[512,1664]{1,0:T(8,128)(2,1)} %collective-permute-done.23.refs_2_, bf16[512,1664]{1,0:T(8,128)(2,1)} %collective-permute-done.24.refs_3_, ...), custom_call_target="tpu_custom_call" | custom-call | tf_op jit(solution)/shard_map/pallas_call | solution.py:97
  374.9 12.7 %shard_map.121 = (bf16[32,64,256]{2,1,0:T(8,128)(2,1)}, bf16[32,64,256]{2,1,0:T(8,128)(2,1)}, bf16[32,64,256]{2,1,0:T(8,128)(2,1)}, bf16[32,64,256]{2,1,0:T(8,128)(2,1)}) custom-call(s32[2,2]{1,0:T(2,128)} %get-tuple-element.120.places_ref, s32[16,8]{1,0:T(8,128)} %copy.42.mask_ref, bf16[1024,256]{1,0:T(8,128)(2,1)} %fusion.25.screened_ref, ...), custom_call_target="tpu_custom_call" | custom-call | tf_op jit(solution)/shard_map/pallas_call | solution.py:184
  391.1 19.9 %collective-permute-done.34 = bf16[1024,256]{1,0:T(8,128)(2,1)S(1)} collective-permute-done((bf16[1024,256]{1,0:T(8,128)(2,1)S(1)}, bf16[1024,256]{1,0:T(8,128)(2,1)S(1)}, u32[]{:S(2)}, u32[]{:S(2)}) %collective-permute-start.34) | collective-permute-done | bytes 524320 | tf_op jit(solution)/shard_map/ppermute | solution.py:20
  412.0 12.6 %shard_map.122 = (bf16[32,64,256]{2,1,0:T(8,128)(2,1)}, bf16[32,64,256]{2,1,0:T(8,128)(2,1)}, bf16[32,64,256]{2,1,0:T(8,128)(2,1)}, bf16[32,64,256]{2,1,0:T(8,128)(2,1)}) custom-call(s32[2,2]{1,0:T(2,128)} %get-tuple-element.111.places_ref, s32[16,8]{1,0:T(8,128)} %copy.42.mask_ref, bf16[1024,256]{1,0:T(8,128)(2,1)} %fusion.24.screened_ref, ...), custom_call_target="tpu_custom_call" | custom-call | tf_op jit(solution)/shard_map/pallas_call | solution.py:184
  425.8 2.8 fusion.42
  428.6 12.5 %shard_map.123 = (bf16[32,64,256]{2,1,0:T(8,128)(2,1)}, bf16[32,64,256]{2,1,0:T(8,128)(2,1)}, bf16[32,64,256]{2,1,0:T(8,128)(2,1)}, bf16[32,64,256]{2,1,0:T(8,128)(2,1)}) custom-call(s32[2,2]{1,0:T(2,128)} %get-tuple-element.120.places_ref, s32[16,8]{1,0:T(8,128)} %copy.42.mask_ref, bf16[1024,256]{1,0:T(8,128)(2,1)} %fusion.24.screened_ref, ...), custom_call_target="tpu_custom_call" | custom-call | tf_op jit(solution)/shard_map/pallas_call | solution.py:184
  441.1 1.6 collective-permute-start.44
  444.1 2.5 add_convert_fusion.6
  446.6 4.4 collective-permute-done.42
  451.1 1.6 add_convert_fusion.1
  453.7 2.6 add_convert_fusion.9
  457.3 3.5 fusion.12
  460.8 3.5 fusion.15
  464.2 9.2 %collective-permute-done.44 = bf16[32,64,256]{2,1,0:T(8,128)(2,1)S(1)} collective-permute-done((bf16[32,64,256]{2,1,0:T(8,128)(2,1)}, bf16[32,64,256]{2,1,0:T(8,128)(2,1)S(1)}, u32[]{:S(2)}, u32[]{:S(2)}) %collective-permute-start.44) | collective-permute-done | bytes 1048608 | tf_op jit(solution)/shard_map/ppermute | solution.py:20
  473.4 19.9 %collective-permute-done.45 = bf16[32,64,256]{2,1,0:T(8,128)(2,1)S(1)} collective-permute-done((bf16[32,64,256]{2,1,0:T(8,128)(2,1)S(1)}, bf16[32,64,256]{2,1,0:T(8,128)(2,1)S(1)}, u32[]{:S(2)}, u32[]{:S(2)}) %collective-permute-start.45) | collective-permute-done | bytes 1048608 | tf_op jit(solution)/shard_map/ppermute | solution.py:20
  493.9 3.5 fusion.18
  498.2 3.5 fusion.21
  503.2 2.3 collective-permute-done.46
  506.2 3.5 maximum_bitcast_fusion
  509.9 4.5 collective-permute-done.48
  515.3 2.9 collective-permute-done.49
  (180 shorter events, 41.8 us)
Async XLA Ops:
  0.6 202.8 %copy-start = (bf16[256,256]{1,0:T(8,128)(2,1)S(1)}, bf16[256,256]{1,0:T(8,128)(2,1)}, u32[]{:S(2)}) copy-start(bf16[256,256]{1,0:T(8,128)(2,1)} %param.13) | copy-start | bytes 393220
  5.9 236.0 %copy-start.3 = (bf16[512,1664]{1,0:T(8,128)(2,1)}, bf16[512,1664]{1,0:T(8,128)(2,1)S(1)}, u32[]{:S(2)}) copy-start(bf16[512,1664]{1,0:T(8,128)(2,1)S(1)} %get-tuple-element.146.refs_0_) | copy-start | bytes 5111812
  5.9 236.2 %copy-start.2 = (bf16[512,1664]{1,0:T(8,128)(2,1)}, bf16[512,1664]{1,0:T(8,128)(2,1)S(1)}, u32[]{:S(2)}) copy-start(bf16[512,1664]{1,0:T(8,128)(2,1)S(1)} %get-tuple-element.80.refs_1_) | copy-start | bytes 5111812
  6.0 40.3 %collective-permute-start.2 = (bf16[512,1664]{1,0:T(8,128)(2,1)S(1)}, bf16[512,1664]{1,0:T(8,128)(2,1)}, u32[]{:S(2)}, u32[]{:S(2)}) collective-permute-start(bf16[512,1664]{1,0:T(8,128)(2,1)S(1)} %get-tuple-element.146.refs_0_), channel_id=1, source_target_pairs={{0,2},{1,3},{2,0},{3,1},{4,6},{5,7},{6,4},{7,5},{8,10},{9,11},{10,... | collective-permute-start | bytes 5111816 | tf_op jit(solution)/shard_map/ppermute | solution.py:20
  16.0 20.5 %collective-permute-start = (bf16[2,1664,128]{2,1,0:T(8,128)(2,1)S(1)}, bf16[2,1664,128]{2,1,0:T(8,128)(2,1)}, u32[]{:S(2)}, u32[]{:S(2)}) collective-permute-start(bf16[2,1664,128]{2,1,0:T(8,128)(2,1)S(1)} %get-tuple-element.163), channel_id=1, source_target_pairs={{0,16},{8,24},{16,0},{24,8},{1,17},{9,25},{17,1},{25,9},{2,18},{10... | collective-permute-start | bytes 2555912 | tf_op jit(solution)/shard_map/ppermute | solution.py:20
  36.5 40.5 %collective-permute-start.1 = (bf16[512,1664]{1,0:T(8,128)(2,1)}, bf16[512,1664]{1,0:T(8,128)(2,1)}, u32[]{:S(2)}, u32[]{:S(2)}) collective-permute-start(bf16[512,1664]{1,0:T(8,128)(2,1)} %get-tuple-element.74), channel_id=1, source_target_pairs={{0,16},{8,24},{16,0},{24,8},{1,17},{9,25},{17,1},{25,9},{2,18},{10... | collective-permute-start | bytes 5111816 | tf_op jit(solution)/shard_map/ppermute | solution.py:20
  38.0 14.2 %copy-start.33 = (bf16[2,1664,128]{2,1,0:T(8,128)(2,1)S(1)}, bf16[2,1664,128]{2,1,0:T(8,128)(2,1)}, u32[]{:S(2)}) copy-start(bf16[2,1664,128]{2,1,0:T(8,128)(2,1)} %get-tuple-element.77) | copy-start | bytes 2555908
  46.3 63.0 %collective-permute-start.5 = (bf16[512,1664]{1,0:T(8,128)(2,1)S(1)}, bf16[512,1664]{1,0:T(8,128)(2,1)}, u32[]{:S(2)}, u32[]{:S(2)}) collective-permute-start(bf16[512,1664]{1,0:T(8,128)(2,1)S(1)} %get-tuple-element.80.refs_1_), channel_id=1, source_target_pairs={{0,2},{1,3},{2,0},{3,1},{4,6},{5,7},{6,4},{7,5},{8,10},{9,11},{10,... | collective-permute-start | bytes 5111816 | tf_op jit(solution)/shard_map/ppermute | solution.py:20
  49.6 16.6 %copy-start.7 = (bf16[2,1664,128]{2,1,0:T(8,128)(2,1)}, bf16[2,1664,128]{2,1,0:T(8,128)(2,1)S(1)}, u32[]{:S(2)}) copy-start(bf16[2,1664,128]{2,1,0:T(8,128)(2,1)S(1)} %get-tuple-element.157.refs_8_) | copy-start | bytes 2555908
  49.6 52.3 %collective-permute-start.6 = (bf16[2,1664,128]{2,1,0:T(8,128)(2,1)S(1)}, bf16[2,1664,128]{2,1,0:T(8,128)(2,1)S(1)}, u32[]{:S(2)}, u32[]{:S(2)}) collective-permute-start(bf16[2,1664,128]{2,1,0:T(8,128)(2,1)S(1)} %get-tuple-element.158), channel_id=1, source_target_pairs={{0,4},{1,5},{2,6},{3,7},{4,0},{5,1},{6,2},{7,3},{8,12},{9,13},{10,... | collective-permute-start | bytes 2555912 | tf_op jit(solution)/shard_map/ppermute | solution.py:20
  52.2 51.1 %collective-permute-start.4 = (bf16[2,1664,128]{2,1,0:T(8,128)(2,1)S(1)}, bf16[2,1664,128]{2,1,0:T(8,128)(2,1)}, u32[]{:S(2)}, u32[]{:S(2)}) collective-permute-start(bf16[2,1664,128]{2,1,0:T(8,128)(2,1)S(1)} %copy-done.33), channel_id=1, source_target_pairs={{0,16},{8,24},{16,0},{24,8},{1,17},{9,25},{17,1},{25,9},{2,18},{10... | collective-permute-start | bytes 2555912 | tf_op jit(solution)/shard_map/ppermute | solution.py:20
  53.7 55.5 %collective-permute-start.7 = (bf16[2,1664,128]{2,1,0:T(8,128)(2,1)S(1)}, bf16[2,1664,128]{2,1,0:T(8,128)(2,1)S(1)}, u32[]{:S(2)}, u32[]{:S(2)}) collective-permute-start(bf16[2,1664,128]{2,1,0:T(8,128)(2,1)S(1)} %get-tuple-element.157.refs_8_), channel_id=1, source_target_pairs={{0,8},{8,0},{16,24},{24,16},{1,9},{9,1},{17,25},{25,17},{2,10},{10... | collective-permute-start | bytes 2555912 | tf_op jit(solution)/shard_map/ppermute | solution.py:20
  76.9 89.5 %collective-permute-start.3 = (bf16[512,1664]{1,0:T(8,128)(2,1)}, bf16[512,1664]{1,0:T(8,128)(2,1)}, u32[]{:S(2)}, u32[]{:S(2)}) collective-permute-start(bf16[512,1664]{1,0:T(8,128)(2,1)} %get-tuple-element.76), channel_id=1, source_target_pairs={{0,16},{8,24},{16,0},{24,8},{1,17},{9,25},{17,1},{25,9},{2,18},{10... | collective-permute-start | bytes 5111816 | tf_op jit(solution)/shard_map/ppermute | solution.py:20
  101.9 18.3 %copy-start.17 = (bf16[2,1664,128]{2,1,0:T(8,128)(2,1)}, bf16[2,1664,128]{2,1,0:T(8,128)(2,1)S(1)}, u32[]{:S(2)}) copy-start(bf16[2,1664,128]{2,1,0:T(8,128)(2,1)S(1)} %collective-permute-done.6.refs_10_) | copy-start | bytes 2555908
  101.9 19.9 %collective-permute-start.13 = (bf16[2,1664,128]{2,1,0:T(8,128)(2,1)S(1)}, bf16[2,1664,128]{2,1,0:T(8,128)(2,1)S(1)}, u32[]{:S(2)}, u32[]{:S(2)}) collective-permute-start(bf16[2,1664,128]{2,1,0:T(8,128)(2,1)S(1)} %collective-permute-done.6.refs_10_), channel_id=1, source_target_pairs={{0,8},{8,0},{16,24},{24,16},{1,9},{9,1},{17,25},{25,17},{2,10},{10... | collective-permute-start | bytes 2555912 | tf_op jit(solution)/shard_map/ppermute | solution.py:20
  105.9 38.7 %collective-permute-start.12 = (bf16[2,1664,128]{2,1,0:T(8,128)(2,1)S(1)}, bf16[2,1664,128]{2,1,0:T(8,128)(2,1)}, u32[]{:S(2)}, u32[]{:S(2)}) collective-permute-start(bf16[2,1664,128]{2,1,0:T(8,128)(2,1)S(1)} %get-tuple-element.88), channel_id=1, source_target_pairs={{0,4},{1,5},{2,6},{3,7},{4,0},{5,1},{6,2},{7,3},{8,12},{9,13},{10,... | collective-permute-start | bytes 2555912 | tf_op jit(solution)/shard_map/ppermute | solution.py:20
  109.2 66.0 %collective-permute-start.11 = (bf16[512,1664]{1,0:T(8,128)(2,1)}, bf16[512,1664]{1,0:T(8,128)(2,1)}, u32[]{:S(2)}, u32[]{:S(2)}) collective-permute-start(bf16[512,1664]{1,0:T(8,128)(2,1)} %collective-permute-done.1.refs_0_), channel_id=1, source_target_pairs={{0,2},{1,3},{2,0},{3,1},{4,6},{5,7},{6,4},{7,5},{8,10},{9,11},{10,... | collective-permute-start | bytes 5111816 | tf_op jit(solution)/shard_map/ppermute | solution.py:20
  120.2 51.8 %collective-permute-start.15 = (bf16[2,1664,128]{2,1,0:T(8,128)(2,1)}, bf16[2,1664,128]{2,1,0:T(8,128)(2,1)}, u32[]{:S(2)}, u32[]{:S(2)}) collective-permute-start(bf16[2,1664,128]{2,1,0:T(8,128)(2,1)} %get-tuple-element.90), channel_id=1, source_target_pairs={{0,16},{8,24},{16,0},{24,8},{1,17},{9,25},{17,1},{25,9},{2,18},{10... | collective-permute-start | bytes 2555912 | tf_op jit(solution)/shard_map/ppermute | solution.py:20
  121.7 34.0 %copy-start.19 = (bf16[2,1664,128]{2,1,0:T(8,128)(2,1)}, bf16[2,1664,128]{2,1,0:T(8,128)(2,1)S(1)}, u32[]{:S(2)}) copy-start(bf16[2,1664,128]{2,1,0:T(8,128)(2,1)S(1)} %collective-permute-done.13.refs_14_) | copy-start | bytes 2555908
  121.7 51.9 %collective-permute-start.17 = (bf16[2,1664,128]{2,1,0:T(8,128)(2,1)}, bf16[2,1664,128]{2,1,0:T(8,128)(2,1)}, u32[]{:S(2)}, u32[]{:S(2)}) collective-permute-start(bf16[2,1664,128]{2,1,0:T(8,128)(2,1)} %get-tuple-element.94.refs_9_), channel_id=1, source_target_pairs={{0,8},{8,0},{16,24},{24,16},{1,9},{9,1},{17,25},{25,17},{2,10},{10... | collective-permute-start | bytes 2555912 | tf_op jit(solution)/shard_map/ppermute | solution.py:20
  144.6 29.1 %collective-permute-start.16 = (bf16[2,1664,128]{2,1,0:T(8,128)(2,1)}, bf16[2,1664,128]{2,1,0:T(8,128)(2,1)}, u32[]{:S(2)}, u32[]{:S(2)}) collective-permute-start(bf16[2,1664,128]{2,1,0:T(8,128)(2,1)} %collective-permute-done.12.refs_11_), channel_id=1, source_target_pairs={{0,8},{8,0},{16,24},{24,16},{1,9},{9,1},{17,25},{25,17},{2,10},{10... | collective-permute-start | bytes 2555912 | tf_op jit(solution)/shard_map/ppermute | solution.py:20
  166.4 18.6 %collective-permute-start.8 = (bf16[2,1664,128]{2,1,0:T(8,128)(2,1)}, bf16[2,1664,128]{2,1,0:T(8,128)(2,1)}, u32[]{:S(2)}, u32[]{:S(2)}) collective-permute-start(bf16[2,1664,128]{2,1,0:T(8,128)(2,1)} %get-tuple-element.84), channel_id=1, source_target_pairs={{0,16},{8,24},{16,0},{24,8},{1,17},{9,25},{17,1},{25,9},{2,18},{10... | collective-permute-start | bytes 2555912 | tf_op jit(solution)/shard_map/ppermute | solution.py:20
  172.0 69.9 %collective-permute-start.9 = (bf16[512,1664]{1,0:T(8,128)(2,1)}, bf16[512,1664]{1,0:T(8,128)(2,1)S(1)}, u32[]{:S(2)}, u32[]{:S(2)}) collective-permute-start(bf16[512,1664]{1,0:T(8,128)(2,1)} %collective-permute-done.1.refs_0_), channel_id=1, source_target_pairs={{0,1},{1,0},{2,3},{3,2},{4,5},{5,4},{6,7},{7,6},{8,9},{9,8},{10,11... | collective-permute-start | bytes 5111816 | tf_op jit(solution)/shard_map/ppermute | solution.py:20
  173.6 25.9 %copy-start.8 = (bf16[2,1664,128]{2,1,0:T(8,128)(2,1)}, bf16[2,1664,128]{2,1,0:T(8,128)(2,1)S(1)}, u32[]{:S(2)}) copy-start(bf16[2,1664,128]{2,1,0:T(8,128)(2,1)S(1)} %get-tuple-element.95.refs_8_) | copy-start | bytes 2555908
  173.6 49.0 %collective-permute-start.20 = (bf16[2,1664,128]{2,1,0:T(8,128)(2,1)S(1)}, bf16[2,1664,128]{2,1,0:T(8,128)(2,1)}, u32[]{:S(2)}, u32[]{:S(2)}) collective-permute-start(bf16[2,1664,128]{2,1,0:T(8,128)(2,1)S(1)} %get-tuple-element.100), channel_id=1, source_target_pairs={{0,4},{1,5},{2,6},{3,7},{4,0},{5,1},{6,2},{7,3},{8,12},{9,13},{10,... | collective-permute-start | bytes 2555912 | tf_op jit(solution)/shard_map/ppermute | solution.py:20
  173.7 28.2 %collective-permute-start.18 = (bf16[2,1664,128]{2,1,0:T(8,128)(2,1)S(1)}, bf16[2,1664,128]{2,1,0:T(8,128)(2,1)S(1)}, u32[]{:S(2)}, u32[]{:S(2)}) collective-permute-start(bf16[2,1664,128]{2,1,0:T(8,128)(2,1)S(1)} %get-tuple-element.95.refs_8_), channel_id=1, source_target_pairs={{0,8},{8,0},{16,24},{24,16},{1,9},{9,1},{17,25},{25,17},{2,10},{10... | collective-permute-start | bytes 2555912 | tf_op jit(solution)/shard_map/ppermute | solution.py:20
  175.2 67.0 %collective-permute-start.10 = (bf16[512,1664]{1,0:T(8,128)(2,1)}, bf16[512,1664]{1,0:T(8,128)(2,1)S(1)}, u32[]{:S(2)}, u32[]{:S(2)}) collective-permute-start(bf16[512,1664]{1,0:T(8,128)(2,1)} %collective-permute-done.3.refs_1_), channel_id=1, source_target_pairs={{0,1},{1,0},{2,3},{3,2},{4,5},{5,4},{6,7},{7,6},{8,9},{9,8},{10,11... | collective-permute-start | bytes 5111816 | tf_op jit(solution)/shard_map/ppermute | solution.py:20
  185.0 54.1 %collective-permute-start.14 = (bf16[512,1664]{1,0:T(8,128)(2,1)}, bf16[512,1664]{1,0:T(8,128)(2,1)S(1)}, u32[]{:S(2)}, u32[]{:S(2)}) collective-permute-start(bf16[512,1664]{1,0:T(8,128)(2,1)} %collective-permute-done.3.refs_1_), channel_id=1, source_target_pairs={{0,2},{1,3},{2,0},{3,1},{4,6},{5,7},{6,4},{7,5},{8,10},{9,11},{10,... | collective-permute-start | bytes 5111816 | tf_op jit(solution)/shard_map/ppermute | solution.py:20
  201.9 20.7 %copy-start.9 = (bf16[2,1664,128]{2,1,0:T(8,128)(2,1)}, bf16[2,1664,128]{2,1,0:T(8,128)(2,1)S(1)}, u32[]{:S(2)}) copy-start(bf16[2,1664,128]{2,1,0:T(8,128)(2,1)S(1)} %get-tuple-element.99.refs_9_) | copy-start | bytes 2555908
  201.9 20.7 %copy-start.20 = (bf16[2,1664,128]{2,1,0:T(8,128)(2,1)}, bf16[2,1664,128]{2,1,0:T(8,128)(2,1)S(1)}, u32[]{:S(2)}) copy-start(bf16[2,1664,128]{2,1,0:T(8,128)(2,1)S(1)} %collective-permute-done.18.refs_12_) | copy-start | bytes 2555908
  201.9 20.8 %collective-permute-start.19 = (bf16[2,1664,128]{2,1,0:T(8,128)(2,1)S(1)}, bf16[2,1664,128]{2,1,0:T(8,128)(2,1)S(1)}, u32[]{:S(2)}, u32[]{:S(2)}) collective-permute-start(bf16[2,1664,128]{2,1,0:T(8,128)(2,1)S(1)} %get-tuple-element.99.refs_9_), channel_id=1, source_target_pairs={{0,8},{8,0},{16,24},{24,16},{1,9},{9,1},{17,25},{25,17},{2,10},{10... | collective-permute-start | bytes 2555912 | tf_op jit(solution)/shard_map/ppermute | solution.py:20
  222.6 20.6 %collective-permute-start.21 = (bf16[512,1664]{1,0:T(8,128)(2,1)}, bf16[512,1664]{1,0:T(8,128)(2,1)S(1)}, u32[]{:S(2)}, u32[]{:S(2)}) collective-permute-start(bf16[512,1664]{1,0:T(8,128)(2,1)} %collective-permute-done.11.refs_4_), channel_id=1, source_target_pairs={{0,1},{1,0},{2,3},{3,2},{4,5},{5,4},{6,7},{7,6},{8,9},{9,8},{10,11... | collective-permute-start | bytes 5111816 | tf_op jit(solution)/shard_map/ppermute | solution.py:20
  239.1 4.8 collective-permute-start.22
  239.1 41.0 %collective-permute-start.27 = (bf16[2,1664,128]{2,1,0:T(8,128)(2,1)}, bf16[2,1664,128]{2,1,0:T(8,128)(2,1)}, u32[]{:S(2)}, u32[]{:S(2)}) collective-permute-start(bf16[2,1664,128]{2,1,0:T(8,128)(2,1)} %get-tuple-element.103), channel_id=1, source_target_pairs={{0,4},{1,5},{2,6},{3,7},{4,0},{5,1},{6,2},{7,3},{8,12},{9,13},{10,... | collective-permute-start | bytes 2555912 | tf_op jit(solution)/shard_map/ppermute | solution.py:20
  241.9 39.7 %collective-permute-start.23 = (bf16[512,1664]{1,0:T(8,128)(2,1)S(1)}, bf16[512,1664]{1,0:T(8,128)(2,1)}, u32[]{:S(2)}, u32[]{:S(2)}) collective-permute-start(bf16[512,1664]{1,0:T(8,128)(2,1)S(1)} %get-tuple-element.146.refs_0_), channel_id=1, source_target_pairs={{0,1},{1,0},{2,3},{3,2},{4,5},{5,4},{6,7},{7,6},{8,9},{9,8},{10,11... | collective-permute-start | bytes 5111816 | tf_op jit(solution)/shard_map/ppermute | solution.py:20
  242.2 40.9 %collective-permute-start.24 = (bf16[512,1664]{1,0:T(8,128)(2,1)S(1)}, bf16[512,1664]{1,0:T(8,128)(2,1)}, u32[]{:S(2)}, u32[]{:S(2)}) collective-permute-start(bf16[512,1664]{1,0:T(8,128)(2,1)S(1)} %get-tuple-element.80.refs_1_), channel_id=1, source_target_pairs={{0,1},{1,0},{2,3},{3,2},{4,5},{5,4},{6,7},{7,6},{8,9},{9,8},{10,11... | collective-permute-start | bytes 5111816 | tf_op jit(solution)/shard_map/ppermute | solution.py:20
  243.7 40.0 %collective-permute-start.25 = (bf16[512,1664]{1,0:T(8,128)(2,1)}, bf16[512,1664]{1,0:T(8,128)(2,1)}, u32[]{:S(2)}, u32[]{:S(2)}) collective-permute-start(bf16[512,1664]{1,0:T(8,128)(2,1)} %collective-permute-done.2.refs_4_), channel_id=1, source_target_pairs={{0,1},{1,0},{2,3},{3,2},{4,5},{5,4},{6,7},{7,6},{8,9},{9,8},{10,11... | collective-permute-start | bytes 5111816 | tf_op jit(solution)/shard_map/ppermute | solution.py:20
  246.0 37.6 %collective-permute-start.26 = (bf16[512,1664]{1,0:T(8,128)(2,1)}, bf16[512,1664]{1,0:T(8,128)(2,1)}, u32[]{:S(2)}, u32[]{:S(2)}) collective-permute-start(bf16[512,1664]{1,0:T(8,128)(2,1)} %collective-permute-done.5.refs_5_), channel_id=1, source_target_pairs={{0,1},{1,0},{2,3},{3,2},{4,5},{5,4},{6,7},{7,6},{8,9},{9,8},{10,11... | collective-permute-start | bytes 5111816 | tf_op jit(solution)/shard_map/ppermute | solution.py:20
  280.1 25.1 %collective-permute-start.28 = (bf16[1024,512]{1,0:T(8,128)(2,1)}, bf16[1024,512]{1,0:T(8,128)(2,1)S(1)}, u32[]{:S(2)}, u32[]{:S(2)}) collective-permute-start(bf16[1024,512]{1,0:T(8,128)(2,1)} %shard_map.116), channel_id=1, source_target_pairs={{0,16},{8,24},{16,0},{24,8},{1,17},{9,25},{17,1},{25,9},{2,18},{10... | collective-permute-start | bytes 3145736 | tf_op jit(solution)/shard_map/ppermute | solution.py:20
  281.6 27.0 %collective-permute-start.31 = (bf16[2,1664,128]{2,1,0:T(8,128)(2,1)}, bf16[2,1664,128]{2,1,0:T(8,128)(2,1)S(1)}, u32[]{:S(2)}, u32[]{:S(2)}) collective-permute-start(bf16[2,1664,128]{2,1,0:T(8,128)(2,1)} %collective-permute-done.27.refs_11_), channel_id=1, source_target_pairs={{0,8},{8,0},{16,24},{24,16},{1,9},{9,1},{17,25},{25,17},{2,10},{10... | collective-permute-start | bytes 2555912 | tf_op jit(solution)/shard_map/ppermute | solution.py:20
  283.1 37.5 %collective-permute-start.30 = (bf16[2,1664,128]{2,1,0:T(8,128)(2,1)}, bf16[2,1664,128]{2,1,0:T(8,128)(2,1)}, u32[]{:S(2)}, u32[]{:S(2)}) collective-permute-start(bf16[2,1664,128]{2,1,0:T(8,128)(2,1)} %collective-permute-done.20.refs_10_), channel_id=1, source_target_pairs={{0,8},{8,0},{16,24},{24,16},{1,9},{9,1},{17,25},{25,17},{2,10},{10... | collective-permute-start | bytes 2555912 | tf_op jit(solution)/shard_map/ppermute | solution.py:20
  308.0 27.2 %collective-permute-start.29 = (bf16[1024,256]{1,0:T(8,128)(2,1)}, bf16[1024,256]{1,0:T(8,128)(2,1)}, u32[]{:S(2)}, u32[]{:S(2)}) collective-permute-start(bf16[1024,256]{1,0:T(8,128)(2,1)} %slice.85), channel_id=1, source_target_pairs={{0,4},{1,5},{2,6},{3,7},{4,0},{5,1},{6,2},{7,3},{8,12},{9,13},{10,... | collective-permute-start | bytes 1572872 | tf_op jit(solution)/shard_map/ppermute | solution.py:20
  308.6 25.8 %copy-start.34 = (s32[64,8]{0,1:T(8,128)S(1)}, s32[64,8]{0,1:T(8,128)}, u32[]{:S(2)}) copy-start(s32[64,8]{0,1:T(8,128)} %param.14) | copy-start | bytes 6148
  333.8 23.9 %collective-permute-start.32 = (bf16[1024,512]{1,0:T(8,128)(2,1)}, bf16[1024,512]{1,0:T(8,128)(2,1)S(1)}, u32[]{:S(2)}, u32[]{:S(2)}) collective-permute-start(bf16[1024,512]{1,0:T(8,128)(2,1)} %shard_map.118), channel_id=1, source_target_pairs={{0,16},{8,24},{16,0},{24,8},{1,17},{9,25},{17,1},{25,9},{2,18},{10... | collective-permute-start | bytes 3145736 | tf_op jit(solution)/shard_map/ppermute | solution.py:20
  349.7 38.0 %collective-permute-start.33 = (bf16[32,64,256]{2,1,0:T(8,128)(2,1)}, bf16[32,64,256]{2,1,0:T(8,128)(2,1)S(1)}, u32[]{:S(2)}, u32[]{:S(2)}) collective-permute-start(bf16[32,64,256]{2,1,0:T(8,128)(2,1)} %get-tuple-element.113), channel_id=1, source_target_pairs={{0,8},{8,0},{16,24},{24,16},{1,9},{9,1},{17,25},{25,17},{2,10},{10... | collective-permute-start | bytes 3145736 | tf_op jit(solution)/shard_map/ppermute | solution.py:20
  357.7 31.5 %collective-permute-start.36 = (bf16[32,64,256]{2,1,0:T(8,128)(2,1)}, bf16[32,64,256]{2,1,0:T(8,128)(2,1)S(1)}, u32[]{:S(2)}, u32[]{:S(2)}) collective-permute-start(bf16[32,64,256]{2,1,0:T(8,128)(2,1)} %get-tuple-element.119), channel_id=1, source_target_pairs={{0,16},{8,24},{16,0},{24,8},{1,17},{9,25},{17,1},{25,9},{2,18},{10... | collective-permute-start | bytes 3145736 | tf_op jit(solution)/shard_map/ppermute | solution.py:20
  358.3 66.9 %collective-permute-start.35 = (bf16[32,64,256]{2,1,0:T(8,128)(2,1)}, bf16[32,64,256]{2,1,0:T(8,128)(2,1)}, u32[]{:S(2)}, u32[]{:S(2)}) collective-permute-start(bf16[32,64,256]{2,1,0:T(8,128)(2,1)} %get-tuple-element.112), channel_id=1, source_target_pairs={{0,8},{8,0},{16,24},{24,16},{1,9},{9,1},{17,25},{25,17},{2,10},{10... | collective-permute-start | bytes 3145736 | tf_op jit(solution)/shard_map/ppermute | solution.py:20
  359.8 64.7 %collective-permute-start.38 = (bf16[32,64,256]{2,1,0:T(8,128)(2,1)}, bf16[32,64,256]{2,1,0:T(8,128)(2,1)}, u32[]{:S(2)}, u32[]{:S(2)}) collective-permute-start(bf16[32,64,256]{2,1,0:T(8,128)(2,1)} %get-tuple-element.118), channel_id=1, source_target_pairs={{0,16},{8,24},{16,0},{24,8},{1,17},{9,25},{17,1},{25,9},{2,18},{10... | collective-permute-start | bytes 3145736 | tf_op jit(solution)/shard_map/ppermute | solution.py:20
  388.1 22.9 %collective-permute-start.34 = (bf16[1024,256]{1,0:T(8,128)(2,1)S(1)}, bf16[1024,256]{1,0:T(8,128)(2,1)S(1)}, u32[]{:S(2)}, u32[]{:S(2)}) collective-permute-start(bf16[1024,256]{1,0:T(8,128)(2,1)S(1)} %slice.84), channel_id=1, source_target_pairs={{0,4},{1,5},{2,6},{3,7},{4,0},{5,1},{6,2},{7,3},{8,12},{9,13},{10,... | collective-permute-start | bytes 1572872 | tf_op jit(solution)/shard_map/ppermute | solution.py:20
  389.3 51.8 %collective-permute-start.37 = (bf16[32,64,256]{2,1,0:T(8,128)(2,1)S(1)}, bf16[32,64,256]{2,1,0:T(8,128)(2,1)}, u32[]{:S(2)}, u32[]{:S(2)}) collective-permute-start(bf16[32,64,256]{2,1,0:T(8,128)(2,1)S(1)} %add_convert_fusion.10), channel_id=1, source_target_pairs={{0,16},{8,24},{16,0},{24,8},{1,17},{9,25},{17,1},{25,9},{2,18},{10... | collective-permute-start | bytes 3145736 | tf_op jit(solution)/shard_map/ppermute | solution.py:20
  390.4 52.3 %collective-permute-start.39 = (bf16[32,64,256]{2,1,0:T(8,128)(2,1)S(1)}, bf16[32,64,256]{2,1,0:T(8,128)(2,1)}, u32[]{:S(2)}, u32[]{:S(2)}) collective-permute-start(bf16[32,64,256]{2,1,0:T(8,128)(2,1)S(1)} %add_convert_fusion.7), channel_id=1, source_target_pairs={{0,8},{8,0},{16,24},{24,16},{1,9},{9,1},{17,25},{25,17},{2,10},{10... | collective-permute-start | bytes 3145736 | tf_op jit(solution)/shard_map/ppermute | solution.py:20
  424.6 26.5 %collective-permute-start.42 = (bf16[32,64,256]{2,1,0:T(8,128)(2,1)}, bf16[32,64,256]{2,1,0:T(8,128)(2,1)}, u32[]{:S(2)}, u32[]{:S(2)}) collective-permute-start(bf16[32,64,256]{2,1,0:T(8,128)(2,1)} %get-tuple-element.136), channel_id=1, source_target_pairs={{0,16},{8,24},{16,0},{24,8},{1,17},{9,25},{17,1},{25,9},{2,18},{10... | collective-permute-start | bytes 3145736 | tf_op jit(solution)/shard_map/ppermute | solution.py:20
  425.2 27.5 %collective-permute-start.41 = (bf16[32,64,256]{2,1,0:T(8,128)(2,1)}, bf16[32,64,256]{2,1,0:T(8,128)(2,1)S(1)}, u32[]{:S(2)}, u32[]{:S(2)}) collective-permute-start(bf16[32,64,256]{2,1,0:T(8,128)(2,1)} %get-tuple-element.135), channel_id=1, source_target_pairs={{0,8},{8,0},{16,24},{24,16},{1,9},{9,1},{17,25},{25,17},{2,10},{10... | collective-permute-start | bytes 3145736 | tf_op jit(solution)/shard_map/ppermute | solution.py:20
  441.1 32.3 %collective-permute-start.44 = (bf16[32,64,256]{2,1,0:T(8,128)(2,1)}, bf16[32,64,256]{2,1,0:T(8,128)(2,1)S(1)}, u32[]{:S(2)}, u32[]{:S(2)}) collective-permute-start(bf16[32,64,256]{2,1,0:T(8,128)(2,1)} %get-tuple-element.139), channel_id=1, source_target_pairs={{0,16},{8,24},{16,0},{24,8},{1,17},{9,25},{17,1},{25,9},{2,18},{10... | collective-permute-start | bytes 3145736 | tf_op jit(solution)/shard_map/ppermute | solution.py:20
  442.7 54.7 %collective-permute-start.40 = (bf16[32,64,256]{2,1,0:T(8,128)(2,1)}, bf16[32,64,256]{2,1,0:T(8,128)(2,1)S(1)}, u32[]{:S(2)}, u32[]{:S(2)}) collective-permute-start(bf16[32,64,256]{2,1,0:T(8,128)(2,1)} %get-tuple-element.133), channel_id=1, source_target_pairs={{0,8},{8,0},{16,24},{24,16},{1,9},{9,1},{17,25},{25,17},{2,10},{10... | collective-permute-start | bytes 3145736 | tf_op jit(solution)/shard_map/ppermute | solution.py:20
  452.7 40.6 %collective-permute-start.45 = (bf16[32,64,256]{2,1,0:T(8,128)(2,1)S(1)}, bf16[32,64,256]{2,1,0:T(8,128)(2,1)S(1)}, u32[]{:S(2)}, u32[]{:S(2)}) collective-permute-start(bf16[32,64,256]{2,1,0:T(8,128)(2,1)S(1)} %add_convert_fusion.1), channel_id=1, source_target_pairs={{0,8},{8,0},{16,24},{24,16},{1,9},{9,1},{17,25},{25,17},{2,10},{10... | collective-permute-start | bytes 3145736 | tf_op jit(solution)/shard_map/ppermute | solution.py:20
  456.7 40.7 %collective-permute-start.43 = (bf16[32,64,256]{2,1,0:T(8,128)(2,1)S(1)}, bf16[32,64,256]{2,1,0:T(8,128)(2,1)S(1)}, u32[]{:S(2)}, u32[]{:S(2)}) collective-permute-start(bf16[32,64,256]{2,1,0:T(8,128)(2,1)S(1)} %add_convert_fusion.4), channel_id=1, source_target_pairs={{0,16},{8,24},{16,0},{24,8},{1,17},{9,25},{17,1},{25,9},{2,18},{10... | collective-permute-start | bytes 3145736 | tf_op jit(solution)/shard_map/ppermute | solution.py:20
  460.8 32.5 %copy-start.32 = (bf16[32,64,256]{2,1,0:T(8,128)(2,1)S(1)}, bf16[32,64,256]{2,1,0:T(8,128)(2,1)}, u32[]{:S(2)}) copy-start(bf16[32,64,256]{2,1,0:T(8,128)(2,1)} %get-tuple-element.138) | copy-start | bytes 3145732
  501.7 3.8 collective-permute-start.46
  505.5 4.1 collective-permute-start.47
  506.1 13.8 %copy-start.1 = (bf16[256,256]{1,0:T(8,128)(2,1)S(1)}, bf16[256,256]{1,0:T(8,128)(2,1)}, u32[]{:S(2)}) copy-start(bf16[256,256]{1,0:T(8,128)(2,1)} %param.13) | copy-start | bytes 393220
  509.7 4.6 collective-permute-start.48
  514.5 3.7 collective-permute-start.49
  518.2 1.2 collective-permute-start.50
  (25 other events, 153.8 us)

commit v9 on v8

--- a/solution.py
+++ b/solution.py
@@ -396,8 +396,8 @@
 
     for j, (front, back) in enumerate(contracted_chunks):
         beside = dressed[:, :, j * wide : (j + 1) * wide]
-        of_back = jnp.einsum("mlq,nlq->mn", back, beside, preferred_element_type=jnp.float32)
-        of_front = jnp.einsum("mlq,nlq->mn", after(front, of_back), beside, preferred_element_type=jnp.float32)
+        of_front = jnp.einsum("mlq,nlq->mn", front, beside, preferred_element_type=jnp.float32)
+        of_back = jnp.einsum("mlq,nlq->mn", after(back, of_front), beside, preferred_element_type=jnp.float32)
         energy = energy - jnp.concatenate([of_front, of_back])
 
     contracted = jnp.transpose(jnp.concatenate([jnp.concatenate(halves) for halves in contracted_chunks], axis=2), (2, 0, 1))

time: 524 us -> 527 us (level)
  transfers between devices with their start and end apart: 51 -> 51, of which waited for: 19 -> 20; matrix products, arithmetic and copies ran while one was open for 17% -> 17% of each run, Pallas kernels for 28% -> 28%
where the time goes in v9:
time: 527 us; the launch traced here: 523 us
  waiting for transfers between devices  218 us (41%)
  Pallas kernels  147 us (28%)
  starting transfers between devices  53.6 us (10%)
  other arithmetic  42.8 us (8%)
  matrix products  33 us (6%)
  local copies, waits for them, and re-layouts  27 us (5%)
    ppermute x51, waiting for transfers between devices, swap(): return lax.ppermute(value, axis, [(i, i ^ bit) for i in range(size)])  218 us
    pallas_call x4, Pallas kernels, product(): pl.pallas_call(functools.partial(product_kernel, count, parts, per_block)...  53.6 us
    ppermute x51, starting transfers between devices, swap(): return lax.ppermute(value, axis, [(i, i ^ bit) for i in range(size)])  53.6 us
    pallas_call x4, Pallas kernels, contract(): pl.pallas_call(functools.partial(contract_kernel, rb, ab), in_specs=[in_s...  50.3 us
    pallas_call x4, Pallas kernels, turn(): pl.pallas_call(turn_kernel, grid=(rows // wide, tile // tall), in_specs=[...  42.9 us
    dot_general x1, matrix products, per_device(): jnp.einsum('qns,ls->nlq', near, green, preferred_element_type=jnp.float32)  19.1 us
    mul x1, other arithmetic, per_device(): after(three_near, near_crossed_first, came[1][1]) * near_mask[:, None, :]  13.8 us
  transfers between devices with their start and end apart: 51, of which 20 were waited for; matrix products, arithmetic and copies ran while one was open for 17% of the time, Pallas kernels for 28%

profile of v9, /device:TPU:0, one launch (start us, length us, event | category | flops | bytes accessed | tf_op | source)
XLA Modules:
  0.0 523.0 jit_solution(9671719100044690460)
XLA Ops:
  0.7 5.3 %fusion.41 = (bf16[512,1664]{1,0:T(8,128)(2,1)S(1)}, bf16[512,1664]{1,0:T(8,128)(2,1)S(1)}, bf16[512,1664]{1,0:T(8,128)(2,1)}, bf16[512,1664]{1,0:T(8,128)(2,1)}) fusion(bf16[1024,3328]{1,0:T(8,128)(2,1)} %param.9, s32[]{:T(128)S(6)} %add.207, s32[]{:T(128)S(6)} %select_n.156, s32[]{:T(128)S(6)} %select_n.155), kind=kLoop, calls=%fused_computation.86 | loop fusion | bytes 13631500 | tf_op jit(solution)/shard_map/split | solution.py:231
  6.0 3.0 collective-permute-start.2
  9.0 5.2 dynamic-slice_bitcast_fusion
  14.2 1.8 fusion.43
  17.5 19.0 %collective-permute-done = bf16[2,1664,128]{2,1,0:T(8,128)(2,1)} collective-permute-done((bf16[2,1664,128]{2,1,0:T(8,128)(2,1)S(1)}, bf16[2,1664,128]{2,1,0:T(8,128)(2,1)}, u32[]{:S(2)}, u32[]{:S(2)}) %collective-permute-start) | collective-permute-done | bytes 852000 | tf_op jit(solution)/shard_map/ppermute | solution.py:20
  38.0 8.3 %collective-permute-done.2.refs_4_ = bf16[512,1664]{1,0:T(8,128)(2,1)} collective-permute-done((bf16[512,1664]{1,0:T(8,128)(2,1)S(1)}, bf16[512,1664]{1,0:T(8,128)(2,1)}, u32[]{:S(2)}, u32[]{:S(2)}) %collective-permute-start.2) | collective-permute-done | bytes 1703968 | tf_op jit(solution)/shard_map/ppermute | solution.py:20
  46.3 1.7 collective-permute-start.5
  48.0 1.5 broadcast_select_fusion.5
  49.6 2.7 collective-permute-start.6
  52.2 1.5 collective-permute-start.4
  55.2 10.9 %shard_map.112.refs_0_ = bf16[64,256,256]{2,1,0:T(8,128)(2,1)} custom-call(bf16[1024,64,256]{2,1,0:T(8,128)(2,1)} %panel_ref.3), custom_call_target="tpu_custom_call" | custom-call | bytes 33554432 | tf_op jit(solution)/shard_map/pallas_call | solution.py:122
  66.1 10.8 %collective-permute-done.1.refs_0_ = bf16[512,1664]{1,0:T(8,128)(2,1)} collective-permute-done((bf16[512,1664]{1,0:T(8,128)(2,1)}, bf16[512,1664]{1,0:T(8,128)(2,1)}, u32[]{:S(2)}, u32[]{:S(2)}) %collective-permute-start.1) | collective-permute-done | bytes 1703968 | tf_op jit(solution)/shard_map/ppermute | solution.py:20
  78.5 23.4 %collective-permute-done.6.refs_10_ = bf16[2,1664,128]{2,1,0:T(8,128)(2,1)S(1)} collective-permute-done((bf16[2,1664,128]{2,1,0:T(8,128)(2,1)S(1)}, bf16[2,1664,128]{2,1,0:T(8,128)(2,1)S(1)}, u32[]{:S(2)}, u32[]{:S(2)}) %collective-permute-start.6) | collective-permute-done | bytes 852000 | tf_op jit(solution)/shard_map/ppermute | solution.py:20
  103.4 2.4 broadcast_select_fusion.2
  105.8 3.4 collective-permute-start.12
  109.4 10.8 %shard_map.113.refs_1_ = bf16[64,256,256]{2,1,0:T(8,128)(2,1)} custom-call(bf16[1024,64,256]{2,1,0:T(8,128)(2,1)} %panel_ref.3), custom_call_target="tpu_custom_call" | custom-call | bytes 33554432 | tf_op jit(solution)/shard_map/pallas_call | solution.py:122
  120.2 1.5 collective-permute-start.15
  122.3 22.3 %collective-permute-done.12.refs_11_ = bf16[2,1664,128]{2,1,0:T(8,128)(2,1)} collective-permute-done((bf16[2,1664,128]{2,1,0:T(8,128)(2,1)S(1)}, bf16[2,1664,128]{2,1,0:T(8,128)(2,1)}, u32[]{:S(2)}, u32[]{:S(2)}) %collective-permute-start.12) | collective-permute-done | bytes 852000 | tf_op jit(solution)/shard_map/ppermute | solution.py:20
  145.1 10.6 %shard_map.114.refs_2_ = bf16[64,256,256]{2,1,0:T(8,128)(2,1)} custom-call(bf16[1024,64,256]{2,1,0:T(8,128)(2,1)} %panel_ref.3), custom_call_target="tpu_custom_call" | custom-call | bytes 33554432 | tf_op jit(solution)/shard_map/pallas_call | solution.py:122
  155.7 10.6 %shard_map.115.refs_3_ = bf16[64,256,256]{2,1,0:T(8,128)(2,1)} custom-call(bf16[1024,64,256]{2,1,0:T(8,128)(2,1)} %panel_ref.3), custom_call_target="tpu_custom_call" | custom-call | bytes 33554432 | tf_op jit(solution)/shard_map/pallas_call | solution.py:122
  166.4 1.5 collective-permute-start.8
  170.2 1.8 copy.27
  172.0 1.6 broadcast_select_fusion
  175.4 9.6 %collective-permute-done.8 = bf16[2,1664,128]{2,1,0:T(8,128)(2,1)} collective-permute-done((bf16[2,1664,128]{2,1,0:T(8,128)(2,1)}, bf16[2,1664,128]{2,1,0:T(8,128)(2,1)}, u32[]{:S(2)}, u32[]{:S(2)}) %collective-permute-start.8) | collective-permute-done | bytes 852000 | tf_op jit(solution)/shard_map/ppermute | solution.py:20
  185.6 13.8 %broadcast_multiply_fusion = bf16[512,64,256]{2,1,0:T(8,128)(2,1)} fusion(bf16[512,64,256]{2,1,0:T(8,128)(2,1)} %param.12, bf16[512,256]{1,0:T(8,128)(2,1)S(1)} %copy-done.23), kind=kLoop, calls=%fused_computation.2 | loop fusion | flops 8388608 | bytes 33816576 | tf_op jit(solution)/shard_map/mul | solution.py:317
  199.4 2.4 broadcast_select_fusion.1
  203.4 19.1 %convert_bitcast_fusion = bf16[64,64,512]{2,1,0:T(8,128)(2,1)} fusion(bf16[512,64,256]{2,1,0:T(8,128)(2,1)} %broadcast_multiply_fusion, bf16[256,256]{1,0:T(8,128)(2,1)S(1)} %copy-done, s32[]{:T(128)S(6)} %select_n.164), kind=kOutput, calls=%fused_computation.4 | convolution fusion | flops 1075838976 | bytes 21004292 | tf_op jit(solution)/shard_map/qns,ls->nlq/dot_general | solution.py:320
  223.6 15.5 %collective-permute-done.14.refs_5_ = bf16[512,1664]{1,0:T(8,128)(2,1)S(1)} collective-permute-done((bf16[512,1664]{1,0:T(8,128)(2,1)}, bf16[512,1664]{1,0:T(8,128)(2,1)S(1)}, u32[]{:S(2)}, u32[]{:S(2)}) %collective-permute-start.14) | collective-permute-done | bytes 1703968 | tf_op jit(solution)/shard_map/ppermute | solution.py:20
  240.9 2.8 collective-permute-start.27
  246.7 13.2 %shard_map.116 = bf16[1024,512]{1,0:T(8,128)(2,1)} custom-call(s32[4]{0:T(128)} %fusion.40.order_ref, bf16[512,1664]{1,0:T(8,128)(2,1)} %collective-permute-done.1.refs_0_, bf16[512,1664]{1,0:T(8,128)(2,1)} %collective-permute-done.3.refs_1_, bf16[512,1664]{1,0:T(8,128)(2,1)} %copy-done.10, bf16[512,1664]{1,0:T(8,128)(2,1)} %collective-permute-done.10.refs_3_, ...), custom_call_target="tpu_custom_call" | custom-call | tf_op jit(solution)/shard_map/pallas_call | solution.py:97
  259.9 21.4 %collective-permute-done.27.refs_11_ = bf16[2,1664,128]{2,1,0:T(8,128)(2,1)} collective-permute-done((bf16[2,1664,128]{2,1,0:T(8,128)(2,1)}, bf16[2,1664,128]{2,1,0:T(8,128)(2,1)}, u32[]{:S(2)}, u32[]{:S(2)}) %collective-permute-start.27) | collective-permute-done | bytes 852000 | tf_op jit(solution)/shard_map/ppermute | solution.py:20
  284.9 13.6 %shard_map.117 = f32[1024,512]{1,0:T(8,128)} custom-call(s32[4]{0:T(128)} %fusion.40.order_ref, bf16[512,1664]{1,0:T(8,128)(2,1)} %copy-done.3, bf16[512,1664]{1,0:T(8,128)(2,1)} %copy-done.2, bf16[512,1664]{1,0:T(8,128)(2,1)} %collective-permute-done.23.refs_2_, bf16[512,1664]{1,0:T(8,128)(2,1)} %collective-permute-done.24.refs_3_, ...), custom_call_target="tpu_custom_call" | custom-call | tf_op jit(solution)/shard_map/pallas_call | solution.py:97
  298.5 7.4 %collective-permute-done.28 = bf16[1024,512]{1,0:T(8,128)(2,1)S(1)} collective-permute-done((bf16[1024,512]{1,0:T(8,128)(2,1)}, bf16[1024,512]{1,0:T(8,128)(2,1)S(1)}, u32[]{:S(2)}, u32[]{:S(2)}) %collective-permute-start.28) | collective-permute-done | bytes 1048608 | tf_op jit(solution)/shard_map/ppermute | solution.py:20
  305.9 1.9 convert_add_fusion.1
  308.7 12.5 %collective-permute-done.30.refs_14_ = bf16[2,1664,128]{2,1,0:T(8,128)(2,1)S(1)} collective-permute-done((bf16[2,1664,128]{2,1,0:T(8,128)(2,1)}, bf16[2,1664,128]{2,1,0:T(8,128)(2,1)S(1)}, u32[]{:S(2)}, u32[]{:S(2)}) %collective-permute-start.30) | collective-permute-done | bytes 852000 | tf_op jit(solution)/shard_map/ppermute | solution.py:20
  322.1 13.2 %shard_map.118 = bf16[1024,512]{1,0:T(8,128)(2,1)} custom-call(s32[4]{0:T(128)} %fusion.40.order_ref, bf16[512,1664]{1,0:T(8,128)(2,1)} %collective-permute-done.1.refs_0_, bf16[512,1664]{1,0:T(8,128)(2,1)} %collective-permute-done.3.refs_1_, bf16[512,1664]{1,0:T(8,128)(2,1)} %copy-done.10, bf16[512,1664]{1,0:T(8,128)(2,1)} %collective-permute-done.10.refs_3_, ...), custom_call_target="tpu_custom_call" | custom-call | tf_op jit(solution)/shard_map/pallas_call | solution.py:97
  337.3 2.0 fusion.25.screened_ref
  339.3 12.5 %shard_map.119 = (bf16[32,64,256]{2,1,0:T(8,128)(2,1)}, bf16[32,64,256]{2,1,0:T(8,128)(2,1)}, bf16[32,64,256]{2,1,0:T(8,128)(2,1)}, bf16[32,64,256]{2,1,0:T(8,128)(2,1)}) custom-call(s32[2,2]{1,0:T(2,128)} %get-tuple-element.111.places_ref, s32[16,8]{1,0:T(8,128)} %copy.42.mask_ref, bf16[1024,256]{1,0:T(8,128)(2,1)} %fusion.25.screened_ref, ...), custom_call_target="tpu_custom_call" | custom-call | tf_op jit(solution)/shard_map/pallas_call | solution.py:184
  351.8 1.6 collective-permute-start.33
  353.5 5.3 %collective-permute-done.32 = bf16[1024,512]{1,0:T(8,128)(2,1)S(1)} collective-permute-done((bf16[1024,512]{1,0:T(8,128)(2,1)}, bf16[1024,512]{1,0:T(8,128)(2,1)S(1)}, u32[]{:S(2)}, u32[]{:S(2)}) %collective-permute-start.32) | collective-permute-done | bytes 1048608 | tf_op jit(solution)/shard_map/ppermute | solution.py:20
  359.2 1.6 collective-permute-start.35
  362.3 13.6 %shard_map.120 = f32[1024,512]{1,0:T(8,128)} custom-call(s32[4]{0:T(128)} %fusion.40.order_ref, bf16[512,1664]{1,0:T(8,128)(2,1)} %copy-done.3, bf16[512,1664]{1,0:T(8,128)(2,1)} %copy-done.2, bf16[512,1664]{1,0:T(8,128)(2,1)} %collective-permute-done.23.refs_2_, bf16[512,1664]{1,0:T(8,128)(2,1)} %collective-permute-done.24.refs_3_, ...), custom_call_target="tpu_custom_call" | custom-call | tf_op jit(solution)/shard_map/pallas_call | solution.py:97
  375.9 12.7 %shard_map.121 = (bf16[32,64,256]{2,1,0:T(8,128)(2,1)}, bf16[32,64,256]{2,1,0:T(8,128)(2,1)}, bf16[32,64,256]{2,1,0:T(8,128)(2,1)}, bf16[32,64,256]{2,1,0:T(8,128)(2,1)}) custom-call(s32[2,2]{1,0:T(2,128)} %get-tuple-element.120.places_ref, s32[16,8]{1,0:T(8,128)} %copy.42.mask_ref, bf16[1024,256]{1,0:T(8,128)(2,1)} %fusion.25.screened_ref, ...), custom_call_target="tpu_custom_call" | custom-call | tf_op jit(solution)/shard_map/pallas_call | solution.py:184
  392.0 19.4 %collective-permute-done.34 = bf16[1024,256]{1,0:T(8,128)(2,1)S(1)} collective-permute-done((bf16[1024,256]{1,0:T(8,128)(2,1)S(1)}, bf16[1024,256]{1,0:T(8,128)(2,1)S(1)}, u32[]{:S(2)}, u32[]{:S(2)}) %collective-permute-start.34) | collective-permute-done | bytes 524320 | tf_op jit(solution)/shard_map/ppermute | solution.py:20
  412.5 12.5 %shard_map.122 = (bf16[32,64,256]{2,1,0:T(8,128)(2,1)}, bf16[32,64,256]{2,1,0:T(8,128)(2,1)}, bf16[32,64,256]{2,1,0:T(8,128)(2,1)}, bf16[32,64,256]{2,1,0:T(8,128)(2,1)}) custom-call(s32[2,2]{1,0:T(2,128)} %get-tuple-element.111.places_ref, s32[16,8]{1,0:T(8,128)} %copy.42.mask_ref, bf16[1024,256]{1,0:T(8,128)(2,1)} %fusion.24.screened_ref, ...), custom_call_target="tpu_custom_call" | custom-call | tf_op jit(solution)/shard_map/pallas_call | solution.py:184
  426.2 2.8 fusion.42
  429.0 12.5 %shard_map.123 = (bf16[32,64,256]{2,1,0:T(8,128)(2,1)}, bf16[32,64,256]{2,1,0:T(8,128)(2,1)}, bf16[32,64,256]{2,1,0:T(8,128)(2,1)}, bf16[32,64,256]{2,1,0:T(8,128)(2,1)}) custom-call(s32[2,2]{1,0:T(2,128)} %get-tuple-element.120.places_ref, s32[16,8]{1,0:T(8,128)} %copy.42.mask_ref, bf16[1024,256]{1,0:T(8,128)(2,1)} %fusion.24.screened_ref, ...), custom_call_target="tpu_custom_call" | custom-call | tf_op jit(solution)/shard_map/pallas_call | solution.py:184
  441.5 1.5 collective-permute-start.40
  444.6 2.5 add_convert_fusion.9
  447.1 4.4 collective-permute-done.41
  451.5 1.6 add_convert_fusion.4
  454.1 2.6 add_convert_fusion.6
  457.8 3.5 fusion.12
  461.2 3.5 fusion.15
  464.7 9.2 %collective-permute-done.40 = bf16[32,64,256]{2,1,0:T(8,128)(2,1)S(1)} collective-permute-done((bf16[32,64,256]{2,1,0:T(8,128)(2,1)}, bf16[32,64,256]{2,1,0:T(8,128)(2,1)S(1)}, u32[]{:S(2)}, u32[]{:S(2)}) %collective-permute-start.40) | collective-permute-done | bytes 1048608 | tf_op jit(solution)/shard_map/ppermute | solution.py:20
  473.9 19.7 %collective-permute-done.43 = bf16[32,64,256]{2,1,0:T(8,128)(2,1)S(1)} collective-permute-done((bf16[32,64,256]{2,1,0:T(8,128)(2,1)S(1)}, bf16[32,64,256]{2,1,0:T(8,128)(2,1)S(1)}, u32[]{:S(2)}, u32[]{:S(2)}) %collective-permute-start.43) | collective-permute-done | bytes 1048608 | tf_op jit(solution)/shard_map/ppermute | solution.py:20
  494.2 3.5 fusion.18
  498.4 3.5 fusion.21
  502.5 3.2 collective-permute-done.46
  505.8 1.6 collective-permute-start.47
  507.4 3.5 maximum_bitcast_fusion
  511.1 4.5 collective-permute-done.48
  515.8 3.6 collective-permute-start.49
  519.4 1.6 collective-permute-done.49
  (180 shorter events, 43.5 us)
Async XLA Ops:
  0.6 202.7 %copy-start = (bf16[256,256]{1,0:T(8,128)(2,1)S(1)}, bf16[256,256]{1,0:T(8,128)(2,1)}, u32[]{:S(2)}) copy-start(bf16[256,256]{1,0:T(8,128)(2,1)} %param.13) | copy-start | bytes 393220
  5.9 233.1 %copy-start.3 = (bf16[512,1664]{1,0:T(8,128)(2,1)}, bf16[512,1664]{1,0:T(8,128)(2,1)S(1)}, u32[]{:S(2)}) copy-start(bf16[512,1664]{1,0:T(8,128)(2,1)S(1)} %get-tuple-element.146.refs_0_) | copy-start | bytes 5111812
  5.9 233.6 %copy-start.2 = (bf16[512,1664]{1,0:T(8,128)(2,1)}, bf16[512,1664]{1,0:T(8,128)(2,1)S(1)}, u32[]{:S(2)}) copy-start(bf16[512,1664]{1,0:T(8,128)(2,1)S(1)} %get-tuple-element.80.refs_1_) | copy-start | bytes 5111812
  6.0 40.3 %collective-permute-start.2 = (bf16[512,1664]{1,0:T(8,128)(2,1)S(1)}, bf16[512,1664]{1,0:T(8,128)(2,1)}, u32[]{:S(2)}, u32[]{:S(2)}) collective-permute-start(bf16[512,1664]{1,0:T(8,128)(2,1)S(1)} %get-tuple-element.146.refs_0_), channel_id=1, source_target_pairs={{0,2},{1,3},{2,0},{3,1},{4,6},{5,7},{6,4},{7,5},{8,10},{9,11},{10,... | collective-permute-start | bytes 5111816 | tf_op jit(solution)/shard_map/ppermute | solution.py:20
  16.0 20.5 %collective-permute-start = (bf16[2,1664,128]{2,1,0:T(8,128)(2,1)S(1)}, bf16[2,1664,128]{2,1,0:T(8,128)(2,1)}, u32[]{:S(2)}, u32[]{:S(2)}) collective-permute-start(bf16[2,1664,128]{2,1,0:T(8,128)(2,1)S(1)} %get-tuple-element.163), channel_id=1, source_target_pairs={{0,16},{8,24},{16,0},{24,8},{1,17},{9,25},{17,1},{25,9},{2,18},{10... | collective-permute-start | bytes 2555912 | tf_op jit(solution)/shard_map/ppermute | solution.py:20
  36.5 40.5 %collective-permute-start.1 = (bf16[512,1664]{1,0:T(8,128)(2,1)}, bf16[512,1664]{1,0:T(8,128)(2,1)}, u32[]{:S(2)}, u32[]{:S(2)}) collective-permute-start(bf16[512,1664]{1,0:T(8,128)(2,1)} %get-tuple-element.74), channel_id=1, source_target_pairs={{0,16},{8,24},{16,0},{24,8},{1,17},{9,25},{17,1},{25,9},{2,18},{10... | collective-permute-start | bytes 5111816 | tf_op jit(solution)/shard_map/ppermute | solution.py:20
  46.3 62.9 %collective-permute-start.5 = (bf16[512,1664]{1,0:T(8,128)(2,1)S(1)}, bf16[512,1664]{1,0:T(8,128)(2,1)}, u32[]{:S(2)}, u32[]{:S(2)}) collective-permute-start(bf16[512,1664]{1,0:T(8,128)(2,1)S(1)} %get-tuple-element.80.refs_1_), channel_id=1, source_target_pairs={{0,2},{1,3},{2,0},{3,1},{4,6},{5,7},{6,4},{7,5},{8,10},{9,11},{10,... | collective-permute-start | bytes 5111816 | tf_op jit(solution)/shard_map/ppermute | solution.py:20
  49.6 16.6 %copy-start.7 = (bf16[2,1664,128]{2,1,0:T(8,128)(2,1)}, bf16[2,1664,128]{2,1,0:T(8,128)(2,1)S(1)}, u32[]{:S(2)}) copy-start(bf16[2,1664,128]{2,1,0:T(8,128)(2,1)S(1)} %get-tuple-element.157.refs_8_) | copy-start | bytes 2555908
  49.6 52.3 %collective-permute-start.6 = (bf16[2,1664,128]{2,1,0:T(8,128)(2,1)S(1)}, bf16[2,1664,128]{2,1,0:T(8,128)(2,1)S(1)}, u32[]{:S(2)}, u32[]{:S(2)}) collective-permute-start(bf16[2,1664,128]{2,1,0:T(8,128)(2,1)S(1)} %get-tuple-element.158), channel_id=1, source_target_pairs={{0,4},{1,5},{2,6},{3,7},{4,0},{5,1},{6,2},{7,3},{8,12},{9,13},{10,... | collective-permute-start | bytes 2555912 | tf_op jit(solution)/shard_map/ppermute | solution.py:20
  52.2 51.1 %collective-permute-start.4 = (bf16[2,1664,128]{2,1,0:T(8,128)(2,1)S(1)}, bf16[2,1664,128]{2,1,0:T(8,128)(2,1)}, u32[]{:S(2)}, u32[]{:S(2)}) collective-permute-start(bf16[2,1664,128]{2,1,0:T(8,128)(2,1)S(1)} %copy-done.33), channel_id=1, source_target_pairs={{0,16},{8,24},{16,0},{24,8},{1,17},{9,25},{17,1},{25,9},{2,18},{10... | collective-permute-start | bytes 2555912 | tf_op jit(solution)/shard_map/ppermute | solution.py:20
  53.7 55.4 %collective-permute-start.7 = (bf16[2,1664,128]{2,1,0:T(8,128)(2,1)S(1)}, bf16[2,1664,128]{2,1,0:T(8,128)(2,1)S(1)}, u32[]{:S(2)}, u32[]{:S(2)}) collective-permute-start(bf16[2,1664,128]{2,1,0:T(8,128)(2,1)S(1)} %get-tuple-element.157.refs_8_), channel_id=1, source_target_pairs={{0,8},{8,0},{16,24},{24,16},{1,9},{9,1},{17,25},{25,17},{2,10},{10... | collective-permute-start | bytes 2555912 | tf_op jit(solution)/shard_map/ppermute | solution.py:20
  76.9 89.4 %collective-permute-start.3 = (bf16[512,1664]{1,0:T(8,128)(2,1)}, bf16[512,1664]{1,0:T(8,128)(2,1)}, u32[]{:S(2)}, u32[]{:S(2)}) collective-permute-start(bf16[512,1664]{1,0:T(8,128)(2,1)} %get-tuple-element.76), channel_id=1, source_target_pairs={{0,16},{8,24},{16,0},{24,8},{1,17},{9,25},{17,1},{25,9},{2,18},{10... | collective-permute-start | bytes 5111816 | tf_op jit(solution)/shard_map/ppermute | solution.py:20
  101.9 18.3 %copy-start.16 = (bf16[2,1664,128]{2,1,0:T(8,128)(2,1)}, bf16[2,1664,128]{2,1,0:T(8,128)(2,1)S(1)}, u32[]{:S(2)}) copy-start(bf16[2,1664,128]{2,1,0:T(8,128)(2,1)S(1)} %collective-permute-done.6.refs_10_) | copy-start | bytes 2555908
  101.9 19.8 %collective-permute-start.13 = (bf16[2,1664,128]{2,1,0:T(8,128)(2,1)S(1)}, bf16[2,1664,128]{2,1,0:T(8,128)(2,1)S(1)}, u32[]{:S(2)}, u32[]{:S(2)}) collective-permute-start(bf16[2,1664,128]{2,1,0:T(8,128)(2,1)S(1)} %collective-permute-done.6.refs_10_), channel_id=1, source_target_pairs={{0,8},{8,0},{16,24},{24,16},{1,9},{9,1},{17,25},{25,17},{2,10},{10... | collective-permute-start | bytes 2555912 | tf_op jit(solution)/shard_map/ppermute | solution.py:20
  105.8 38.7 %collective-permute-start.12 = (bf16[2,1664,128]{2,1,0:T(8,128)(2,1)S(1)}, bf16[2,1664,128]{2,1,0:T(8,128)(2,1)}, u32[]{:S(2)}, u32[]{:S(2)}) collective-permute-start(bf16[2,1664,128]{2,1,0:T(8,128)(2,1)S(1)} %get-tuple-element.88), channel_id=1, source_target_pairs={{0,4},{1,5},{2,6},{3,7},{4,0},{5,1},{6,2},{7,3},{8,12},{9,13},{10,... | collective-permute-start | bytes 2555912 | tf_op jit(solution)/shard_map/ppermute | solution.py:20
  109.2 66.0 %collective-permute-start.11 = (bf16[512,1664]{1,0:T(8,128)(2,1)}, bf16[512,1664]{1,0:T(8,128)(2,1)}, u32[]{:S(2)}, u32[]{:S(2)}) collective-permute-start(bf16[512,1664]{1,0:T(8,128)(2,1)} %collective-permute-done.1.refs_0_), channel_id=1, source_target_pairs={{0,2},{1,3},{2,0},{3,1},{4,6},{5,7},{6,4},{7,5},{8,10},{9,11},{10,... | collective-permute-start | bytes 5111816 | tf_op jit(solution)/shard_map/ppermute | solution.py:20
  120.2 51.8 %collective-permute-start.15 = (bf16[2,1664,128]{2,1,0:T(8,128)(2,1)}, bf16[2,1664,128]{2,1,0:T(8,128)(2,1)}, u32[]{:S(2)}, u32[]{:S(2)}) collective-permute-start(bf16[2,1664,128]{2,1,0:T(8,128)(2,1)} %get-tuple-element.90), channel_id=1, source_target_pairs={{0,16},{8,24},{16,0},{24,8},{1,17},{9,25},{17,1},{25,9},{2,18},{10... | collective-permute-start | bytes 2555912 | tf_op jit(solution)/shard_map/ppermute | solution.py:20
  121.7 34.0 %copy-start.18 = (bf16[2,1664,128]{2,1,0:T(8,128)(2,1)}, bf16[2,1664,128]{2,1,0:T(8,128)(2,1)S(1)}, u32[]{:S(2)}) copy-start(bf16[2,1664,128]{2,1,0:T(8,128)(2,1)S(1)} %collective-permute-done.13.refs_14_) | copy-start | bytes 2555908
  121.7 51.9 %collective-permute-start.17 = (bf16[2,1664,128]{2,1,0:T(8,128)(2,1)}, bf16[2,1664,128]{2,1,0:T(8,128)(2,1)}, u32[]{:S(2)}, u32[]{:S(2)}) collective-permute-start(bf16[2,1664,128]{2,1,0:T(8,128)(2,1)} %get-tuple-element.94.refs_9_), channel_id=1, source_target_pairs={{0,8},{8,0},{16,24},{24,16},{1,9},{9,1},{17,25},{25,17},{2,10},{10... | collective-permute-start | bytes 2555912 | tf_op jit(solution)/shard_map/ppermute | solution.py:20
  144.5 29.1 %collective-permute-start.16 = (bf16[2,1664,128]{2,1,0:T(8,128)(2,1)}, bf16[2,1664,128]{2,1,0:T(8,128)(2,1)}, u32[]{:S(2)}, u32[]{:S(2)}) collective-permute-start(bf16[2,1664,128]{2,1,0:T(8,128)(2,1)} %collective-permute-done.12.refs_11_), channel_id=1, source_target_pairs={{0,8},{8,0},{16,24},{24,16},{1,9},{9,1},{17,25},{25,17},{2,10},{10... | collective-permute-start | bytes 2555912 | tf_op jit(solution)/shard_map/ppermute | solution.py:20
  166.4 18.6 %collective-permute-start.8 = (bf16[2,1664,128]{2,1,0:T(8,128)(2,1)}, bf16[2,1664,128]{2,1,0:T(8,128)(2,1)}, u32[]{:S(2)}, u32[]{:S(2)}) collective-permute-start(bf16[2,1664,128]{2,1,0:T(8,128)(2,1)} %get-tuple-element.84), channel_id=1, source_target_pairs={{0,16},{8,24},{16,0},{24,8},{1,17},{9,25},{17,1},{25,9},{2,18},{10... | collective-permute-start | bytes 2555912 | tf_op jit(solution)/shard_map/ppermute | solution.py:20
  172.0 67.6 %collective-permute-start.9 = (bf16[512,1664]{1,0:T(8,128)(2,1)}, bf16[512,1664]{1,0:T(8,128)(2,1)S(1)}, u32[]{:S(2)}, u32[]{:S(2)}) collective-permute-start(bf16[512,1664]{1,0:T(8,128)(2,1)} %collective-permute-done.1.refs_0_), channel_id=1, source_target_pairs={{0,1},{1,0},{2,3},{3,2},{4,5},{5,4},{6,7},{7,6},{8,9},{9,8},{10,11... | collective-permute-start | bytes 5111816 | tf_op jit(solution)/shard_map/ppermute | solution.py:20
  173.5 25.9 %copy-start.8 = (bf16[2,1664,128]{2,1,0:T(8,128)(2,1)}, bf16[2,1664,128]{2,1,0:T(8,128)(2,1)S(1)}, u32[]{:S(2)}) copy-start(bf16[2,1664,128]{2,1,0:T(8,128)(2,1)S(1)} %get-tuple-element.95.refs_8_) | copy-start | bytes 2555908
  173.6 49.0 %collective-permute-start.20 = (bf16[2,1664,128]{2,1,0:T(8,128)(2,1)S(1)}, bf16[2,1664,128]{2,1,0:T(8,128)(2,1)}, u32[]{:S(2)}, u32[]{:S(2)}) collective-permute-start(bf16[2,1664,128]{2,1,0:T(8,128)(2,1)S(1)} %get-tuple-element.100), channel_id=1, source_target_pairs={{0,4},{1,5},{2,6},{3,7},{4,0},{5,1},{6,2},{7,3},{8,12},{9,13},{10,... | collective-permute-start | bytes 2555912 | tf_op jit(solution)/shard_map/ppermute | solution.py:20
  173.7 28.2 %collective-permute-start.18 = (bf16[2,1664,128]{2,1,0:T(8,128)(2,1)S(1)}, bf16[2,1664,128]{2,1,0:T(8,128)(2,1)S(1)}, u32[]{:S(2)}, u32[]{:S(2)}) collective-permute-start(bf16[2,1664,128]{2,1,0:T(8,128)(2,1)S(1)} %get-tuple-element.95.refs_8_), channel_id=1, source_target_pairs={{0,8},{8,0},{16,24},{24,16},{1,9},{9,1},{17,25},{25,17},{2,10},{10... | collective-permute-start | bytes 2555912 | tf_op jit(solution)/shard_map/ppermute | solution.py:20
  175.2 65.7 %collective-permute-start.10 = (bf16[512,1664]{1,0:T(8,128)(2,1)}, bf16[512,1664]{1,0:T(8,128)(2,1)}, u32[]{:S(2)}, u32[]{:S(2)}) collective-permute-start(bf16[512,1664]{1,0:T(8,128)(2,1)} %collective-permute-done.3.refs_1_), channel_id=1, source_target_pairs={{0,1},{1,0},{2,3},{3,2},{4,5},{5,4},{6,7},{7,6},{8,9},{9,8},{10,11... | collective-permute-start | bytes 5111816 | tf_op jit(solution)/shard_map/ppermute | solution.py:20
  184.9 54.1 %collective-permute-start.14 = (bf16[512,1664]{1,0:T(8,128)(2,1)}, bf16[512,1664]{1,0:T(8,128)(2,1)S(1)}, u32[]{:S(2)}, u32[]{:S(2)}) collective-permute-start(bf16[512,1664]{1,0:T(8,128)(2,1)} %collective-permute-done.3.refs_1_), channel_id=1, source_target_pairs={{0,2},{1,3},{2,0},{3,1},{4,6},{5,7},{6,4},{7,5},{8,10},{9,11},{10,... | collective-permute-start | bytes 5111816 | tf_op jit(solution)/shard_map/ppermute | solution.py:20
  201.8 20.7 %copy-start.9 = (bf16[2,1664,128]{2,1,0:T(8,128)(2,1)}, bf16[2,1664,128]{2,1,0:T(8,128)(2,1)S(1)}, u32[]{:S(2)}) copy-start(bf16[2,1664,128]{2,1,0:T(8,128)(2,1)S(1)} %get-tuple-element.99.refs_9_) | copy-start | bytes 2555908
  201.8 20.7 %copy-start.19 = (bf16[2,1664,128]{2,1,0:T(8,128)(2,1)}, bf16[2,1664,128]{2,1,0:T(8,128)(2,1)S(1)}, u32[]{:S(2)}) copy-start(bf16[2,1664,128]{2,1,0:T(8,128)(2,1)S(1)} %collective-permute-done.18.refs_12_) | copy-start | bytes 2555908
  201.8 20.8 %collective-permute-start.19 = (bf16[2,1664,128]{2,1,0:T(8,128)(2,1)S(1)}, bf16[2,1664,128]{2,1,0:T(8,128)(2,1)S(1)}, u32[]{:S(2)}, u32[]{:S(2)}) collective-permute-start(bf16[2,1664,128]{2,1,0:T(8,128)(2,1)S(1)} %get-tuple-element.99.refs_9_), channel_id=1, source_target_pairs={{0,8},{8,0},{16,24},{24,16},{1,9},{9,1},{17,25},{25,17},{2,10},{10... | collective-permute-start | bytes 2555912 | tf_op jit(solution)/shard_map/ppermute | solution.py:20
  222.5 21.2 %collective-permute-start.21 = (bf16[512,1664]{1,0:T(8,128)(2,1)}, bf16[512,1664]{1,0:T(8,128)(2,1)S(1)}, u32[]{:S(2)}, u32[]{:S(2)}) collective-permute-start(bf16[512,1664]{1,0:T(8,128)(2,1)} %collective-permute-done.11.refs_4_), channel_id=1, source_target_pairs={{0,1},{1,0},{2,3},{3,2},{4,5},{5,4},{6,7},{7,6},{8,9},{9,8},{10,11... | collective-permute-start | bytes 5111816 | tf_op jit(solution)/shard_map/ppermute | solution.py:20
  239.0 5.3 %collective-permute-start.22 = (bf16[512,1664]{1,0:T(8,128)(2,1)S(1)}, bf16[512,1664]{1,0:T(8,128)(2,1)S(1)}, u32[]{:S(2)}, u32[]{:S(2)}) collective-permute-start(bf16[512,1664]{1,0:T(8,128)(2,1)S(1)} %collective-permute-done.14.refs_5_), channel_id=1, source_target_pairs={{0,1},{1,0},{2,3},{3,2},{4,5},{5,4},{6,7},{7,6},{8,9},{9,8},{10,11... | collective-permute-start | bytes 5111816 | tf_op jit(solution)/shard_map/ppermute | solution.py:20
  239.1 43.8 %collective-permute-start.23 = (bf16[512,1664]{1,0:T(8,128)(2,1)S(1)}, bf16[512,1664]{1,0:T(8,128)(2,1)}, u32[]{:S(2)}, u32[]{:S(2)}) collective-permute-start(bf16[512,1664]{1,0:T(8,128)(2,1)S(1)} %get-tuple-element.146.refs_0_), channel_id=1, source_target_pairs={{0,1},{1,0},{2,3},{3,2},{4,5},{5,4},{6,7},{7,6},{8,9},{9,8},{10,11... | collective-permute-start | bytes 5111816 | tf_op jit(solution)/shard_map/ppermute | solution.py:20
  239.6 44.7 %collective-permute-start.24 = (bf16[512,1664]{1,0:T(8,128)(2,1)S(1)}, bf16[512,1664]{1,0:T(8,128)(2,1)}, u32[]{:S(2)}, u32[]{:S(2)}) collective-permute-start(bf16[512,1664]{1,0:T(8,128)(2,1)S(1)} %get-tuple-element.80.refs_1_), channel_id=1, source_target_pairs={{0,1},{1,0},{2,3},{3,2},{4,5},{5,4},{6,7},{7,6},{8,9},{9,8},{10,11... | collective-permute-start | bytes 5111816 | tf_op jit(solution)/shard_map/ppermute | solution.py:20
  240.9 40.4 %collective-permute-start.27 = (bf16[2,1664,128]{2,1,0:T(8,128)(2,1)}, bf16[2,1664,128]{2,1,0:T(8,128)(2,1)}, u32[]{:S(2)}, u32[]{:S(2)}) collective-permute-start(bf16[2,1664,128]{2,1,0:T(8,128)(2,1)} %get-tuple-element.103), channel_id=1, source_target_pairs={{0,4},{1,5},{2,6},{3,7},{4,0},{5,1},{6,2},{7,3},{8,12},{9,13},{10,... | collective-permute-start | bytes 2555912 | tf_op jit(solution)/shard_map/ppermute | solution.py:20
  243.7 41.2 %collective-permute-start.25 = (bf16[512,1664]{1,0:T(8,128)(2,1)}, bf16[512,1664]{1,0:T(8,128)(2,1)}, u32[]{:S(2)}, u32[]{:S(2)}) collective-permute-start(bf16[512,1664]{1,0:T(8,128)(2,1)} %collective-permute-done.2.refs_4_), channel_id=1, source_target_pairs={{0,1},{1,0},{2,3},{3,2},{4,5},{5,4},{6,7},{7,6},{8,9},{9,8},{10,11... | collective-permute-start | bytes 5111816 | tf_op jit(solution)/shard_map/ppermute | solution.py:20
  246.1 38.8 %collective-permute-start.26 = (bf16[512,1664]{1,0:T(8,128)(2,1)}, bf16[512,1664]{1,0:T(8,128)(2,1)}, u32[]{:S(2)}, u32[]{:S(2)}) collective-permute-start(bf16[512,1664]{1,0:T(8,128)(2,1)} %collective-permute-done.5.refs_5_), channel_id=1, source_target_pairs={{0,1},{1,0},{2,3},{3,2},{4,5},{5,4},{6,7},{7,6},{8,9},{9,8},{10,11... | collective-permute-start | bytes 5111816 | tf_op jit(solution)/shard_map/ppermute | solution.py:20
  281.3 24.5 %collective-permute-start.28 = (bf16[1024,512]{1,0:T(8,128)(2,1)}, bf16[1024,512]{1,0:T(8,128)(2,1)S(1)}, u32[]{:S(2)}, u32[]{:S(2)}) collective-permute-start(bf16[1024,512]{1,0:T(8,128)(2,1)} %shard_map.116), channel_id=1, source_target_pairs={{0,16},{8,24},{16,0},{24,8},{1,17},{9,25},{17,1},{25,9},{2,18},{10... | collective-permute-start | bytes 3145736 | tf_op jit(solution)/shard_map/ppermute | solution.py:20
  282.9 25.8 %collective-permute-start.31 = (bf16[2,1664,128]{2,1,0:T(8,128)(2,1)}, bf16[2,1664,128]{2,1,0:T(8,128)(2,1)S(1)}, u32[]{:S(2)}, u32[]{:S(2)}) collective-permute-start(bf16[2,1664,128]{2,1,0:T(8,128)(2,1)} %collective-permute-done.27.refs_11_), channel_id=1, source_target_pairs={{0,8},{8,0},{16,24},{24,16},{1,9},{9,1},{17,25},{25,17},{2,10},{10... | collective-permute-start | bytes 2555912 | tf_op jit(solution)/shard_map/ppermute | solution.py:20
  284.3 36.9 %collective-permute-start.30 = (bf16[2,1664,128]{2,1,0:T(8,128)(2,1)}, bf16[2,1664,128]{2,1,0:T(8,128)(2,1)S(1)}, u32[]{:S(2)}, u32[]{:S(2)}) collective-permute-start(bf16[2,1664,128]{2,1,0:T(8,128)(2,1)} %collective-permute-done.20.refs_10_), channel_id=1, source_target_pairs={{0,8},{8,0},{16,24},{24,16},{1,9},{9,1},{17,25},{25,17},{2,10},{10... | collective-permute-start | bytes 2555912 | tf_op jit(solution)/shard_map/ppermute | solution.py:20
  308.7 27.2 %copy-start.34 = (s32[64,8]{0,1:T(8,128)S(1)}, s32[64,8]{0,1:T(8,128)}, u32[]{:S(2)}) copy-start(s32[64,8]{0,1:T(8,128)} %param.14) | copy-start | bytes 6148
  308.7 28.0 %copy-start.36 = (s32[2,2]{1,0:T(2,128)S(1)}, s32[2,2]{1,0:T(2,128)}, u32[]{:S(2)}) copy-start(s32[2,2]{1,0:T(2,128)} %constant.176.clone) | copy-start | bytes 52
  308.7 28.0 %copy-start.37 = (s32[2]{0:T(128)S(1)}, s32[2]{0:T(128)}, u32[]{:S(2)}) copy-start(s32[2]{0:T(128)} %constant.178) | copy-start | bytes 28
  308.7 28.6 %collective-permute-start.29 = (bf16[1024,256]{1,0:T(8,128)(2,1)}, bf16[1024,256]{1,0:T(8,128)(2,1)}, u32[]{:S(2)}, u32[]{:S(2)}) collective-permute-start(bf16[1024,256]{1,0:T(8,128)(2,1)} %slice.85), channel_id=1, source_target_pairs={{0,4},{1,5},{2,6},{3,7},{4,0},{5,1},{6,2},{7,3},{8,12},{9,13},{10,... | collective-permute-start | bytes 1572872 | tf_op jit(solution)/shard_map/ppermute | solution.py:20
  335.3 23.4 %collective-permute-start.32 = (bf16[1024,512]{1,0:T(8,128)(2,1)}, bf16[1024,512]{1,0:T(8,128)(2,1)S(1)}, u32[]{:S(2)}, u32[]{:S(2)}) collective-permute-start(bf16[1024,512]{1,0:T(8,128)(2,1)} %shard_map.118), channel_id=1, source_target_pairs={{0,16},{8,24},{16,0},{24,8},{1,17},{9,25},{17,1},{25,9},{2,18},{10... | collective-permute-start | bytes 3145736 | tf_op jit(solution)/shard_map/ppermute | solution.py:20
  351.8 36.8 %collective-permute-start.33 = (bf16[32,64,256]{2,1,0:T(8,128)(2,1)}, bf16[32,64,256]{2,1,0:T(8,128)(2,1)S(1)}, u32[]{:S(2)}, u32[]{:S(2)}) collective-permute-start(bf16[32,64,256]{2,1,0:T(8,128)(2,1)} %get-tuple-element.113), channel_id=1, source_target_pairs={{0,8},{8,0},{16,24},{24,16},{1,9},{9,1},{17,25},{25,17},{2,10},{10... | collective-permute-start | bytes 3145736 | tf_op jit(solution)/shard_map/ppermute | solution.py:20
  358.7 30.4 %collective-permute-start.36 = (bf16[32,64,256]{2,1,0:T(8,128)(2,1)}, bf16[32,64,256]{2,1,0:T(8,128)(2,1)S(1)}, u32[]{:S(2)}, u32[]{:S(2)}) collective-permute-start(bf16[32,64,256]{2,1,0:T(8,128)(2,1)} %get-tuple-element.119), channel_id=1, source_target_pairs={{0,16},{8,24},{16,0},{24,8},{1,17},{9,25},{17,1},{25,9},{2,18},{10... | collective-permute-start | bytes 3145736 | tf_op jit(solution)/shard_map/ppermute | solution.py:20
  359.2 65.8 %collective-permute-start.35 = (bf16[32,64,256]{2,1,0:T(8,128)(2,1)}, bf16[32,64,256]{2,1,0:T(8,128)(2,1)}, u32[]{:S(2)}, u32[]{:S(2)}) collective-permute-start(bf16[32,64,256]{2,1,0:T(8,128)(2,1)} %get-tuple-element.112), channel_id=1, source_target_pairs={{0,8},{8,0},{16,24},{24,16},{1,9},{9,1},{17,25},{25,17},{2,10},{10... | collective-permute-start | bytes 3145736 | tf_op jit(solution)/shard_map/ppermute | solution.py:20
  360.8 64.8 %collective-permute-start.38 = (bf16[32,64,256]{2,1,0:T(8,128)(2,1)}, bf16[32,64,256]{2,1,0:T(8,128)(2,1)}, u32[]{:S(2)}, u32[]{:S(2)}) collective-permute-start(bf16[32,64,256]{2,1,0:T(8,128)(2,1)} %get-tuple-element.118), channel_id=1, source_target_pairs={{0,16},{8,24},{16,0},{24,8},{1,17},{9,25},{17,1},{25,9},{2,18},{10... | collective-permute-start | bytes 3145736 | tf_op jit(solution)/shard_map/ppermute | solution.py:20
  389.1 22.3 %collective-permute-start.34 = (bf16[1024,256]{1,0:T(8,128)(2,1)S(1)}, bf16[1024,256]{1,0:T(8,128)(2,1)S(1)}, u32[]{:S(2)}, u32[]{:S(2)}) collective-permute-start(bf16[1024,256]{1,0:T(8,128)(2,1)S(1)} %slice.84), channel_id=1, source_target_pairs={{0,4},{1,5},{2,6},{3,7},{4,0},{5,1},{6,2},{7,3},{8,12},{9,13},{10,... | collective-permute-start | bytes 1572872 | tf_op jit(solution)/shard_map/ppermute | solution.py:20
  390.3 51.3 %collective-permute-start.39 = (bf16[32,64,256]{2,1,0:T(8,128)(2,1)S(1)}, bf16[32,64,256]{2,1,0:T(8,128)(2,1)}, u32[]{:S(2)}, u32[]{:S(2)}) collective-permute-start(bf16[32,64,256]{2,1,0:T(8,128)(2,1)S(1)} %add_convert_fusion.7), channel_id=1, source_target_pairs={{0,8},{8,0},{16,24},{24,16},{1,9},{9,1},{17,25},{25,17},{2,10},{10... | collective-permute-start | bytes 3145736 | tf_op jit(solution)/shard_map/ppermute | solution.py:20
  391.5 51.6 %collective-permute-start.37 = (bf16[32,64,256]{2,1,0:T(8,128)(2,1)S(1)}, bf16[32,64,256]{2,1,0:T(8,128)(2,1)}, u32[]{:S(2)}, u32[]{:S(2)}) collective-permute-start(bf16[32,64,256]{2,1,0:T(8,128)(2,1)S(1)} %add_convert_fusion.10), channel_id=1, source_target_pairs={{0,16},{8,24},{16,0},{24,8},{1,17},{9,25},{17,1},{25,9},{2,18},{10... | collective-permute-start | bytes 3145736 | tf_op jit(solution)/shard_map/ppermute | solution.py:20
  425.0 26.5 %collective-permute-start.41 = (bf16[32,64,256]{2,1,0:T(8,128)(2,1)}, bf16[32,64,256]{2,1,0:T(8,128)(2,1)}, u32[]{:S(2)}, u32[]{:S(2)}) collective-permute-start(bf16[32,64,256]{2,1,0:T(8,128)(2,1)} %get-tuple-element.135), channel_id=1, source_target_pairs={{0,8},{8,0},{16,24},{24,16},{1,9},{9,1},{17,25},{25,17},{2,10},{10... | collective-permute-start | bytes 3145736 | tf_op jit(solution)/shard_map/ppermute | solution.py:20
  425.7 27.4 %collective-permute-start.42 = (bf16[32,64,256]{2,1,0:T(8,128)(2,1)}, bf16[32,64,256]{2,1,0:T(8,128)(2,1)S(1)}, u32[]{:S(2)}, u32[]{:S(2)}) collective-permute-start(bf16[32,64,256]{2,1,0:T(8,128)(2,1)} %get-tuple-element.136), channel_id=1, source_target_pairs={{0,16},{8,24},{16,0},{24,8},{1,17},{9,25},{17,1},{25,9},{2,18},{10... | collective-permute-start | bytes 3145736 | tf_op jit(solution)/shard_map/ppermute | solution.py:20
  441.5 32.3 %collective-permute-start.40 = (bf16[32,64,256]{2,1,0:T(8,128)(2,1)}, bf16[32,64,256]{2,1,0:T(8,128)(2,1)S(1)}, u32[]{:S(2)}, u32[]{:S(2)}) collective-permute-start(bf16[32,64,256]{2,1,0:T(8,128)(2,1)} %get-tuple-element.133), channel_id=1, source_target_pairs={{0,8},{8,0},{16,24},{24,16},{1,9},{9,1},{17,25},{25,17},{2,10},{10... | collective-permute-start | bytes 3145736 | tf_op jit(solution)/shard_map/ppermute | solution.py:20
  443.1 54.6 %collective-permute-start.44 = (bf16[32,64,256]{2,1,0:T(8,128)(2,1)}, bf16[32,64,256]{2,1,0:T(8,128)(2,1)S(1)}, u32[]{:S(2)}, u32[]{:S(2)}) collective-permute-start(bf16[32,64,256]{2,1,0:T(8,128)(2,1)} %get-tuple-element.139), channel_id=1, source_target_pairs={{0,16},{8,24},{16,0},{24,8},{1,17},{9,25},{17,1},{25,9},{2,18},{10... | collective-permute-start | bytes 3145736 | tf_op jit(solution)/shard_map/ppermute | solution.py:20
  453.1 40.5 %collective-permute-start.43 = (bf16[32,64,256]{2,1,0:T(8,128)(2,1)S(1)}, bf16[32,64,256]{2,1,0:T(8,128)(2,1)S(1)}, u32[]{:S(2)}, u32[]{:S(2)}) collective-permute-start(bf16[32,64,256]{2,1,0:T(8,128)(2,1)S(1)} %add_convert_fusion.4), channel_id=1, source_target_pairs={{0,16},{8,24},{16,0},{24,8},{1,17},{9,25},{17,1},{25,9},{2,18},{10... | collective-permute-start | bytes 3145736 | tf_op jit(solution)/shard_map/ppermute | solution.py:20
  457.1 40.5 %collective-permute-start.45 = (bf16[32,64,256]{2,1,0:T(8,128)(2,1)S(1)}, bf16[32,64,256]{2,1,0:T(8,128)(2,1)S(1)}, u32[]{:S(2)}, u32[]{:S(2)}) collective-permute-start(bf16[32,64,256]{2,1,0:T(8,128)(2,1)S(1)} %add_convert_fusion.1), channel_id=1, source_target_pairs={{0,8},{8,0},{16,24},{24,16},{1,9},{9,1},{17,25},{25,17},{2,10},{10... | collective-permute-start | bytes 3145736 | tf_op jit(solution)/shard_map/ppermute | solution.py:20
  461.2 32.3 %copy-start.32 = (bf16[32,64,256]{2,1,0:T(8,128)(2,1)S(1)}, bf16[32,64,256]{2,1,0:T(8,128)(2,1)}, u32[]{:S(2)}) copy-start(bf16[32,64,256]{2,1,0:T(8,128)(2,1)} %get-tuple-element.132) | copy-start | bytes 3145732
  501.9 3.8 collective-permute-start.46
  505.8 5.1 collective-permute-start.47
  511.0 4.6 collective-permute-start.48
  515.8 5.2 collective-permute-start.49
  521.0 1.2 collective-permute-start.50
  (25 other events, 164.1 us)
